TPU v7x, 32 devices: a whole 2x2x4 slice. The times are simulated.
32 devices in a mesh: fsdp: 8 (over z, core), sp: 4 (over y, x).
Axes of the slice: x: 2, y: 2, z: 4, core: 2. Of those that a mesh axis runs over, the one named last changes fastest.
Arguments:
- layer_input: bfloat16 [8192, 2048], P(('fsdp', 'sp')), may hold values from -6 to 6
- output_grad: bfloat16 [8192, 2048], P(('fsdp', 'sp')), may hold values from -6 to 6
- w_query: bfloat16 [2048, 2048], P(('fsdp', 'sp')), may hold values from -0.125 to 0.125
- w_key: bfloat16 [2048, 2048], P(('fsdp', 'sp')), may hold values from -0.125 to 0.125
- w_value: bfloat16 [2048, 2048], P(('fsdp', 'sp')), may hold values from -0.125 to 0.125
- w_output: bfloat16 [2048, 2048], P(('fsdp', 'sp')), may hold values from -1 to 1
- w_router: bfloat16 [2048, 16], P(('fsdp', 'sp')), may hold values from -0.0625 to 0.0625
- norm_gains: bfloat16 [4, 2048], P(None, ('fsdp', 'sp')), may hold values from 0.5 to 1.5
- w_gate: bfloat16 [16, 2048, 1024], P('fsdp', 'sp'), may hold values from -0.125 to 0.125
- w_up: bfloat16 [16, 2048, 1024], P('fsdp', 'sp'), may hold values from -0.125 to 0.125
- w_down: bfloat16 [16, 1024, 2048], P('fsdp', 'sp'), may hold values from -3 to 3
- expert_routes: int32 [8192, 8], P(('fsdp', 'sp')), may hold values from 0 to 15, all different within a row; in each aligned block of 256 rows (0 to 255, 256 to 511, ...) at most 136 rows name the same one
Outputs:
- layer_out: bfloat16 [8192, 2048], P(('fsdp', 'sp'))
- input_grad: float32 [8192, 2048], P(('fsdp', 'sp'))
- grad_query: float32 [2048, 2048], P(('fsdp', 'sp'))
- grad_key: float32 [2048, 2048], P(('fsdp', 'sp'))
- grad_value: float32 [2048, 2048], P(('fsdp', 'sp'))
- grad_output: float32 [2048, 2048], P(('fsdp', 'sp'))
- grad_router: float32 [2048, 16], P(('fsdp', 'sp'))
- grad_gains: float32 [4, 2048], P(None, ('fsdp', 'sp'))
- grad_gate: float32 [16, 2048, 1024], P('fsdp', 'sp')
- grad_up: float32 [16, 2048, 1024], P('fsdp', 'sp')
- grad_down: float32 [16, 1024, 2048], P('fsdp', 'sp')
Inputs may be any that keep to these rules, and one draw needn't show every extreme that they name: `expert_routes`: among the 256 tokens of one device no expert is named more than 136 times, a bound that some block reaches; every token names 8 different experts.
All inputs are finite; a program needn't handle non-finite values.
Results may differ from a plain program's by a relative error of at most 0.02.
Values may be sent and summed in bfloat16 or wider, within the bound.
A program may use at most 320 MiB of HBM per device.

v0:
```python
import jax
import jax.numpy as jnp
from jax import lax
from jax.sharding import PartitionSpec as P

D = 2048
HEADS = 16
HEAD_DIM = 128
TOP = 8
EXP_DEV = 2
BLK = 256
TOK_DEV = 256


EPSILON = 1e-05
ROPE_BASE = 10000.0
MASKED = -1000000000.0


def rms_parts(values_in):
    inverse = lax.rsqrt(jnp.mean(values_in * values_in, axis=-1, keepdims=True) + EPSILON)
    return (values_in * inverse, inverse)


def rms_back(grad_out, normed, inverse, gain_row):
    scaled = grad_out * gain_row
    grad_in = inverse * (scaled - normed * jnp.mean(scaled * normed, axis=-1, keepdims=True))
    return (grad_in, jnp.sum(grad_out * normed, axis=0))


def angles(positions):
    freqs = ROPE_BASE ** (-2.0 * jnp.arange(HEAD_DIM // 2, dtype=jnp.float32) / HEAD_DIM)
    turned = positions.astype(jnp.float32)[:, None] * freqs[None, :]
    return (jnp.cos(turned)[:, None, :], jnp.sin(turned)[:, None, :])


def rotate(values_in, cosine_table, sine_table):
    row_count = values_in.shape[0]
    pieces = values_in.reshape(row_count, HEADS, HEAD_DIM)
    front = pieces[:, :, : HEAD_DIM // 2]
    behind = pieces[:, :, HEAD_DIM // 2 :]
    joined = jnp.concatenate(
        [front * cosine_table - behind * sine_table, behind * cosine_table + front * sine_table],
        axis=-1,
    )
    return joined.reshape(row_count, HEADS * HEAD_DIM)


def split_heads(values_in):
    row_count = values_in.shape[0]
    return values_in.reshape(row_count, HEADS, HEAD_DIM).transpose(1, 0, 2)


def merge_heads(values_in):
    row_count = values_in.shape[1]
    return values_in.transpose(1, 0, 2).reshape(row_count, HEADS * HEAD_DIM)


def body(
    layer_input,
    output_grad,
    w_query,
    w_key,
    w_value,
    w_output,
    w_router,
    norm_gains,
    w_gate,
    w_up,
    w_down,
    expert_routes,
):
    fsdp_count = lax.axis_size("fsdp")
    sp_count = lax.axis_size("sp")
    expert_count = EXP_DEV * fsdp_count
    capacity = TOK_DEV * TOP // expert_count * 17 // 16
    seq_len = TOK_DEV * sp_count
    score_scale = HEAD_DIM ** (-0.5)
    layer_set = (
        lax.all_gather(w_query, ("fsdp", "sp"), axis=0, tiled=True),
        lax.all_gather(w_key, ("fsdp", "sp"), axis=0, tiled=True),
        lax.all_gather(w_value, ("fsdp", "sp"), axis=0, tiled=True),
        lax.all_gather(w_output, ("fsdp", "sp"), axis=0, tiled=True),
        lax.all_gather(w_router, ("fsdp", "sp"), axis=0, tiled=True),
        lax.all_gather(norm_gains, ("fsdp", "sp"), axis=1, tiled=True),
    )
    query_w, key_w, value_w, output_w, router_w, gains_w = layer_set
    gains32 = gains_w.astype(jnp.float32)
    expert_set = (
        lax.all_gather(w_gate, "sp", axis=1, tiled=True),
        lax.all_gather(w_up, "sp", axis=1, tiled=True),
        lax.all_gather(w_down, "sp", axis=1, tiled=True),
    )
    inputs = layer_input.astype(jnp.float32)
    normed_a, inverse_a = rms_parts(inputs)
    first_in = (normed_a * gains32[0]).astype(jnp.bfloat16)
    q_raw = jnp.dot(first_in, query_w, preferred_element_type=jnp.float32)
    k_raw = jnp.dot(first_in, key_w, preferred_element_type=jnp.float32)
    v_raw = jnp.dot(first_in, value_w, preferred_element_type=jnp.float32)
    positions = lax.axis_index("sp") * TOK_DEV + jnp.arange(TOK_DEV, dtype=jnp.int32)
    cosine_table, sine_table = angles(positions)
    q_normed, q_inverse = rms_parts(q_raw)
    queries = rotate(q_normed * gains32[2], cosine_table, sine_table).astype(jnp.bfloat16)
    k_normed, k_inverse = rms_parts(k_raw)
    keys_local = rotate(k_normed * gains32[3], cosine_table, sine_table).astype(jnp.bfloat16)
    values_local = v_raw.astype(jnp.bfloat16)
    all_keys, all_values = (
        lax.all_gather(keys_local, "sp", axis=0, tiled=True),
        lax.all_gather(values_local, "sp", axis=0, tiled=True),
    )
    q_heads = split_heads(queries)
    k_heads = split_heads(all_keys)
    v_heads = split_heads(all_values)
    query_block = positions // BLK
    key_block = jnp.arange(seq_len, dtype=jnp.int32) // BLK
    allowed = key_block[None, :] <= query_block[:, None]

    def head_forward(pieces):
        q_head, k_head, v_head = pieces
        scores = (
            jnp.einsum("qd,kd->qk", q_head, k_head, preferred_element_type=jnp.float32)
            * score_scale
        )
        scores = jnp.where(allowed, scores, MASKED)
        row_max = jnp.max(scores, axis=-1, keepdims=True)
        exp_rows = jnp.exp(scores - row_max)
        row_sum = jnp.sum(exp_rows, axis=-1, keepdims=True)
        weights = (exp_rows / row_sum).astype(jnp.bfloat16)
        mixed = jnp.dot(weights, v_head, preferred_element_type=jnp.float32)
        return (mixed, (row_max + jnp.log(row_sum))[:, 0])

    mixed_heads, log_sum = lax.map(head_forward, (q_heads, k_heads, v_heads))
    attended = merge_heads(mixed_heads).astype(jnp.bfloat16)
    mid = inputs + jnp.dot(attended, output_w, preferred_element_type=jnp.float32)
    normed_m, inverse_m = rms_parts(mid)
    second_in = (normed_m * gains32[1]).astype(jnp.bfloat16)
    second32 = second_in.astype(jnp.float32)
    logits = jnp.dot(second_in, router_w, preferred_element_type=jnp.float32)
    exp_logits = jnp.exp(logits - jnp.max(logits, axis=1, keepdims=True))
    router_probs = exp_logits / jnp.sum(exp_logits, axis=1, keepdims=True)
    gates = jnp.take_along_axis(router_probs, expert_routes, axis=1)
    flat_routes = expert_routes.reshape(TOK_DEV * TOP)
    onehot = (flat_routes[:, None] == jnp.arange(expert_count, dtype=jnp.int32)[None, :]).astype(
        jnp.int32
    )
    slot_index = jnp.sum((jnp.cumsum(onehot, axis=0) - onehot) * onehot, axis=1)
    token_ids = jnp.arange(TOK_DEV * TOP, dtype=jnp.int32) // TOP
    token_of = (
        jnp.full((expert_count, capacity), TOK_DEV, jnp.int32)
        .at[flat_routes, slot_index]
        .set(token_ids)
    )
    picked = flat_routes * capacity + slot_index
    padded_in = jnp.concatenate([second_in, jnp.zeros((1, D), jnp.bfloat16)], axis=0)
    send_rows = padded_in[token_of].reshape(fsdp_count, EXP_DEV, capacity, D)
    gate_full, up_full, down_full = expert_set
    received = lax.all_to_all(send_rows, "fsdp", split_axis=0, concat_axis=0, tiled=True)
    gate_pre = jnp.einsum("secd,edf->secf", received, gate_full, preferred_element_type=jnp.float32)
    up_pre = jnp.einsum("secd,edf->secf", received, up_full, preferred_element_type=jnp.float32)
    hidden = (gate_pre * jax.nn.sigmoid(gate_pre) * up_pre).astype(jnp.bfloat16)
    result = jnp.einsum(
        "secf,efd->secd", hidden, down_full, preferred_element_type=jnp.float32
    ).astype(jnp.bfloat16)
    returned = lax.all_to_all(result, "fsdp", split_axis=0, concat_axis=0, tiled=True)
    returned, received, gate_pre, up_pre = (returned, received, gate_pre, up_pre)
    back_rows = (
        returned.reshape(expert_count * capacity, D)[picked]
        .astype(jnp.float32)
        .reshape(TOK_DEV, TOP, D)
    )
    final = mid + jnp.sum(back_rows * gates[:, :, None], axis=1)
    layer_out = final.astype(jnp.bfloat16)
    grad_final = output_grad.astype(jnp.float32)
    grad_gates = jnp.sum(back_rows * grad_final[:, None, :], axis=2)
    slot_gates = (
        jnp.zeros((expert_count, capacity), jnp.float32)
        .at[flat_routes, slot_index]
        .set(gates.reshape(TOK_DEV * TOP))
    )
    padded_grad = jnp.concatenate([grad_final, jnp.zeros((1, D), jnp.float32)], axis=0)
    grad_send = (
        (padded_grad[token_of] * slot_gates[:, :, None])
        .astype(jnp.bfloat16)
        .reshape(fsdp_count, EXP_DEV, capacity, D)
    )
    grad_recv = lax.all_to_all(grad_send, "fsdp", split_axis=0, concat_axis=0, tiled=True)
    back_experts = (
        lax.all_gather(w_gate, "sp", axis=1, tiled=True),
        lax.all_gather(w_up, "sp", axis=1, tiled=True),
        lax.all_gather(w_down, "sp", axis=1, tiled=True),
    )
    gate_back, up_back, down_back = back_experts
    grad_hidden = jnp.einsum(
        "secd,efd->secf", grad_recv, down_back, preferred_element_type=jnp.float32
    )
    sigmoid_g = jax.nn.sigmoid(gate_pre)
    silu_g = gate_pre * sigmoid_g
    grad_gate_pre = (
        grad_hidden * up_pre * sigmoid_g * (1.0 + gate_pre * (1.0 - sigmoid_g))
    ).astype(jnp.bfloat16)
    grad_up_pre = (grad_hidden * silu_g).astype(jnp.bfloat16)
    hidden = (silu_g * up_pre).astype(jnp.bfloat16)
    grad_w_down = jnp.einsum(
        "secf,secd->efd", hidden, grad_recv, preferred_element_type=jnp.float32
    )
    grad_w_gate = jnp.einsum(
        "secd,secf->edf", received, grad_gate_pre, preferred_element_type=jnp.float32
    )
    grad_w_up = jnp.einsum(
        "secd,secf->edf", received, grad_up_pre, preferred_element_type=jnp.float32
    )
    grad_rows = jnp.einsum(
        "secf,edf->secd", grad_gate_pre, gate_back, preferred_element_type=jnp.float32
    )
    grad_rows = (
        grad_rows
        + jnp.einsum("secf,edf->secd", grad_up_pre, up_back, preferred_element_type=jnp.float32)
    ).astype(jnp.bfloat16)
    expert_grads = (
        lax.psum_scatter(
            grad_w_gate.astype(jnp.bfloat16), "sp", scatter_dimension=1, tiled=True
        ).astype(jnp.float32),
        lax.psum_scatter(
            grad_w_up.astype(jnp.bfloat16), "sp", scatter_dimension=1, tiled=True
        ).astype(jnp.float32),
        lax.psum_scatter(
            grad_w_down.astype(jnp.bfloat16), "sp", scatter_dimension=1, tiled=True
        ).astype(jnp.float32),
    )
    grad_back = lax.all_to_all(grad_rows, "fsdp", split_axis=0, concat_axis=0, tiled=True)
    grad_second = jnp.sum(
        grad_back.reshape(expert_count * capacity, D)[picked]
        .astype(jnp.float32)
        .reshape(TOK_DEV, TOP, D),
        axis=1,
    )
    back_set = (
        lax.all_gather(w_query, ("fsdp", "sp"), axis=0, tiled=True),
        lax.all_gather(w_key, ("fsdp", "sp"), axis=0, tiled=True),
        lax.all_gather(w_value, ("fsdp", "sp"), axis=0, tiled=True),
        lax.all_gather(w_output, ("fsdp", "sp"), axis=0, tiled=True),
        lax.all_gather(w_router, ("fsdp", "sp"), axis=0, tiled=True),
        lax.all_gather(norm_gains, ("fsdp", "sp"), axis=1, tiled=True),
    )
    query_b, key_b, value_b, output_b, router_b, gains_b = back_set
    router_back = router_b.astype(jnp.float32)
    expert_ids = jnp.arange(expert_count, dtype=jnp.int32)
    choice_grad = jnp.sum(
        jnp.where(
            expert_routes[:, :, None] == expert_ids[None, None, :], grad_gates[:, :, None], 0.0
        ),
        axis=1,
    )
    grad_logits = router_probs * (
        choice_grad - jnp.sum(router_probs * choice_grad, axis=1, keepdims=True)
    )
    grad_router = jnp.einsum(
        "td,te->de",
        second32,
        grad_logits,
        precision=lax.Precision.HIGHEST,
        preferred_element_type=jnp.float32,
    )
    grad_second = grad_second + jnp.einsum(
        "te,de->td",
        grad_logits,
        router_back,
        precision=lax.Precision.HIGHEST,
        preferred_element_type=jnp.float32,
    )
    grad_mid_norm, gain_m = rms_back(grad_second, normed_m, inverse_m, gains32[1])
    grad_mid = grad_final + grad_mid_norm
    grad_branch = grad_mid.astype(jnp.bfloat16)
    grad_w_output = jnp.einsum(
        "td,te->de", attended, grad_branch, preferred_element_type=jnp.float32
    )
    grad_attended = jnp.einsum(
        "te,de->td", grad_branch, output_b, preferred_element_type=jnp.float32
    ).astype(jnp.bfloat16)
    grad_heads = split_heads(grad_attended)

    def head_query(pieces):
        q_head, k_head, v_head, g_head, sum_head = pieces
        scores = (
            jnp.einsum("qd,kd->qk", q_head, k_head, preferred_element_type=jnp.float32)
            * score_scale
        )
        scores = jnp.where(allowed, scores, MASKED)
        weights = jnp.exp(scores - sum_head[:, None])
        grad_weights = jnp.einsum("qd,kd->qk", g_head, v_head, preferred_element_type=jnp.float32)
        row_dot = jnp.sum(weights * grad_weights, axis=1, keepdims=True)
        grad_scores = (weights * (grad_weights - row_dot)).astype(jnp.bfloat16)
        grad_q_head = jnp.dot(grad_scores, k_head, preferred_element_type=jnp.float32) * score_scale
        return (grad_q_head, row_dot[:, 0])

    grad_q_heads, row_dots = lax.map(head_query, (q_heads, k_heads, v_heads, grad_heads, log_sum))
    every_query, every_grad = (
        lax.all_gather(queries, "sp", axis=0, tiled=True),
        lax.all_gather(grad_attended, "sp", axis=0, tiled=True),
    )
    every_sum, every_dot = (
        lax.all_gather(log_sum, "sp", axis=1, tiled=True),
        lax.all_gather(row_dots, "sp", axis=1, tiled=True),
    )
    own_allowed = query_block[None, :] <= key_block[:, None]

    def head_keys(pieces):
        q_head, k_head, v_head, g_head, sum_head, dot_head = pieces
        scores = (
            jnp.einsum("qd,kd->qk", q_head, k_head, preferred_element_type=jnp.float32)
            * score_scale
        )
        scores = jnp.where(own_allowed, scores, MASKED)
        weights = jnp.exp(scores - sum_head[:, None])
        grad_weights = jnp.einsum("qd,kd->qk", g_head, v_head, preferred_element_type=jnp.float32)
        grad_v_head = jnp.einsum(
            "qk,qd->kd", weights.astype(jnp.bfloat16), g_head, preferred_element_type=jnp.float32
        )
        grad_scores = (weights * (grad_weights - dot_head[:, None])).astype(jnp.bfloat16)
        grad_k_head = (
            jnp.einsum("qk,qd->kd", grad_scores, q_head, preferred_element_type=jnp.float32)
            * score_scale
        )
        return (grad_k_head, grad_v_head)

    grad_k_heads, grad_v_heads = lax.map(
        head_keys,
        (
            split_heads(every_query),
            split_heads(keys_local),
            split_heads(values_local),
            split_heads(every_grad),
            every_sum,
            every_dot,
        ),
    )
    grad_keys = merge_heads(grad_k_heads)
    grad_values = merge_heads(grad_v_heads)
    grad_q_normed = rotate(merge_heads(grad_q_heads), cosine_table, -sine_table)
    grad_q_raw, gain_q = rms_back(grad_q_normed, q_normed, q_inverse, gains32[2])
    grad_k_normed = rotate(grad_keys, cosine_table, -sine_table)
    grad_k_raw, gain_k = rms_back(grad_k_normed, k_normed, k_inverse, gains32[3])
    grad_q_low = grad_q_raw.astype(jnp.bfloat16)
    grad_k_low = grad_k_raw.astype(jnp.bfloat16)
    grad_v_low = grad_values.astype(jnp.bfloat16)
    grad_w_query = jnp.einsum("td,te->de", first_in, grad_q_low, preferred_element_type=jnp.float32)
    grad_w_key = jnp.einsum("td,te->de", first_in, grad_k_low, preferred_element_type=jnp.float32)
    grad_w_value = jnp.einsum("td,te->de", first_in, grad_v_low, preferred_element_type=jnp.float32)
    grad_first = jnp.einsum("te,de->td", grad_q_low, query_b, preferred_element_type=jnp.float32)
    grad_first = grad_first + jnp.einsum(
        "te,de->td", grad_k_low, key_b, preferred_element_type=jnp.float32
    )
    grad_first = grad_first + jnp.einsum(
        "te,de->td", grad_v_low, value_b, preferred_element_type=jnp.float32
    )
    grad_in_norm, gain_a = rms_back(grad_first, normed_a, inverse_a, gains32[0])
    input_grad = grad_mid + grad_in_norm
    gain_grads = jnp.stack([gain_a, gain_m, gain_q, gain_k], axis=0)
    layer_grads = (
        lax.psum_scatter(grad_w_query, ("fsdp", "sp"), scatter_dimension=0, tiled=True),
        lax.psum_scatter(grad_w_key, ("fsdp", "sp"), scatter_dimension=0, tiled=True),
        lax.psum_scatter(grad_w_value, ("fsdp", "sp"), scatter_dimension=0, tiled=True),
        lax.psum_scatter(grad_w_output, ("fsdp", "sp"), scatter_dimension=0, tiled=True),
        lax.psum_scatter(grad_router, ("fsdp", "sp"), scatter_dimension=0, tiled=True),
        lax.psum_scatter(gain_grads, ("fsdp", "sp"), scatter_dimension=1, tiled=True),
    )
    grad_query, grad_key, grad_value, grad_output, grad_router_own, grad_gains = layer_grads
    grad_gate, grad_up, grad_down = expert_grads
    return (
        layer_out,
        input_grad,
        grad_query,
        grad_key,
        grad_value,
        grad_output,
        grad_router_own,
        grad_gains,
        grad_gate,
        grad_up,
        grad_down,
    )


def solution(mesh):
    return jax.shard_map(
        body,
        mesh=mesh,
        in_specs=(
            P(("fsdp", "sp"), None),
            P(("fsdp", "sp"), None),
            P(("fsdp", "sp"), None),
            P(("fsdp", "sp"), None),
            P(("fsdp", "sp"), None),
            P(("fsdp", "sp"), None),
            P(("fsdp", "sp"), None),
            P(None, ("fsdp", "sp")),
            P("fsdp", "sp", None),
            P("fsdp", "sp", None),
            P("fsdp", "sp", None),
            P(("fsdp", "sp"), None),
        ),
        out_specs=(
            P(("fsdp", "sp"), None),
            P(("fsdp", "sp"), None),
            P(("fsdp", "sp"), None),
            P(("fsdp", "sp"), None),
            P(("fsdp", "sp"), None),
            P(("fsdp", "sp"), None),
            P(("fsdp", "sp"), None),
            P(None, ("fsdp", "sp")),
            P("fsdp", "sp", None),
            P("fsdp", "sp", None),
            P("fsdp", "sp", None),
        ),
        check_vma=False,
    )
```

profile of v0, /device:TPU:12, one launch (start us, length us, event | category | flops | bytes accessed | tf_op | source)
XLA Modules:
  0.0 3529.9 jit_solution(7070439323896605279)
XLA Ops:
  9.4 54.2 %all-gather = bf16[32,64,4]{1,2,0:T(4,128)(2,1)S(1)} all-gather(bf16[1,64,4]{1,2,0:T(4,128)(2,1)} %bitcast.378), channel_id=1, replica_groups=mesh['fsdp'=8,'sp'=4] {'fsdp','sp'}, dimensions={0}, use_global_device_ids=true | all-gather | bytes 16896 | tf_op jit(solution)/shard_map/all_gather | solution.py:85
  66.3 23.4 all-gather.14.cloned.1.call-done
  100.7 68.0 %all-gather.16.cloned.1.call-done = bf16[2048,2048]{1,0:T(8,128)(2,1)} async-done(((bf16[64,2048]{1,0:T(8,128)(2,1)}), bf16[2048,2048]{1,0:T(8,128)(2,1)}) %all-gather.16.cloned.1.call-update) | async-done | bytes 8388624 | tf_op jit(solution)/shard_map/all_gather | solution.py:81
  185.5 62.4 %all-gather.20.cloned.1.call-done = bf16[2048,2048]{1,0:T(8,128)(2,1)} async-done(((bf16[64,2048]{1,0:T(8,128)(2,1)}), bf16[2048,2048]{1,0:T(8,128)(2,1)}) %all-gather.20.cloned.1.call-update) | async-done | bytes 8388624 | tf_op jit(solution)/shard_map/all_gather | solution.py:82
  274.6 26.7 all-gather.18.cloned.1.call-done
  307.7 48.0 %all-gather.22.cloned.1.call-done = bf16[1024,2048]{1,0:T(8,128)(2,1)} async-done(((bf16[256,2048]{1,0:T(8,128)(2,1)}), bf16[1024,2048]{1,0:T(8,128)(2,1)}) %all-gather.22.cloned.1.call-update) | async-done | bytes 4194320 | tf_op jit(solution)/shard_map/all_gather | solution.py:109
  361.1 50.5 %while.39 = (s32[]{:T(128)}, bf16[16,256,128]{1,2,0:T(8,128)(2,1)S(1)}, f32[16,256]{1,0:T(8,128)S(1)}, bf16[16,256,128]{2,1,0:T(8,128)(2,1)}, bf16[16,1024,128]{...) while((s32[]{:T(128)}, ...), condition=%wide.region_6.7_spmd.clone, body=%wide.region_3.6_spmd.clone.sunk | while | flops 136576768 | bytes 3884137 | solution.py:132
  411.7 24.4 all-gather.24.cloned.1.call-done
  443.6 9.6 gather_fusion
  459.6 234.7 %all-gather.1 = bf16[32,64,16]{1,2,0:T(8,128)(2,1)S(1)} all-gather(bf16[1,64,16]{1,2,0:T(8,128)(2,1)S(1)} %bitcast.377), channel_id=1, replica_groups=mesh['fsdp'=8,'sp'=4] {'fsdp','sp'}, dimensions={0}, use_global_device_ids=true | all-gather | bytes 67584 | tf_op jit(solution)/shard_map/all_gather | solution.py:84
  696.2 11.2 gather_fusion.2
  708.5 16.8 gather_fusion.4
  733.9 9.4 multiply_convert_fusion.2
  751.6 16.5 fusion.87
  768.1 16.5 fusion.83
  784.6 56.5 %all-gather.30.cloned.1.call-done = bf16[2,1024,2048]{2,1,0:T(8,128)(2,1)} async-done(((bf16[2,256,2048]{2,1,0:T(8,128)(2,1)}), bf16[2,1024,2048]{2,1,0:T(8,128)(2,1)}) %all-gather.30.cloned.1.call-update) | async-done | bytes 8388624 | tf_op jit(solution)/shard_map/all_gather | solution.py:92
  841.1 101.4 %all-to-all-done.2 = bf16[8,2,136,2048]{3,2,1,0:T(8,128)(2,1)} async-done(((bf16[8,2,136,2048]{3,2,1,0:T(8,128)(2,1)}), bf16[8,2,136,2048]{3,2,1,0:T(8,128)(2,1)}, u32[]{:S(2)}, u32[]{:S(2)}) %all-to-all-start.2) | async-done | bytes 8912928 | tf_op jit(solution)/shard_map/all_to_all | solution.py:186
  942.5 22.4 fusion.74
  964.9 15.8 convert_bitcast_fusion
  980.8 8.8 copy.201
  989.5 8.5 all-to-all-start.1
  998.1 17.1 fusion.81
  1015.1 17.9 fusion.71
  1033.1 8.8 copy.208
  1041.9 147.8 %all-to-all-done.1 = bf16[8,2,136,2048]{3,2,1,0:T(8,128)(2,1)} async-done(((bf16[8,2,136,2048]{3,2,1,0:T(8,128)(2,1)}), bf16[8,2,136,2048]{3,2,1,0:T(8,128)(2,1)}, u32[]{:S(2)}, u32[]{:S(2)}) %all-to-all-start.1) | async-done | bytes 8912928 | tf_op jit(solution)/shard_map/all_to_all | solution.py:164
  1198.5 21.4 gather_fusion.1
  1219.9 9.5 fusion.70
  1229.6 160.2 %all-to-all-done.3 = bf16[8,2,136,2048]{3,2,1,0:T(8,128)(2,1)} async-done(((bf16[8,2,136,2048]{3,2,1,0:T(8,128)(2,1)}), bf16[8,2,136,2048]{3,2,1,0:T(8,128)(2,1)}, u32[]{:S(2)}, u32[]{:S(2)}) %all-to-all-start.3) | async-done | bytes 8912928 | tf_op jit(solution)/shard_map/all_to_all | solution.py:230
  1389.8 21.0 gather_fusion.3
  1410.9 11.4 convert_reduce_fusion
  1436.5 17.6 bitcast_convert_fusion
  1454.1 17.7 bitcast_convert_fusion.2
  1475.4 9.3 all_gather.65
  1484.7 17.6 bitcast_convert_fusion.1
  1504.1 68.8 %while.40 = (s32[]{:T(128)}, f32[16,256,128]{1,2,0:T(8,128)S(1)}, f32[16,256]{1,0:T(8,128)S(1)}, bf16[16,256,128]{2,1,0:T(8,128)(2,1)}, bf16[16,1024,128]{2,1,0:...) while((s32[]{:T(128)}, f32[16,256,128]{1,2,0:T(8,128)S(1)}, ...), condition=%wide.region_23.24_spmd.clone, body=%wide.region_21.23_spmd.clone.sunk | while | flops 203718400 | bytes 6830721 | solution.py:296
  1588.3 83.0 %while.41 = (s32[]{:T(128)}, f32[16,256,128]{1,2,0:T(8,128)}, bf16[16,256,128]{1,2,0:T(8,128)(2,1)S(1)}, bf16[16,1024,128]{1,2,0:T(8,128)(2,1)}, bf16[16,256,128...) while((s32[]{:T(128)}, f32[16,256,128]{1,2,0:T(8,128)}, ...), condition=%wide.region_26.27_spmd.clone, body=%wide.region_25.26_spmd.clone.sunk | while | flops 270565376 | bytes 5145721 | solution.py:326
  1707.6 9.8 fusion.117
  1717.7 9.7 fusion.141
  1727.4 9.5 fusion.143
  1737.0 9.5 fusion.139
  1748.0 16.6 reduce-scatter.26.cloned.1.call-done
  1768.7 85.2 %reduce-scatter.22.cloned.1.call-done = bf16[2,512,1024]{2,1,0:T(8,128)(2,1)} async-done(((bf16[2,2048,1024]{2,1,0:T(8,128)(2,1)}), bf16[2,512,1024]{2,1,0:T(8,128)(2,1)}) %reduce-scatter.22.cloned.1.call-update) | async-done | bytes 2097168 | tf_op jit(solution)/shard_map/reduce_scatter | solution.py:220
  1858.0 85.6 %reduce-scatter.24.cloned.1.call-done = bf16[2,512,1024]{2,1,0:T(8,128)(2,1)} async-done(((bf16[2,2048,1024]{2,1,0:T(8,128)(2,1)}), bf16[2,512,1024]{2,1,0:T(8,128)(2,1)}) %reduce-scatter.24.cloned.1.call-update) | async-done | bytes 2097168 | tf_op jit(solution)/shard_map/reduce_scatter | solution.py:223
  1949.7 116.1 %reduce-scatter.30.cloned.1.call-done = f32[64,4]{1,0:T(8,128)} async-done(((f32[2048,4]{1,0:T(8,128)}), f32[64,4]{1,0:T(8,128)}) %reduce-scatter.30.cloned.1.call-update) | async-done | bytes 1040
  2067.2 369.8 %reduce-scatter.20.cloned.1.call-done = f32[64,2048]{1,0:T(8,128)} async-done(((f32[2048,2048]{1,0:T(8,128)}), f32[64,2048]{1,0:T(8,128)}) %reduce-scatter.20.cloned.1.call-update) | async-done | bytes 524304 | tf_op jit(solution)/shard_map/reduce_scatter | solution.py:363
  2437.0 361.9 %reduce-scatter.16.cloned.1.call-done = f32[64,2048]{1,0:T(8,128)} async-done(((f32[2048,2048]{1,0:T(8,128)}), f32[64,2048]{1,0:T(8,128)}) %reduce-scatter.16.cloned.1.call-update) | async-done | bytes 524304 | tf_op jit(solution)/shard_map/reduce_scatter | solution.py:361
  2798.9 362.0 %reduce-scatter.14.cloned.1.call-done = f32[64,2048]{1,0:T(8,128)} async-done(((f32[2048,2048]{1,0:T(8,128)}), f32[64,2048]{1,0:T(8,128)}) %reduce-scatter.14.cloned.1.call-update) | async-done | bytes 524304 | tf_op jit(solution)/shard_map/reduce_scatter | solution.py:360
  3161.0 361.9 %reduce-scatter.18.cloned.1.call-done = f32[64,2048]{1,0:T(8,128)} async-done(((f32[2048,2048]{1,0:T(8,128)}), f32[64,2048]{1,0:T(8,128)}) %reduce-scatter.18.cloned.1.call-update) | async-done | bytes 524304 | tf_op jit(solution)/shard_map/reduce_scatter | solution.py:362
  (622 shorter events, 401.6 us)
Async XLA Ops:
  7.2 82.5 %all-gather.14.cloned.1.call-start = ((), (), s32[]{:S(2)}) async-start(), calls=%async_computation.13 | async-start | bytes 8650752 | tf_op jit(solution)/shard_map/all_gather | solution.py:80
  7.9 160.9 %all-gather.16.cloned.1.call-start = ((), (), s32[]{:S(2)}) async-start(), calls=%async_computation.14 | async-start | bytes 8650752 | tf_op jit(solution)/shard_map/all_gather | solution.py:81
  8.7 239.2 %all-gather.20.cloned.1.call-start = ((), (), s32[]{:S(2)}) async-start(), calls=%async_computation.16 | async-start | bytes 8650752 | tf_op jit(solution)/shard_map/all_gather | solution.py:82
  9.4 291.9 %all-gather.18.cloned.1.call-start = ((), (), s32[]{:S(2)}) async-start(), calls=%async_computation.15 | async-start | bytes 5242880 | tf_op jit(solution)/shard_map/all_gather | solution.py:108
  65.3 182.6 %copy-start.62 = (f32[256]{0:T(256)}, f32[256]{0:T(256)S(1)}, u32[]{:S(2)}) copy-start(f32[256]{0:T(256)S(1)} %add_rsqrt_fusion.3) | copy-start | bytes 3076
  66.2 114.2 %copy-start.41 = (f32[256,64]{0,1:T(8,128)}, f32[256,64]{0,1:T(8,128)S(1)}, u32[]{:S(2)}) copy-start(f32[256,64]{0,1:T(8,128)S(1)} %get-tuple-element.473) | copy-start | bytes 196612
  66.3 29.7 copy-start.52
  66.3 108.4 %copy-start.54 = (f32[1,2048]{1,0:T(1,128)}, f32[1,2048]{1,0:T(1,128)S(1)}, u32[]{:S(2)}) copy-start(f32[1,2048]{1,0:T(1,128)S(1)} %get-tuple-element.465) | copy-start | bytes 24580
  66.3 181.6 %copy-start.45 = (f32[1,2048]{1,0:T(1,128)}, f32[1,2048]{1,0:T(1,128)S(1)}, u32[]{:S(2)}) copy-start(f32[1,2048]{1,0:T(1,128)S(1)} %get-tuple-element.467) | copy-start | bytes 24580
  66.3 375.7 %copy-start.56 = (f32[1,2048]{1,0:T(1,128)}, f32[1,2048]{1,0:T(1,128)S(1)}, u32[]{:S(2)}) copy-start(f32[1,2048]{1,0:T(1,128)S(1)} %get-tuple-element.464) | copy-start | bytes 24580
  97.2 71.6 %copy-start.2 = (bf16[256,2048]{1,0:T(8,128)(2,1)S(1)}, bf16[256,2048]{1,0:T(8,128)(2,1)}, u32[]{:S(2)}) copy-start(bf16[256,2048]{1,0:T(8,128)(2,1)} %param.18) | copy-start | bytes 3145732
  185.4 170.3 %all-gather.22.cloned.1.call-start = ((), (), s32[]{:S(2)}) async-start(), calls=%async_computation.17 | async-start | bytes 5242880 | tf_op jit(solution)/shard_map/all_gather | solution.py:109
  254.6 16.7 copy-start.29
  254.6 16.7 copy-start.31
  254.7 181.4 %all-gather.24.cloned.1.call-start = ((), (), s32[]{:S(2)}) async-start(), calls=%async_computation.18 | async-start | bytes 8650752 | tf_op jit(solution)/shard_map/all_gather | solution.py:83
  255.2 496.4 %all-gather.26.cloned.1.call-start = ((), (), s32[]{:S(2)}) async-start(), calls=%async_computation.19 | async-start | bytes 10485760 | tf_op jit(solution)/shard_map/all_gather | solution.py:90
  256.1 51.6 %copy-start.16 = (bf16[16,256,128]{1,2,0:T(8,128)(2,1)}, bf16[16,256,128]{1,2,0:T(8,128)(2,1)S(1)}, u32[]{:S(2)}) copy-start(bf16[16,256,128]{1,2,0:T(8,128)(2,1)S(1)} %fusion.151) | copy-start | bytes 3145732
  411.7 30.3 copy-start.20
  411.7 30.3 copy-start.50
  411.7 30.3 copy-start.60
  411.7 30.3 copy-start.66
  443.5 263.9 %copy-start.14 = (bf16[256,2048]{1,0:T(8,128)(2,1)}, bf16[256,2048]{1,0:T(8,128)(2,1)S(1)}, u32[]{:S(2)}) copy-start(bf16[256,2048]{1,0:T(8,128)(2,1)S(1)} %multiply_convert_fusion.5) | copy-start | bytes 3145732
  453.3 290.0 %all-to-all-start = ((bf16[8,2,136,2048]{3,2,1,0:T(8,128)(2,1)}), bf16[8,2,136,2048]{3,2,1,0:T(8,128)(2,1)}, u32[]{:S(2)}, u32[]{:S(2)}) async-start(bf16[8,2,136,2048]{3,2,1,0:T(8,128)(2,1)} %bitcast.327), calls=%async_computation | async-start | bytes 17825792 | tf_op jit(solution)/shard_map/all_to_all | solution.py:157
  458.9 309.3 %all-gather.28.cloned.1.call-start = ((), (), s32[]{:S(2)}) async-start(), calls=%async_computation.20 | async-start | bytes 10485760 | tf_op jit(solution)/shard_map/all_gather | solution.py:91
  707.8 17.4 copy-start.70
  708.4 16.8 copy-start.76
  708.5 16.8 copy-start
  725.6 17.7 copy-start.39
  743.3 199.2 %all-to-all-start.2 = ((bf16[8,2,136,2048]{3,2,1,0:T(8,128)(2,1)}), bf16[8,2,136,2048]{3,2,1,0:T(8,128)(2,1)}, u32[]{:S(2)}, u32[]{:S(2)}) async-start(bf16[8,2,136,2048]{3,2,1,0:T(8,128)(2,1)} %multiply_convert_fusion.2), calls=%async_computation.2 | async-start | bytes 17825792 | tf_op jit(solution)/shard_map/all_to_all | solution.py:186
  750.9 90.3 %all-gather.30.cloned.1.call-start = ((), (), s32[]{:S(2)}) async-start(), calls=%async_computation.21 | async-start | bytes 10485760 | tf_op jit(solution)/shard_map/all_gather | solution.py:92
  989.5 200.2 %all-to-all-start.1 = ((bf16[8,2,136,2048]{3,2,1,0:T(8,128)(2,1)}), bf16[8,2,136,2048]{3,2,1,0:T(8,128)(2,1)}, u32[]{:S(2)}, u32[]{:S(2)}) async-start(bf16[8,2,136,2048]{3,2,1,0:T(8,128)(2,1)} %copy.201), calls=%async_computation.1 | async-start | bytes 17825792 | tf_op jit(solution)/shard_map/all_to_all | solution.py:164
  1041.9 156.3 %copy-start.22 = (bf16[256,2048]{1,0:T(8,128)(2,1)S(1)}, bf16[256,2048]{1,0:T(8,128)(2,1)}, u32[]{:S(2)}) copy-start(bf16[256,2048]{1,0:T(8,128)(2,1)} %param.19) | copy-start | bytes 3145732
  1041.9 156.5 %copy-start.65 = (s32[2048,1]{0,1:T(1,128)S(1)}, s32[2048,1]{0,1:T(1,128)}, u32[]{:S(2)}) copy-start(s32[2048,1]{0,1:T(1,128)} %get-tuple-element.468) | copy-start | bytes 24580
  1189.7 200.1 %all-to-all-start.3 = ((bf16[8,2,136,2048]{3,2,1,0:T(8,128)(2,1)}), bf16[8,2,136,2048]{3,2,1,0:T(8,128)(2,1)}, u32[]{:S(2)}, u32[]{:S(2)}) async-start(bf16[8,2,136,2048]{3,2,1,0:T(8,128)(2,1)} %copy.208), calls=%async_computation.3 | async-start | bytes 17825792 | tf_op jit(solution)/shard_map/all_to_all | solution.py:230
  1198.2 383.2 %all-gather.34.cloned.1.call-start = ((), (), s32[]{:S(2)}) async-start(), calls=%async_computation.23 | async-start | bytes 5242880 | tf_op jit(solution)/shard_map/all_gather | solution.py:299
  1198.5 21.5 copy-start.40
  1432.8 154.0 %all-gather.32.cloned.1.call-start = ((), (), s32[]{:S(2)}) async-start(), calls=%async_computation.22 | async-start | bytes 5242880 | tf_op jit(solution)/shard_map/all_gather | solution.py:298
  1434.0 312.6 %reduce-scatter.28.cloned.1.call-start = ((), (), s32[]{:S(2)}) async-start(), calls=%async_computation.31 | async-start | bytes 1081344
  1436.4 328.1 %reduce-scatter.26.cloned.1.call-start = ((), (), s32[]{:S(2)}) async-start(), calls=%async_computation.30 | async-start | bytes 10485760 | tf_op jit(solution)/shard_map/reduce_scatter | solution.py:226
  1454.1 399.8 %reduce-scatter.22.cloned.1.call-start = ((), (), s32[]{:S(2)}) async-start(), calls=%async_computation.28 | async-start | bytes 10485760 | tf_op jit(solution)/shard_map/reduce_scatter | solution.py:220
  1471.9 471.7 %reduce-scatter.24.cloned.1.call-start = ((), (), s32[]{:S(2)}) async-start(), calls=%async_computation.29 | async-start | bytes 10485760 | tf_op jit(solution)/shard_map/reduce_scatter | solution.py:223
  1502.4 563.4 %reduce-scatter.30.cloned.1.call-start = ((), (), s32[]{:S(2)}) async-start(), calls=%async_computation.32 | async-start | bytes 1081344
  1588.3 83.0 %copy-start.42 = (f32[256,64]{0,1:T(8,128)S(1)}, f32[256,64]{0,1:T(8,128)}, u32[]{:S(2)}) copy-start(f32[256,64]{0,1:T(8,128)} %copy-done.41) | copy-start | bytes 196612
  1588.3 83.0 %copy-start.47 = (f32[256,64]{0,1:T(8,128)S(1)}, f32[256,64]{0,1:T(8,128)}, u32[]{:S(2)}) copy-start(f32[256,64]{0,1:T(8,128)} %get-tuple-element.471) | copy-start | bytes 196612
  1707.5 729.5 %reduce-scatter.20.cloned.1.call-start = ((), (), s32[]{:S(2)}) async-start(), calls=%async_computation.27 | async-start | bytes 17301504 | tf_op jit(solution)/shard_map/reduce_scatter | solution.py:363
  1717.4 1081.5 %reduce-scatter.16.cloned.1.call-start = ((), (), s32[]{:S(2)}) async-start(), calls=%async_computation.25 | async-start | bytes 17301504 | tf_op jit(solution)/shard_map/reduce_scatter | solution.py:361
  1727.4 1433.6 %reduce-scatter.14.cloned.1.call-start = ((), (), s32[]{:S(2)}) async-start(), calls=%async_computation.24 | async-start | bytes 17301504 | tf_op jit(solution)/shard_map/reduce_scatter | solution.py:360
  1736.9 1785.9 %reduce-scatter.18.cloned.1.call-start = ((), (), s32[]{:S(2)}) async-start(), calls=%async_computation.26 | async-start | bytes 17301504 | tf_op jit(solution)/shard_map/reduce_scatter | solution.py:362
  (63 other events, 326.3 us)
Sparse Core Ops, SparseCore 0:
  10.9 78.7 all-gather.13
  92.6 76.1 all-gather.15
  171.7 76.1 all-gather.19
  250.1 51.1 all-gather.17
  303.0 52.6 all-gather.21
  358.5 77.6 all-gather.23
  438.0 86.3 all-gather.25
  526.2 87.7 all-gather.27
  753.5 87.5 all-gather.29
  1432.9 54.1 all-gather.33
  1489.0 52.5 all-gather.31
  1543.7 120.1 reduce-scatter.27
  1667.3 97.2 reduce-scatter.25
  1767.5 86.3 reduce-scatter.21
  1857.1 86.3 reduce-scatter.23
  1945.7 120.0 reduce-scatter.29
  2068.6 368.3 reduce-scatter.19
  2439.9 359.0 reduce-scatter.15
  2801.9 359.0 reduce-scatter.13
  3163.8 359.0 reduce-scatter.17
where the time goes:
time: 3540 us; the launch traced here: 3530 us
  waiting for transfers between devices  2480 us (70%)
  matrix products  425 us (12%)
  blocking collectives  305 us (9%)
  local copies, waits for them, and re-layouts  182 us (5%)
  other arithmetic  85.2 us (2%)
    reduce_scatter x1, waiting for transfers between devices, body(): lax.psum_scatter(grad_w_output, ('fsdp', 'sp'), scatter_dimension=0, tile...  370 us
    reduce_scatter x1, waiting for transfers between devices, body(): lax.psum_scatter(grad_w_query, ('fsdp', 'sp'), scatter_dimension=0, tiled...  362 us
    reduce_scatter x1, waiting for transfers between devices, body(): lax.psum_scatter(grad_w_key, ('fsdp', 'sp'), scatter_dimension=0, tiled=T...  362 us
    reduce_scatter x1, waiting for transfers between devices, body(): lax.psum_scatter(grad_w_value, ('fsdp', 'sp'), scatter_dimension=0, tiled...  362 us
    all_gather x1, blocking collectives, body(): lax.all_gather(w_router, ('fsdp', 'sp'), axis=0, tiled=True)  235 us
    all_to_all x1, waiting for transfers between devices, body(): lax.all_to_all(grad_rows, 'fsdp', split_axis=0, concat_axis=0, tiled=True)  160 us
    all_to_all x1, waiting for transfers between devices, body(): lax.all_to_all(result, 'fsdp', split_axis=0, concat_axis=0, tiled=True)  148 us
    unnamed x22, waiting for transfers between devices  121 us
  transfers between devices with their start and end apart: 24, of which 18 were waited for; matrix products, arithmetic and copies ran while one was open for 17% of the time, Pallas kernels for 0%

commit v1 on v0

v1 whole, which is shorter than its diff:
```python
import functools

import jax
import jax.numpy as jnp
from jax import lax
from jax.experimental import pallas as pl
from jax.experimental.pallas import tpu as pltpu
from jax.sharding import PartitionSpec as P

D = 2048
HEADS = 16
HEAD_DIM = 128
TOP = 8
EXP_DEV = 2
BLK = 256
TOK_DEV = 256
EPSILON = 1e-05
ROPE_BASE = 10000.0
MASKED = -1000000000.0
SCALE = HEAD_DIM ** (-0.5)
MESH = pl.DeviceIdType.MESH
ANY = pl.BlockSpec(memory_space=pl.ANY)
VMEM = pl.BlockSpec(memory_space=pltpu.VMEM)
VLIM = 56 * 1024 * 1024
F32 = jnp.float32
BF16 = jnp.bfloat16


def remote(src, dst, send_sem, recv_sem, device):
    return pltpu.make_async_remote_copy(
        src_ref=src,
        dst_ref=dst,
        send_sem=send_sem,
        recv_sem=recv_sem,
        device_id=device,
        device_id_type=MESH,
    )


def landed(ref, sem):
    pltpu.make_async_copy(ref, ref, sem).wait()


def signal(sem, device):
    pl.semaphore_signal(sem, inc=1, device_id=device, device_id_type=MESH)


def greet_line(barrier, lines, f, s):
    place, core = f // 2, f % 2
    signal(barrier, (f + 1 - 2 * core, s))

    @pl.when(place > 0)
    def _():
        signal(barrier, (f - 2, s))

    @pl.when(place < lines - 1)
    def _():
        signal(barrier, (f + 2, s))

    return 1 + jnp.where(place > 0, 1, 0) + jnp.where(place < lines - 1, 1, 0)


class LineGather:
    def __init__(self, views, lines, f, s, send, recv):
        self.views, self.lines, self.f, self.s = views, lines, f, s
        self.send, self.recv = send, recv
        self.place, self.core = f // 2, f % 2

    def copy(self, v, block, slot, way):
        device = {
            "right": (self.f + 2, self.s),
            "left": (self.f - 2, self.s),
            "partner": (self.f + 1 - 2 * self.core, self.s),
        }[way]
        index = {"right": 0, "left": 1, "partner": 2}[way]
        ref = self.views[v](block)
        return remote(ref, ref, self.send.at[v, slot, index], self.recv.at[v, block], device)

    def each(self, v, action):
        pass

    def start_own(self, v):
        self.copy(v, self.f, 0, "partner").start()

        @pl.when(self.place < self.lines - 1)
        def _():
            self.copy(v, self.f, 0, "right").start()

        @pl.when(self.place > 0)
        def _():
            self.copy(v, self.f, 0, "left").start()

    def forward(self, v, k):
        place, lines = self.place, self.lines

        @pl.when(place >= k)
        def _():
            block = self.f - 2 * k
            landed(self.views[v](block), self.recv.at[v, block])

            @pl.when(place < lines - 1)
            def _():
                self.copy(v, block, k, "right").start()

            self.copy(v, block, k, "partner").start()

        @pl.when(place + k < lines)
        def _():
            block = self.f + 2 * k
            landed(self.views[v](block), self.recv.at[v, block])

            @pl.when(place > 0)
            def _():
                self.copy(v, block, lines - 1 + k, "left").start()

            self.copy(v, block, lines - 1 + k, "partner").start()

    def finish(self, v):
        place, lines = self.place, self.lines
        for line in range(lines):
            block = 2 * line + 1 - self.core
            landed(self.views[v](block), self.recv.at[v, block])
        self.copy(v, self.f, 0, "partner").wait_send()

        @pl.when(place < lines - 1)
        def _():
            self.copy(v, self.f, 0, "right").wait_send()

        @pl.when(place > 0)
        def _():
            self.copy(v, self.f, 0, "left").wait_send()

        for k in range(1, lines):

            @pl.when(place >= k)
            def _():
                block = self.f - 2 * k

                @pl.when(place < lines - 1)
                def _():
                    self.copy(v, block, k, "right").wait_send()

                self.copy(v, block, k, "partner").wait_send()

            @pl.when(place + k < lines)
            def _():
                block = self.f + 2 * k

                @pl.when(place > 0)
                def _():
                    self.copy(v, block, lines - 1 + k, "left").wait_send()

                self.copy(v, block, lines - 1 + k, "partner").wait_send()


def line_sems(arrays, fsdp):
    lines = fsdp // 2
    return [
        pltpu.SemaphoreType.DMA((arrays, 2 * lines, 3)),
        pltpu.SemaphoreType.DMA((arrays, fsdp)),
    ]


def start_kernel(
    fsdp, sp, x_ref, w_ref, wo_ref, misc_ref, routes_ref,
    x_all, w_all, wo_all, misc_all, routes_all,
    send, recv, xsend, xrecv, psend, precv, wsend, wrecv, msend, mrecv, rsend, rrecv, local,
):
    f, s = lax.axis_index("fsdp"), lax.axis_index("sp")
    count, lines = fsdp * sp, fsdp // 2
    me = f * sp + s
    rows = w_ref.shape[1]
    cols = D // sp
    half = TOK_DEV // 2
    barrier = pltpu.get_barrier_semaphore()

    def greet(i, carry):
        other = lax.rem(me + i, count)
        signal(barrier, (other // sp, lax.rem(other, sp)))
        return carry

    lax.fori_loop(1, count, greet, 0)
    pl.semaphore_wait(barrier, count - 1)

    def w_block(i, s_to):
        return w_ref.at[:, :, pl.ds(pl.multiple_of(s_to * cols, cols), cols)]

    def w_rows(i):
        return w_all.at[:, pl.ds(pl.multiple_of(i * rows, rows), rows), :]

    def w_view(b):
        size = rows * sp
        return w_all.at[:, pl.ds(pl.multiple_of(b * size, size), size), :]

    def wo_view(b):
        return wo_all.at[pl.ds(pl.multiple_of(b * rows, rows), rows), :]

    def x_rows(place, first, size):
        return x_all.at[pl.ds(pl.multiple_of(place * TOK_DEV + first, half), size), :]

    w_own = pltpu.make_async_copy(w_block(me, s), w_rows(me), local.at[0])
    w_own.start()
    w_copies = []
    for k in range(1, sp):
        s_to = s ^ k
        copy = remote(w_block(me, s_to), w_rows(me), psend.at[k], precv.at[k], (f, s_to))
        copy.start()
        w_copies.append(copy)
    target_s, target_f = me // fsdp, lax.rem(me, fsdp)
    stays = jnp.logical_and(target_s == s, target_f == f)
    wo_copy = remote(wo_ref, wo_view(target_f), wsend, wrecv, (target_f, target_s))
    wo_own = pltpu.make_async_copy(wo_ref, wo_view(f), wrecv)

    @pl.when(stays)
    def _():
        wo_own.start()

    @pl.when(jnp.logical_not(stays))
    def _():
        wo_copy.start()

    x_own = pltpu.make_async_copy(x_ref, x_rows(s, 0, TOK_DEV), local.at[1])
    x_own.start()
    x_near = []
    for k in (1, 2):
        copy = remote(x_ref, x_rows(s, 0, TOK_DEV), xsend.at[k - 1], xrecv.at[k - 1], (f, s ^ k))
        copy.start()
        x_near.append(copy)
    misc_own = pltpu.make_async_copy(misc_ref, misc_all.at[me], local.at[2])
    misc_own.start()

    def misc_copy(i):
        other = lax.rem(me + i, count)
        return remote(
            misc_ref, misc_all.at[me], msend.at[i], mrecv.at[me], (other // sp, lax.rem(other, sp))
        )

    def misc_go(i, carry):
        misc_copy(i).start()
        return carry

    lax.fori_loop(1, count, misc_go, 0)

    routes_own = pltpu.make_async_copy(routes_ref, routes_all.at[f], local.at[3])
    routes_own.start()

    def routes_copy(i):
        other = lax.rem(f + i, fsdp)
        return remote(routes_ref, routes_all.at[f], rsend.at[i], rrecv.at[f], (other, s))

    def routes_go(i, carry):
        routes_copy(i).start()
        return carry

    lax.fori_loop(1, fsdp, routes_go, 0)

    w_own.wait()
    for k in range(1, sp):
        landed(w_rows(f * sp + (s ^ k)), precv.at[k])
    line = LineGather([w_view, wo_view], lines, f, s, send, recv)
    line.start_own(0)
    landed(wo_view(f), wrecv)
    line.start_own(1)

    landed(x_rows(s ^ 1, 0, TOK_DEV), xrecv.at[0])
    x_on_a = remote(
        x_rows(s ^ 1, 0, half), x_rows(s ^ 1, 0, half), xsend.at[2], xrecv.at[2], (f, s ^ 2)
    )
    x_on_a.start()
    landed(x_rows(s ^ 2, 0, TOK_DEV), xrecv.at[1])
    x_on_b = remote(
        x_rows(s ^ 2, half, half), x_rows(s ^ 2, half, half), xsend.at[3], xrecv.at[3], (f, s ^ 1)
    )
    x_on_b.start()

    for k in range(1, lines):
        line.forward(0, k)
        line.forward(1, k)
    line.finish(0)
    line.finish(1)
    landed(x_rows(s ^ 3, 0, half), xrecv.at[2])
    landed(x_rows(s ^ 3, half, half), xrecv.at[3])

    def misc_end(i, carry):
        misc_copy(i).wait_send()
        other = lax.rem(me + i, count)
        landed(misc_all.at[other], mrecv.at[other])
        return carry

    lax.fori_loop(1, count, misc_end, 0)

    def routes_end(i, carry):
        routes_copy(i).wait_send()
        other = lax.rem(f + i, fsdp)
        landed(routes_all.at[other], rrecv.at[other])
        return carry

    lax.fori_loop(1, fsdp, routes_end, 0)
    for copy in w_copies + x_near + [x_on_a, x_on_b]:
        copy.wait_send()

    @pl.when(jnp.logical_not(stays))
    def _():
        wo_copy.wait_send()

    x_own.wait()
    misc_own.wait()
    routes_own.wait()


def gather_start(fsdp, sp, x, w, wo, misc, routes):
    count = fsdp * sp
    dma = pltpu.SemaphoreType.DMA
    return pl.pallas_call(
        functools.partial(start_kernel, fsdp, sp),
        out_shape=(
            jax.ShapeDtypeStruct((sp * TOK_DEV, D), BF16),
            jax.ShapeDtypeStruct((3, D, D // sp), BF16),
            jax.ShapeDtypeStruct((D // sp, D), BF16),
            jax.ShapeDtypeStruct((count,) + misc.shape, BF16),
            jax.ShapeDtypeStruct((fsdp,) + routes.shape, jnp.int32),
        ),
        in_specs=[ANY] * 5,
        out_specs=[ANY] * 5,
        scratch_shapes=line_sems(2, fsdp)
        + [
            dma((4,)), dma((4,)), dma((sp,)), dma((sp,)), dma, dma,
            dma((count,)), dma((count,)), dma((fsdp,)), dma((fsdp,)), dma((4,)),
        ],
        compiler_params=pltpu.CompilerParams(collective_id=0, has_side_effects=True),
        name="gather_start",
    )(x, w, wo, misc, routes)


def line_gather_kernel(fsdp, parts, x_ref, out_ref, send, recv, local):
    f, s = lax.axis_index("fsdp"), lax.axis_index("sp")
    lines = fsdp // 2
    rows = x_ref.shape[0]
    size = rows // parts
    barrier = pltpu.get_barrier_semaphore()
    expected = greet_line(barrier, lines, f, s)
    own = pltpu.make_async_copy(x_ref, out_ref.at[pl.ds(pl.multiple_of(f * rows, rows), rows)], local)
    own.start()
    pl.semaphore_wait(barrier, expected)
    own.wait()

    def view(part):
        return lambda b: out_ref.at[pl.ds(pl.multiple_of(b * rows + part * size, size), size)]

    line = LineGather([view(p) for p in range(parts)], lines, f, s, send, recv)
    for p in range(parts):
        line.start_own(p)
    for k in range(1, lines):
        for p in range(parts):
            line.forward(p, k)
    for p in range(parts):
        line.finish(p)


def line_gather(fsdp, x, number, name):
    parts = 2
    return pl.pallas_call(
        functools.partial(line_gather_kernel, fsdp, parts),
        out_shape=jax.ShapeDtypeStruct((fsdp * x.shape[0], x.shape[1]), x.dtype),
        in_specs=[ANY],
        out_specs=ANY,
        scratch_shapes=line_sems(parts, fsdp) + [pltpu.SemaphoreType.DMA],
        compiler_params=pltpu.CompilerParams(collective_id=number, has_side_effects=True),
        name=name,
    )(x)


def add_rows(dst, a, b, rows):
    def step(i, carry):
        at = pl.ds(pl.multiple_of(i * 32, 32), 32)
        dst[at, :] = (a[at, :].astype(F32) + b[at, :].astype(F32)).astype(dst.dtype)
        return carry

    lax.fori_loop(0, rows // 32, step, 0)


def line_reduce_kernel(
    fsdp, p_ref, out_ref, own, paired, from_left, from_right, psend, precv, send, lrecv, rrecv, local
):
    f, s = lax.axis_index("fsdp"), lax.axis_index("sp")
    lines = fsdp // 2
    place, core = f // 2, f % 2
    rows = out_ref.shape[0]
    barrier = pltpu.get_barrier_semaphore()
    expected = greet_line(barrier, lines, f, s)
    order_right = [(n, lines - 1 - n) for n in range(lines)]

    def load(i):
        return pltpu.make_async_copy(p_ref.at[2 * i + core], own.at[i], local.at[i])

    def swap(i):
        return remote(
            p_ref.at[2 * i + 1 - core], paired.at[i], psend.at[i], precv.at[i], (f + 1 - 2 * core, s)
        )

    for n in range(lines):
        load(n).start()
    pl.semaphore_wait(barrier, expected)
    for n in range(lines):
        swap(lines - 1 - n if n % 2 == 0 else n // 2 if False else lines - 1 - n).start()
    for n in range(lines):
        i = lines - 1 - n
        load(i).wait()
        landed(paired.at[i], precv.at[i])
        add_rows(own.at[i], own.at[i], paired.at[i], rows)

    def right(d):
        return remote(own.at[d], from_left.at[d], send.at[d], lrecv.at[d], (f + 2, s))

    def left(d):
        return remote(own.at[d], from_right.at[d], send.at[d], rrecv.at[d], (f - 2, s))

    for n in range(lines - 1):
        d_right = lines - 1 - n

        @pl.when(place < d_right)
        def _():
            @pl.when(place > 0)
            def _():
                landed(from_left.at[d_right], lrecv.at[d_right])
                add_rows(own.at[d_right], own.at[d_right], from_left.at[d_right], rows)

            right(d_right).start()

        d_left = n

        @pl.when(place > d_left)
        def _():
            @pl.when(place < lines - 1)
            def _():
                landed(from_right.at[d_left], rrecv.at[d_left])
                add_rows(own.at[d_left], own.at[d_left], from_right.at[d_left], rows)

            left(d_left).start()

    add_rows(out_ref, own.at[place], own.at[place], rows) if False else None

    def first(i, carry):
        at = pl.ds(pl.multiple_of(i * 32, 32), 32)
        out_ref[at, :] = own[place, at, :].astype(F32)
        return carry

    lax.fori_loop(0, rows // 32, first, 0)

    @pl.when(place > 0)
    def _():
        landed(from_left.at[place], lrecv.at[place])
        add_rows(out_ref, out_ref, from_left.at[place], rows)

    @pl.when(place < lines - 1)
    def _():
        landed(from_right.at[place], rrecv.at[place])
        add_rows(out_ref, out_ref, from_right.at[place], rows)

    for i in range(lines):
        swap(i).wait_send()

        @pl.when(place < i)
        def _():
            right(i).wait_send()

        @pl.when(place > i)
        def _():
            left(i).wait_send()


def line_reduce(fsdp, partial, number, name):
    lines = fsdp // 2
    block = partial.shape[1:]
    dma = pltpu.SemaphoreType.DMA
    return pl.pallas_call(
        functools.partial(line_reduce_kernel, fsdp),
        out_shape=jax.ShapeDtypeStruct(block, F32),
        in_specs=[ANY],
        out_specs=VMEM,
        scratch_shapes=[pltpu.VMEM((lines,) + block, BF16) for _ in range(4)]
        + [dma((lines,)) for _ in range(6)],
        compiler_params=pltpu.CompilerParams(
            collective_id=number, has_side_effects=True, vmem_limit_bytes=VLIM
        ),
        name=name,
    )(partial)


def greet_plane(f, s):
    barrier = pltpu.get_barrier_semaphore()
    for k in (1, 2):
        signal(barrier, (f, s ^ k))
    pl.semaphore_wait(barrier, 2)


def plane_gather_kernel(x_ref, out_ref, send, recv, local):
    f, s = lax.axis_index("fsdp"), lax.axis_index("sp")
    rows = x_ref.shape[0]
    half = rows // 2

    def at(place, first, size):
        return out_ref.at[pl.ds(pl.multiple_of(place * rows + first, half), size), :]

    own = pltpu.make_async_copy(x_ref, at(s, 0, rows), local)
    own.start()
    greet_plane(f, s)
    near = [
        remote(x_ref, at(s, 0, rows), send.at[k - 1], recv.at[k - 1], (f, s ^ k)) for k in (1, 2)
    ]
    for copy in near:
        copy.start()
    landed(at(s ^ 1, 0, rows), recv.at[0])
    on_a = remote(at(s ^ 1, 0, half), at(s ^ 1, 0, half), send.at[2], recv.at[2], (f, s ^ 2))
    on_a.start()
    landed(at(s ^ 2, 0, rows), recv.at[1])
    on_b = remote(at(s ^ 2, half, half), at(s ^ 2, half, half), send.at[3], recv.at[3], (f, s ^ 1))
    on_b.start()
    landed(at(s ^ 3, 0, half), recv.at[2])
    landed(at(s ^ 3, half, half), recv.at[3])
    own.wait()
    for copy in near + [on_a, on_b]:
        copy.wait_send()


def plane_gather(sp, x, number, name):
    dma = pltpu.SemaphoreType.DMA
    return pl.pallas_call(
        plane_gather_kernel,
        out_shape=jax.ShapeDtypeStruct((sp * x.shape[0], x.shape[1]), x.dtype),
        in_specs=[ANY],
        out_specs=ANY,
        scratch_shapes=[dma((4,)), dma((4,)), dma],
        compiler_params=pltpu.CompilerParams(collective_id=number, has_side_effects=True),
        name=name,
    )(x)


def plane_reduce_kernel(p_ref, out_ref, own, got, got_on, send, recv, local):
    f, s = lax.axis_index("fsdp"), lax.axis_index("sp")
    rows = out_ref.shape[0]
    half = rows // 2

    def part(ref, h):
        return ref.at[pl.ds(h * half, half), :]

    loads = []
    for n, d in enumerate((s, s ^ 2, s ^ 1)):
        load = pltpu.make_async_copy(p_ref.at[d], own.at[n], local.at[n])
        load.start()
        loads.append(load)
    greet_plane(f, s)
    hops = []
    for h, k in ((0, 1), (1, 2)):
        far = remote(
            part(p_ref.at[s ^ 3], h), part(got.at[1], h), send.at[h, 0], recv.at[h, 0], (f, s ^ k)
        )
        far.start()
        hops.append(far)
    for h, k in ((0, 1), (1, 2)):
        near = remote(
            part(p_ref.at[s ^ k], h), part(got.at[0], h), send.at[h, 1], recv.at[h, 1], (f, s ^ k)
        )
        near.start()
        hops.append(near)
    for load in loads:
        load.wait()
    for h, k, n in ((0, 1, 1), (1, 2, 2)):
        landed(part(got.at[1], h), recv.at[h, 0])
        add_rows(part(own.at[n], h), part(own.at[n], h), part(got.at[1], h), half)
        on = remote(
            part(own.at[n], h), part(got_on, h), send.at[h, 2], recv.at[h, 2], (f, s ^ (3 - k))
        )
        on.start()
        hops.append(on)
    for h in (0, 1):
        landed(part(got.at[0], h), recv.at[h, 1])
        add_rows(part(out_ref, h), part(own.at[0], h), part(got.at[0], h), half)
    for h in (0, 1):
        landed(part(got_on, h), recv.at[h, 2])
        add_rows(part(out_ref, h), part(out_ref, h), part(got_on, h), half)
    for copy in hops:
        copy.wait_send()


def plane_reduce(sp, partial, number, name):
    block = partial.shape[1:]
    dma = pltpu.SemaphoreType.DMA
    return pl.pallas_call(
        plane_reduce_kernel,
        out_shape=jax.ShapeDtypeStruct(block, F32),
        in_specs=[ANY],
        out_specs=VMEM,
        scratch_shapes=[
            pltpu.VMEM((3,) + block, BF16),
            pltpu.VMEM((2,) + block, BF16),
            pltpu.VMEM(block, BF16),
            dma((2, 3)),
            dma((2, 3)),
            dma((3,)),
        ],
        compiler_params=pltpu.CompilerParams(
            collective_id=number, has_side_effects=True, vmem_limit_bytes=VLIM
        ),
        name=name,
    )(partial)


def plane_sum_kernel(x_ref, out_ref, got, send, recv):
    f, s = lax.axis_index("fsdp"), lax.axis_index("sp")
    barrier = pltpu.get_barrier_semaphore()
    for k in (1, 2, 3):
        signal(barrier, (f, s ^ k))
    pl.semaphore_wait(barrier, 3)
    copies = []
    for k in (1, 2, 3):
        copy = remote(x_ref, got.at[k - 1], send.at[k - 1], recv.at[k - 1], (f, s ^ k))
        copy.start()
        copies.append(copy)
    for copy in copies:
        copy.wait()
    near = x_ref[...] + got[0]
    far = got[1] + got[2]
    out_ref[...] = near + far


def plane_sum(x, number, name):
    dma = pltpu.SemaphoreType.DMA
    return pl.pallas_call(
        plane_sum_kernel,
        out_shape=jax.ShapeDtypeStruct(x.shape, F32),
        in_specs=[VMEM],
        out_specs=VMEM,
        scratch_shapes=[pltpu.VMEM((3,) + x.shape, F32), dma((3,)), dma((3,))],
        compiler_params=pltpu.CompilerParams(collective_id=number, has_side_effects=True),
        name=name,
    )(x)


def end_kernel(
    fsdp, sp, q_ref, o_ref, m_ref, q_out, o_out, m_out,
    qsend, qrecv, osend, orecv, msend, mrecv, local,
):
    f, s = lax.axis_index("fsdp"), lax.axis_index("sp")
    count = fsdp * sp
    me = f * sp + s
    rows = o_ref.shape[0]
    barrier = pltpu.get_barrier_semaphore()

    def greet(i, carry):
        other = lax.rem(me + i, count)
        signal(barrier, (other // sp, lax.rem(other, sp)))
        return carry

    lax.fori_loop(1, count, greet, 0)
    pl.semaphore_wait(barrier, count - 1)

    def q_from(place):
        return q_ref.at[:, pl.ds(pl.multiple_of(place * rows, rows), rows), :]

    q_own = pltpu.make_async_copy(q_from(s), q_out.at[s], local.at[0])
    q_own.start()
    copies = []
    for k in range(1, sp):
        copy = remote(q_from(s ^ k), q_out.at[s], qsend.at[k], qrecv.at[k], (f, s ^ k))
        copy.start()
        copies.append(copy)
    flat = s * fsdp + f
    target_f, target_s = flat // sp, lax.rem(flat, sp)
    stays = jnp.logical_and(target_s == s, target_f == f)
    o_copy = remote(o_ref, o_out, osend, orecv, (target_f, target_s))
    o_own = pltpu.make_async_copy(o_ref, o_out, orecv)

    @pl.when(stays)
    def _():
        o_own.start()

    @pl.when(jnp.logical_not(stays))
    def _():
        o_copy.start()

    m_own = pltpu.make_async_copy(m_ref.at[me], m_out.at[me], local.at[1])
    m_own.start()

    def m_copy(i):
        other = lax.rem(me + i, count)
        return remote(
            m_ref.at[other], m_out.at[me], msend.at[i], mrecv.at[me], (other // sp, lax.rem(other, sp))
        )

    def m_go(i, carry):
        m_copy(i).start()
        return carry

    lax.fori_loop(1, count, m_go, 0)

    def m_end(i, carry):
        m_copy(i).wait_send()
        other = lax.rem(me + i, count)
        landed(m_out.at[other], mrecv.at[other])
        return carry

    lax.fori_loop(1, count, m_end, 0)
    landed(o_out, orecv)

    @pl.when(jnp.logical_not(stays))
    def _():
        o_copy.wait_send()

    for k in range(1, sp):
        landed(q_out.at[s ^ k], qrecv.at[k])
    for copy in copies:
        copy.wait_send()
    q_own.wait()
    m_own.wait()


def exchange_end(fsdp, sp, q, o, m, number):
    count = fsdp * sp
    rows = o.shape[0]
    dma = pltpu.SemaphoreType.DMA
    return pl.pallas_call(
        functools.partial(end_kernel, fsdp, sp),
        out_shape=(
            jax.ShapeDtypeStruct((sp, 3, rows, D // sp), q.dtype),
            jax.ShapeDtypeStruct(o.shape, o.dtype),
            jax.ShapeDtypeStruct(m.shape, m.dtype),
        ),
        in_specs=[ANY] * 3,
        out_specs=[ANY] * 3,
        scratch_shapes=[
            dma((sp,)), dma((sp,)), dma, dma, dma((count,)), dma((count,)), dma((2,)),
        ],
        compiler_params=pltpu.CompilerParams(collective_id=number, has_side_effects=True),
        name="exchange_end",
    )(q, o, m)


def dot_nt(a, b):
    return lax.dot_general(a, b, (((1,), (1,)), ((), ())), preferred_element_type=F32)


def dot_tn(a, b):
    return lax.dot_general(a, b, (((0,), (0,)), ((), ())), preferred_element_type=F32)


def dot_nn(a, b):
    return jnp.dot(a, b, preferred_element_type=F32)


def attend_kernel(q_ref, k_ref, v_ref, o_ref, sum_ref):
    for i in range(q_ref.shape[0] // BLK):
        rows, seen = pl.ds(i * BLK, BLK), pl.ds(0, (i + 1) * BLK)
        scores = dot_nt(q_ref[rows, :], k_ref[seen, :]) * SCALE
        row_max = jnp.max(scores, axis=-1, keepdims=True)
        exp_rows = jnp.exp(scores - row_max)
        row_sum = jnp.sum(exp_rows, axis=-1, keepdims=True)
        probs = (exp_rows / row_sum).astype(BF16)
        o_ref[rows, :] = dot_nn(probs, v_ref[seen, :]).astype(BF16)
        sum_ref[0, rows, :] = row_max + jnp.log(row_sum)


def attend(q, k, v):
    seq, width = q.shape
    heads = width // HEAD_DIM
    spec = pl.BlockSpec((seq, HEAD_DIM), lambda h: (0, h))
    return pl.pallas_call(
        attend_kernel,
        grid=(heads,),
        out_shape=(
            jax.ShapeDtypeStruct((seq, width), BF16),
            jax.ShapeDtypeStruct((heads, seq, 1), F32),
        ),
        in_specs=[spec] * 3,
        out_specs=[spec, pl.BlockSpec((1, seq, 1), lambda h: (h, 0, 0))],
        compiler_params=pltpu.CompilerParams(vmem_limit_bytes=VLIM),
        cost_estimate=pl.CostEstimate(
            flops=4 * seq * seq * width * 5 // 8, bytes_accessed=12 * seq * width,
            transcendentals=heads * seq * seq * 5 // 8,
        ),
        name="attend",
    )(q, k, v)


def attend_back_kernel(q_ref, k_ref, v_ref, g_ref, sum_ref, dq_ref, dk_ref, dv_ref):
    dk_ref[...] = jnp.zeros_like(dk_ref)
    dv_ref[...] = jnp.zeros_like(dv_ref)
    for i in range(q_ref.shape[0] // BLK):
        rows, seen = pl.ds(i * BLK, BLK), pl.ds(0, (i + 1) * BLK)
        q, g, keys = q_ref[rows, :], g_ref[rows, :], k_ref[seen, :]
        scores = dot_nt(q, keys) * SCALE
        probs = jnp.exp(scores - sum_ref[0, rows, :])
        grad_probs = dot_nt(g, v_ref[seen, :])
        row_dot = jnp.sum(probs * grad_probs, axis=-1, keepdims=True)
        grad_scores = (probs * (grad_probs - row_dot)).astype(BF16)
        dq_ref[rows, :] = dot_nn(grad_scores, keys) * SCALE
        dk_ref[seen, :] += dot_tn(grad_scores, q) * SCALE
        dv_ref[seen, :] += dot_tn(probs.astype(BF16), g)


def attend_back(q, k, v, g, log_sum):
    seq, width = q.shape
    heads = width // HEAD_DIM
    spec = pl.BlockSpec((seq, HEAD_DIM), lambda h: (0, h))
    return pl.pallas_call(
        attend_back_kernel,
        grid=(heads,),
        out_shape=tuple(jax.ShapeDtypeStruct((seq, width), F32) for _ in range(3)),
        in_specs=[spec] * 4 + [pl.BlockSpec((1, seq, 1), lambda h: (h, 0, 0))],
        out_specs=[spec] * 3,
        compiler_params=pltpu.CompilerParams(vmem_limit_bytes=VLIM),
        cost_estimate=pl.CostEstimate(
            flops=10 * seq * seq * width * 5 // 8, bytes_accessed=20 * seq * width,
            transcendentals=heads * seq * seq * 5 // 8,
        ),
        name="attend_back",
    )(q, k, v, g, log_sum)


def rms_parts(values_in):
    inverse = lax.rsqrt(jnp.mean(values_in * values_in, axis=-1, keepdims=True) + EPSILON)
    return (values_in * inverse, inverse)


def rms_back(grad_out, normed, inverse, gain_row):
    scaled = grad_out * gain_row
    grad_in = inverse * (scaled - normed * jnp.mean(scaled * normed, axis=-1, keepdims=True))
    return (grad_in, jnp.sum(grad_out * normed, axis=0))


def angles(positions):
    freqs = ROPE_BASE ** (-2.0 * jnp.arange(HEAD_DIM // 2, dtype=F32) / HEAD_DIM)
    turned = positions.astype(F32)[:, None] * freqs[None, :]
    return (jnp.cos(turned)[:, None, :], jnp.sin(turned)[:, None, :])


def rotate(values_in, cosine_table, sine_table):
    row_count, width = values_in.shape
    pieces = values_in.reshape(row_count, width // HEAD_DIM, HEAD_DIM)
    front = pieces[:, :, : HEAD_DIM // 2]
    behind = pieces[:, :, HEAD_DIM // 2 :]
    joined = jnp.concatenate(
        [front * cosine_table - behind * sine_table, behind * cosine_table + front * sine_table],
        axis=-1,
    )
    return joined.reshape(row_count, width)


def two_row_sums(first, second, number, name):
    seq = first.shape[0]
    packed = jnp.concatenate([first, second], axis=0).reshape(2 * seq // 128, 128)
    total = plane_sum(packed, number, name).reshape(2, seq, 1)
    return total[0], total[1]


def spread(x, fsdp):
    f = lax.axis_index("fsdp")
    lines = fsdp // 2
    pieces = [x]
    for k in range(1, lines):
        pieces.append(lax.ppermute(x, "fsdp", [(i, i ^ (2 * k)) for i in range(fsdp)]))
    own = jnp.stack(pieces)
    other = lax.ppermute(own, "fsdp", [(i, i ^ 1) for i in range(fsdp)])
    place, core = f // 2, f % 2
    both = jnp.where(core == 0, jnp.stack([own, other], axis=1), jnp.stack([other, own], axis=1))
    order = jnp.arange(lines, dtype=jnp.int32) ^ place
    return both[order].reshape((fsdp * x.shape[0],) + x.shape[1:])


def gather_back(partial, fsdp):
    f = lax.axis_index("fsdp")
    lines = fsdp // 2
    place, core = f // 2, f % 2
    pairs = partial.reshape((lines, 2) + partial.shape[1:])
    keep = lax.dynamic_index_in_dim(pairs, core, axis=1, keepdims=False)
    give = lax.dynamic_index_in_dim(pairs, 1 - core, axis=1, keepdims=False)
    got = lax.ppermute(give, "fsdp", [(i, i ^ 1) for i in range(fsdp)])
    both = (keep.astype(F32) + got.astype(F32)).astype(BF16)
    total = lax.dynamic_index_in_dim(both, place, axis=0, keepdims=False).astype(F32)
    for k in range(1, lines):
        piece = lax.dynamic_index_in_dim(both, place ^ k, axis=0, keepdims=False)
        moved = lax.ppermute(piece, "fsdp", [(i, i ^ (2 * k)) for i in range(fsdp)])
        total = total + moved.astype(F32)
    return total


def body(
    layer_input, output_grad, w_query, w_key, w_value, w_output, w_router, norm_gains,
    w_gate, w_up, w_down, expert_routes,
):
    fsdp, sp = lax.axis_size("fsdp"), lax.axis_size("sp")
    f, s = lax.axis_index("fsdp"), lax.axis_index("sp")
    count = fsdp * sp
    experts = EXP_DEV * fsdp
    capacity = TOK_DEV * TOP // experts * 17 // 16
    slots = -(-capacity // 16) * 16
    seq = TOK_DEV * sp
    cols = D // sp
    rows = D // count
    tokens = fsdp * TOK_DEV

    expert_set = (
        lax.all_gather(w_gate, "sp", axis=1, tiled=True),
        lax.all_gather(w_up, "sp", axis=1, tiled=True),
        lax.all_gather(w_down, "sp", axis=1, tiled=True),
    )
    grad_tok = spread(output_grad, fsdp)

    router_size = rows * experts
    misc = jnp.concatenate([w_router.reshape(router_size), norm_gains.reshape(4 * rows)])
    misc_rows = -(-misc.shape[0] // 2048) * 16
    misc = jnp.pad(misc, (0, misc_rows * 128 - misc.shape[0])).reshape(misc_rows, 128)
    routes = expert_routes.reshape(TOK_DEV * TOP // 128, 128)
    x_all, w_all, wo_s, misc_all, routes_all = gather_start(
        fsdp, sp, layer_input, jnp.stack([w_query, w_key, w_value]), w_output, misc, routes
    )
    misc_all = misc_all.reshape(count, misc_rows * 128)
    router_w = misc_all[:, :router_size].reshape(D, experts)
    gains_w = misc_all[:, router_size : router_size + 4 * rows].reshape(count, 4, rows)
    gains32 = gains_w.transpose(1, 0, 2).reshape(4, D).astype(F32)
    gains_own = lax.dynamic_slice_in_dim(gains32, s * cols, cols, axis=1)
    routes_tok = routes_all.reshape(tokens, TOP)

    normed_a, _ = rms_parts(x_all.astype(F32))
    first_in = (normed_a * gains32[0]).astype(BF16)
    q_raw = dot_nn(first_in, w_all[0])
    k_raw = dot_nn(first_in, w_all[1])
    values = dot_nn(first_in, w_all[2]).astype(BF16)
    q_square, k_square = two_row_sums(
        jnp.sum(q_raw * q_raw, axis=-1, keepdims=True),
        jnp.sum(k_raw * k_raw, axis=-1, keepdims=True),
        1,
        "norm_sums",
    )
    q_inverse = lax.rsqrt(q_square / D + EPSILON)
    k_inverse = lax.rsqrt(k_square / D + EPSILON)
    q_normed, k_normed = q_raw * q_inverse, k_raw * k_inverse
    cosine_table, sine_table = angles(jnp.arange(seq, dtype=jnp.int32))
    queries = rotate(q_normed * gains_own[2], cosine_table, sine_table).astype(BF16)
    keys = rotate(k_normed * gains_own[3], cosine_table, sine_table).astype(BF16)
    attended, log_sum = attend(queries, keys, values)
    branch = dot_nn(attended, wo_s).astype(BF16).reshape(sp, TOK_DEV, D)
    inputs = layer_input.astype(F32)
    mid = inputs + plane_reduce(sp, branch, 2, "branch_sum")
    normed_m, inverse_m = rms_parts(mid)
    second_in = (normed_m * gains32[1]).astype(BF16)

    second_tok = line_gather(fsdp, second_in, 3, "token_gather")
    logits = dot_nn(second_tok, router_w)
    exp_logits = jnp.exp(logits - jnp.max(logits, axis=1, keepdims=True))
    router_probs = exp_logits / jnp.sum(exp_logits, axis=1, keepdims=True)
    own_ids = f * EXP_DEV + jnp.arange(EXP_DEV, dtype=jnp.int32)
    chosen = jnp.any(routes_tok[:, :, None] == own_ids[None, None, :], axis=1)
    columns = jnp.arange(experts, dtype=jnp.int32)[:, None] == own_ids[None, :]
    gate_tok = jnp.sum(
        jnp.where(columns[None, :, :], router_probs[:, :, None], 0.0), axis=1
    )
    chosen_block = chosen.reshape(fsdp, TOK_DEV, EXP_DEV)
    before = jnp.arange(TOK_DEV)[:, None] > jnp.arange(TOK_DEV)[None, :]
    place = jnp.einsum(
        "ut,fte->fue", before.astype(BF16), chosen_block.astype(BF16), preferred_element_type=F32
    ).astype(jnp.int32)
    slot_ids = jnp.arange(slots, dtype=jnp.int32)
    picks = (
        (place.transpose(0, 2, 1)[:, :, None, :] == slot_ids[None, None, :, None])
        & chosen_block.transpose(0, 2, 1)[:, :, None, :]
    )
    picks_low = picks.astype(BF16)
    gate_block = gate_tok.reshape(fsdp, TOK_DEV, EXP_DEV).transpose(0, 2, 1)
    slot_gates = jnp.sum(jnp.where(picks, gate_block[:, :, None, :], 0.0), axis=3)
    slot_gates = slot_gates.transpose(1, 0, 2).reshape(EXP_DEV, fsdp * slots, 1)
    total = fsdp * slots

    def take(rows_in):
        return (
            jnp.einsum(
                "fect,ftd->efcd", picks_low, rows_in.reshape(fsdp, TOK_DEV, D),
                preferred_element_type=F32,
            )
            .astype(BF16)
            .reshape(EXP_DEV, total, D)
        )

    received = take(second_tok)
    grad_rows_in = take(grad_tok)
    gate_full, up_full, down_full = expert_set
    gate_pre = jnp.einsum("erd,edf->erf", received, gate_full, preferred_element_type=F32)
    up_pre = jnp.einsum("erd,edf->erf", received, up_full, preferred_element_type=F32)
    sigmoid_g = jax.nn.sigmoid(gate_pre)
    silu_g = gate_pre * sigmoid_g
    hidden = (silu_g * up_pre).astype(BF16)
    grad_expert = (slot_gates * grad_rows_in.astype(F32)).astype(BF16)
    grad_hidden = jnp.einsum("erd,efd->erf", grad_expert, down_full, preferred_element_type=F32)
    grad_gate_pre = (grad_hidden * up_pre * sigmoid_g * (1.0 + gate_pre * (1.0 - sigmoid_g))).astype(
        BF16
    )
    grad_up_pre = (grad_hidden * silu_g).astype(BF16)

    def shed(grad):
        return lax.psum_scatter(grad.astype(BF16), "sp", scatter_dimension=1, tiled=True).astype(F32)

    grad_down = shed(jnp.einsum("erf,erd->efd", hidden, grad_expert, preferred_element_type=F32))
    grad_gate = shed(jnp.einsum("erd,erf->edf", received, grad_gate_pre, preferred_element_type=F32))
    grad_up = shed(jnp.einsum("erd,erf->edf", received, grad_up_pre, preferred_element_type=F32))

    expert_out = jnp.einsum("erf,efd->erd", hidden, down_full, preferred_element_type=F32).astype(BF16)
    slot_dots = jnp.sum(expert_out.astype(F32) * grad_rows_in.astype(F32), axis=2)
    slot_dots = slot_dots.reshape(EXP_DEV, fsdp, 1, slots).transpose(1, 0, 3, 2)
    gate_grads = jnp.sum(jnp.where(picks, slot_dots, 0.0), axis=2)
    gate_grads = gate_grads.transpose(0, 2, 1).reshape(tokens, EXP_DEV)
    choice_grad = jnp.sum(jnp.where(columns[None, :, :], gate_grads[:, None, :], 0.0), axis=2)
    grad_logits = router_probs * (
        choice_grad - jnp.sum(router_probs * choice_grad, axis=1, keepdims=True)
    )
    logits_high = grad_logits.astype(BF16)
    logits_low = (grad_logits - logits_high.astype(F32)).astype(BF16)
    logits_two = jnp.concatenate([logits_high, logits_low], axis=1)
    router_two = jnp.einsum("td,te->de", second_tok, logits_two, preferred_element_type=F32)
    grad_router = router_two[:, :experts] + router_two[:, experts:]

    grad_rows = jnp.einsum("erf,edf->erd", grad_gate_pre, gate_full, preferred_element_type=F32)
    grad_rows = (
        grad_rows + jnp.einsum("erf,edf->erd", grad_up_pre, up_full, preferred_element_type=F32)
    ).astype(BF16)
    second_part = jnp.einsum(
        "fect,efcd->ftd", picks_low, grad_rows.reshape(EXP_DEV, fsdp, slots, D),
        preferred_element_type=F32,
    )
    second_part = second_part + jnp.einsum(
        "te,de->td", logits_two, jnp.concatenate([router_w, router_w], axis=1),
        preferred_element_type=F32,
    ).reshape(fsdp, TOK_DEV, D)
    grad_second = line_reduce(fsdp, second_part.astype(BF16), 4, "token_grads")

    out_part = jnp.zeros((fsdp, TOK_DEV, D), F32)
    for e in range(EXP_DEV):
        back = jnp.einsum(
            "fct,fcd->ftd", picks_low[:, e], expert_out[e].reshape(fsdp, slots, D),
            preferred_element_type=F32,
        )
        out_part = out_part + back * gate_block[:, e, :, None]
    layer_out = (mid + gather_back(out_part.astype(BF16), fsdp)).astype(BF16)

    grad_final = output_grad.astype(F32)
    grad_mid_norm, gain_m = rms_back(grad_second, normed_m, inverse_m, gains32[1])
    grad_mid = grad_final + grad_mid_norm
    grad_branch = plane_gather(sp, grad_mid.astype(BF16), 5, "branch_grads")
    grad_attended = dot_nt(grad_branch, wo_s).astype(BF16)
    grad_w_output = dot_tn(attended, grad_branch)
    grad_queries, grad_keys, grad_values = attend_back(queries, keys, values, grad_attended, log_sum)
    grad_q_normed = rotate(grad_queries, cosine_table, -sine_table)
    grad_k_normed = rotate(grad_keys, cosine_table, -sine_table)
    q_scaled, k_scaled = grad_q_normed * gains_own[2], grad_k_normed * gains_own[3]
    q_mean, k_mean = two_row_sums(
        jnp.sum(q_scaled * q_normed, axis=-1, keepdims=True),
        jnp.sum(k_scaled * k_normed, axis=-1, keepdims=True),
        6,
        "norm_grad_sums",
    )
    grad_q_low = (q_inverse * (q_scaled - q_normed * (q_mean / D))).astype(BF16)
    grad_k_low = (k_inverse * (k_scaled - k_normed * (k_mean / D))).astype(BF16)
    grad_v_low = grad_values.astype(BF16)
    gain_q = jnp.sum(grad_q_normed * q_normed, axis=0)
    gain_k = jnp.sum(grad_k_normed * k_normed, axis=0)
    grad_first = dot_nt(grad_q_low, w_all[0]) + dot_nt(grad_k_low, w_all[1])
    grad_first = (grad_first + dot_nt(grad_v_low, w_all[2])).astype(BF16)
    grad_first = plane_reduce(sp, grad_first.reshape(sp, TOK_DEV, D), 7, "input_grads")
    normed_own, inverse_own = rms_parts(inputs)
    grad_in_norm, gain_a = rms_back(grad_first, normed_own, inverse_own, gains32[0])
    input_grad = grad_mid + grad_in_norm

    parts = [
        dot_tn(first_in, low).astype(BF16).reshape(fsdp, D // fsdp, cols)
        for low in (grad_q_low, grad_k_low, grad_v_low)
    ]
    output_part = grad_w_output.astype(BF16).reshape(fsdp, rows, sp, cols).transpose(0, 2, 1, 3)
    parts.append(output_part.reshape(fsdp, sp * rows, cols))
    summed = line_reduce(fsdp, jnp.concatenate(parts, axis=1), 8, "weight_grads")
    height = D // fsdp
    qkv = summed[: 3 * height].reshape(3, height, cols)
    out_rows = summed[3 * height :].reshape(sp, rows, cols).transpose(1, 0, 2).reshape(rows, D)
    wide = jnp.zeros((2, D), F32)
    wide = lax.dynamic_update_slice(wide, jnp.stack([gain_q, gain_k]), (0, s * cols))
    gain_rows = jnp.concatenate([jnp.stack([gain_a, gain_m]), wide], axis=0)
    small = jnp.concatenate(
        [
            grad_router.reshape(count, router_size),
            gain_rows.reshape(4, count, rows).transpose(1, 0, 2).reshape(count, 4 * rows),
        ],
        axis=1,
    )
    small = jnp.pad(small, ((0, 0), (0, misc_rows * 128 - small.shape[1])))
    qkv_own, grad_output, small_all = exchange_end(
        fsdp, sp, qkv, out_rows, small.reshape(count, misc_rows, 128), 9
    )
    qkv_own = qkv_own.transpose(1, 2, 0, 3).reshape(3, rows, D)
    small_sum = jnp.sum(small_all, axis=0).reshape(misc_rows * 128)
    grad_router_own = small_sum[:router_size].reshape(rows, experts)
    grad_gains = small_sum[router_size : router_size + 4 * rows].reshape(4, rows)
    return (
        layer_out, input_grad, qkv_own[0], qkv_own[1], qkv_own[2], grad_output,
        grad_router_own, grad_gains, grad_gate, grad_up, grad_down,
    )


def solution(mesh):
    both, split = P(("fsdp", "sp"), None), P("fsdp", "sp", None)
    gains = P(None, ("fsdp", "sp"))
    return jax.shard_map(
        body,
        mesh=mesh,
        in_specs=(both,) * 7 + (gains,) + (split,) * 3 + (both,),
        out_specs=(both,) * 7 + (gains,) + (split,) * 3,
        check_vma=False,
    )
```

time: 3540 us -> 1300 us (0.37)
  waiting for transfers between devices: 2480 us -> 1.47 us
  Pallas kernels: 0 us -> 745 us
  blocking collectives: 305 us -> 0 us
  matrix products: 425 us -> 295 us
  local copies, waits for them, and re-layouts: 182 us -> 119 us
    reduce_scatter x7 -> x3, waiting for transfers between devices: 1640 us -> 0.01 us  [shed(): lax.psum_scatter(grad.astype(BF16), 'sp', scatter_dimension=1, tiled=True)]
    pallas_call x0 -> x12, Pallas kernels: none -> 745 us  [the longest x2 263 us: line_reduce(): pl.pallas_call(functools.partial(line_reduce_kernel, fsdp), out_shape=jax...]
    all_to_all x4 -> x0, waiting for transfers between devices: 409 us -> none  [the longest x1 160 us: body(): lax.all_to_all(grad_rows, 'fsdp', split_axis=0, concat_axis=0, tiled=True)]
    all_gather x4 -> x0, blocking collectives: 305 us -> none  [the longest x1 235 us: body(): lax.all_gather(w_router, ('fsdp', 'sp'), axis=0, tiled=True)]
    all_gather x8 -> x0, waiting for transfers between devices: 253 us -> none  [the longest x1 68 us: body(): lax.all_gather(w_key, ('fsdp', 'sp'), axis=0, tiled=True)]
    dot_general x151 -> x30, matrix products: 423 us -> 295 us  [the longest x5 28.7 us: dot_nn(): return jnp.dot(a, b, preferred_element_type=F32)]
    unnamed x22 -> x6, waiting for transfers between devices: 121 us -> 1.44 us
    gather x9 -> x3, local copies, waits for them, and re-layouts: 80.5 us -> 13.9 us  [spread(): return both[order].reshape((fsdp * x.shape[0],) + x.shape[1:])]
  transfers between devices with their start and end apart: 24 -> 14, of which waited for: 18 -> 0; matrix products, arithmetic and copies ran while one was open for 17% -> 36% of each run, Pallas kernels for 0% -> 58%
where the time goes in v1:
time: 1300 us; the launch traced here: 1290 us
  Pallas kernels  745 us (57%)
  matrix products  295 us (23%)
  local copies, waits for them, and re-layouts  119 us (9%)
  other arithmetic  106 us (8%)
  between operations  15.7 us (1%)
    pallas_call x2, Pallas kernels, line_reduce(): pl.pallas_call(functools.partial(line_reduce_kernel, fsdp), out_shape=jax...  263 us
    pallas_call x1, Pallas kernels, gather_start(): pl.pallas_call(functools.partial(start_kernel, fsdp, sp), out_shape=(jax....  161 us
    pallas_call x1, Pallas kernels, line_gather(): pl.pallas_call(functools.partial(line_gather_kernel, fsdp, parts), out_sh...  102 us
    pallas_call x2, Pallas kernels, plane_reduce(): pl.pallas_call(plane_reduce_kernel, out_shape=jax.ShapeDtypeStruct(block,...  96.4 us
    pallas_call x1, Pallas kernels, exchange_end(): pl.pallas_call(functools.partial(end_kernel, fsdp, sp), out_shape=(jax.Sh...  46.8 us
    pallas_call x1, Pallas kernels, plane_gather(): pl.pallas_call(plane_gather_kernel, out_shape=jax.ShapeDtypeStruct((sp *...  38.3 us
    unnamed x171, local copies, waits for them, and re-layouts  32.4 us
    dot_general x5, matrix products, dot_nn(): return jnp.dot(a, b, preferred_element_type=F32)  28.7 us
  transfers between devices with their start and end apart: 14, of which 0 were waited for; matrix products, arithmetic and copies ran while one was open for 36% of the time, Pallas kernels for 58%

profile of v1, /device:TPU:12, one launch (start us, length us, event | category | flops | bytes accessed | tf_op | source)
XLA Modules:
  0.0 1289.1 jit_solution(9902590683121606461)
XLA Ops:
  15.1 160.5 %gather_start.1 = (bf16[1024,2048]{1,0:T(8,128)(2,1)}, bf16[3,2048,512]{2,1,0:T(8,128)(2,1)}, bf16[512,2048]{1,0:T(8,128)(2,1)}, bf16[32,16,128]{2,1,0:T(8,128)(2,1)}, s32[8,16,128]{2,1,0:T(8,128)}) custom-call(bf16[256,2048]{1,0:T(8,128)(2,1)} %x_ref.1, bf16[3,64,2048]{2,1,0:T(8,128)(2,1)} %pad_maximum_fusion.7.w_ref, bf16[64,2048]{1,0:T(8,128)(2,1)} %wo_ref.1, ...), custom_call_target="tpu_custom_call" | custom-call | tf_op jit(solution)/shard_map/gather_start/pallas_call | solution.py:314
  179.1 5.5 multiply_reduce_fusion.6
  184.6 6.7 multiply_reduce_fusion.5
  192.0 6.3 norm_sums.1
  226.4 5.0 fusion.43.v_ref
  231.4 11.2 attend.1
  242.6 5.7 convolution_convert_fusion.4
  248.3 63.9 %branch_sum.1 = f32[256,2048]{1,0:T(8,128)} custom-call(bf16[4,256,2048]{2,1,0:T(8,128)(2,1)} %bitcast.263), custom_call_target="tpu_custom_call" | custom-call | tf_op jit(solution)/shard_map/branch_sum/pallas_call | solution.py:589
  312.3 5.2 fusion.72
  320.6 102.1 %token_gather.1 = bf16[2048,2048]{1,0:T(8,128)(2,1)} custom-call(bf16[256,2048]{1,0:T(8,128)(2,1)} %multiply_convert_fusion.5.x_ref), custom_call_target="tpu_custom_call" | custom-call | tf_op jit(solution)/shard_map/token_gather/pallas_call | solution.py:362
  423.9 8.8 convert_bitcast_fusion.1
  432.7 9.3 copy.107
  442.4 5.9 fusion.86
  449.1 8.1 maximum_select_fusion
  461.1 5.0 gather_fusion
  466.1 5.0 gather_fusion.1
  471.2 8.2 pad_maximum_fusion
  479.4 11.4 convert_bitcast_fusion
  490.8 12.9 %copy.110 = f32[2,8,144,2048]{3,2,1,0:T(8,128)} copy(f32[2,8,144,2048]{3,2,0,1:T(8,128)} %convert_bitcast_fusion) | data formatting | bytes 37748736 | tf_op jit(solution)/shard_map/convert_element_type | solution.py:992
  503.7 17.2 %fusion.87 = f32[2,1152,1024]{2,1,0:T(8,128)} fusion(bf16[2,1152,2048]{2,1,0:T(8,128)(2,1)} %bitcast.253, bf16[2,2048,1024]{2,1,0:T(8,128)(2,1)} %all-gather.4.cloned.1.call-done), kind=kOutput, calls=%fused_computation.195 | convolution fusion | flops 9663676416 | bytes 27262976 | tf_op jit(solution)/shard_map/erd,edf->erf/dot_general | solution.py:987
  520.9 19.8 %multiply_convert_fusion.2 = (bf16[2,1152,1024]{2,1,0:T(8,128)(2,1)}, f32[2,1152,1024]{2,1,0:T(8,128)}) fusion(f32[2,1152,1024]{2,1,0:T(8,128)} %fusion.87, bf16[2,1152,2048]{2,1,0:T(8,128)(2,1)} %bitcast.254, bf16[2,2048,1024]{2,1,0:T(8,128)(2,1)} %all-gather.6.cloned.1.call-done), kind=kOutput, calls=%fused_computation.16 | convolution fusion | flops 9677832192 | bytes 41418752 | tf_op jit(solution)/shard_map/erd,edf->erf/dot_general | solution.py:988
  540.7 19.1 %fusion.1 = (f32[2,1152]{1,0:T(2,128)S(1)}, bf16[2,1152,2048]{2,1,0:T(8,128)(2,1)}) fusion(f32[2,8,144,2048]{3,2,1,0:T(8,128)} %copy.110, bf16[2,1152,1024]{2,1,0:T(8,128)(2,1)} %get-tuple-element.136, bf16[2,1024,2048]{2,1,0:T(8,128)(2,1)} %all-gather.8.cloned.1.call-done), kind=kOutput, calls=%fused_computation.5 | convolution fusion | flops 9682548736 | bytes 41427968 | tf_op jit(solution)/shard_map/erf,efd->erd/dot_general | solution.py:1006
  561.5 7.8 fusion
  573.0 13.6 %convolution_convert_fusion.1 = bf16[2,1024,2048]{2,1,0:T(8,128)(2,1)} fusion(bf16[2,1152,1024]{2,1,0:T(8,128)(2,1)S(1)} %copy-done.69, bf16[2,1152,2048]{2,1,0:T(8,128)(2,1)S(1)} %fusion), kind=kOutput, calls=%fused_computation.29 | convolution fusion | flops 9667870720 | bytes 22544384 | tf_op jit(solution)/shard_map/erf,erd->efd/dot_general | solution.py:1002
  586.7 21.2 %multiply_convert_fusion = (bf16[2,1152,1024]{2,1,0:T(8,128)(2,1)}, bf16[2,1152,1024]{2,1,0:T(8,128)(2,1)}) fusion(f32[2,1152,1024]{2,1,0:T(8,128)} %fusion.87, f32[2,1152,1024]{2,1,0:T(8,128)} %get-tuple-element.137, bf16[2,1152,2048]{2,1,0:T(8,128)(2,1)} %copy-done.12, bf16[2,1024,2048]{2,1,0:T(8,128)(2,1)} %all-gather.8.cloned.1.call-done), kind=kOutput, calls=%fused_computation.14 | convolution fusion | flops 9694347264 | bytes 46137344 | tf_op jit(solution)/shard_map/erd,efd->erf/dot_general | solution.py:993
  607.9 17.4 %convolution_convert_fusion.3 = bf16[2,2048,1024]{2,1,0:T(8,128)(2,1)} fusion(bf16[2,1152,2048]{2,1,0:T(8,128)(2,1)} %bitcast.255, bf16[2,1152,1024]{2,1,0:T(8,128)(2,1)} %get-tuple-element.83), kind=kOutput, calls=%fused_computation.31 | convolution fusion | flops 9667870720 | bytes 22544384 | tf_op jit(solution)/shard_map/erd,erf->edf/dot_general | solution.py:1003
  628.4 8.3 fusion.53
  636.7 16.3 %fusion.88 = f32[2,1152,2048]{2,1,0:T(8,128)} fusion(bf16[2,1152,1024]{2,1,0:T(8,128)(2,1)S(1)} %bitcast.321, bf16[2,2048,1024]{2,1,0:T(8,128)(2,1)} %all-gather.4.cloned.1.call-done), kind=kOutput, calls=%fused_computation.196 | convolution fusion | flops 9663676416 | bytes 31981568 | tf_op jit(solution)/shard_map/erf,edf->erd/dot_general | solution.py:1021
  653.0 19.2 %add_convert_fusion = bf16[2,1152,2048]{2,1,0:T(8,128)(2,1)} fusion(f32[2,1152,2048]{2,1,0:T(8,128)} %fusion.88, bf16[2,1152,1024]{2,1,0:T(8,128)(2,1)} %get-tuple-element.82, bf16[2,2048,1024]{2,1,0:T(8,128)(2,1)} %all-gather.6.cloned.1.call-done), kind=kOutput, calls=%fused_computation.7 | convolution fusion | flops 9673113600 | bytes 41418752 | tf_op jit(solution)/shard_map/erf,edf->erd/dot_general | solution.py:1023
  672.2 13.2 %fusion.2.p_ref = bf16[8,256,2048]{2,1,0:T(8,128)(2,1)} fusion(f32[8,256,2048]{2,1,0:T(8,128)} %bitcast.244, bf16[2,8,144,2048]{3,2,1,0:T(8,128)(2,1)} %bitcast.251, s32[8,2,256]{2,0,1:T(8,128)S(1)} %convolution_convert_fusion.10, pred[8,2,256]{2,0,1:T(8,128)(4,1)S(1)} %bitcast.283), kind=kOutput, calls=%fused_computation.9 | convolution fusion | flops 2425487360 | bytes 34623488 | tf_op jit(solution)/shard_map/fect,efcd->ftd/dot_general | solution.py:1025
  685.4 108.4 %token_grads.1 = f32[256,2048]{1,0:T(8,128)} custom-call(bf16[8,256,2048]{2,1,0:T(8,128)(2,1)} %fusion.2.p_ref), custom_call_target="tpu_custom_call" | custom-call | tf_op jit(solution)/shard_map/token_grads/pallas_call | solution.py:476
  798.0 38.3 %branch_grads.1 = bf16[1024,2048]{1,0:T(8,128)(2,1)} custom-call(bf16[256,2048]{1,0:T(8,128)(2,1)} %fusion.70.x_ref), custom_call_target="tpu_custom_call" | custom-call | tf_op jit(solution)/shard_map/branch_grads/pallas_call | solution.py:528
  836.3 17.3 %convolution_convert_fusion.2 = bf16[2,2048,1024]{2,1,0:T(8,128)(2,1)} fusion(bf16[2,1152,2048]{2,1,0:T(8,128)(2,1)} %bitcast.256, bf16[2,1152,1024]{2,1,0:T(8,128)(2,1)} %get-tuple-element.82), kind=kOutput, calls=%fused_computation.30 | convolution fusion | flops 9667870720 | bytes 22544384 | tf_op jit(solution)/shard_map/erd,erf->edf/dot_general | solution.py:1004
  853.6 6.2 convolution_convert_fusion.9.g_ref
  859.8 14.0 %attend_back.1 = (f32[1024,512]{1,0:T(8,128)}, f32[1024,512]{1,0:T(8,128)}, f32[1024,512]{1,0:T(8,128)}) custom-call(bf16[1024,512]{1,0:T(8,128)(2,1)} %bitcast.278, bf16[1024,512]{1,0:T(8,128)(2,1)} %bitcast.276, bf16[1024,512]{1,0:T(8,128)(2,1)} %fusion.43.v_ref, bf16[1024,512]{1,0:T(8,128)(2,1)} %convolution_convert_fusion.9.g_ref, ...), custom_call_target="tpu_custom_call" | custom-call | flops 3355443200 | bytes 10485760 | tf_op jit(solution)/shard_map/attend_back/pallas_call | solution.py:805
  879.7 7.6 multiply_subtract_fusion
  906.0 6.0 norm_grad_sums.1
  912.0 6.9 convolution_convert_fusion.5
  926.9 7.7 fusion.79
  934.6 8.2 fusion.46
  942.9 9.1 add_convert_fusion.1
  961.4 5.7 fusion.27
  967.1 5.7 fusion.31
  985.4 10.8 add_convert_fusion.2
  1007.5 154.6 %weight_grads.1 = f32[1024,512]{1,0:T(8,128)} custom-call(bf16[8,1024,512]{2,1,0:T(8,128)(2,1)} %pad_maximum_fusion.1.p_ref), custom_call_target="tpu_custom_call" | custom-call | tf_op jit(solution)/shard_map/weight_grads/pallas_call | solution.py:476
  1169.9 32.5 %input_grads.1 = f32[256,2048]{1,0:T(8,128)} custom-call(bf16[4,256,2048]{2,1,0:T(8,128)(2,1)} %bitcast.250), custom_call_target="tpu_custom_call" | custom-call | tf_op jit(solution)/shard_map/input_grads/pallas_call | solution.py:589
  1208.1 46.8 %exchange_end.1 = (f32[4,3,64,512]{3,2,1,0:T(8,128)}, f32[64,2048]{1,0:T(8,128)}, f32[32,16,128]{2,1,0:T(8,128)}) custom-call(f32[3,256,512]{2,1,0:T(8,128)} %bitcast.260, f32[64,2048]{1,0:T(8,128)} %bitcast.269, f32[32,16,128]{2,1,0:T(8,128)} %bitcast.274), custom_call_target="tpu_custom_call" | custom-call | tf_op jit(solution)/shard_map/exchange_end/pallas_call | solution.py:722
  1262.8 5.9 fusion.15
  (315 shorter events, 161.9 us)
Async XLA Ops:
  7.2 6.3 copy-start.68
  7.2 6.9 copy-start.35
  7.2 6.9 copy-start.34
  7.2 6.9 copy-start.33
  7.3 496.4 %all-gather.4.cloned.1.call-start = ((), (), s32[]{:S(2)}) async-start(), calls=%async_computation.3 | async-start | bytes 10485760 | tf_op jit(solution)/shard_map/all_gather | solution.py:903
  8.0 512.9 %all-gather.6.cloned.1.call-start = ((), (), s32[]{:S(2)}) async-start(), calls=%async_computation.4 | async-start | bytes 10485760 | tf_op jit(solution)/shard_map/all_gather | solution.py:904
  8.7 532.0 %all-gather.8.cloned.1.call-start = ((), (), s32[]{:S(2)}) async-start(), calls=%async_computation.5 | async-start | bytes 10485760 | tf_op jit(solution)/shard_map/all_gather | solution.py:905
  8.8 303.4 %collective-permute-start.4 = (bf16[256,2048]{1,0:T(8,128)(2,1)S(1)}, bf16[256,2048]{1,0:T(8,128)(2,1)}, u32[]{:S(2)}, u32[]{:S(2)}) collective-permute-start(bf16[256,2048]{1,0:T(8,128)(2,1)S(1)} %copy-done.13), channel_id=1, source_target_pairs={{0,8},{4,12},{8,0},{12,4},{16,24},{20,28},{24,16},{28,20},{1,9},{5... | collective-permute-start | bytes 3145736 | tf_op jit(solution)/shard_map/ppermute | solution.py:861
  9.3 302.9 %collective-permute-start.5 = (bf16[256,2048]{1,0:T(8,128)(2,1)S(1)}, bf16[256,2048]{1,0:T(8,128)(2,1)}, u32[]{:S(2)}, u32[]{:S(2)}) collective-permute-start(bf16[256,2048]{1,0:T(8,128)(2,1)S(1)} %copy-done.13), channel_id=1, source_target_pairs={{0,16},{4,20},{8,24},{12,28},{16,0},{20,4},{24,8},{28,12},{1,17},{... | collective-permute-start | bytes 3145736 | tf_op jit(solution)/shard_map/ppermute | solution.py:861
  11.9 300.4 %collective-permute-start.6 = (bf16[256,2048]{1,0:T(8,128)(2,1)S(1)}, bf16[256,2048]{1,0:T(8,128)(2,1)}, u32[]{:S(2)}, u32[]{:S(2)}) collective-permute-start(bf16[256,2048]{1,0:T(8,128)(2,1)S(1)} %copy-done.13), channel_id=1, source_target_pairs={{0,24},{4,28},{8,16},{12,20},{16,8},{20,12},{24,0},{28,4},{1,25},{... | collective-permute-start | bytes 3145736 | tf_op jit(solution)/shard_map/ppermute | solution.py:861
  12.4 1256.4 %reduce-scatter.8.cloned.1.call-start = ((), (), s32[]{:S(2)}) async-start(), calls=%async_computation.8 | async-start | bytes 10485760 | tf_op jit(solution)/shard_map/reduce_scatter | solution.py:1000
  178.8 47.6 %copy-start.63 = (f32[1024]{0:T(1024)}, f32[1024]{0:T(1024)S(1)}, u32[]{:S(2)}) copy-start(f32[1024]{0:T(1024)S(1)} %add_rsqrt_fusion) | copy-start | bytes 12292
  179.1 47.3 %copy-start.43 = (f32[2048]{0:T(1024)}, f32[2048]{0:T(1024)S(1)}, u32[]{:S(2)}) copy-start(f32[2048]{0:T(1024)S(1)} %mul.515) | copy-start | bytes 24580
  184.6 14.5 %copy-start.3 = (f32[1024,512]{0,1:T(8,128)}, f32[1024,512]{0,1:T(8,128)S(1)}, u32[]{:S(2)}) copy-start(f32[1024,512]{0,1:T(8,128)S(1)} %get-tuple-element.133) | copy-start | bytes 6291460
  199.0 7.4 copy-start.47
  199.1 7.3 copy-start.52
  208.2 8.5 copy-start.16
  231.4 11.2 copy-start.67
  317.5 131.7 %collective-permute-start.7 = (bf16[4,256,2048]{2,1,0:T(8,128)(2,1)}, bf16[4,256,2048]{2,1,0:T(8,128)(2,1)}, u32[]{:S(2)}, u32[]{:S(2)}) collective-permute-start(bf16[4,256,2048]{2,1,0:T(8,128)(2,1)} %get-tuple-element.93), channel_id=1, source_target_pairs={{0,4},{4,0},{8,12},{12,8},{16,20},{20,16},{24,28},{28,24},{1,5},{5... | collective-permute-start | bytes 12582920 | tf_op jit(solution)/shard_map/ppermute | solution.py:863
  318.6 104.1 %copy-start = (f32[256,2048]{1,0:T(8,128)}, f32[256,2048]{1,0:T(8,128)S(1)}, u32[]{:S(2)}) copy-start(f32[256,2048]{1,0:T(8,128)S(1)} %get-tuple-element.81) | copy-start | bytes 6291460
  318.7 104.0 %copy-start.36 = (f32[2048]{0:T(1024)}, f32[2048]{0:T(1024)S(1)}, u32[]{:S(2)}) copy-start(f32[2048]{0:T(1024)S(1)} %mul.548) | copy-start | bytes 24580
  320.6 102.1 %copy-start.49 = (s32[8,16,128]{2,1,0:T(8,128)S(1)}, s32[8,16,128]{2,1,0:T(8,128)}, u32[]{:S(2)}) copy-start(s32[8,16,128]{2,1,0:T(8,128)} %get-tuple-element.29) | copy-start | bytes 196612
  448.3 9.0 copy-start.38
  448.3 8.9 copy-start.40
  448.9 8.4 copy-start.65
  561.5 11.5 copy-start.69
  586.6 686.2 %reduce-scatter.4.cloned.1.call-start = ((), (), s32[]{:S(2)}) async-start(), calls=%async_computation.6 | async-start | bytes 10485760 | tf_op jit(solution)/shard_map/reduce_scatter | solution.py:1000
  625.3 651.6 %reduce-scatter.6.cloned.1.call-start = ((), (), s32[]{:S(2)}) async-start(), calls=%async_computation.7 | async-start | bytes 10485760 | tf_op jit(solution)/shard_map/reduce_scatter | solution.py:1000
  627.7 9.0 slice-start.4
  628.3 8.3 copy-start.28
  628.4 8.3 copy-start.30
  628.4 8.3 slice-start.5
  685.4 108.4 %copy-start.1 = (f32[256,2048]{1,0:T(8,128)S(1)}, f32[256,2048]{1,0:T(8,128)}, u32[]{:S(2)}) copy-start(f32[256,2048]{1,0:T(8,128)} %copy-done) | copy-start | bytes 6291460
  685.4 108.5 %copy-start.37 = (f32[2048]{0:T(1024)S(1)}, f32[2048]{0:T(1024)}, u32[]{:S(2)}) copy-start(f32[2048]{0:T(1024)} %copy-done.36) | copy-start | bytes 24580
  685.4 108.5 %copy-start.58 = (f32[256]{0:T(256)S(1)}, f32[256]{0:T(256)}, u32[]{:S(2)}) copy-start(f32[256]{0:T(256)} %copy-done.57) | copy-start | bytes 3076
  892.9 7.8 copy-start.46
  892.9 7.8 copy-start.48
  892.9 7.8 copy-start.51
  892.9 7.8 copy-start.53
  934.6 8.3 copy-start.55
  934.6 8.3 copy-start.56
  942.9 11.6 copy-start.54
  954.4 41.7 %collective-permute-start = (bf16[4,256,2048]{2,1,0:T(8,128)(2,1)}, bf16[4,256,2048]{2,1,0:T(8,128)(2,1)}, u32[]{:S(2)}, u32[]{:S(2)}) collective-permute-start(bf16[4,256,2048]{2,1,0:T(8,128)(2,1)} %dynamic-slice_bitcast_fusion), channel_id=1, source_target_pairs={{0,4},{4,0},{8,12},{12,8},{16,20},{20,16},{24,28},{28,24},{1,5},{5... | collective-permute-start | bytes 12582920 | tf_op jit(solution)/shard_map/ppermute | solution.py:877
  1004.0 258.8 %collective-permute-start.1 = (bf16[256,2048]{1,0:T(8,128)(2,1)}, bf16[256,2048]{1,0:T(8,128)(2,1)}, u32[]{:S(2)}, u32[]{:S(2)}) collective-permute-start(bf16[256,2048]{1,0:T(8,128)(2,1)} %get-tuple-element.94), channel_id=1, source_target_pairs={{0,8},{4,12},{8,0},{12,4},{16,24},{20,28},{24,16},{28,20},{1,9},{5... | collective-permute-start | bytes 3145736 | tf_op jit(solution)/shard_map/ppermute | solution.py:882
  1004.0 258.8 %collective-permute-start.2 = (bf16[256,2048]{1,0:T(8,128)(2,1)}, bf16[256,2048]{1,0:T(8,128)(2,1)}, u32[]{:S(2)}, u32[]{:S(2)}) collective-permute-start(bf16[256,2048]{1,0:T(8,128)(2,1)} %get-tuple-element.96), channel_id=1, source_target_pairs={{0,16},{4,20},{8,24},{12,28},{16,0},{20,4},{24,8},{28,12},{1,17},{... | collective-permute-start | bytes 3145736 | tf_op jit(solution)/shard_map/ppermute | solution.py:882
  1006.1 256.7 %collective-permute-start.3 = (bf16[256,2048]{1,0:T(8,128)(2,1)}, bf16[256,2048]{1,0:T(8,128)(2,1)}, u32[]{:S(2)}, u32[]{:S(2)}) collective-permute-start(bf16[256,2048]{1,0:T(8,128)(2,1)} %get-tuple-element.95), channel_id=1, source_target_pairs={{0,24},{4,28},{8,16},{12,20},{16,8},{20,12},{24,0},{28,4},{1,25},{... | collective-permute-start | bytes 3145736 | tf_op jit(solution)/shard_map/ppermute | solution.py:882
  1166.6 35.8 %copy-start.10 = (bf16[256,2048]{1,0:T(8,128)(2,1)S(1)}, bf16[256,2048]{1,0:T(8,128)(2,1)}, u32[]{:S(2)}) copy-start(bf16[256,2048]{1,0:T(8,128)(2,1)} %x_ref.1) | copy-start | bytes 3145732
  1166.6 35.8 %copy-start.59 = (f32[256]{0:T(256)S(1)}, f32[256]{0:T(256)}, u32[]{:S(2)}) copy-start(f32[256]{0:T(256)} %add_rsqrt_fusion.1) | copy-start | bytes 3076
  (42 other events, 148.7 us)
Sparse Core Ops, SparseCore 0:
  9.9 134.0 all-gather.3
  145.9 86.1 all-gather.5
  233.9 113.1 all-gather.7
  586.7 88.3 reduce-scatter.7
  678.3 86.4 reduce-scatter.3
  853.7 85.2 reduce-scatter.5

commit v2 on v1

v2 whole, which is shorter than its diff:
```python
import functools

import jax
import jax.numpy as jnp
from jax import lax
from jax.experimental import pallas as pl
from jax.experimental.pallas import tpu as pltpu
from jax.sharding import PartitionSpec as P

D = 2048
HEADS = 16
HEAD_DIM = 128
TOP = 8
EXP_DEV = 2
BLK = 256
TOK_DEV = 256
EPSILON = 1e-05
ROPE_BASE = 10000.0
MASKED = -1000000000.0
SCALE = HEAD_DIM ** (-0.5)
MESH = pl.DeviceIdType.MESH
ANY = pl.BlockSpec(memory_space=pl.ANY)
VMEM = pl.BlockSpec(memory_space=pltpu.VMEM)
VLIM = 60 * 1024 * 1024
F32 = jnp.float32
BF16 = jnp.bfloat16


def remote(src, dst, send_sem, recv_sem, device):
    return pltpu.make_async_remote_copy(
        src_ref=src,
        dst_ref=dst,
        send_sem=send_sem,
        recv_sem=recv_sem,
        device_id=device,
        device_id_type=MESH,
    )


def landed(ref, sem):
    pltpu.make_async_copy(ref, ref, sem).wait()


def signal(sem, device):
    pl.semaphore_signal(sem, inc=1, device_id=device, device_id_type=MESH)


def greet_line(barrier, lines, f, s):
    place, core = f // 2, f % 2
    signal(barrier, (f + 1 - 2 * core, s))

    @pl.when(place > 0)
    def _():
        signal(barrier, (f - 2, s))

    @pl.when(place < lines - 1)
    def _():
        signal(barrier, (f + 2, s))

    return 1 + jnp.where(place > 0, 1, 0) + jnp.where(place < lines - 1, 1, 0)


class LineGather:
    def __init__(self, views, owns, lines, f, s, send, recv):
        self.views, self.owns, self.lines, self.f, self.s = views, owns, lines, f, s
        self.send, self.recv = send, recv
        self.place, self.core = f // 2, f % 2

    def copy(self, v, block, slot, way):
        device = {
            "right": (self.f + 2, self.s),
            "left": (self.f - 2, self.s),
            "partner": (self.f + 1 - 2 * self.core, self.s),
        }[way]
        index = {"right": 0, "left": 1, "partner": 2}[way]
        ref = self.views[v](block)
        own = self.owns[v] if slot == 0 and self.owns[v] is not None else ref
        return remote(own, ref, self.send.at[v, slot, index], self.recv.at[v, block], device)

    def start_own(self, v):
        @pl.when(self.place < self.lines - 1)
        def _():
            self.copy(v, self.f, 0, "right").start()

        @pl.when(self.place > 0)
        def _():
            self.copy(v, self.f, 0, "left").start()

        self.copy(v, self.f, 0, "partner").start()

    def forward(self, v, k):
        place, lines = self.place, self.lines

        @pl.when(place >= k)
        def _():
            block = self.f - 2 * k
            landed(self.views[v](block), self.recv.at[v, block])

            @pl.when(place < lines - 1)
            def _():
                self.copy(v, block, k, "right").start()

            self.copy(v, block, k, "partner").start()

        @pl.when(place + k < lines)
        def _():
            block = self.f + 2 * k
            landed(self.views[v](block), self.recv.at[v, block])

            @pl.when(place > 0)
            def _():
                self.copy(v, block, lines - 1 + k, "left").start()

            self.copy(v, block, lines - 1 + k, "partner").start()

    def finish(self, v):
        place, lines = self.place, self.lines
        for line in range(lines):
            block = 2 * line + 1 - self.core
            landed(self.views[v](block), self.recv.at[v, block])
        self.copy(v, self.f, 0, "partner").wait_send()

        @pl.when(place < lines - 1)
        def _():
            self.copy(v, self.f, 0, "right").wait_send()

        @pl.when(place > 0)
        def _():
            self.copy(v, self.f, 0, "left").wait_send()

        for k in range(1, lines):

            @pl.when(place >= k)
            def _():
                block = self.f - 2 * k

                @pl.when(place < lines - 1)
                def _():
                    self.copy(v, block, k, "right").wait_send()

                self.copy(v, block, k, "partner").wait_send()

            @pl.when(place + k < lines)
            def _():
                block = self.f + 2 * k

                @pl.when(place > 0)
                def _():
                    self.copy(v, block, lines - 1 + k, "left").wait_send()

                self.copy(v, block, lines - 1 + k, "partner").wait_send()


def line_sems(arrays, fsdp):
    lines = fsdp // 2
    return [
        pltpu.SemaphoreType.DMA((arrays, 2 * lines, 3)),
        pltpu.SemaphoreType.DMA((arrays, fsdp)),
    ]


def add_rows(dst, a, b, rows):
    def step(i, carry):
        at = pl.ds(pl.multiple_of(i * 32, 32), 32)
        dst[at, :] = a[at, :].astype(dst.dtype) + b[at, :].astype(dst.dtype)
        return carry

    lax.fori_loop(0, rows // 32, step, 0)


class LineReduce:
    def __init__(self, p_ref, scratch, lines, f, s):
        self.p_ref, self.lines, self.f, self.s = p_ref, lines, f, s
        self.own, self.paired, self.got, self.last = scratch[:4]
        self.psend, self.precv, self.send, self.recv, self.final, self.local = scratch[4:]
        self.place, self.core = f // 2, f % 2
        self.rows = p_ref.shape[1]
        self.order = []
        for n in range(lines):
            for d in (lines - 1 - n, n):
                if d not in self.order:
                    self.order.append(d)

    @staticmethod
    def scratch(fsdp, block):
        lines = fsdp // 2
        dma = pltpu.SemaphoreType.DMA
        return [
            pltpu.VMEM((lines,) + block, BF16),
            pltpu.VMEM((lines,) + block, BF16),
            pltpu.VMEM((lines,) + block, BF16),
            pltpu.VMEM(block, BF16),
            dma((lines,)), dma((lines,)), dma((lines,)), dma((lines,)), dma, dma((lines,)),
        ]

    def load(self, i):
        return pltpu.make_async_copy(self.p_ref.at[2 * i + self.core], self.own.at[i], self.local.at[i])

    def swap(self, i):
        return remote(
            self.p_ref.at[2 * i + 1 - self.core], self.paired.at[i], self.psend.at[i],
            self.precv.at[i], (self.f + 1 - 2 * self.core, self.s),
        )

    def right(self, d, last):
        dst = self.last if last else self.got.at[d]
        sem = self.final if last else self.recv.at[d]
        return remote(self.own.at[d], dst, self.send.at[d], sem, (self.f + 2, self.s))

    def left(self, d):
        return remote(
            self.own.at[d], self.got.at[d], self.send.at[d], self.recv.at[d], (self.f - 2, self.s)
        )

    def start(self):
        for i in self.order:
            self.swap(i).start()
        for i in self.order:
            self.load(i).start()
        for i in self.order:
            self.load(i).wait()
            landed(self.paired.at[i], self.precv.at[i])
            add_rows(self.own.at[i], self.own.at[i], self.paired.at[i], self.rows)

    def step(self, t):
        place, lines = self.place, self.lines
        d = lines - 1 - t + place

        @pl.when(t >= place)
        def _():
            @pl.when(place > 0)
            def _():
                landed(self.got.at[d], self.recv.at[d])
                add_rows(self.own.at[d], self.own.at[d], self.got.at[d], self.rows)

            @pl.when(d == place + 1)
            def _():
                self.right(d, True).start()

            @pl.when(d != place + 1)
            def _():
                self.right(d, False).start()

        e = t - (lines - 1 - place)

        @pl.when(e >= 0)
        def _():
            @pl.when(place < lines - 1)
            def _():
                landed(self.got.at[e], self.recv.at[e])
                add_rows(self.own.at[e], self.own.at[e], self.got.at[e], self.rows)

            self.left(e).start()

    def finish(self, out_ref):
        place, lines, rows = self.place, self.lines, self.rows

        def first(i, carry):
            at = pl.ds(pl.multiple_of(i * 32, 32), 32)
            out_ref[at, :] = self.own[place, at, :].astype(F32)
            return carry

        lax.fori_loop(0, rows // 32, first, 0)

        @pl.when(place > 0)
        def _():
            landed(self.last, self.final)
            add_rows(out_ref, out_ref, self.last, rows)

        @pl.when(place < lines - 1)
        def _():
            landed(self.got.at[place], self.recv.at[place])
            add_rows(out_ref, out_ref, self.got.at[place], rows)

        for i in range(lines):
            self.swap(i).wait_send()

            @pl.when(place < i)
            def _():
                self.right(i, False).wait_send()

            @pl.when(place > i)
            def _():
                self.left(i).wait_send()


class PlaneGather:
    def __init__(self, own, out, f, s, send, recv):
        self.own, self.out, self.f, self.s, self.send, self.recv = own, out, f, s, send, recv
        self.rows = own.shape[0]
        self.half = self.rows // 2

    def at(self, place, first, size):
        return self.out.at[pl.ds(pl.multiple_of(place * self.rows + first, self.half), size), :]

    def near(self, k):
        return remote(
            self.own, self.at(self.s, 0, self.rows), self.send.at[k - 1], self.recv.at[k - 1],
            (self.f, self.s ^ k),
        )

    def on(self, k):
        ref = self.at(self.s ^ k, (k - 1) * self.half, self.half)
        return remote(ref, ref, self.send.at[k + 1], self.recv.at[k + 1], (self.f, self.s ^ (3 - k)))

    def start(self):
        self.near(1).start()
        self.near(2).start()

    def forward(self):
        for k in (1, 2):
            landed(self.at(self.s ^ k, 0, self.rows), self.recv.at[k - 1])
            self.on(k).start()

    def finish(self):
        landed(self.at(self.s ^ 3, 0, self.half), self.recv.at[2])
        landed(self.at(self.s ^ 3, self.half, self.half), self.recv.at[3])
        for k in (1, 2):
            self.near(k).wait_send()
            self.on(k).wait_send()


class PlaneReduce:
    WAYS = ((0, 1, 1), (1, 2, 2))

    def __init__(self, p_ref, out_ref, scratch, f, s):
        self.p_ref, self.out_ref, self.f, self.s = p_ref, out_ref, f, s
        self.own, self.got, self.got_on, self.send, self.recv, self.local = scratch
        self.half = p_ref.shape[1] // 2

    @staticmethod
    def scratch(block):
        dma = pltpu.SemaphoreType.DMA
        return [
            pltpu.VMEM((3,) + block, BF16), pltpu.VMEM((2,) + block, BF16),
            pltpu.VMEM(block, BF16), dma((2, 3)), dma((2, 3)), dma((3,)),
        ]

    def part(self, ref, h):
        return ref.at[pl.ds(h * self.half, self.half), :]

    def load(self, n):
        d = (self.s, self.s ^ 2, self.s ^ 1)[n]
        return pltpu.make_async_copy(self.p_ref.at[d], self.own.at[n], self.local.at[n])

    def hop(self, h, k, far):
        d = self.s ^ 3 if far else self.s ^ k
        n = 0 if far else 1
        return remote(
            self.part(self.p_ref.at[d], h), self.part(self.got.at[1 - n], h), self.send.at[h, n],
            self.recv.at[h, n], (self.f, self.s ^ k),
        )

    def on(self, h, k, n):
        return remote(
            self.part(self.own.at[n], h), self.part(self.got_on, h), self.send.at[h, 2],
            self.recv.at[h, 2], (self.f, self.s ^ (3 - k)),
        )

    def start(self):
        for far in (True, False):
            for h, k, _ in self.WAYS:
                self.hop(h, k, far).start()
        for n in range(3):
            self.load(n).start()

    def forward(self):
        for n in range(3):
            self.load(n).wait()
        for h, k, n in self.WAYS:
            mine = self.part(self.own.at[n], h)
            landed(self.part(self.got.at[1], h), self.recv.at[h, 0])
            add_rows(mine, mine, self.part(self.got.at[1], h), self.half)
            self.on(h, k, n).start()

    def finish(self):
        for h in (0, 1):
            landed(self.part(self.got.at[0], h), self.recv.at[h, 1])
            add_rows(
                self.part(self.out_ref, h), self.part(self.own.at[0], h), self.part(self.got.at[0], h),
                self.half,
            )
        for h in (0, 1):
            landed(self.part(self.got_on, h), self.recv.at[h, 2])
            out = self.part(self.out_ref, h)
            add_rows(out, out, self.part(self.got_on, h), self.half)
        for h, k, n in self.WAYS:
            self.hop(h, k, True).wait_send()
            self.hop(h, k, False).wait_send()
            self.on(h, k, n).wait_send()


def greet_plane(barrier, f, s):
    for k in (1, 2):
        signal(barrier, (f, s ^ k))
    return 2


def rows_view(ref, rows):
    return lambda b: ref.at[pl.ds(pl.multiple_of(b * rows, rows), rows), :]


def block_view(ref):
    return lambda b: ref.at[b]


def comm_params(number):
    return pltpu.CompilerParams(
        collective_id=number, has_side_effects=True, vmem_limit_bytes=VLIM
    )


def start_kernel(
    fsdp, sp, x_ref, w_ref, wo_ref, g_ref, misc_ref, routes_ref,
    x_all, w_all, wo_all, g_all, misc_all, routes_all,
    send, recv, xsend, xrecv, psend, precv, wsend, wrecv, msend, mrecv, rsend, rrecv, local,
):
    f, s = lax.axis_index("fsdp"), lax.axis_index("sp")
    count, lines = fsdp * sp, fsdp // 2
    me = f * sp + s
    rows = w_ref.shape[1]
    cols = D // sp
    barrier = pltpu.get_barrier_semaphore()

    def greet(i, carry):
        other = lax.rem(me + i, count)
        signal(barrier, (other // sp, lax.rem(other, sp)))
        return carry

    def w_block(s_to):
        return w_ref.at[:, :, pl.ds(pl.multiple_of(s_to * cols, cols), cols)]

    def w_rows(i):
        return w_all.at[:, pl.ds(pl.multiple_of(i * rows, rows), rows), :]

    def w_view(b):
        size = rows * sp
        return w_all.at[:, pl.ds(pl.multiple_of(b * size, size), size), :]

    wo_view = rows_view(wo_all, rows)
    x_view = rows_view(x_all, TOK_DEV)
    owns = [
        pltpu.make_async_copy(w_block(s), w_rows(me), local.at[0]),
        pltpu.make_async_copy(x_ref, x_view(s), local.at[1]),
        pltpu.make_async_copy(misc_ref, misc_all.at[me], local.at[2]),
        pltpu.make_async_copy(routes_ref, routes_all.at[f], local.at[3]),
        pltpu.make_async_copy(g_ref, g_all.at[f], local.at[4]),
    ]
    for copy in owns:
        copy.start()
    lax.fori_loop(1, count, greet, 0)
    pl.semaphore_wait(barrier, count - 1)

    line = LineGather([w_view, wo_view, block_view(g_all)], [None, None, g_ref], lines, f, s, send, recv)
    line.start_own(2)
    w_copies = []
    for k in (3, 1, 2):
        s_to = s ^ k
        copy = remote(w_block(s_to), w_rows(me), psend.at[k], precv.at[k], (f, s_to))
        copy.start()
        w_copies.append(copy)
    target_s, target_f = me // fsdp, lax.rem(me, fsdp)
    stays = jnp.logical_and(target_s == s, target_f == f)
    wo_copy = remote(wo_ref, wo_view(target_f), wsend, wrecv, (target_f, target_s))
    wo_own = pltpu.make_async_copy(wo_ref, wo_view(f), wrecv)

    @pl.when(stays)
    def _():
        wo_own.start()

    @pl.when(jnp.logical_not(stays))
    def _():
        wo_copy.start()

    def misc_copy(i):
        other = lax.rem(me + i, count)
        return remote(
            misc_ref, misc_all.at[me], msend.at[i], mrecv.at[me], (other // sp, lax.rem(other, sp))
        )

    def misc_go(i, carry):
        misc_copy(i).start()
        return carry

    lax.fori_loop(1, count, misc_go, 0)

    def routes_copy(i):
        other = lax.rem(f + i, fsdp)
        return remote(routes_ref, routes_all.at[f], rsend.at[i], rrecv.at[f], (other, s))

    def routes_go(i, carry):
        routes_copy(i).start()
        return carry

    lax.fori_loop(1, fsdp, routes_go, 0)

    owns[0].wait()
    for k in range(1, sp):
        landed(w_rows(f * sp + (s ^ k)), precv.at[k])
    line.start_own(0)
    tokens = PlaneGather(x_ref, x_all, f, s, xsend, xrecv)
    tokens.start()
    landed(wo_view(f), wrecv)
    line.start_own(1)
    for k in range(1, lines):
        for v in (2, 0, 1):
            line.forward(v, k)
        if k == min(2, lines - 1):
            tokens.forward()
    for v in range(3):
        line.finish(v)
    tokens.finish()

    def misc_end(i, carry):
        misc_copy(i).wait_send()
        other = lax.rem(me + i, count)
        landed(misc_all.at[other], mrecv.at[other])
        return carry

    lax.fori_loop(1, count, misc_end, 0)

    def routes_end(i, carry):
        routes_copy(i).wait_send()
        other = lax.rem(f + i, fsdp)
        landed(routes_all.at[other], rrecv.at[other])
        return carry

    lax.fori_loop(1, fsdp, routes_end, 0)
    for copy in w_copies:
        copy.wait_send()

    @pl.when(jnp.logical_not(stays))
    def _():
        wo_copy.wait_send()

    for copy in owns[1:]:
        copy.wait()


def gather_start(fsdp, sp, x, w, wo, g, misc, routes):
    count = fsdp * sp
    dma = pltpu.SemaphoreType.DMA
    return pl.pallas_call(
        functools.partial(start_kernel, fsdp, sp),
        out_shape=(
            jax.ShapeDtypeStruct((sp * TOK_DEV, D), BF16),
            jax.ShapeDtypeStruct((3, D, D // sp), BF16),
            jax.ShapeDtypeStruct((D // sp, D), BF16),
            jax.ShapeDtypeStruct((fsdp,) + g.shape, BF16),
            jax.ShapeDtypeStruct((count,) + misc.shape, BF16),
            jax.ShapeDtypeStruct((fsdp,) + routes.shape, jnp.int32),
        ),
        in_specs=[VMEM] * 6,
        out_specs=[ANY] * 6,
        scratch_shapes=line_sems(3, fsdp)
        + [
            dma((4,)), dma((4,)), dma((sp,)), dma((sp,)), dma, dma,
            dma((count,)), dma((count,)), dma((fsdp,)), dma((fsdp,)), dma((5,)),
        ],
        compiler_params=comm_params(0),
        name="gather_start",
    )(x, w, wo, g, misc, routes)


def branch_kernel(fsdp, p_ref, g_ref, out_ref, g_all, *scratch):
    f, s = lax.axis_index("fsdp"), lax.axis_index("sp")
    lines = fsdp // 2
    barrier = pltpu.get_barrier_semaphore()
    expected = greet_line(barrier, lines, f, s) + greet_plane(barrier, f, s)
    send, recv, own_sem = scratch[-3:]
    own = pltpu.make_async_copy(g_ref, g_all.at[f], own_sem)
    own.start()
    pl.semaphore_wait(barrier, expected)
    plane = PlaneReduce(p_ref, out_ref, scratch[:-3], f, s)
    line = LineGather([block_view(g_all)], [g_ref], lines, f, s, send, recv)
    plane.start()
    line.start_own(0)
    for k in range(1, lines):
        line.forward(0, k)
        if k == min(2, lines - 1):
            plane.forward()
    plane.finish()
    line.finish(0)
    own.wait()


def branch_sum(fsdp, partial, g):
    block = partial.shape[1:]
    return pl.pallas_call(
        functools.partial(branch_kernel, fsdp),
        out_shape=(jax.ShapeDtypeStruct(block, F32), jax.ShapeDtypeStruct((fsdp,) + g.shape, BF16)),
        in_specs=[ANY, VMEM],
        out_specs=[VMEM, ANY],
        scratch_shapes=PlaneReduce.scratch(block) + line_sems(1, fsdp) + [pltpu.SemaphoreType.DMA],
        compiler_params=comm_params(2),
        name="branch_sum",
    )(partial, g)


def token_kernel(
    fsdp, x_ref, g_first, g_second, picks, w_ref, out_ref, taken_ref, back_ref,
    g_buf, w_buf, taken, back, send, recv, local, loads, stores, back_sem,
):
    f, s = lax.axis_index("fsdp"), lax.axis_index("sp")
    lines = fsdp // 2
    parts = 2
    size = TOK_DEV // parts
    early, later = g_first.shape[1], g_second.shape[1]
    slots = picks.shape[1] // EXP_DEV
    ff = w_ref.shape[1]
    barrier = pltpu.get_barrier_semaphore()
    expected = greet_line(barrier, lines, f, s)
    own = pltpu.make_async_copy(x_ref, out_ref.at[f], local)
    own.start()
    reads = [
        pltpu.make_async_copy(g_first, g_buf.at[:, pl.ds(0, early), :], loads.at[0]),
        pltpu.make_async_copy(g_second, g_buf.at[:, pl.ds(early, later), :], loads.at[1]),
        pltpu.make_async_copy(w_ref, w_buf, loads.at[2]),
    ]
    for copy in reads:
        copy.start()
    pl.semaphore_wait(barrier, expected)

    def view(part):
        return lambda b: out_ref.at[b, pl.ds(part * size, size), :]

    owns = [x_ref.at[pl.ds(p * size, size), :] for p in range(parts)]
    line = LineGather([view(p) for p in range(parts)], owns, lines, f, s, send, recv)
    for p in range(parts):
        line.start_own(p)

    def take_all():
        reads[0].wait()
        reads[1].wait()

        def block(b, carry):
            for n in range(D // 512):
                at = pl.ds(n * 512, 512)
                got = dot_nn(picks[b], g_buf[b, :, at]).astype(BF16)
                for e in range(EXP_DEV):
                    to = pl.ds(pl.multiple_of(b * slots, 16), slots)
                    taken[e, to, at] = got[e * slots : (e + 1) * slots]
            return carry

        lax.fori_loop(0, fsdp, block, 0)
        for e in range(EXP_DEV):
            pltpu.make_async_copy(taken.at[e], taken_ref.at[e], stores.at[e]).start()

    def back_copy(e, j, slot):
        at = pl.ds(pl.multiple_of(j * FT, FT), FT)
        return pltpu.make_async_copy(back.at[slot], back_ref.at[e, :, at], back_sem.at[slot])

    def back_of(e):
        if e == 0:
            reads[2].wait()
        for j in range(ff // FT):
            slot = j % 2
            if e > 0 or j > 1:
                back_copy(e, j, slot).wait()
            back[slot] = dot_nt(taken[e], w_buf[e, pl.ds(j * FT, FT), :])
            back_copy(e, j, slot).start()

    work = [take_all] + [functools.partial(back_of, e) for e in range(EXP_DEV)]
    for k in range(1, lines):
        if k - 1 < len(work):
            work[k - 1]()
        for p in range(parts):
            line.forward(p, k)
    for unit in work[lines - 1 :]:
        unit()
    for p in range(parts):
        line.finish(p)
    own.wait()
    for slot in range(2):
        back_copy(0, slot, slot).wait()
    for e in range(EXP_DEV):
        pltpu.make_async_copy(taken.at[e], taken_ref.at[e], stores.at[e]).wait()


def token_gather(fsdp, x, g_first, g_second, picks, w_down):
    slots = picks.shape[1] // EXP_DEV
    total = fsdp * slots
    ff = w_down.shape[1]
    dma = pltpu.SemaphoreType.DMA
    return pl.pallas_call(
        functools.partial(token_kernel, fsdp),
        out_shape=(
            jax.ShapeDtypeStruct((fsdp, TOK_DEV, D), BF16),
            jax.ShapeDtypeStruct((EXP_DEV, total, D), BF16),
            jax.ShapeDtypeStruct((EXP_DEV, total, ff), F32),
        ),
        in_specs=[VMEM, ANY, ANY, VMEM, ANY],
        out_specs=[ANY, ANY, ANY],
        scratch_shapes=[
            pltpu.VMEM((fsdp, TOK_DEV, D), BF16),
            pltpu.VMEM((EXP_DEV, ff, D), BF16),
            pltpu.VMEM((EXP_DEV, total, D), BF16),
            pltpu.VMEM((2, total, FT), F32),
        ]
        + line_sems(2, fsdp)
        + [dma, dma((3,)), dma((EXP_DEV,)), dma((2,))],
        compiler_params=comm_params(3),
        name="token_gather",
    )(x, g_first, g_second, picks, w_down)


def token_back_kernel(
    fsdp, p_ref, gated_ref, w_ref, turned, x_ref, gg_ref, gu_ref,
    out_ref, part_ref, wg_ref, wu_ref,
    wide, narrow, w_buf, tile, grad_tile, loads, tile_sem, grad_sem, *scratch,
):
    f, s = lax.axis_index("fsdp"), lax.axis_index("sp")
    lines = fsdp // 2
    slots = turned.shape[3]
    height = grad_tile.shape[1]
    barrier = pltpu.get_barrier_semaphore()
    expected = greet_line(barrier, lines, f, s)
    reads = [
        pltpu.make_async_copy(gated_ref, narrow, loads.at[0]),
        pltpu.make_async_copy(w_ref, w_buf, loads.at[1]),
        pltpu.make_async_copy(x_ref, wide, loads.at[2]),
        pltpu.make_async_copy(gg_ref.at[0], narrow.at[0], loads.at[3]),
        pltpu.make_async_copy(gu_ref.at[0], narrow.at[1], loads.at[4]),
        pltpu.make_async_copy(gg_ref.at[1], narrow.at[0], loads.at[3]),
        pltpu.make_async_copy(gu_ref.at[1], narrow.at[1], loads.at[4]),
    ]
    reads[0].start()
    reads[1].start()
    pl.semaphore_wait(barrier, expected)
    line = LineReduce(p_ref, scratch, lines, f, s)
    line.start()

    def down_of(e):
        if e == 0:
            reads[0].wait()
            reads[1].wait()

        def columns(n, carry):
            at = pl.ds(pl.multiple_of(n * 512, 512), 512)
            wide[e, :, at] = dot_nn(narrow[e], w_buf[e, :, at]).astype(BF16)
            return carry

        lax.fori_loop(0, D // 512, columns, 0)

    def tile_copy(b, slot):
        return pltpu.make_async_copy(tile.at[slot], part_ref.at[b], tile_sem.at[slot])

    def sum_all():
        reads[3].start()
        reads[4].start()

        def pair(i, carry):
            for slot in range(2):
                b = 2 * i + slot

                @pl.when(i > 0)
                def _():
                    tile_copy(b, slot).wait()

                for n in range(D // 512):
                    at = pl.ds(n * 512, 512)
                    summed = jnp.zeros((TOK_DEV, 512), F32)
                    for e in range(EXP_DEV):
                        rows = wide[e, pl.ds(pl.multiple_of(b * slots, 16), slots), at]
                        summed += dot_nn(turned[b, e], rows)
                    tile[slot, :, at] = summed.astype(BF16)
                tile_copy(b, slot).start()
            return carry

        lax.fori_loop(0, fsdp // 2, pair, 0)
        reads[2].start()

    def grad_copy(to, e, i, slot):
        at = pl.ds(pl.multiple_of(i * height, height), height)
        return pltpu.make_async_copy(grad_tile.at[slot], to.at[e, at, :], grad_sem.at[slot])

    def grad_of(e, n, to, first):
        if n == 0 and e == 0:
            reads[2].wait()
            reads[3].wait()
            reads[4].wait()
        if n == 0 and e == 1:
            reads[5].wait()
            reads[6].wait()

        def pair(i, carry):
            for slot in range(2):
                part = 2 * i + slot

                def before():
                    grad_copy(to, e, part, slot).wait()

                if first:
                    pl.when(i > 0)(before)
                else:
                    before()
                at = pl.ds(pl.multiple_of(part * height, height), height)
                grad_tile[slot] = dot_tn(wide[e, :, at], narrow[n]).astype(BF16)
                grad_copy(to, e, part, slot).start()
            return carry

        lax.fori_loop(0, D // height // 2, pair, 0)
        if n == 1 and e == 0:
            reads[5].start()
            reads[6].start()

    work = [functools.partial(down_of, e) for e in range(EXP_DEV)] + [sum_all]
    for e in range(EXP_DEV):
        for n, to in ((0, wg_ref), (1, wu_ref)):
            work.append(functools.partial(grad_of, e, n, to, e == 0 and n == 0))
    done = 0
    for t in range(lines - 1):
        line.step(t)
        until = (t + 1) * len(work) // (lines - 1)
        for unit in work[done:until]:
            unit()
        done = until
    line.finish(out_ref)
    for slot in range(2):
        tile_copy(slot, slot).wait()
        grad_copy(wg_ref, 0, slot, slot).wait()


def token_back(fsdp, partial, gated, w_down, turned, received, grad_gate_pre, grad_up_pre):
    block = partial.shape[1:]
    total, ff = gated.shape[1:]
    height = 256
    dma = pltpu.SemaphoreType.DMA
    weight = jax.ShapeDtypeStruct((EXP_DEV, D, ff), BF16)
    return pl.pallas_call(
        functools.partial(token_back_kernel, fsdp),
        out_shape=(
            jax.ShapeDtypeStruct(block, F32),
            jax.ShapeDtypeStruct(partial.shape, BF16),
            weight,
            weight,
        ),
        in_specs=[ANY, ANY, ANY, VMEM, ANY, ANY, ANY],
        out_specs=[VMEM, ANY, ANY, ANY],
        scratch_shapes=[
            pltpu.VMEM((EXP_DEV, total, D), BF16),
            pltpu.VMEM((EXP_DEV, total, ff), BF16),
            pltpu.VMEM((EXP_DEV, ff, D), BF16),
            pltpu.VMEM((2,) + block, BF16),
            pltpu.VMEM((2, height, ff), BF16),
            dma((5,)),
            dma((2,)),
            dma((2,)),
        ]
        + LineReduce.scratch(fsdp, block),
        compiler_params=comm_params(4),
        name="token_back",
    )(partial, gated, w_down, turned, received, grad_gate_pre, grad_up_pre)


def branch_back_kernel(fsdp, x_ref, p_ref, all_ref, out_ref, xsend, xrecv, own_sem, *scratch):
    f, s = lax.axis_index("fsdp"), lax.axis_index("sp")
    lines = fsdp // 2
    barrier = pltpu.get_barrier_semaphore()
    expected = greet_line(barrier, lines, f, s) + greet_plane(barrier, f, s)
    plane = PlaneGather(x_ref, all_ref, f, s, xsend, xrecv)
    own = pltpu.make_async_copy(x_ref, plane.at(s, 0, x_ref.shape[0]), own_sem)
    own.start()
    pl.semaphore_wait(barrier, expected)
    plane.start()
    line = LineReduce(p_ref, scratch, lines, f, s)
    line.start()
    for t in range(lines - 1):
        line.step(t)
        if t == min(1, lines - 2):
            plane.forward()
    plane.finish()
    line.finish(out_ref)
    own.wait()


def branch_back(fsdp, sp, x, partial):
    block = partial.shape[1:]
    dma = pltpu.SemaphoreType.DMA
    return pl.pallas_call(
        functools.partial(branch_back_kernel, fsdp),
        out_shape=(
            jax.ShapeDtypeStruct((sp * x.shape[0], x.shape[1]), BF16),
            jax.ShapeDtypeStruct(block, F32),
        ),
        in_specs=[VMEM, ANY],
        out_specs=[ANY, VMEM],
        scratch_shapes=[dma((4,)), dma((4,)), dma] + LineReduce.scratch(fsdp, block),
        compiler_params=comm_params(5),
        name="branch_back",
    )(x, partial)


def line_reduce_kernel(fsdp, p_ref, out_ref, *scratch):
    f, s = lax.axis_index("fsdp"), lax.axis_index("sp")
    lines = fsdp // 2
    barrier = pltpu.get_barrier_semaphore()
    expected = greet_line(barrier, lines, f, s)
    pl.semaphore_wait(barrier, expected)
    line = LineReduce(p_ref, scratch, lines, f, s)
    line.start()
    for t in range(lines - 1):
        line.step(t)
    line.finish(out_ref)


def line_reduce(fsdp, partial, number, name):
    block = partial.shape[1:]
    return pl.pallas_call(
        functools.partial(line_reduce_kernel, fsdp),
        out_shape=jax.ShapeDtypeStruct(block, F32),
        in_specs=[ANY],
        out_specs=VMEM,
        scratch_shapes=LineReduce.scratch(fsdp, block),
        compiler_params=comm_params(number),
        name=name,
    )(partial)


def plane_sum_kernel(x_ref, out_ref, got, send, recv):
    f, s = lax.axis_index("fsdp"), lax.axis_index("sp")
    barrier = pltpu.get_barrier_semaphore()
    for k in (1, 2, 3):
        signal(barrier, (f, s ^ k))
    pl.semaphore_wait(barrier, 3)
    copies = []
    for k in (1, 2, 3):
        copy = remote(x_ref, got.at[k - 1], send.at[k - 1], recv.at[k - 1], (f, s ^ k))
        copy.start()
        copies.append(copy)
    for copy in copies:
        copy.wait()
    near = x_ref[...] + got[0]
    far = got[1] + got[2]
    out_ref[...] = near + far


def plane_sum(x, number, name):
    dma = pltpu.SemaphoreType.DMA
    return pl.pallas_call(
        plane_sum_kernel,
        out_shape=jax.ShapeDtypeStruct(x.shape, F32),
        in_specs=[VMEM],
        out_specs=VMEM,
        scratch_shapes=[pltpu.VMEM((3,) + x.shape, F32), dma((3,)), dma((3,))],
        compiler_params=pltpu.CompilerParams(collective_id=number, has_side_effects=True),
        name=name,
    )(x)


def end_kernel(
    fsdp, sp, q_ref, o_ref, m_ref, q_out, o_out, m_out,
    qsend, qrecv, osend, orecv, msend, mrecv, local,
):
    f, s = lax.axis_index("fsdp"), lax.axis_index("sp")
    count = fsdp * sp
    me = f * sp + s
    rows = o_ref.shape[0]
    barrier = pltpu.get_barrier_semaphore()

    def greet(i, carry):
        other = lax.rem(me + i, count)
        signal(barrier, (other // sp, lax.rem(other, sp)))
        return carry

    lax.fori_loop(1, count, greet, 0)
    pl.semaphore_wait(barrier, count - 1)

    def q_from(place):
        return q_ref.at[:, pl.ds(pl.multiple_of(place * rows, rows), rows), :]

    q_own = pltpu.make_async_copy(q_from(s), q_out.at[s], local.at[0])
    q_own.start()
    copies = []
    for k in range(1, sp):
        copy = remote(q_from(s ^ k), q_out.at[s], qsend.at[k], qrecv.at[k], (f, s ^ k))
        copy.start()
        copies.append(copy)
    flat = s * fsdp + f
    target_f, target_s = flat // sp, lax.rem(flat, sp)
    stays = jnp.logical_and(target_s == s, target_f == f)
    o_copy = remote(o_ref, o_out, osend, orecv, (target_f, target_s))
    o_own = pltpu.make_async_copy(o_ref, o_out, orecv)

    @pl.when(stays)
    def _():
        o_own.start()

    @pl.when(jnp.logical_not(stays))
    def _():
        o_copy.start()

    m_own = pltpu.make_async_copy(m_ref.at[me], m_out.at[me], local.at[1])
    m_own.start()

    def m_copy(i):
        other = lax.rem(me + i, count)
        return remote(
            m_ref.at[other], m_out.at[me], msend.at[i], mrecv.at[me], (other // sp, lax.rem(other, sp))
        )

    def m_go(i, carry):
        m_copy(i).start()
        return carry

    lax.fori_loop(1, count, m_go, 0)

    def m_end(i, carry):
        m_copy(i).wait_send()
        other = lax.rem(me + i, count)
        landed(m_out.at[other], mrecv.at[other])
        return carry

    lax.fori_loop(1, count, m_end, 0)
    landed(o_out, orecv)

    @pl.when(jnp.logical_not(stays))
    def _():
        o_copy.wait_send()

    for k in range(1, sp):
        landed(q_out.at[s ^ k], qrecv.at[k])
    for copy in copies:
        copy.wait_send()
    q_own.wait()
    m_own.wait()


def exchange_end(fsdp, sp, q, o, m, number):
    count = fsdp * sp
    rows = o.shape[0]
    dma = pltpu.SemaphoreType.DMA
    return pl.pallas_call(
        functools.partial(end_kernel, fsdp, sp),
        out_shape=(
            jax.ShapeDtypeStruct((sp, 3, rows, D // sp), q.dtype),
            jax.ShapeDtypeStruct(o.shape, o.dtype),
            jax.ShapeDtypeStruct(m.shape, m.dtype),
        ),
        in_specs=[ANY] * 3,
        out_specs=[ANY] * 3,
        scratch_shapes=[
            dma((sp,)), dma((sp,)), dma, dma, dma((count,)), dma((count,)), dma((2,)),
        ],
        compiler_params=pltpu.CompilerParams(collective_id=number, has_side_effects=True),
        name="exchange_end",
    )(q, o, m)


def dot_nt(a, b):
    return lax.dot_general(a, b, (((1,), (1,)), ((), ())), preferred_element_type=F32)


def dot_tn(a, b):
    return lax.dot_general(a, b, (((0,), (0,)), ((), ())), preferred_element_type=F32)


def dot_nn(a, b):
    return jnp.dot(a, b, preferred_element_type=F32)


def whole(shape):
    return pl.BlockSpec(shape, lambda *_: (0,) * len(shape))


def turn(v, cosine, sine):
    return v * cosine + pltpu.roll(v, HEAD_DIM // 2, 1) * sine


def project_kernel(x_ref, gain, w_ref, first_out, q_out, k_out, v_out, q_square, k_square):
    x = x_ref[...].astype(F32)
    inverse = lax.rsqrt(jnp.mean(x * x, axis=-1, keepdims=True) + EPSILON)
    first = (x * inverse * gain[0:1, :]).astype(BF16)
    first_out[...] = first
    q = dot_nn(first, w_ref[0])
    q_out[...] = q
    q_square[...] = jnp.sum(q * q, axis=-1, keepdims=True)
    k = dot_nn(first, w_ref[1])
    k_out[...] = k
    k_square[...] = jnp.sum(k * k, axis=-1, keepdims=True)
    v_out[...] = dot_nn(first, w_ref[2]).astype(BF16)


def project(x, gains, w):
    seq, cols = x.shape[0], w.shape[2]

    def block(width):
        return pl.BlockSpec((TOK_DEV, width), lambda i: (i, 0))

    return pl.pallas_call(
        project_kernel,
        grid=(seq // TOK_DEV,),
        out_shape=(
            jax.ShapeDtypeStruct((seq, D), BF16),
            jax.ShapeDtypeStruct((seq, cols), F32),
            jax.ShapeDtypeStruct((seq, cols), F32),
            jax.ShapeDtypeStruct((seq, cols), BF16),
            jax.ShapeDtypeStruct((seq, 1), F32),
            jax.ShapeDtypeStruct((seq, 1), F32),
        ),
        in_specs=[block(D), whole(gains.shape), whole(w.shape)],
        out_specs=[block(D), block(cols), block(cols), block(cols), block(1), block(1)],
        compiler_params=pltpu.CompilerParams(vmem_limit_bytes=VLIM),
        name="project",
    )(x, gains, w)


def attend_kernel(
    q_raw, k_raw, v_ref, q_inv, k_inv, gain, cosine, sine, o_ref, sum_ref, q_ref, k_ref
):
    c, d = cosine[...], sine[...]
    q_ref[...] = turn(q_raw[...] * q_inv[...] * gain[2:3, :], c, d).astype(BF16)
    k_ref[...] = turn(k_raw[...] * k_inv[...] * gain[3:4, :], c, d).astype(BF16)
    for i in range(q_ref.shape[0] // BLK):
        rows, seen = pl.ds(i * BLK, BLK), pl.ds(0, (i + 1) * BLK)
        scores = dot_nt(q_ref[rows, :], k_ref[seen, :]) * SCALE
        row_max = jnp.max(scores, axis=-1, keepdims=True)
        exp_rows = jnp.exp(scores - row_max)
        row_sum = jnp.sum(exp_rows, axis=-1, keepdims=True)
        probs = (exp_rows / row_sum).astype(BF16)
        o_ref[rows, :] = dot_nn(probs, v_ref[seen, :]).astype(BF16)
        sum_ref[0, rows, :] = row_max + jnp.log(row_sum)


def attend(q_raw, k_raw, v, q_inv, k_inv, gains, cosine, sine):
    seq, width = v.shape
    heads = width // HEAD_DIM
    spec = pl.BlockSpec((seq, HEAD_DIM), lambda h: (0, h))
    return pl.pallas_call(
        attend_kernel,
        grid=(heads,),
        out_shape=(
            jax.ShapeDtypeStruct((seq, width), BF16),
            jax.ShapeDtypeStruct((heads, seq, 1), F32),
            jax.ShapeDtypeStruct((seq, width), BF16),
            jax.ShapeDtypeStruct((seq, width), BF16),
        ),
        in_specs=[
            spec, spec, spec, whole((seq, 1)), whole((seq, 1)),
            pl.BlockSpec((4, HEAD_DIM), lambda h: (0, h)),
            whole((seq, HEAD_DIM)), whole((seq, HEAD_DIM)),
        ],
        out_specs=[spec, pl.BlockSpec((1, seq, 1), lambda h: (h, 0, 0)), spec, spec],
        compiler_params=pltpu.CompilerParams(vmem_limit_bytes=VLIM),
        name="attend",
    )(q_raw, k_raw, v, q_inv, k_inv, gains, cosine, sine)


def attend_back_kernel(
    q_ref, k_ref, v_ref, g_ref, sum_ref, q_raw, k_raw, q_inv, k_inv, gain, cosine, sine,
    q_scaled, k_scaled, dv_out, q_dots, k_dots, gains_out, dk_ref, dv_ref,
):
    head = pl.program_id(0)

    @pl.when(head == 0)
    def _():
        q_dots[...] = jnp.zeros_like(q_dots)
        k_dots[...] = jnp.zeros_like(k_dots)

    dk_ref[...] = jnp.zeros_like(dk_ref)
    dv_ref[...] = jnp.zeros_like(dv_ref)
    gain_q, gain_k = gain[2:3, :], gain[3:4, :]
    gain_sum = jnp.zeros((1, HEAD_DIM), F32)
    for i in range(q_ref.shape[0] // BLK):
        rows, seen = pl.ds(i * BLK, BLK), pl.ds(0, (i + 1) * BLK)
        q, g, keys = q_ref[rows, :], g_ref[rows, :], k_ref[seen, :]
        scores = dot_nt(q, keys) * SCALE
        probs = jnp.exp(scores - sum_ref[0, rows, :])
        grad_probs = dot_nt(g, v_ref[seen, :])
        row_dot = jnp.sum(probs * grad_probs, axis=-1, keepdims=True)
        grad_scores = (probs * (grad_probs - row_dot)).astype(BF16)
        dk_ref[seen, :] += dot_tn(grad_scores, q)
        dv_ref[seen, :] += dot_tn(probs.astype(BF16), g)
        grad_y = turn(dot_nn(grad_scores, keys) * SCALE, cosine[rows, :], -sine[rows, :])
        normed = q_raw[rows, :] * q_inv[rows, :]
        scaled = grad_y * gain_q
        q_scaled[rows, :] = scaled
        q_dots[rows, :] += jnp.sum(scaled * normed, axis=-1, keepdims=True)
        gain_sum += jnp.sum(grad_y * normed, axis=0, keepdims=True)
    grad_y = turn(dk_ref[...] * SCALE, cosine[...], -sine[...])
    normed = k_raw[...] * k_inv[...]
    scaled = grad_y * gain_k
    k_scaled[...] = scaled
    k_dots[...] += jnp.sum(scaled * normed, axis=-1, keepdims=True)
    gains_out[0:1, :] = gain_sum
    gains_out[1:2, :] = jnp.sum(grad_y * normed, axis=0, keepdims=True)
    dv_out[...] = dv_ref[...].astype(BF16)


def attend_back(q, k, v, g, log_sum, q_raw, k_raw, q_inv, k_inv, gains, cosine, sine):
    seq, width = q.shape
    heads = width // HEAD_DIM
    spec = pl.BlockSpec((seq, HEAD_DIM), lambda h: (0, h))
    column, table = whole((seq, 1)), whole((seq, HEAD_DIM))
    return pl.pallas_call(
        attend_back_kernel,
        grid=(heads,),
        out_shape=(
            jax.ShapeDtypeStruct((seq, width), F32),
            jax.ShapeDtypeStruct((seq, width), F32),
            jax.ShapeDtypeStruct((seq, width), BF16),
            jax.ShapeDtypeStruct((seq, 1), F32),
            jax.ShapeDtypeStruct((seq, 1), F32),
            jax.ShapeDtypeStruct((2, width), F32),
        ),
        in_specs=[spec] * 4
        + [pl.BlockSpec((1, seq, 1), lambda h: (h, 0, 0)), spec, spec, column, column]
        + [pl.BlockSpec((4, HEAD_DIM), lambda h: (0, h)), table, table],
        out_specs=[spec] * 3 + [column, column, pl.BlockSpec((2, HEAD_DIM), lambda h: (0, h))],
        scratch_shapes=[pltpu.VMEM((seq, HEAD_DIM), F32)] * 2,
        compiler_params=pltpu.CompilerParams(vmem_limit_bytes=VLIM),
        name="attend_back",
    )(q, k, v, g, log_sum, q_raw, k_raw, q_inv, k_inv, gains, cosine, sine)


def two_parts(x, axis):
    high = x.astype(BF16)
    return jnp.concatenate([high, (x - high.astype(F32)).astype(BF16)], axis=axis)


def blocks_of(shape):
    return pl.BlockSpec((1,) + shape, lambda b: (b,) + (0,) * len(shape))


def slots_of(slots, width):
    return pl.BlockSpec((EXP_DEV, slots, width), lambda b: (0, b, 0))


def route_kernel(picks, rows_in, router, columns, out, probs_out, gates_out):
    slots = out.shape[1]
    for n in range(D // 512):
        at = pl.ds(n * 512, 512)
        got = dot_nn(picks[0], rows_in[0, :, at]).astype(BF16)
        for e in range(EXP_DEV):
            out[e, :, at] = got[e * slots : (e + 1) * slots]
    logits = dot_nt(rows_in[0], router[...])
    exp_logits = jnp.exp(logits - jnp.max(logits, axis=1, keepdims=True))
    probs = exp_logits / jnp.sum(exp_logits, axis=1, keepdims=True)
    probs_out[0] = probs
    both = two_parts(probs, 1)
    for e in range(EXP_DEV):
        moved = dot_nn(picks[0, e * slots : (e + 1) * slots, :], both)
        mask = columns[e : e + 1, :]
        gates_out[e] = jnp.sum(moved * jnp.concatenate([mask, mask], axis=1), axis=1, keepdims=True)


def route(picks, tokens, router_t, columns):
    blocks = tokens.shape[0]
    slots = picks.shape[1] // EXP_DEV
    total = blocks * slots
    experts = router_t.shape[0]
    return pl.pallas_call(
        route_kernel,
        grid=(blocks,),
        out_shape=(
            jax.ShapeDtypeStruct((EXP_DEV, total, D), BF16),
            jax.ShapeDtypeStruct((blocks, TOK_DEV, experts), F32),
            jax.ShapeDtypeStruct((EXP_DEV, total, 1), F32),
        ),
        in_specs=[
            blocks_of(picks.shape[1:]), blocks_of((TOK_DEV, D)), whole(router_t.shape),
            whole(columns.shape),
        ],
        out_specs=[slots_of(slots, D), blocks_of((TOK_DEV, experts)), slots_of(slots, 1)],
        compiler_params=pltpu.CompilerParams(vmem_limit_bytes=VLIM),
        name="route",
    )(picks, tokens, router_t, columns)


FT = 256


def active_kernel(x_ref, g_ref, w_ref, u_ref, gates, gated, grad_gate, grad_up, dots):
    @pl.when(pl.program_id(1) == 0)
    def _():
        dots[...] = jnp.zeros_like(dots)

    gate_pre = dot_nn(x_ref[0], g_ref[0])
    up_pre = dot_nn(x_ref[0], w_ref[0])
    sig = jax.nn.sigmoid(gate_pre)
    silu = gate_pre * sig
    hidden = silu * up_pre
    back = u_ref[0]
    gate = gates[0]
    dots[0] += jnp.sum(hidden * back, axis=1, keepdims=True)
    gated[0] = (hidden * gate).astype(BF16)
    back = back * gate
    grad_gate[0] = (back * up_pre * (sig * (1.0 + gate_pre * (1.0 - sig)))).astype(BF16)
    grad_up[0] = (back * silu).astype(BF16)


def active(x, w_gate, w_up, u, gates):
    _, total, _ = x.shape
    ff = w_up.shape[2]
    tile = pl.BlockSpec((1, total, FT), lambda e, j: (e, 0, j))
    weight = pl.BlockSpec((1, D, FT), lambda e, j: (e, 0, j))
    column = pl.BlockSpec((1, total, 1), lambda e, j: (e, 0, 0))
    low = jax.ShapeDtypeStruct((EXP_DEV, total, ff), BF16)
    return pl.pallas_call(
        active_kernel,
        grid=(EXP_DEV, ff // FT),
        out_shape=(low, low, low, jax.ShapeDtypeStruct((EXP_DEV, total, 1), F32)),
        in_specs=[
            pl.BlockSpec((1, total, D), lambda e, j: (e, 0, 0)), weight, weight, tile, column,
        ],
        out_specs=[tile, tile, tile, column],
        compiler_params=pltpu.CompilerParams(vmem_limit_bytes=VLIM),
        name="active",
    )(x, w_gate, w_up, u, gates)


def rows_back_kernel(a_ref, b_ref, g_ref, w_ref, out):
    out[0] = (dot_nt(a_ref[0], g_ref[0]) + dot_nt(b_ref[0], w_ref[0])).astype(BF16)


def rows_back(grad_gate_pre, grad_up_pre, w_gate, w_up):
    _, total, ff = grad_up_pre.shape
    size = 512
    row = pl.BlockSpec((1, total, ff), lambda e, j: (e, 0, 0))
    weight = pl.BlockSpec((1, size, ff), lambda e, j: (e, j, 0))
    return pl.pallas_call(
        rows_back_kernel,
        grid=(EXP_DEV, D // size),
        out_shape=jax.ShapeDtypeStruct((EXP_DEV, total, D), BF16),
        in_specs=[row, row, weight, weight],
        out_specs=pl.BlockSpec((1, total, size), lambda e, j: (e, 0, j)),
        compiler_params=pltpu.CompilerParams(vmem_limit_bytes=VLIM),
        name="rows_back",
    )(grad_gate_pre, grad_up_pre, w_gate, w_up)


def combine_kernel(turned, rows_ref, tokens, probs, dots, router, columns, out, router_out):
    @pl.when(pl.program_id(0) == 0)
    def _():
        router_out[...] = jnp.zeros_like(router_out)

    choice = jnp.zeros(probs.shape[1:], F32)
    for e in range(EXP_DEV):
        moved = dot_nn(turned[0, e], dots[e])
        choice += jnp.sum(moved, axis=1, keepdims=True) * columns[e : e + 1, :]
    p = probs[0]
    grad_logits = p * (choice - jnp.sum(p * choice, axis=1, keepdims=True))
    both = two_parts(grad_logits, 1)
    for n in range(D // 512):
        at = pl.ds(n * 512, 512)
        total = dot_nn(both, router[:, at])
        for e in range(EXP_DEV):
            total += dot_nn(turned[0, e], rows_ref[e, :, at])
        out[0, :, at] = total.astype(BF16)
    router_out[...] += dot_tn(both, tokens[0])


def combine(turned, grad_rows, tokens, probs, dots, router_two, columns):
    blocks = tokens.shape[0]
    slots = turned.shape[3]
    return pl.pallas_call(
        combine_kernel,
        grid=(blocks,),
        out_shape=(
            jax.ShapeDtypeStruct((blocks, TOK_DEV, D), BF16),
            jax.ShapeDtypeStruct((router_two.shape[0], D), F32),
        ),
        in_specs=[
            blocks_of(turned.shape[1:]), slots_of(slots, D), blocks_of((TOK_DEV, D)),
            blocks_of(probs.shape[1:]), slots_of(slots, 128), whole(router_two.shape),
            whole(columns.shape),
        ],
        out_specs=[blocks_of((TOK_DEV, D)), whole((router_two.shape[0], D))],
        compiler_params=pltpu.CompilerParams(vmem_limit_bytes=VLIM),
        name="combine",
    )(turned, grad_rows, tokens, probs, dots, router_two, columns)


def rms_parts(values_in):
    inverse = lax.rsqrt(jnp.mean(values_in * values_in, axis=-1, keepdims=True) + EPSILON)
    return (values_in * inverse, inverse)


def rms_back(grad_out, normed, inverse, gain_row):
    scaled = grad_out * gain_row
    grad_in = inverse * (scaled - normed * jnp.mean(scaled * normed, axis=-1, keepdims=True))
    return (grad_in, jnp.sum(grad_out * normed, axis=0))


def angles(positions):
    freqs = ROPE_BASE ** (-2.0 * jnp.arange(HEAD_DIM // 2, dtype=F32) / HEAD_DIM)
    turned = positions.astype(F32)[:, None] * freqs[None, :]
    cosine, sine = jnp.cos(turned), jnp.sin(turned)
    return (jnp.concatenate([cosine, cosine], axis=1), jnp.concatenate([-sine, sine], axis=1))


def two_row_sums(first, second, number, name):
    seq = first.shape[0]
    packed = jnp.concatenate([first, second], axis=0).reshape(2 * seq // 128, 128)
    total = plane_sum(packed, number, name).reshape(2, seq, 1)
    return total[0], total[1]


def plane_back(partial, s, sp):
    total = lax.dynamic_index_in_dim(partial, s, axis=0, keepdims=False).astype(F32)
    for k in (3, 1, 2):
        piece = lax.dynamic_index_in_dim(partial, s ^ k, axis=0, keepdims=False)
        total = total + lax.ppermute(piece, "sp", [(i, i ^ k) for i in range(sp)]).astype(F32)
    return total


def body(
    layer_input, output_grad, w_query, w_key, w_value, w_output, w_router, norm_gains,
    w_gate, w_up, w_down, expert_routes,
):
    fsdp, sp = lax.axis_size("fsdp"), lax.axis_size("sp")
    f, s = lax.axis_index("fsdp"), lax.axis_index("sp")
    count = fsdp * sp
    experts = EXP_DEV * fsdp
    capacity = TOK_DEV * TOP // experts * 17 // 16
    slots = -(-capacity // 16) * 16
    seq = TOK_DEV * sp
    cols = D // sp
    rows = D // count

    down_full = lax.all_gather(w_down, "sp", axis=1, tiled=True)
    gate_full = lax.all_gather(w_gate, "sp", axis=1, tiled=True)
    up_full = lax.all_gather(w_up, "sp", axis=1, tiled=True)

    router_size = rows * experts
    misc = jnp.concatenate([w_router.reshape(router_size), norm_gains.reshape(4 * rows)])
    misc_rows = -(-misc.shape[0] // 2048) * 16
    misc = jnp.pad(misc, (0, misc_rows * 128 - misc.shape[0])).reshape(misc_rows, 128)
    routes = expert_routes.reshape(TOK_DEV * TOP // 128, 128)
    early = TOK_DEV // 4
    x_all, w_all, wo_s, grad_first_half, misc_all, routes_all = gather_start(
        fsdp, sp, layer_input, jnp.stack([w_query, w_key, w_value]), w_output, output_grad[:early],
        misc, routes,
    )
    misc_all = misc_all.reshape(count, misc_rows * 128)
    router_w = misc_all[:, :router_size].reshape(D, experts)
    router_t = router_w.T
    gains_w = misc_all[:, router_size : router_size + 4 * rows].reshape(count, 4, rows)
    gains32 = gains_w.transpose(1, 0, 2).reshape(4, D).astype(F32)
    gains_own = lax.dynamic_slice_in_dim(gains32, s * cols, cols, axis=1)

    routes_block = routes_all.reshape(fsdp, TOK_DEV, TOP)
    own_ids = f * EXP_DEV + jnp.arange(EXP_DEV, dtype=jnp.int32)
    chosen = jnp.any(routes_block[:, :, :, None] == own_ids, axis=2)
    before = jnp.arange(TOK_DEV)[:, None] > jnp.arange(TOK_DEV)[None, :]
    place = jnp.einsum(
        "ut,fte->feu", before.astype(BF16), chosen.astype(BF16), preferred_element_type=F32
    ).astype(jnp.int32)
    slot_ids = jnp.arange(slots, dtype=jnp.int32)
    picks = (
        (place[:, :, None, :] == slot_ids[:, None]) & chosen.transpose(0, 2, 1)[:, :, None, :]
    ).astype(BF16).reshape(fsdp, EXP_DEV * slots, TOK_DEV)
    turned = (
        (place[:, :, :, None] == slot_ids) & chosen.transpose(0, 2, 1)[:, :, :, None]
    ).astype(BF16)
    columns = (jnp.arange(experts, dtype=jnp.int32)[None, :] == own_ids[:, None]).astype(F32)

    first_in, q_raw, k_raw, values, q_square, k_square = project(x_all, gains32, w_all)
    q_square, k_square = two_row_sums(q_square, k_square, 1, "norm_sums")
    q_inverse = lax.rsqrt(q_square / D + EPSILON)
    k_inverse = lax.rsqrt(k_square / D + EPSILON)
    cosine, sine = angles(jnp.arange(seq, dtype=jnp.int32))
    attended, log_sum, queries, keys = attend(
        q_raw, k_raw, values, q_inverse, k_inverse, gains_own, cosine, sine
    )
    branch = dot_nn(attended, wo_s).astype(BF16).reshape(sp, TOK_DEV, D)
    inputs = layer_input.astype(F32)
    branch, grad_second_half = branch_sum(fsdp, branch, output_grad[early:])
    mid = inputs + branch
    normed_m, inverse_m = rms_parts(mid)
    second_in = (normed_m * gains32[1]).astype(BF16)

    tokens, grad_taken, unscaled = token_gather(
        fsdp, second_in, grad_first_half, grad_second_half, picks, down_full
    )
    received, probs, slot_gates = route(picks, tokens, router_t, columns)
    gated, grad_gate_pre, grad_up_pre, slot_dots = active(
        received, gate_full, up_full, unscaled, slot_gates
    )
    dots_two = jnp.pad(two_parts(slot_dots, 2), ((0, 0), (0, 0), (0, 126)))
    grad_rows = rows_back(grad_gate_pre, grad_up_pre, gate_full, up_full)
    second_part, router_two = combine(
        turned, grad_rows, tokens, probs, dots_two, jnp.concatenate([router_t, router_t], axis=0),
        columns,
    )
    grad_router = (router_two[:experts] + router_two[experts:]).T

    def shed(grad):
        return lax.psum_scatter(grad, "sp", scatter_dimension=1, tiled=True).astype(F32)

    down_part = jnp.einsum("erf,erd->efd", gated, grad_taken, preferred_element_type=F32).astype(BF16)
    grad_down = shed(down_part)
    grad_second, out_part, gate_part, up_part = token_back(
        fsdp, second_part, gated, down_full, turned, received, grad_gate_pre, grad_up_pre
    )
    grad_gate, grad_up = shed(gate_part), shed(up_part)

    grad_final = output_grad.astype(F32)
    grad_mid_norm, gain_m = rms_back(grad_second, normed_m, inverse_m, gains32[1])
    grad_mid = grad_final + grad_mid_norm
    grad_branch, out_sum = branch_back(fsdp, sp, grad_mid.astype(BF16), out_part)
    layer_out = (mid + out_sum).astype(BF16)
    grad_attended = dot_nt(grad_branch, wo_s).astype(BF16)
    grad_w_output = dot_tn(attended, grad_branch).astype(BF16)
    q_scaled, k_scaled, grad_v_low, q_dots, k_dots, gain_qk = attend_back(
        queries, keys, values, grad_attended, log_sum, q_raw, k_raw, q_inverse, k_inverse,
        gains_own, cosine, sine,
    )
    q_mean, k_mean = two_row_sums(q_dots, k_dots, 6, "norm_grad_sums")
    grad_q_low = (q_inverse * (q_scaled - q_raw * (q_inverse * (q_mean / D)))).astype(BF16)
    grad_k_low = (k_inverse * (k_scaled - k_raw * (k_inverse * (k_mean / D)))).astype(BF16)
    grad_first = dot_nt(grad_q_low, w_all[0]) + dot_nt(grad_k_low, w_all[1])
    grad_first = (grad_first + dot_nt(grad_v_low, w_all[2])).astype(BF16)
    grad_first, grad_q_low, grad_k_low, grad_v_low, grad_w_output = lax.optimization_barrier(
        (grad_first, grad_q_low, grad_k_low, grad_v_low, grad_w_output)
    )
    grad_first = plane_back(grad_first.reshape(sp, TOK_DEV, D), s, sp)
    normed_own, inverse_own = rms_parts(inputs)
    grad_in_norm, gain_a = rms_back(grad_first, normed_own, inverse_own, gains32[0])
    input_grad = grad_mid + grad_in_norm

    parts = [
        dot_tn(first_in, low).astype(BF16).reshape(fsdp, D // fsdp, cols)
        for low in (grad_q_low, grad_k_low, grad_v_low)
    ]
    output_part = grad_w_output.reshape(fsdp, rows, sp, cols).transpose(0, 2, 1, 3)
    parts.append(output_part.reshape(fsdp, sp * rows, cols))
    summed = line_reduce(fsdp, jnp.concatenate(parts, axis=1), 8, "weight_grads")
    summed, grad_gate, grad_up, grad_down = lax.optimization_barrier(
        (summed, grad_gate, grad_up, grad_down)
    )
    summed = summed.astype(BF16)
    height = D // fsdp
    qkv = summed[: 3 * height].reshape(3, height, cols)
    out_rows = summed[3 * height :].reshape(sp, rows, cols).transpose(1, 0, 2).reshape(rows, D)
    wide = jnp.zeros((2, D), F32)
    wide = lax.dynamic_update_slice(wide, gain_qk, (0, s * cols))
    gain_rows = jnp.concatenate([jnp.stack([gain_a, gain_m]), wide], axis=0)
    small = jnp.concatenate(
        [
            grad_router.reshape(count, router_size),
            gain_rows.reshape(4, count, rows).transpose(1, 0, 2).reshape(count, 4 * rows),
        ],
        axis=1,
    )
    small = jnp.pad(small, ((0, 0), (0, misc_rows * 128 - small.shape[1])))
    qkv_own, grad_output, small_all = exchange_end(
        fsdp, sp, qkv, out_rows, small.reshape(count, misc_rows, 128), 9
    )
    qkv_own = qkv_own.transpose(1, 2, 0, 3).reshape(3, rows, D).astype(F32)
    grad_output = grad_output.astype(F32)
    small_sum = jnp.sum(small_all, axis=0).reshape(misc_rows * 128)
    grad_router_own = small_sum[:router_size].reshape(rows, experts)
    grad_gains = small_sum[router_size : router_size + 4 * rows].reshape(4, rows)
    return (
        layer_out, input_grad, qkv_own[0], qkv_own[1], qkv_own[2], grad_output,
        grad_router_own, grad_gains, grad_gate, grad_up, grad_down,
    )


def solution(mesh):
    both, split = P(("fsdp", "sp"), None), P("fsdp", "sp", None)
    gains = P(None, ("fsdp", "sp"))
    return jax.shard_map(
        body,
        mesh=mesh,
        in_specs=(both,) * 7 + (gains,) + (split,) * 3 + (both,),
        out_specs=(both,) * 7 + (gains,) + (split,) * 3,
        check_vma=False,
    )
```

time: 1300 us -> 894 us (0.69)
  matrix products: 295 us -> 65.4 us
  local copies, waits for them, and re-layouts: 119 us -> 39 us
  Pallas kernels: 745 us -> 693 us
  other arithmetic: 106 us -> 58.8 us
    dot_general x17 -> x2, matrix products: 222 us -> 17.9 us  [the longest x1 17.7 us: body(): jnp.einsum('erf,erd->efd', gated, grad_taken, preferred_element_type=F32)]
    pallas_call x5 -> x10, Pallas kernels: 251 us -> 443 us  [the longest x1 85.8 us: token_back(): pl.pallas_call(functools.partial(token_back_kernel, fsdp), out_shape=(jax...]
    pallas_call x2 -> x1, Pallas kernels: 263 us -> 83.1 us  [line_reduce(): pl.pallas_call(functools.partial(line_reduce_kernel, fsdp), out_shape=jax...]
    pallas_call x1, Pallas kernels: 161 us -> 110 us  [gather_start(): pl.pallas_call(functools.partial(start_kernel, fsdp, sp), out_shape=(jax....]
    unnamed x171 -> x85, local copies, waits for them, and re-layouts: 32.4 us -> 8.48 us
    dot_general x5 -> x1, matrix products: 28.7 us -> 5.58 us  [dot_nn(): return jnp.dot(a, b, preferred_element_type=F32)]
    convert_element_type x2 -> x1, local copies, waits for them, and re-layouts: 22.1 us -> 0.04 us  [body(): place = jnp.einsum('ut,fte->feu', before.astype(BF16), chosen.astype(BF16...]
    pallas_call x1, Pallas kernels: 46.8 us -> 27.9 us  [exchange_end(): pl.pallas_call(functools.partial(end_kernel, fsdp, sp), out_shape=(jax.Sh...]
  transfers between devices with their start and end apart: 14 -> 9, of which waited for: 0 -> 1; matrix products, arithmetic and copies ran while one was open for 36% -> 15% of each run, Pallas kernels for 58% -> 72%
where the time goes in v2:
time: 894 us; the launch traced here: 882 us
  Pallas kernels  693 us (78%)
  matrix products  65.4 us (7%)
  other arithmetic  58.8 us (7%)
  local copies, waits for them, and re-layouts  39 us (4%)
  between operations  15 us (2%)
    pallas_call x1, Pallas kernels, gather_start(): pl.pallas_call(functools.partial(start_kernel, fsdp, sp), out_shape=(jax....  110 us
    pallas_call x1, Pallas kernels, token_back(): pl.pallas_call(functools.partial(token_back_kernel, fsdp), out_shape=(jax...  85.8 us
    pallas_call x1, Pallas kernels, branch_back(): pl.pallas_call(functools.partial(branch_back_kernel, fsdp), out_shape=(ja...  84.2 us
    pallas_call x1, Pallas kernels, line_reduce(): pl.pallas_call(functools.partial(line_reduce_kernel, fsdp), out_shape=jax...  83.1 us
    pallas_call x1, Pallas kernels, branch_sum(): pl.pallas_call(functools.partial(branch_kernel, fsdp), out_shape=(jax.Sha...  76.9 us
    pallas_call x1, Pallas kernels, token_gather(): pl.pallas_call(functools.partial(token_kernel, fsdp), out_shape=(jax.Shap...  71.1 us
    pallas_call x1, Pallas kernels, active(): pl.pallas_call(active_kernel, grid=(EXP_DEV, ff // FT), out_shape=(low, l...  31.9 us
    dot_general x4, matrix products, dot_nt(): lax.dot_general(a, b, (((1,), (1,)), ((), ())), preferred_element_type=F32)  28.7 us
  transfers between devices with their start and end apart: 9, of which 1 were waited for; matrix products, arithmetic and copies ran while one was open for 15% of the time, Pallas kernels for 72%

profile of v2, /device:TPU:12, one launch (start us, length us, event | category | flops | bytes accessed | tf_op | source)
XLA Modules:
  0.0 882.1 jit_solution(1733196514857659307)
XLA Ops:
  13.9 109.6 %gather_start.1 = (bf16[1024,2048]{1,0:T(8,128)(2,1)}, bf16[3,2048,512]{2,1,0:T(8,128)(2,1)}, bf16[512,2048]{1,0:T(8,128)(2,1)}, bf16[8,64,2048]{2,1,0:T(8,128)(...) custom-call(bf16[256,2048]{1,0:T(8,128)(2,1)} %x_ref.1, bf16[3,64,2048]{2,1,0:T(8,128)(2,1)} %pad_maximum_fusion.1.w_ref, ...), custom_call_target="tpu_custom_call" | custom-call | tf_op jit(solution)/shard_map/gather_start/pallas_call | solution.py:543
  125.3 12.1 %project.1 = (bf16[1024,2048]{1,0:T(8,128)(2,1)}, f32[1024,512]{1,0:T(8,128)}, f32[1024,512]{1,0:T(8,128)}, bf16[1024,512]{1,0:T(8,128)(2,1)}, f32[1024,1]{1,0:T(8,128)}, /*index=5*/f32[1024,1]{1,0:T(8,128)}) custom-call(bf16[1024,2048]{1,0:T(8,128)(2,1)} %get-tuple-element.65.x_ref, f32[4,2048]{1,0:T(4,128)} %convert_element_type.138.gain, ...), custom_call_target="tpu_custom_call" | custom-call | tf_op jit(solution)/shard_map/project/pallas_call | solution.py:1090
  140.5 6.0 norm_sums.1
  153.3 1.9 fusion.29
  157.2 15.9 %attend.1 = (bf16[1024,512]{1,0:T(8,128)(2,1)}, f32[4,1024,1]{2,1,0:T(8,128)}, bf16[1024,512]{1,0:T(8,128)(2,1)}, bf16[1024,512]{1,0:T(8,128)(2,1)}) custom-call(f32[1024,512]{1,0:T(8,128)} %get-tuple-element.68.q_raw, f32[1024,512]{1,0:T(8,128)} %get-tuple-element.69.k_raw, bf16[1024,512]{1,0:T(8,128)(2,1)} %get-tuple-element.70.v_ref, ...), custom_call_target="tpu_custom_call" | custom-call | tf_op jit(solution)/shard_map/attend/pallas_call | solution.py:1129
  173.1 5.6 convolution_convert_fusion.1
  178.7 76.9 %branch_sum.1 = (f32[256,2048]{1,0:T(8,128)}, bf16[8,192,2048]{2,1,0:T(8,128)(2,1)}) custom-call(bf16[4,256,2048]{2,1,0:T(8,128)(2,1)} %bitcast.109, bf16[192,2048]{1,0:T(8,128)(2,1)} %slice.82.g_ref), custom_call_target="tpu_custom_call" | custom-call | tf_op jit(solution)/shard_map/branch_sum/pallas_call | solution.py:589
  255.5 1.4 fusion.6.picks
  257.6 2.1 multiply_reduce_fusion.2
  260.9 71.1 %token_gather.1 = (bf16[8,256,2048]{2,1,0:T(8,128)(2,1)}, bf16[2,1152,2048]{2,1,0:T(8,128)(2,1)}, f32[2,1152,1024]{2,1,0:T(8,128)}) custom-call(bf16[256,2048]{1,0:T(8,128)(2,1)} %multiply_convert_fusion.2.x_ref, bf16[8,64,2048]{2,1,0:T(8,128)(2,1)} %get-tuple-element.77.g_first, bf16[8,192,2048]{2,1,0:T(8,128)(2,1)} %get-tuple-element.78.g_second, ...), custom_call_target="tpu_custom_call" | custom-call | tf_op jit(solution)/shard_map/token_gather/pallas_call | solution.py:685
  332.1 15.0 %route.1 = (bf16[2,1152,2048]{2,1,0:T(8,128)(2,1)}, f32[8,256,16]{2,1,0:T(8,128)}, f32[2,1152,1]{2,1,0:T(8,128)}) custom-call(bf16[8,288,256]{2,1,0:T(8,128)(2,1)} %fusion.6.picks, bf16[8,256,2048]{2,1,0:T(8,128)(2,1)} %get-tuple-element.79.rows_in.tokens, bf16[16,2048]{1,0:T(8,128)(2,1)} %bitcast.121, f32[2,16]{1,0:T(2,128)} %compare_convert_fusion.columns), custom_call_target="tpu_custom_call" | custom-call | tf_op jit(solution)/shard_map/route/pallas_call | solution.py:1252
  347.0 4.7 all-gather.8.cloned.1.call-done.w_ref
  351.8 31.9 %active.1 = (bf16[2,1152,1024]{2,1,0:T(8,128)(2,1)}, bf16[2,1152,1024]{2,1,0:T(8,128)(2,1)}, bf16[2,1152,1024]{2,1,0:T(8,128)(2,1)}, f32[2,1152,1]{2,1,0:T(8,128)}) custom-call(bf16[2,1152,2048]{2,1,0:T(8,128)(2,1)} %get-tuple-element.80.x_ref, bf16[2,2048,1024]{2,1,0:T(8,128)(2,1)} %all-gather.6.cloned.1.call-done.g_ref, ...), custom_call_target="tpu_custom_call" | custom-call | tf_op jit(solution)/shard_map/active/pallas_call | solution.py:1299
  383.7 17.7 %convolution_convert_fusion = bf16[2,1024,2048]{2,1,0:T(8,128)(2,1)} fusion(bf16[2,1152,1024]{2,1,0:T(8,128)(2,1)} %get-tuple-element.88.gated_ref, bf16[2,1152,2048]{2,1,0:T(8,128)(2,1)} %get-tuple-element.109), kind=kOutput, calls=%fused_computation.2 | convolution fusion | flops 9667870720 | bytes 22544384 | tf_op jit(solution)/shard_map/erf,erd->efd/dot_general | solution.py:1491
  402.9 2.8 fusion.1.turned
  405.7 26.4 %rows_back.1.rows_ref = bf16[2,1152,2048]{2,1,0:T(8,128)(2,1)} custom-call(bf16[2,1152,1024]{2,1,0:T(8,128)(2,1)} %get-tuple-element.83.a_ref.gg_ref, bf16[2,1152,1024]{2,1,0:T(8,128)(2,1)} %get-tuple-element.84.b_ref.gu_ref, bf16[2,2048,1024]{2,1,0:T(8,128)(2,1)} %all-gather.6.cloned.1.call-done.g_ref, bf16[2,2048,1024]{2,1,0:T(8,128)(2,1)} %all-gather.8.cloned.1.call-done.w_ref), custom_call_target="tpu_custom_call" | custom-call | tf_op jit(solution)/shard_map/rows_back/pallas_call | solution.py:1321
  432.1 1.9 subtract_convert_fusion
  435.2 16.5 %combine.1 = (bf16[8,256,2048]{2,1,0:T(8,128)(2,1)}, f32[32,2048]{1,0:T(8,128)}) custom-call(bf16[8,2,256,144]{3,2,1,0:T(8,128)(2,1)} %fusion.1.turned, bf16[2,1152,2048]{2,1,0:T(8,128)(2,1)} %rows_back.1.rows_ref, bf16[8,256,2048]{2,1,0:T(8,128)(2,1)} %get-tuple-element.79.rows_in.tokens, f32[8,256,16]{2,1,0:T(8,128)} %get-tuple-element.85.probs, ...), custom_call_target="tpu_custom_call" | custom-call | tf_op jit(solution)/shard_map/combine/pallas_call | solution.py:1356
  451.7 85.8 %token_back.1 = (f32[256,2048]{1,0:T(8,128)}, bf16[8,256,2048]{2,1,0:T(8,128)(2,1)}, bf16[2,2048,1024]{2,1,0:T(8,128)(2,1)}, bf16[2,2048,1024]{2,1,0:T(8,128)(2,1)}) custom-call(bf16[8,256,2048]{2,1,0:T(8,128)(2,1)} %get-tuple-element.87.p_ref, bf16[2,1152,1024]{2,1,0:T(8,128)(2,1)} %get-tuple-element.88.gated_ref, ...), custom_call_target="tpu_custom_call" | custom-call | tf_op jit(solution)/shard_map/token_back/pallas_call | solution.py:830
  538.8 2.3 multiply_reduce_fusion
  541.3 1.6 fusion.37.x_ref
  542.9 84.2 %branch_back.1 = (bf16[1024,2048]{1,0:T(8,128)(2,1)}, f32[256,2048]{1,0:T(8,128)}) custom-call(bf16[256,2048]{1,0:T(8,128)(2,1)} %fusion.37.x_ref, bf16[8,256,2048]{2,1,0:T(8,128)(2,1)} %get-tuple-element.90.p_ref), custom_call_target="tpu_custom_call" | custom-call | tf_op jit(solution)/shard_map/branch_back/pallas_call | solution.py:880
  627.2 6.2 convolution_convert_fusion.6.g_ref
  633.4 22.9 %attend_back.1 = (f32[1024,512]{1,0:T(8,128)}, f32[1024,512]{1,0:T(8,128)}, bf16[1024,512]{1,0:T(8,128)(2,1)}, f32[1024,1]{1,0:T(8,128)}, f32[1024,1]{1,0:T(8,128)}, /*index=5*/f32[2,512]{1,0:T(2,128)}) custom-call(bf16[1024,512]{1,0:T(8,128)(2,1)} %get-tuple-element.92.q_ref, bf16[1024,512]{1,0:T(8,128)(2,1)} %get-tuple-element.93.k_ref, ...), custom_call_target="tpu_custom_call" | custom-call | tf_op jit(solution)/shard_map/attend_back/pallas_call | solution.py:1195
  659.4 7.5 norm_grad_sums.1
  667.6 4.4 multiply_convert_fusion
  672.1 8.1 fusion.16
  680.2 5.7 fusion.18
  685.9 3.7 convolution_convert_fusion.5
  689.6 8.7 add_convert_fusion
  698.4 1.7 dynamic-slice_bitcast_fusion.2
  701.3 1.5 collective-permute-start
  702.7 1.5 collective-permute-start.1
  707.5 1.8 reshape.289
  709.4 4.6 reshape.284
  714.0 2.2 copy.100
  716.2 4.7 convolution_convert_fusion.4
  721.0 2.4 convolution_convert_fusion.3
  723.4 2.4 convolution_convert_fusion.2
  725.9 3.7 pad_maximum_fusion.p_ref
  729.5 83.1 %weight_grads.1 = f32[1024,512]{1,0:T(8,128)} custom-call(bf16[8,1024,512]{2,1,0:T(8,128)(2,1)} %pad_maximum_fusion.p_ref), custom_call_target="tpu_custom_call" | custom-call | tf_op jit(solution)/shard_map/weight_grads/pallas_call | solution.py:909
  812.7 4.3 fusion.11
  818.1 5.9 fusion.10
  824.0 4.1 convert_element_type.168
  828.1 4.1 convert_element_type.165
  832.2 4.2 convert_element_type.166
  838.5 27.9 %exchange_end.1 = (bf16[4,3,64,512]{3,2,1,0:T(8,128)(2,1)}, bf16[64,2048]{1,0:T(8,128)(2,1)}, f32[32,16,128]{2,1,0:T(8,128)}) custom-call(bf16[3,256,512]{2,1,0:T(8,128)(2,1)} %bitcast.110, bf16[64,2048]{1,0:T(8,128)(2,1)} %bitcast.118, f32[32,16,128]{2,1,0:T(8,128)} %bitcast.117), custom_call_target="tpu_custom_call" | custom-call | tf_op jit(solution)/shard_map/exchange_end/pallas_call | solution.py:1033
  867.4 1.3 convert_bitcast_fusion
  (182 shorter events, 44.8 us)
Async XLA Ops:
  7.2 253.8 %all-gather.4.cloned.1.call-start = ((), (), s32[]{:S(2)}) async-start(), calls=%async_computation.3 | async-start | bytes 10485760 | tf_op jit(solution)/shard_map/all_gather | solution.py:1421
  7.9 1.6 copy-start.3
  7.9 339.1 %all-gather.6.cloned.1.call-start = ((), (), s32[]{:S(2)}) async-start(), calls=%async_computation.4 | async-start | bytes 10485760 | tf_op jit(solution)/shard_map/all_gather | solution.py:1422
  8.7 2.5 copy-start.28
  8.7 3.4 copy-start.29
  8.7 3.5 copy-start.35
  8.7 4.2 copy-start.15
  8.7 4.2 copy-start.16
  8.7 4.2 copy-start.17
  8.7 343.0 %all-gather.8.cloned.1.call-start = ((), (), s32[]{:S(2)}) async-start(), calls=%async_computation.5 | async-start | bytes 10485760 | tf_op jit(solution)/shard_map/all_gather | solution.py:1423
  9.5 814.5 %reduce-scatter.8.cloned.1.call-start = ((), (), s32[]{:S(2)}) async-start(), calls=%async_computation.8 | async-start | bytes 10485760 | tf_op jit(solution)/shard_map/reduce_scatter | solution.py:1489
  137.4 12.0 %copy-start.20 = (s32[8,16,128]{2,1,0:T(8,128)S(1)}, s32[8,16,128]{2,1,0:T(8,128)}, u32[]{:S(2)}) copy-start(s32[8,16,128]{2,1,0:T(8,128)} %get-tuple-element.76) | copy-start | bytes 196612
  157.2 15.9 %copy-start.33 = (bf16[512,2048]{1,0:T(8,128)(2,1)S(1)}, bf16[512,2048]{1,0:T(8,128)(2,1)}, u32[]{:S(2)}) copy-start(bf16[512,2048]{1,0:T(8,128)(2,1)} %get-tuple-element.74) | copy-start | bytes 6291460
  178.7 79.0 %copy-start.1 = (bf16[256,2048]{1,0:T(8,128)(2,1)S(1)}, bf16[256,2048]{1,0:T(8,128)(2,1)}, u32[]{:S(2)}) copy-start(bf16[256,2048]{1,0:T(8,128)(2,1)} %x_ref.1) | copy-start | bytes 3145732
  259.7 281.4 %copy-start.22 = (f32[256]{0:T(256)}, f32[256]{0:T(256)S(1)}, u32[]{:S(2)}) copy-start(f32[256]{0:T(256)S(1)} %add_rsqrt_fusion.3) | copy-start | bytes 3076
  401.4 426.7 %reduce-scatter.4.cloned.1.call-start = ((), (), s32[]{:S(2)}) async-start(), calls=%async_computation.6 | async-start | bytes 10485760 | tf_op jit(solution)/shard_map/reduce_scatter | solution.py:1489
  537.5 294.7 %reduce-scatter.6.cloned.1.call-start = ((), (), s32[]{:S(2)}) async-start(), calls=%async_computation.7 | async-start | bytes 10485760 | tf_op jit(solution)/shard_map/reduce_scatter | solution.py:1489
  538.8 2.3 copy-start
  538.8 2.5 copy-start.4
  541.3 1.6 copy-start.26
  633.4 33.5 %copy-start.19 = (f32[16,128]{1,0:T(8,128)S(1)}, f32[16,128]{1,0:T(8,128)}, u32[]{:S(2)}) copy-start(f32[16,128]{1,0:T(8,128)} %norm_sums.1) | copy-start | bytes 24580
  667.6 12.6 %slice-start = ((s8[6291456]{0:T(1024)(128)(4,1)}), s8[4194304]{0:T(1024)(128)(4,1)S(1)}, s32[]{:S(2)}) async-start(s8[6291456]{0:T(1024)(128)(4,1)} %bitcast.106), calls=%async_computation.9 | async-start | bytes 8388608
  672.1 8.1 copy-start.8
  672.1 8.1 copy-start.10
  672.1 8.1 slice-start.1
  680.2 5.7 copy-start.32
  680.2 5.7 copy-start.34
  685.9 3.7 copy-start.6
  698.3 3.0 copy-start.2
  698.3 6.4 copy-start.30
  698.3 7.8 copy-start.14
  701.3 111.4 %collective-permute-start = (bf16[256,2048]{1,0:T(8,128)(2,1)}, bf16[256,2048]{1,0:T(8,128)(2,1)}, u32[]{:S(2)}, u32[]{:S(2)}) collective-permute-start(bf16[256,2048]{1,0:T(8,128)(2,1)} %get-tuple-element.163), channel_id=1, source_target_pairs={{0,3},{1,2},{2,1},{3,0},{4,7},{5,6},{6,5},{7,4},{8,11},{9,10},{10,... | collective-permute-start | bytes 3145736 | tf_op jit(solution)/shard_map/ppermute | solution.py:1403
  702.7 109.9 %collective-permute-start.1 = (bf16[256,2048]{1,0:T(8,128)(2,1)}, bf16[256,2048]{1,0:T(8,128)(2,1)}, u32[]{:S(2)}, u32[]{:S(2)}) collective-permute-start(bf16[256,2048]{1,0:T(8,128)(2,1)} %get-tuple-element.165), channel_id=1, source_target_pairs={{0,1},{1,0},{2,3},{3,2},{4,5},{5,4},{6,7},{7,6},{8,9},{9,8},{10,11... | collective-permute-start | bytes 3145736 | tf_op jit(solution)/shard_map/ppermute | solution.py:1403
  704.2 108.5 %collective-permute-start.2 = (bf16[256,2048]{1,0:T(8,128)(2,1)}, bf16[256,2048]{1,0:T(8,128)(2,1)}, u32[]{:S(2)}, u32[]{:S(2)}) collective-permute-start(bf16[256,2048]{1,0:T(8,128)(2,1)} %get-tuple-element.164), channel_id=1, source_target_pairs={{0,2},{1,3},{2,0},{3,1},{4,6},{5,7},{6,4},{7,5},{8,10},{9,11},{10,... | collective-permute-start | bytes 3145736 | tf_op jit(solution)/shard_map/ppermute | solution.py:1403
  714.0 2.2 copy-start.11
  716.2 4.8 copy-start.9
  716.2 4.8 copy-start.31
  721.0 2.4 copy-start.7
  729.5 83.2 %copy-start.25 = (f32[256]{0:T(256)S(1)}, f32[256]{0:T(256)}, u32[]{:S(2)}) copy-start(f32[256]{0:T(256)} %add_rsqrt_fusion.2) | copy-start | bytes 3076
  812.6 4.5 copy-start.18
  812.6 4.5 copy-start.21
  812.6 5.4 copy-start.23
  812.6 5.4 copy-start.27
  832.2 4.2 copy-start.5
  867.4 1.5 copy-start.24
  870.2 2.6 copy-start.13
  870.6 3.1 slice-start.2
  870.6 3.9 slice-start.3
  (1 other events, 0.8 us)
Sparse Core Ops, SparseCore 0:
  9.9 129.1 all-gather.3
  140.9 121.3 all-gather.5
  264.1 87.6 all-gather.7
  401.5 86.7 reduce-scatter.7
  537.7 118.6 reduce-scatter.3
  659.3 122.4 reduce-scatter.5

commit v3 on v2

--- a/solution.py
+++ b/solution.py
@@ -2,6 +2,7 @@
 
 import jax
 import jax.numpy as jnp
+import numpy as np
 from jax import lax
 from jax.experimental import pallas as pl
 from jax.experimental.pallas import tpu as pltpu
@@ -217,10 +218,15 @@
             self.swap(i).start()
         for i in self.order:
             self.load(i).start()
-        for i in self.order:
+        self.added = 0
+        self.add_pairs(2)
+
+    def add_pairs(self, until):
+        for i in self.order[self.added : until]:
             self.load(i).wait()
             landed(self.paired.at[i], self.precv.at[i])
             add_rows(self.own.at[i], self.own.at[i], self.paired.at[i], self.rows)
+        self.added = max(self.added, until)
 
     def step(self, t):
         place, lines = self.place, self.lines
@@ -252,6 +258,8 @@
 
             self.left(e).start()
 
+        self.add_pairs(2 * t + 4)
+
     def finish(self, out_ref):
         place, lines, rows = self.place, self.lines, self.rows
 
@@ -318,6 +326,86 @@
         for k in (1, 2):
             self.near(k).wait_send()
             self.on(k).wait_send()
+
+
+class AnyGather:
+    def __init__(self, own, out, f, s, sp, send, recv):
+        self.own, self.out, self.f, self.s, self.sp = own, out, f, s, sp
+        self.send, self.recv = send, recv
+        self.rows = own.shape[0]
+
+    def at(self, place, first, size):
+        return self.out.at[pl.ds(pl.multiple_of(place * self.rows + first, size), size), :]
+
+    def copy(self, k):
+        dst = self.at(self.s, 0, self.rows)
+        return remote(self.own, dst, self.send.at[k], self.recv.at[k], (self.f, self.s ^ k))
+
+    def start(self):
+        for k in range(1, self.sp):
+            self.copy(k).start()
+
+    def forward(self):
+        pass
+
+    def finish(self):
+        for k in range(1, self.sp):
+            landed(self.at(self.s ^ k, 0, self.rows), self.recv.at[k])
+            self.copy(k).wait_send()
+
+
+class AnyReduce:
+    def __init__(self, p_ref, out_ref, scratch, f, s, sp):
+        self.p_ref, self.out_ref, self.f, self.s, self.sp = p_ref, out_ref, f, s, sp
+        self.own, self.got, self.send, self.recv, self.local = scratch
+
+    @staticmethod
+    def scratch(block, sp):
+        dma = pltpu.SemaphoreType.DMA
+        return [
+            pltpu.VMEM(block, BF16), pltpu.VMEM((sp,) + block, BF16), dma((sp,)), dma((sp,)), dma,
+        ]
+
+    def copy(self, k):
+        d = self.s ^ k
+        return remote(
+            self.p_ref.at[d], self.got.at[k], self.send.at[k], self.recv.at[k], (self.f, d)
+        )
+
+    def load(self):
+        return pltpu.make_async_copy(self.p_ref.at[self.s], self.own, self.local)
+
+    def start(self):
+        for k in range(1, self.sp):
+            self.copy(k).start()
+        self.load().start()
+
+    def forward(self):
+        self.load().wait()
+
+    def finish(self):
+        rows = self.own.shape[0]
+        for k in range(1, self.sp):
+            landed(self.got.at[k], self.recv.at[k])
+            add_rows(self.out_ref, self.own if k == 1 else self.out_ref, self.got.at[k], rows)
+        for k in range(1, self.sp):
+            self.copy(k).wait_send()
+
+
+def plane_gather_of(own, out, f, s, sp, send, recv):
+    if sp == 4:
+        return PlaneGather(own, out, f, s, send, recv)
+    return AnyGather(own, out, f, s, sp, send, recv)
+
+
+def plane_reduce_of(p_ref, out_ref, scratch, f, s, sp):
+    if sp == 4:
+        return PlaneReduce(p_ref, out_ref, scratch, f, s)
+    return AnyReduce(p_ref, out_ref, scratch, f, s, sp)
+
+
+def plane_scratch(block, sp):
+    return PlaneReduce.scratch(block) if sp == 4 else AnyReduce.scratch(block, sp)
 
 
 class PlaneReduce:
@@ -390,10 +478,20 @@
             self.on(h, k, n).wait_send()
 
 
-def greet_plane(barrier, f, s):
-    for k in (1, 2):
+def greet_plane(barrier, f, s, sp):
+    ways = (1, 2) if sp == 4 else range(1, sp)
+    for k in ways:
         signal(barrier, (f, s ^ k))
-    return 2
+    return len(ways)
+
+
+def greet_all(barrier, me, count, sp):
+    def greet(i, carry):
+        other = lax.rem(me + i, count)
+        signal(barrier, (other // sp, lax.rem(other, sp)))
+        return carry
+
+    lax.fori_loop(1, count, greet, 0)
 
 
 def rows_view(ref, rows):
@@ -422,11 +520,6 @@
     cols = D // sp
     barrier = pltpu.get_barrier_semaphore()
 
-    def greet(i, carry):
-        other = lax.rem(me + i, count)
-        signal(barrier, (other // sp, lax.rem(other, sp)))
-        return carry
-
     def w_block(s_to):
         return w_ref.at[:, :, pl.ds(pl.multiple_of(s_to * cols, cols), cols)]
 
@@ -448,13 +541,13 @@
     ]
     for copy in owns:
         copy.start()
-    lax.fori_loop(1, count, greet, 0)
+    greet_all(barrier, me, count, sp)
     pl.semaphore_wait(barrier, count - 1)
 
     line = LineGather([w_view, wo_view, block_view(g_all)], [None, None, g_ref], lines, f, s, send, recv)
     line.start_own(2)
     w_copies = []
-    for k in (3, 1, 2):
+    for k in range(sp - 1, 0, -1):
         s_to = s ^ k
         copy = remote(w_block(s_to), w_rows(me), psend.at[k], precv.at[k], (f, s_to))
         copy.start()
@@ -498,7 +591,7 @@
     for k in range(1, sp):
         landed(w_rows(f * sp + (s ^ k)), precv.at[k])
     line.start_own(0)
-    tokens = PlaneGather(x_ref, x_all, f, s, xsend, xrecv)
+    tokens = plane_gather_of(x_ref, x_all, f, s, sp, xsend, xrecv)
     tokens.start()
     landed(wo_view(f), wrecv)
     line.start_own(1)
@@ -554,7 +647,7 @@
         out_specs=[ANY] * 6,
         scratch_shapes=line_sems(3, fsdp)
         + [
-            dma((4,)), dma((4,)), dma((sp,)), dma((sp,)), dma, dma,
+            dma((sp,)), dma((sp,)), dma((sp,)), dma((sp,)), dma, dma,
             dma((count,)), dma((count,)), dma((fsdp,)), dma((fsdp,)), dma((5,)),
         ],
         compiler_params=comm_params(0),
@@ -562,16 +655,16 @@
     )(x, w, wo, g, misc, routes)
 
 
-def branch_kernel(fsdp, p_ref, g_ref, out_ref, g_all, *scratch):
+def branch_kernel(fsdp, sp, p_ref, g_ref, out_ref, g_all, *scratch):
     f, s = lax.axis_index("fsdp"), lax.axis_index("sp")
     lines = fsdp // 2
     barrier = pltpu.get_barrier_semaphore()
-    expected = greet_line(barrier, lines, f, s) + greet_plane(barrier, f, s)
+    expected = greet_line(barrier, lines, f, s) + greet_plane(barrier, f, s, sp)
     send, recv, own_sem = scratch[-3:]
     own = pltpu.make_async_copy(g_ref, g_all.at[f], own_sem)
     own.start()
     pl.semaphore_wait(barrier, expected)
-    plane = PlaneReduce(p_ref, out_ref, scratch[:-3], f, s)
+    plane = plane_reduce_of(p_ref, out_ref, scratch[:-3], f, s, sp)
     line = LineGather([block_view(g_all)], [g_ref], lines, f, s, send, recv)
     plane.start()
     line.start_own(0)
@@ -585,13 +678,13 @@
 
 
 def branch_sum(fsdp, partial, g):
-    block = partial.shape[1:]
+    sp, block = partial.shape[0], partial.shape[1:]
     return pl.pallas_call(
-        functools.partial(branch_kernel, fsdp),
+        functools.partial(branch_kernel, fsdp, sp),
         out_shape=(jax.ShapeDtypeStruct(block, F32), jax.ShapeDtypeStruct((fsdp,) + g.shape, BF16)),
         in_specs=[ANY, VMEM],
         out_specs=[VMEM, ANY],
-        scratch_shapes=PlaneReduce.scratch(block) + line_sems(1, fsdp) + [pltpu.SemaphoreType.DMA],
+        scratch_shapes=plane_scratch(block, sp) + line_sems(1, fsdp) + [pltpu.SemaphoreType.DMA],
         compiler_params=comm_params(2),
         name="branch_sum",
     )(partial, g)
@@ -853,134 +946,160 @@
     )(partial, gated, w_down, turned, received, grad_gate_pre, grad_up_pre)
 
 
-def branch_back_kernel(fsdp, x_ref, p_ref, all_ref, out_ref, xsend, xrecv, own_sem, *scratch):
+class PlaneSum:
+    def __init__(self, scratch, f, s, sp):
+        self.own, self.got, self.send, self.recv = scratch
+        self.f, self.s, self.sp = f, s, sp
+
+    @staticmethod
+    def scratch(seq, sp):
+        dma = pltpu.SemaphoreType.DMA
+        return [
+            pltpu.VMEM((8, seq), F32), pltpu.VMEM((sp, 8, seq), F32), dma((sp,)), dma((sp,)),
+        ]
+
+    def greet(self, barrier):
+        for k in range(1, self.sp):
+            signal(barrier, (self.f, self.s ^ k))
+        return self.sp - 1
+
+    def copy(self, k):
+        return remote(
+            self.own, self.got.at[k], self.send.at[k], self.recv.at[k], (self.f, self.s ^ k)
+        )
+
+    def start(self, x_ref):
+        self.own[...] = x_ref[...].T[:8]
+        for k in range(1, self.sp):
+            self.copy(k).start()
+
+    def finish(self, out_ref):
+        for k in range(1, self.sp):
+            self.copy(k).wait()
+        terms = [self.own[...]] + [self.got[k] for k in range(1, self.sp)]
+        while len(terms) > 1:
+            terms = [terms[i] + terms[i + 1] for i in range(0, len(terms), 2)]
+        seq = out_ref.shape[0]
+        out_ref[...] = jnp.concatenate([terms[0], jnp.zeros((120, seq), F32)], axis=0).T
+
+
+def plane_sum_kernel(sp, x_ref, out_ref, *scratch):
     f, s = lax.axis_index("fsdp"), lax.axis_index("sp")
-    lines = fsdp // 2
+    total = PlaneSum(scratch, f, s, sp)
     barrier = pltpu.get_barrier_semaphore()
-    expected = greet_line(barrier, lines, f, s) + greet_plane(barrier, f, s)
-    plane = PlaneGather(x_ref, all_ref, f, s, xsend, xrecv)
-    own = pltpu.make_async_copy(x_ref, plane.at(s, 0, x_ref.shape[0]), own_sem)
-    own.start()
-    pl.semaphore_wait(barrier, expected)
+    pl.semaphore_wait(barrier, total.greet(barrier))
+    total.start(x_ref)
+    total.finish(out_ref)
+
+
+def plane_sum(sp, x, number, name):
+    seq = x.shape[0]
+    return pl.pallas_call(
+        functools.partial(plane_sum_kernel, sp),
+        out_shape=jax.ShapeDtypeStruct(x.shape, F32),
+        in_specs=[VMEM],
+        out_specs=VMEM,
+        scratch_shapes=PlaneSum.scratch(seq, sp),
+        compiler_params=comm_params(number),
+        name=name,
+    )(x)
+
+
+def end_kernel(
+    fsdp, sp, p_ref, b_ref, x_ref, mid_ref, gain, gains_in, router_ref,
+    grad_out, qkv_0, qkv_1, qkv_2, o_out, small_out,
+    back, summed, low, o_low, gain_sum, pay, small,
+    qsend, qrecv, osend, orecv, msend, mrecv, local, *scratch,
+):
+    f, s = lax.axis_index("fsdp"), lax.axis_index("sp")
+    count, lines = fsdp * sp, fsdp // 2
+    me = f * sp + s
+    rows, cols = o_low.shape[0], D // sp
+    height = D // fsdp
+    barrier = pltpu.get_barrier_semaphore()
+    greet_all(barrier, me, count, sp)
+    pl.semaphore_wait(barrier, count - 1)
+    plane_parts = 6 if sp == 4 else 5
+    plane = plane_reduce_of(b_ref, back, scratch[:plane_parts], f, s, sp)
+    line = LineReduce(p_ref, scratch[plane_parts:], lines, f, s)
     plane.start()
-    line = LineReduce(p_ref, scratch, lines, f, s)
     line.start()
+
+    def input_grads():
+        gain_sum[...] = jnp.zeros_like(gain_sum)
+
+        def chunk(i, carry):
+            at = pl.ds(pl.multiple_of(i * 32, 32), 32)
+            x = x_ref[at, :].astype(F32)
+            inverse = lax.rsqrt(jnp.mean(x * x, axis=-1, keepdims=True) + EPSILON)
+            normed = x * inverse
+            grad_y = back[at, :]
+            scaled = grad_y * gain[0:1, :]
+            mean = jnp.mean(scaled * normed, axis=-1, keepdims=True)
+            grad_out[at, :] = mid_ref[at, :] + inverse * (scaled - normed * mean)
+            gain_sum[0:1, :] += jnp.sum(grad_y * normed, axis=0, keepdims=True)
+            return carry
+
+        lax.fori_loop(0, TOK_DEV // 32, chunk, 0)
+        gain_sum[...] += gains_in[...]
+
+        def fill(i, carry):
+            at = pl.ds(pl.multiple_of(i * rows // 128 * 128, 128), 128)
+            pay[i, 0:8, :] = router_ref[i]
+            pay[i, 8:16, :] = gain_sum[:, at]
+            return carry
+
+        lax.fori_loop(0, count, fill, 0)
+
+    def m_copy(i):
+        other = lax.rem(me + i, count)
+        return remote(
+            pay.at[other], small.at[me], msend.at[i], mrecv.at[me], (other // sp, lax.rem(other, sp))
+        )
+
+    def m_go(i, carry):
+        m_copy(i).start()
+        return carry
+
     for t in range(lines - 1):
         line.step(t)
         if t == min(1, lines - 2):
             plane.forward()
     plane.finish()
-    line.finish(out_ref)
-    own.wait()
-
-
-def branch_back(fsdp, sp, x, partial):
-    block = partial.shape[1:]
-    dma = pltpu.SemaphoreType.DMA
-    return pl.pallas_call(
-        functools.partial(branch_back_kernel, fsdp),
-        out_shape=(
-            jax.ShapeDtypeStruct((sp * x.shape[0], x.shape[1]), BF16),
-            jax.ShapeDtypeStruct(block, F32),
-        ),
-        in_specs=[VMEM, ANY],
-        out_specs=[ANY, VMEM],
-        scratch_shapes=[dma((4,)), dma((4,)), dma] + LineReduce.scratch(fsdp, block),
-        compiler_params=comm_params(5),
-        name="branch_back",
-    )(x, partial)
-
-
-def line_reduce_kernel(fsdp, p_ref, out_ref, *scratch):
-    f, s = lax.axis_index("fsdp"), lax.axis_index("sp")
-    lines = fsdp // 2
-    barrier = pltpu.get_barrier_semaphore()
-    expected = greet_line(barrier, lines, f, s)
-    pl.semaphore_wait(barrier, expected)
-    line = LineReduce(p_ref, scratch, lines, f, s)
-    line.start()
-    for t in range(lines - 1):
-        line.step(t)
-    line.finish(out_ref)
-
-
-def line_reduce(fsdp, partial, number, name):
-    block = partial.shape[1:]
-    return pl.pallas_call(
-        functools.partial(line_reduce_kernel, fsdp),
-        out_shape=jax.ShapeDtypeStruct(block, F32),
-        in_specs=[ANY],
-        out_specs=VMEM,
-        scratch_shapes=LineReduce.scratch(fsdp, block),
-        compiler_params=comm_params(number),
-        name=name,
-    )(partial)
-
-
-def plane_sum_kernel(x_ref, out_ref, got, send, recv):
-    f, s = lax.axis_index("fsdp"), lax.axis_index("sp")
-    barrier = pltpu.get_barrier_semaphore()
-    for k in (1, 2, 3):
-        signal(barrier, (f, s ^ k))
-    pl.semaphore_wait(barrier, 3)
-    copies = []
-    for k in (1, 2, 3):
-        copy = remote(x_ref, got.at[k - 1], send.at[k - 1], recv.at[k - 1], (f, s ^ k))
-        copy.start()
-        copies.append(copy)
-    for copy in copies:
-        copy.wait()
-    near = x_ref[...] + got[0]
-    far = got[1] + got[2]
-    out_ref[...] = near + far
-
-
-def plane_sum(x, number, name):
-    dma = pltpu.SemaphoreType.DMA
-    return pl.pallas_call(
-        plane_sum_kernel,
-        out_shape=jax.ShapeDtypeStruct(x.shape, F32),
-        in_specs=[VMEM],
-        out_specs=VMEM,
-        scratch_shapes=[pltpu.VMEM((3,) + x.shape, F32), dma((3,)), dma((3,))],
-        compiler_params=pltpu.CompilerParams(collective_id=number, has_side_effects=True),
-        name=name,
-    )(x)
-
-
-def end_kernel(
-    fsdp, sp, q_ref, o_ref, m_ref, q_out, o_out, m_out,
-    qsend, qrecv, osend, orecv, msend, mrecv, local,
-):
-    f, s = lax.axis_index("fsdp"), lax.axis_index("sp")
-    count = fsdp * sp
-    me = f * sp + s
-    rows = o_ref.shape[0]
-    barrier = pltpu.get_barrier_semaphore()
-
-    def greet(i, carry):
-        other = lax.rem(me + i, count)
-        signal(barrier, (other // sp, lax.rem(other, sp)))
+    input_grads()
+    lax.fori_loop(1, count, m_go, 0)
+    line.finish(summed)
+
+    def cast(i, carry):
+        at = pl.ds(pl.multiple_of(i * 32, 32), 32)
+        low[at, :] = summed[at, :].astype(BF16)
         return carry
 
-    lax.fori_loop(1, count, greet, 0)
-    pl.semaphore_wait(barrier, count - 1)
-
-    def q_from(place):
-        return q_ref.at[:, pl.ds(pl.multiple_of(place * rows, rows), rows), :]
-
-    q_own = pltpu.make_async_copy(q_from(s), q_out.at[s], local.at[0])
-    q_own.start()
-    copies = []
-    for k in range(1, sp):
-        copy = remote(q_from(s ^ k), q_out.at[s], qsend.at[k], qrecv.at[k], (f, s ^ k))
-        copy.start()
-        copies.append(copy)
+    lax.fori_loop(0, summed.shape[0] // 32, cast, 0)
+    for c in range(sp):
+        first = 3 * height + c * rows
+        o_low[:, c * cols : (c + 1) * cols] = low[first : first + rows, :]
+
+    def q_from(i, place):
+        return low.at[pl.ds(pl.multiple_of(i * height + place * rows, rows), rows), :]
+
+    def q_to(i, place):
+        return (qkv_0, qkv_1, qkv_2)[i].at[:, pl.ds(pl.multiple_of(place * cols, cols), cols)]
+
+    def q_copy(i, k):
+        return remote(q_from(i, s ^ k), q_to(i, s), qsend.at[k, i], qrecv.at[k, i], (f, s ^ k))
+
+    def q_own(i):
+        return pltpu.make_async_copy(q_from(i, s), q_to(i, s), local.at[i])
+
+    for k in range(sp - 1, 0, -1):
+        for i in range(3):
+            q_copy(i, k).start()
     flat = s * fsdp + f
     target_f, target_s = flat // sp, lax.rem(flat, sp)
     stays = jnp.logical_and(target_s == s, target_f == f)
-    o_copy = remote(o_ref, o_out, osend, orecv, (target_f, target_s))
-    o_own = pltpu.make_async_copy(o_ref, o_out, orecv)
+    o_copy = remote(o_low, o_out, osend, orecv, (target_f, target_s))
+    o_own = pltpu.make_async_copy(o_low, o_out, orecv)
 
     @pl.when(stays)
     def _():
@@ -990,61 +1109,62 @@
     def _():
         o_copy.start()
 
-    m_own = pltpu.make_async_copy(m_ref.at[me], m_out.at[me], local.at[1])
-    m_own.start()
-
-    def m_copy(i):
-        other = lax.rem(me + i, count)
-        return remote(
-            m_ref.at[other], m_out.at[me], msend.at[i], mrecv.at[me], (other // sp, lax.rem(other, sp))
-        )
-
-    def m_go(i, carry):
-        m_copy(i).start()
-        return carry
-
-    lax.fori_loop(1, count, m_go, 0)
+    for i in range(3):
+        q_own(i).start()
 
     def m_end(i, carry):
         m_copy(i).wait_send()
         other = lax.rem(me + i, count)
-        landed(m_out.at[other], mrecv.at[other])
-        return carry
-
-    lax.fori_loop(1, count, m_end, 0)
+        landed(small.at[other], mrecv.at[other])
+        return carry + small[other]
+
+    small_out[...] = lax.fori_loop(1, count, m_end, pay[me])
+    for k in range(1, sp):
+        for i in range(3):
+            landed(q_to(i, s ^ k), qrecv.at[k, i])
+            q_copy(i, k).wait_send()
     landed(o_out, orecv)
 
     @pl.when(jnp.logical_not(stays))
     def _():
         o_copy.wait_send()
 
-    for k in range(1, sp):
-        landed(q_out.at[s ^ k], qrecv.at[k])
-    for copy in copies:
-        copy.wait_send()
-    q_own.wait()
-    m_own.wait()
-
-
-def exchange_end(fsdp, sp, q, o, m, number):
+    for i in range(3):
+        q_own(i).wait()
+
+
+def end_exchange(fsdp, sp, partial, back, x, grad_mid, gains, gains_in, router, number):
     count = fsdp * sp
-    rows = o.shape[0]
+    block = partial.shape[1:]
+    rows = D // count
     dma = pltpu.SemaphoreType.DMA
     return pl.pallas_call(
         functools.partial(end_kernel, fsdp, sp),
         out_shape=(
-            jax.ShapeDtypeStruct((sp, 3, rows, D // sp), q.dtype),
-            jax.ShapeDtypeStruct(o.shape, o.dtype),
-            jax.ShapeDtypeStruct(m.shape, m.dtype),
+            jax.ShapeDtypeStruct((TOK_DEV, D), F32),
+            jax.ShapeDtypeStruct((rows, D), BF16),
+            jax.ShapeDtypeStruct((rows, D), BF16),
+            jax.ShapeDtypeStruct((rows, D), BF16),
+            jax.ShapeDtypeStruct((rows, D), BF16),
+            jax.ShapeDtypeStruct((16, 128), F32),
         ),
-        in_specs=[ANY] * 3,
-        out_specs=[ANY] * 3,
+        in_specs=[ANY, ANY, VMEM, VMEM, VMEM, VMEM, VMEM],
+        out_specs=[VMEM, ANY, ANY, ANY, ANY, VMEM],
         scratch_shapes=[
-            dma((sp,)), dma((sp,)), dma, dma, dma((count,)), dma((count,)), dma((2,)),
-        ],
-        compiler_params=pltpu.CompilerParams(collective_id=number, has_side_effects=True),
-        name="exchange_end",
-    )(q, o, m)
+            pltpu.VMEM((TOK_DEV, D), F32),
+            pltpu.VMEM(block, F32),
+            pltpu.VMEM(block, BF16),
+            pltpu.VMEM((rows, D), BF16),
+            pltpu.VMEM((8, D), F32),
+            pltpu.VMEM((count, 16, 128), F32),
+            pltpu.VMEM((count, 16, 128), F32),
+            dma((sp, 3)), dma((sp, 3)), dma, dma, dma((count,)), dma((count,)), dma((3,)),
+        ]
+        + plane_scratch((TOK_DEV, D), sp)
+        + LineReduce.scratch(fsdp, block),
+        compiler_params=comm_params(number),
+        name="end_exchange",
+    )(partial, back, x, grad_mid, gains, gains_in, router)
 
 
 def dot_nt(a, b):
@@ -1063,21 +1183,40 @@
     return pl.BlockSpec(shape, lambda *_: (0,) * len(shape))
 
 
-def turn(v, cosine, sine):
-    return v * cosine + pltpu.roll(v, HEAD_DIM // 2, 1) * sine
-
-
-def project_kernel(x_ref, gain, w_ref, first_out, q_out, k_out, v_out, q_square, k_square):
+def lanes(first, second):
+    lane = lax.broadcasted_iota(jnp.int32, (first.shape[0], 128), 1)
+    return jnp.where(lane == 0, first, jnp.where(lane == 1, second, 0.0))
+
+
+def inverse_of(sums, lane):
+    return lax.rsqrt(sums[:, lane : lane + 1] / D + EPSILON)
+
+
+def turn(v, table, sign=1.0):
+    half = HEAD_DIM // 2
+    front = lax.broadcasted_iota(jnp.int32, table.shape, 1) < half
+    turned = pltpu.roll(table, half, 1)
+    cosine = jnp.where(front, table, turned)
+    sine = jnp.where(front, -turned, table)
+    return v * cosine + pltpu.roll(v, half, 1) * (sine * sign)
+
+
+def turn_back(v, table):
+    return turn(v, table, -1.0)
+
+
+def project_kernel(x_ref, gain, w_ref, first_out, q_out, k_out, v_out, squares):
     x = x_ref[...].astype(F32)
     inverse = lax.rsqrt(jnp.mean(x * x, axis=-1, keepdims=True) + EPSILON)
     first = (x * inverse * gain[0:1, :]).astype(BF16)
     first_out[...] = first
     q = dot_nn(first, w_ref[0])
     q_out[...] = q
-    q_square[...] = jnp.sum(q * q, axis=-1, keepdims=True)
     k = dot_nn(first, w_ref[1])
     k_out[...] = k
-    k_square[...] = jnp.sum(k * k, axis=-1, keepdims=True)
+    squares[...] = lanes(
+        jnp.sum(q * q, axis=-1, keepdims=True), jnp.sum(k * k, axis=-1, keepdims=True)
+    )
     v_out[...] = dot_nn(first, w_ref[2]).astype(BF16)
 
 
@@ -1095,22 +1234,27 @@
             jax.ShapeDtypeStruct((seq, cols), F32),
             jax.ShapeDtypeStruct((seq, cols), F32),
             jax.ShapeDtypeStruct((seq, cols), BF16),
-            jax.ShapeDtypeStruct((seq, 1), F32),
-            jax.ShapeDtypeStruct((seq, 1), F32),
+            jax.ShapeDtypeStruct((seq, 128), F32),
         ),
         in_specs=[block(D), whole(gains.shape), whole(w.shape)],
-        out_specs=[block(D), block(cols), block(cols), block(cols), block(1), block(1)],
+        out_specs=[block(D), block(cols), block(cols), block(cols), block(128)],
         compiler_params=pltpu.CompilerParams(vmem_limit_bytes=VLIM),
         name="project",
     )(x, gains, w)
 
 
 def attend_kernel(
-    q_raw, k_raw, v_ref, q_inv, k_inv, gain, cosine, sine, o_ref, sum_ref, q_ref, k_ref
+    q_raw, k_raw, v_ref, squares, gain, table, o_ref, sum_ref, q_ref, k_ref
 ):
-    c, d = cosine[...], sine[...]
-    q_ref[...] = turn(q_raw[...] * q_inv[...] * gain[2:3, :], c, d).astype(BF16)
-    k_ref[...] = turn(k_raw[...] * k_inv[...] * gain[3:4, :], c, d).astype(BF16)
+    head = pl.program_id(0)
+
+    @pl.when(head == 0)
+    def _():
+        sum_ref[...] = squares[...]
+
+    q_inv, k_inv = inverse_of(squares, 0), inverse_of(squares, 1)
+    q_ref[...] = turn(q_raw[...] * q_inv * gain[2:3, :], table[...]).astype(BF16)
+    k_ref[...] = turn(k_raw[...] * k_inv * gain[3:4, :], table[...]).astype(BF16)
     for i in range(q_ref.shape[0] // BLK):
         rows, seen = pl.ds(i * BLK, BLK), pl.ds(0, (i + 1) * BLK)
         scores = dot_nt(q_ref[rows, :], k_ref[seen, :]) * SCALE
@@ -1119,10 +1263,11 @@
         row_sum = jnp.sum(exp_rows, axis=-1, keepdims=True)
         probs = (exp_rows / row_sum).astype(BF16)
         o_ref[rows, :] = dot_nn(probs, v_ref[seen, :]).astype(BF16)
-        sum_ref[0, rows, :] = row_max + jnp.log(row_sum)
-
-
-def attend(q_raw, k_raw, v, q_inv, k_inv, gains, cosine, sine):
+        lane = lax.broadcasted_iota(jnp.int32, (BLK, 128), 1)
+        sum_ref[rows, :] += jnp.where(lane == head + 2, row_max + jnp.log(row_sum), 0.0)
+
+
+def attend(q_raw, k_raw, v, squares, gains, table):
     seq, width = v.shape
     heads = width // HEAD_DIM
     spec = pl.BlockSpec((seq, HEAD_DIM), lambda h: (0, h))
@@ -1131,86 +1276,198 @@
         grid=(heads,),
         out_shape=(
             jax.ShapeDtypeStruct((seq, width), BF16),
-            jax.ShapeDtypeStruct((heads, seq, 1), F32),
+            jax.ShapeDtypeStruct((seq, 128), F32),
             jax.ShapeDtypeStruct((seq, width), BF16),
             jax.ShapeDtypeStruct((seq, width), BF16),
         ),
         in_specs=[
-            spec, spec, spec, whole((seq, 1)), whole((seq, 1)),
+            spec, spec, spec, whole((seq, 128)),
             pl.BlockSpec((4, HEAD_DIM), lambda h: (0, h)),
-            whole((seq, HEAD_DIM)), whole((seq, HEAD_DIM)),
+            whole((seq, HEAD_DIM)),
         ],
-        out_specs=[spec, pl.BlockSpec((1, seq, 1), lambda h: (h, 0, 0)), spec, spec],
+        out_specs=[spec, whole((seq, 128)), spec, spec],
         compiler_params=pltpu.CompilerParams(vmem_limit_bytes=VLIM),
         name="attend",
-    )(q_raw, k_raw, v, q_inv, k_inv, gains, cosine, sine)
-
-
-def attend_back_kernel(
-    q_ref, k_ref, v_ref, g_ref, sum_ref, q_raw, k_raw, q_inv, k_inv, gain, cosine, sine,
-    q_scaled, k_scaled, dv_out, q_dots, k_dots, gains_out, dk_ref, dv_ref,
+    )(q_raw, k_raw, v, squares, gains, table)
+
+
+def attend_back_head(
+    h, q_ref, k_ref, v_ref, sums, q_raw, k_raw, gain, table,
+    q_scaled, k_scaled, dv_out, dots, gains_out, dv_ref,
 ):
-    head = pl.program_id(0)
-
-    @pl.when(head == 0)
-    def _():
-        q_dots[...] = jnp.zeros_like(q_dots)
-        k_dots[...] = jnp.zeros_like(k_dots)
-
-    dk_ref[...] = jnp.zeros_like(dk_ref)
+    head = slice(h * HEAD_DIM, (h + 1) * HEAD_DIM)
+    k_scaled[:, head] = jnp.zeros(k_raw[:, head].shape, F32)
     dv_ref[...] = jnp.zeros_like(dv_ref)
-    gain_q, gain_k = gain[2:3, :], gain[3:4, :]
+    gain_q, gain_k = gain[2:3, head], gain[3:4, head]
     gain_sum = jnp.zeros((1, HEAD_DIM), F32)
-    for i in range(q_ref.shape[0] // BLK):
-        rows, seen = pl.ds(i * BLK, BLK), pl.ds(0, (i + 1) * BLK)
-        q, g, keys = q_ref[rows, :], g_ref[rows, :], k_ref[seen, :]
+    size = BLK if q_ref.shape[0] <= 4 * BLK else BLK // 2
+    for i in range(q_ref.shape[0] // size):
+        rows, seen = pl.ds(i * size, size), pl.ds(0, (i * size // BLK + 1) * BLK)
+        q, g, keys = q_ref[rows, head], dv_out[rows, head], k_ref[seen, head]
         scores = dot_nt(q, keys) * SCALE
-        probs = jnp.exp(scores - sum_ref[0, rows, :])
-        grad_probs = dot_nt(g, v_ref[seen, :])
+        probs = jnp.exp(scores - sums[rows, h + 2 : h + 3])
+        grad_probs = dot_nt(g, v_ref[seen, head])
         row_dot = jnp.sum(probs * grad_probs, axis=-1, keepdims=True)
         grad_scores = (probs * (grad_probs - row_dot)).astype(BF16)
-        dk_ref[seen, :] += dot_tn(grad_scores, q)
+        k_scaled[seen, head] += dot_tn(grad_scores, q)
         dv_ref[seen, :] += dot_tn(probs.astype(BF16), g)
-        grad_y = turn(dot_nn(grad_scores, keys) * SCALE, cosine[rows, :], -sine[rows, :])
-        normed = q_raw[rows, :] * q_inv[rows, :]
+        grad_y = turn_back(dot_nn(grad_scores, keys) * SCALE, table[rows, :])
+        normed = q_raw[rows, head] * inverse_of(sums.at[rows, :], 0)
         scaled = grad_y * gain_q
-        q_scaled[rows, :] = scaled
-        q_dots[rows, :] += jnp.sum(scaled * normed, axis=-1, keepdims=True)
+        q_scaled[rows, head] = scaled
+        dots[rows, :] += lanes(jnp.sum(scaled * normed, axis=-1, keepdims=True), 0.0)
         gain_sum += jnp.sum(grad_y * normed, axis=0, keepdims=True)
-    grad_y = turn(dk_ref[...] * SCALE, cosine[...], -sine[...])
-    normed = k_raw[...] * k_inv[...]
+    grad_y = turn_back(k_scaled[:, head] * SCALE, table[...])
+    normed = k_raw[:, head] * inverse_of(sums, 1)
     scaled = grad_y * gain_k
-    k_scaled[...] = scaled
-    k_dots[...] += jnp.sum(scaled * normed, axis=-1, keepdims=True)
-    gains_out[0:1, :] = gain_sum
-    gains_out[1:2, :] = jnp.sum(grad_y * normed, axis=0, keepdims=True)
-    dv_out[...] = dv_ref[...].astype(BF16)
-
-
-def attend_back(q, k, v, g, log_sum, q_raw, k_raw, q_inv, k_inv, gains, cosine, sine):
+    k_scaled[:, head] = scaled
+    k_dots = jnp.sum(scaled * normed, axis=-1, keepdims=True)
+    dots[...] += lanes(jnp.zeros_like(k_dots), k_dots)
+    gains_out[0:1, head] = gain_sum
+    gains_out[1:2, head] = jnp.sum(grad_y * normed, axis=0, keepdims=True)
+    dv_out[:, head] = dv_ref[...].astype(BF16)
+
+
+def branch_back_kernel(
+    fsdp, sp, x_ref, p_ref, wo_ref, q_ref, k_ref, v_ref, sums, q_raw, k_raw, gain, table,
+    all_ref, out_ref, q_scaled, k_scaled, dv_out, dots, gains_out,
+    g_all, dv_ref, xsend, xrecv, own_sem, all_sem, *scratch,
+):
+    f, s = lax.axis_index("fsdp"), lax.axis_index("sp")
+    lines = fsdp // 2
+    barrier = pltpu.get_barrier_semaphore()
+    sums_over = PlaneSum(scratch[:4], f, s, sp)
+    expected = greet_line(barrier, lines, f, s) + sums_over.greet(barrier)
+    plane = plane_gather_of(x_ref, g_all, f, s, sp, xsend, xrecv)
+    own = pltpu.make_async_copy(x_ref, plane.at(s, 0, x_ref.shape[0]), own_sem)
+    own.start()
+    pl.semaphore_wait(barrier, expected)
+    plane.start()
+    line = LineReduce(p_ref, scratch[4:], lines, f, s)
+    line.start()
+    dots[...] = jnp.zeros_like(dots)
+    out_all = pltpu.make_async_copy(g_all, all_ref, all_sem)
+    for t in range(lines - 1):
+        line.step(t)
+        if t == min(1, lines - 2):
+            plane.forward()
+    plane.finish()
+    own.wait()
+    out_all.start()
+
+    def block(i, carry):
+        at = pl.ds(pl.multiple_of(i * TOK_DEV, TOK_DEV), TOK_DEV)
+        dv_out[at, :] = dot_nt(g_all[at, :], wo_ref[...]).astype(BF16)
+        return carry
+
+    lax.fori_loop(0, sp, block, 0)
+    for h in range(q_ref.shape[1] // HEAD_DIM):
+        attend_back_head(
+            h, q_ref, k_ref, v_ref, sums, q_raw, k_raw, gain, table,
+            q_scaled, k_scaled, dv_out, dots, gains_out, dv_ref,
+        )
+    sums_over.start(dots)
+    line.finish(out_ref)
+    sums_over.finish(dots)
+    out_all.wait()
+
+
+def branch_back(fsdp, sp, x, partial, wo, q, k, v, sums, q_raw, k_raw, gains, table):
+    block = partial.shape[1:]
     seq, width = q.shape
-    heads = width // HEAD_DIM
-    spec = pl.BlockSpec((seq, HEAD_DIM), lambda h: (0, h))
-    column, table = whole((seq, 1)), whole((seq, HEAD_DIM))
+    dma = pltpu.SemaphoreType.DMA
     return pl.pallas_call(
-        attend_back_kernel,
-        grid=(heads,),
+        functools.partial(branch_back_kernel, fsdp, sp),
         out_shape=(
+            jax.ShapeDtypeStruct((seq, D), BF16),
+            jax.ShapeDtypeStruct(block, F32),
             jax.ShapeDtypeStruct((seq, width), F32),
             jax.ShapeDtypeStruct((seq, width), F32),
             jax.ShapeDtypeStruct((seq, width), BF16),
-            jax.ShapeDtypeStruct((seq, 1), F32),
-            jax.ShapeDtypeStruct((seq, 1), F32),
+            jax.ShapeDtypeStruct((seq, 128), F32),
             jax.ShapeDtypeStruct((2, width), F32),
         ),
-        in_specs=[spec] * 4
-        + [pl.BlockSpec((1, seq, 1), lambda h: (h, 0, 0)), spec, spec, column, column]
-        + [pl.BlockSpec((4, HEAD_DIM), lambda h: (0, h)), table, table],
-        out_specs=[spec] * 3 + [column, column, pl.BlockSpec((2, HEAD_DIM), lambda h: (0, h))],
-        scratch_shapes=[pltpu.VMEM((seq, HEAD_DIM), F32)] * 2,
+        in_specs=[VMEM, ANY] + [VMEM] * 9,
+        out_specs=[ANY] + [VMEM] * 6,
+        scratch_shapes=[
+            pltpu.VMEM((seq, D), BF16), pltpu.VMEM((seq, HEAD_DIM), F32), dma((sp,)), dma((sp,)), dma, dma,
+        ]
+        + PlaneSum.scratch(seq, sp)
+        + LineReduce.scratch(fsdp, block),
+        compiler_params=comm_params(5),
+        name="branch_back",
+    )(x, partial, wo, q, k, v, sums, q_raw, k_raw, gains, table)
+
+
+def held(shape):
+    return pl.BlockSpec(
+        shape, lambda *_: (0,) * len(shape), pipeline_mode=pl.Buffered(buffer_count=1)
+    )
+
+
+def weight_kernel(
+    q_scaled, k_scaled, q_raw, k_raw, squares, dots, dv_ref, first, attended, g_ref, w_ref,
+    out, back, low, square,
+):
+    f = pl.program_id(0)
+    height = first.shape[1]
+    rows = out.shape[1] - 3 * height
+    cols = out.shape[2]
+    sp = D // cols
+
+    @pl.when(f == 0)
+    def _():
+        for n, scaled, raw in ((0, q_scaled, q_raw), (1, k_scaled, k_raw)):
+            inverse = inverse_of(squares, n)
+            mean = dots[:, n : n + 1] / D
+            low[:, n * cols : (n + 1) * cols] = (
+                inverse * (scaled[...] - raw[...] * (inverse * mean))
+            ).astype(BF16)
+        low[:, 2 * cols :] = dv_ref[...]
+        for c in range(sp):
+            at = slice(c * cols, (c + 1) * cols)
+            square[:, at] = dot_tn(attended[...], g_ref[:, at]).astype(BF16)
+
+    grads = dot_tn(first[...], low[...]).astype(BF16)
+    for n in range(3):
+        out[0, n * height : (n + 1) * height, :] = grads[:, n * cols : (n + 1) * cols]
+    each = rows // sp
+    from_rows = pl.ds(pl.multiple_of(f * each, each), each)
+    for c in range(sp):
+        at = 3 * height + c * each
+        out[0, at : at + each, :] = square[from_rows, c * cols : (c + 1) * cols]
+    total = dot_nt(low[:, :cols], w_ref[0]) + dot_nt(low[:, cols : 2 * cols], w_ref[1])
+    back[...] = (total + dot_nt(low[:, 2 * cols :], w_ref[2])).astype(BF16)
+
+
+def weight_parts(fsdp, q_scaled, k_scaled, q_raw, k_raw, squares, dots, dv, first, attended, g, w):
+    seq, cols = dv.shape
+    height = D // fsdp
+    each = cols // fsdp
+    return pl.pallas_call(
+        weight_kernel,
+        grid=(fsdp,),
+        out_shape=(
+            jax.ShapeDtypeStruct((fsdp, 3 * height + D // cols * each, cols), BF16),
+            jax.ShapeDtypeStruct((seq, D), BF16),
+        ),
+        in_specs=[held((seq, cols))] * 4
+        + [held((seq, 128))] * 2
+        + [
+            held((seq, cols)),
+            pl.BlockSpec((seq, height), lambda f: (0, f)),
+            held((seq, cols)),
+            held((seq, D)),
+            pl.BlockSpec((3, height, cols), lambda f: (0, f, 0)),
+        ],
+        out_specs=[
+            pl.BlockSpec((1, 3 * height + D // cols * each, cols), lambda f: (f, 0, 0)),
+            pl.BlockSpec((seq, height), lambda f: (0, f)),
+        ],
+        scratch_shapes=[pltpu.VMEM((seq, 3 * cols), BF16), pltpu.VMEM((cols, D), BF16)],
         compiler_params=pltpu.CompilerParams(vmem_limit_bytes=VLIM),
-        name="attend_back",
-    )(q, k, v, g, log_sum, q_raw, k_raw, q_inv, k_inv, gains, cosine, sine)
+        name="weight_parts",
+    )(q_scaled, k_scaled, q_raw, k_raw, squares, dots, dv, first, attended, g, w)
 
 
 def two_parts(x, axis):
@@ -1275,30 +1532,35 @@
     def _():
         dots[...] = jnp.zeros_like(dots)
 
-    gate_pre = dot_nn(x_ref[0], g_ref[0])
-    up_pre = dot_nn(x_ref[0], w_ref[0])
-    sig = jax.nn.sigmoid(gate_pre)
-    silu = gate_pre * sig
-    hidden = silu * up_pre
-    back = u_ref[0]
-    gate = gates[0]
-    dots[0] += jnp.sum(hidden * back, axis=1, keepdims=True)
-    gated[0] = (hidden * gate).astype(BF16)
-    back = back * gate
-    grad_gate[0] = (back * up_pre * (sig * (1.0 + gate_pre * (1.0 - sig)))).astype(BF16)
-    grad_up[0] = (back * silu).astype(BF16)
+    total = x_ref.shape[1]
+    chunk = total // 4
+    for first in range(0, total, chunk):
+        at = slice(first, first + chunk)
+        gate_pre = dot_nn(x_ref[0, at, :], g_ref[0])
+        up_pre = dot_nn(x_ref[0, at, :], w_ref[0])
+        sig = jax.nn.sigmoid(gate_pre)
+        silu = gate_pre * sig
+        hidden = silu * up_pre
+        back = u_ref[0, at, :]
+        gate = gates[0, at, :]
+        dots[0, at, :] += jnp.sum(hidden * back, axis=1, keepdims=True)
+        gated[0, at, :] = (hidden * gate).astype(BF16)
+        back = back * gate
+        grad_gate[0, at, :] = (back * up_pre * (sig * (1.0 + gate_pre * (1.0 - sig)))).astype(BF16)
+        grad_up[0, at, :] = (back * silu).astype(BF16)
 
 
 def active(x, w_gate, w_up, u, gates):
     _, total, _ = x.shape
     ff = w_up.shape[2]
-    tile = pl.BlockSpec((1, total, FT), lambda e, j: (e, 0, j))
-    weight = pl.BlockSpec((1, D, FT), lambda e, j: (e, 0, j))
+    wide = 2 * FT
+    tile = pl.BlockSpec((1, total, wide), lambda e, j: (e, 0, j))
+    weight = pl.BlockSpec((1, D, wide), lambda e, j: (e, 0, j))
     column = pl.BlockSpec((1, total, 1), lambda e, j: (e, 0, 0))
     low = jax.ShapeDtypeStruct((EXP_DEV, total, ff), BF16)
     return pl.pallas_call(
         active_kernel,
-        grid=(EXP_DEV, ff // FT),
+        grid=(EXP_DEV, ff // wide),
         out_shape=(low, low, low, jax.ShapeDtypeStruct((EXP_DEV, total, 1), F32)),
         in_specs=[
             pl.BlockSpec((1, total, D), lambda e, j: (e, 0, 0)), weight, weight, tile, column,
@@ -1307,6 +1569,27 @@
         compiler_params=pltpu.CompilerParams(vmem_limit_bytes=VLIM),
         name="active",
     )(x, w_gate, w_up, u, gates)
+
+
+def down_grad_kernel(a_ref, g_ref, out):
+    out[0] = dot_tn(a_ref[0], g_ref[0]).astype(BF16)
+
+
+def down_grad(gated, g):
+    _, total, ff = gated.shape
+    size = D // 2
+    return pl.pallas_call(
+        down_grad_kernel,
+        grid=(EXP_DEV, D // size),
+        out_shape=jax.ShapeDtypeStruct((EXP_DEV, ff, D), BF16),
+        in_specs=[
+            pl.BlockSpec((1, total, ff), lambda e, j: (e, 0, 0)),
+            pl.BlockSpec((1, total, size), lambda e, j: (e, 0, j)),
+        ],
+        out_specs=pl.BlockSpec((1, ff, size), lambda e, j: (e, 0, j)),
+        compiler_params=pltpu.CompilerParams(vmem_limit_bytes=VLIM),
+        name="down_grad",
+    )(gated, g)
 
 
 def rows_back_kernel(a_ref, b_ref, g_ref, w_ref, out):
@@ -1382,26 +1665,10 @@
     return (grad_in, jnp.sum(grad_out * normed, axis=0))
 
 
-def angles(positions):
-    freqs = ROPE_BASE ** (-2.0 * jnp.arange(HEAD_DIM // 2, dtype=F32) / HEAD_DIM)
-    turned = positions.astype(F32)[:, None] * freqs[None, :]
-    cosine, sine = jnp.cos(turned), jnp.sin(turned)
-    return (jnp.concatenate([cosine, cosine], axis=1), jnp.concatenate([-sine, sine], axis=1))
-
-
-def two_row_sums(first, second, number, name):
-    seq = first.shape[0]
-    packed = jnp.concatenate([first, second], axis=0).reshape(2 * seq // 128, 128)
-    total = plane_sum(packed, number, name).reshape(2, seq, 1)
-    return total[0], total[1]
-
-
-def plane_back(partial, s, sp):
-    total = lax.dynamic_index_in_dim(partial, s, axis=0, keepdims=False).astype(F32)
-    for k in (3, 1, 2):
-        piece = lax.dynamic_index_in_dim(partial, s ^ k, axis=0, keepdims=False)
-        total = total + lax.ppermute(piece, "sp", [(i, i ^ k) for i in range(sp)]).astype(F32)
-    return total
+def angles(seq):
+    freqs = np.float32(ROPE_BASE) ** (-2.0 * np.arange(HEAD_DIM // 2, dtype=np.float32) / HEAD_DIM)
+    turned = np.arange(seq, dtype=np.float32)[:, None] * freqs[None, :].astype(np.float32)
+    return jnp.asarray(np.concatenate([np.cos(turned), np.sin(turned)], axis=1), F32)
 
 
 def body(
@@ -1455,13 +1722,11 @@
     ).astype(BF16)
     columns = (jnp.arange(experts, dtype=jnp.int32)[None, :] == own_ids[:, None]).astype(F32)
 
-    first_in, q_raw, k_raw, values, q_square, k_square = project(x_all, gains32, w_all)
-    q_square, k_square = two_row_sums(q_square, k_square, 1, "norm_sums")
-    q_inverse = lax.rsqrt(q_square / D + EPSILON)
-    k_inverse = lax.rsqrt(k_square / D + EPSILON)
-    cosine, sine = angles(jnp.arange(seq, dtype=jnp.int32))
-    attended, log_sum, queries, keys = attend(
-        q_raw, k_raw, values, q_inverse, k_inverse, gains_own, cosine, sine
+    first_in, q_raw, k_raw, values, squares = project(x_all, gains32, w_all)
+    squares = plane_sum(sp, squares, 1, "norm_sums")
+    table = angles(seq)
+    attended, sums, queries, keys = attend(
+        q_raw, k_raw, values, squares, gains_own, table
     )
     branch = dot_nn(attended, wo_s).astype(BF16).reshape(sp, TOK_DEV, D)
     inputs = layer_input.astype(F32)
@@ -1488,8 +1753,7 @@
     def shed(grad):
         return lax.psum_scatter(grad, "sp", scatter_dimension=1, tiled=True).astype(F32)
 
-    down_part = jnp.einsum("erf,erd->efd", gated, grad_taken, preferred_element_type=F32).astype(BF16)
-    grad_down = shed(down_part)
+    grad_down = shed(down_grad(gated, grad_taken))
     grad_second, out_part, gate_part, up_part = token_back(
         fsdp, second_part, gated, down_full, turned, received, grad_gate_pre, grad_up_pre
     )
@@ -1498,62 +1762,30 @@
     grad_final = output_grad.astype(F32)
     grad_mid_norm, gain_m = rms_back(grad_second, normed_m, inverse_m, gains32[1])
     grad_mid = grad_final + grad_mid_norm
-    grad_branch, out_sum = branch_back(fsdp, sp, grad_mid.astype(BF16), out_part)
+    grad_branch, out_sum, q_scaled, k_scaled, grad_values, dots, gain_qk = branch_back(
+        fsdp, sp, grad_mid.astype(BF16), out_part, wo_s, queries, keys, values, sums, q_raw, k_raw,
+        gains_own, table,
+    )
     layer_out = (mid + out_sum).astype(BF16)
-    grad_attended = dot_nt(grad_branch, wo_s).astype(BF16)
-    grad_w_output = dot_tn(attended, grad_branch).astype(BF16)
-    q_scaled, k_scaled, grad_v_low, q_dots, k_dots, gain_qk = attend_back(
-        queries, keys, values, grad_attended, log_sum, q_raw, k_raw, q_inverse, k_inverse,
-        gains_own, cosine, sine,
+    weight_part, first_part = weight_parts(
+        fsdp, q_scaled, k_scaled, q_raw, k_raw, squares, dots, grad_values, first_in, attended,
+        grad_branch, w_all,
     )
-    q_mean, k_mean = two_row_sums(q_dots, k_dots, 6, "norm_grad_sums")
-    grad_q_low = (q_inverse * (q_scaled - q_raw * (q_inverse * (q_mean / D)))).astype(BF16)
-    grad_k_low = (k_inverse * (k_scaled - k_raw * (k_inverse * (k_mean / D)))).astype(BF16)
-    grad_first = dot_nt(grad_q_low, w_all[0]) + dot_nt(grad_k_low, w_all[1])
-    grad_first = (grad_first + dot_nt(grad_v_low, w_all[2])).astype(BF16)
-    grad_first, grad_q_low, grad_k_low, grad_v_low, grad_w_output = lax.optimization_barrier(
-        (grad_first, grad_q_low, grad_k_low, grad_v_low, grad_w_output)
+
+    gain_rows = lax.dynamic_update_slice(jnp.zeros((8, D), F32), gain_qk, (2, s * cols))
+    gain_rows = gain_rows.at[1].set(gain_m)
+    router_part = grad_router.reshape(count, router_size)
+    router_part = jnp.pad(router_part, ((0, 0), (0, 1024 - router_size))).reshape(count, 8, 128)
+    input_grad, *weight_grads, small = end_exchange(
+        fsdp, sp, weight_part, first_part.reshape(sp, TOK_DEV, D), layer_input, grad_mid, gains32,
+        gain_rows, router_part, 8,
     )
-    grad_first = plane_back(grad_first.reshape(sp, TOK_DEV, D), s, sp)
-    normed_own, inverse_own = rms_parts(inputs)
-    grad_in_norm, gain_a = rms_back(grad_first, normed_own, inverse_own, gains32[0])
-    input_grad = grad_mid + grad_in_norm
-
-    parts = [
-        dot_tn(first_in, low).astype(BF16).reshape(fsdp, D // fsdp, cols)
-        for low in (grad_q_low, grad_k_low, grad_v_low)
-    ]
-    output_part = grad_w_output.reshape(fsdp, rows, sp, cols).transpose(0, 2, 1, 3)
-    parts.append(output_part.reshape(fsdp, sp * rows, cols))
-    summed = line_reduce(fsdp, jnp.concatenate(parts, axis=1), 8, "weight_grads")
-    summed, grad_gate, grad_up, grad_down = lax.optimization_barrier(
-        (summed, grad_gate, grad_up, grad_down)
-    )
-    summed = summed.astype(BF16)
-    height = D // fsdp
-    qkv = summed[: 3 * height].reshape(3, height, cols)
-    out_rows = summed[3 * height :].reshape(sp, rows, cols).transpose(1, 0, 2).reshape(rows, D)
-    wide = jnp.zeros((2, D), F32)
-    wide = lax.dynamic_update_slice(wide, gain_qk, (0, s * cols))
-    gain_rows = jnp.concatenate([jnp.stack([gain_a, gain_m]), wide], axis=0)
-    small = jnp.concatenate(
-        [
-            grad_router.reshape(count, router_size),
-            gain_rows.reshape(4, count, rows).transpose(1, 0, 2).reshape(count, 4 * rows),
-        ],
-        axis=1,
-    )
-    small = jnp.pad(small, ((0, 0), (0, misc_rows * 128 - small.shape[1])))
-    qkv_own, grad_output, small_all = exchange_end(
-        fsdp, sp, qkv, out_rows, small.reshape(count, misc_rows, 128), 9
-    )
-    qkv_own = qkv_own.transpose(1, 2, 0, 3).reshape(3, rows, D).astype(F32)
-    grad_output = grad_output.astype(F32)
-    small_sum = jnp.sum(small_all, axis=0).reshape(misc_rows * 128)
-    grad_router_own = small_sum[:router_size].reshape(rows, experts)
-    grad_gains = small_sum[router_size : router_size + 4 * rows].reshape(4, rows)
+    weight_grads = [grad.astype(F32) for grad in weight_grads]
+    grad_router_own = small[:8].reshape(1024)[:router_size].reshape(rows, experts)
+    first_lane = (f * sp + s) * rows % 128
+    grad_gains = lax.dynamic_slice(small[8:12], (0, first_lane), (4, rows))
     return (
-        layer_out, input_grad, qkv_own[0], qkv_own[1], qkv_own[2], grad_output,
+        layer_out, input_grad, *weight_grads,
         grad_router_own, grad_gains, grad_gate, grad_up, grad_down,
     )
 

time: 894 us -> 826 us (0.924)
  matrix products: 65.4 us -> 5.74 us
  Pallas kernels: 693 us -> 726 us
  local copies, waits for them, and re-layouts: 39 us -> 15.8 us
  other arithmetic: 58.8 us -> 37.6 us
  waiting for transfers between devices: 7.14 us -> 17.2 us
    dot_general x9 -> x0, matrix products: 59.7 us -> none  [the longest x4 28.7 us: dot_nt(): lax.dot_general(a, b, (((1,), (1,)), ((), ())), preferred_element_type=F32)]
    pallas_call x8 -> x7, Pallas kernels: 340 us -> 376 us  [the longest x1 117 us: end_exchange(): pl.pallas_call(functools.partial(end_kernel, fsdp, sp), out_shape=(jax.Sh...]
    all_gather x1, waiting for transfers between devices: 4.72 us -> 14.6 us  [body(): up_full = lax.all_gather(w_up, 'sp', axis=1, tiled=True)]
  transfers between devices with their start and end apart: 9 -> 6, of which waited for: 1 -> 1; matrix products, arithmetic and copies ran while one was open for 15% -> 6% of each run, Pallas kernels for 72% -> 83%
where the time goes in v3:
time: 826 us; the launch traced here: 817 us
  Pallas kernels  726 us (88%)
  other arithmetic  37.6 us (5%)
  waiting for transfers between devices  17.2 us (2%)
  local copies, waits for them, and re-layouts  15.8 us (2%)
  between operations  14.9 us (2%)
    pallas_call x1, Pallas kernels, end_exchange(): pl.pallas_call(functools.partial(end_kernel, fsdp, sp), out_shape=(jax.Sh...  117 us
    pallas_call x1, Pallas kernels, branch_back(): pl.pallas_call(functools.partial(branch_back_kernel, fsdp, sp), out_shape...  110 us
    pallas_call x1, Pallas kernels, gather_start(): pl.pallas_call(functools.partial(start_kernel, fsdp, sp), out_shape=(jax....  110 us
    pallas_call x1, Pallas kernels, token_back(): pl.pallas_call(functools.partial(token_back_kernel, fsdp), out_shape=(jax...  82.6 us
    pallas_call x1, Pallas kernels, branch_sum(): pl.pallas_call(functools.partial(branch_kernel, fsdp, sp), out_shape=(jax...  71 us
    pallas_call x1, Pallas kernels, token_gather(): pl.pallas_call(functools.partial(token_kernel, fsdp), out_shape=(jax.Shap...  70.7 us
    pallas_call x1, Pallas kernels, active(): pl.pallas_call(active_kernel, grid=(EXP_DEV, ff // wide), out_shape=(low,...  29.3 us
    pallas_call x1, Pallas kernels, rows_back(): pl.pallas_call(rows_back_kernel, grid=(EXP_DEV, D // size), out_shape=jax...  26.5 us
  transfers between devices with their start and end apart: 6, of which 1 were waited for; matrix products, arithmetic and copies ran while one was open for 6% of the time, Pallas kernels for 83%

profile of v3, /device:TPU:12, one launch (start us, length us, event | category | flops | bytes accessed | tf_op | source)
XLA Modules:
  0.0 817.1 jit_solution(6277574265373222772)
XLA Ops:
  8.0 0.7 all-gather.6.cloned.1.call-update
  8.8 0.7 all-gather.8.cloned.1.call-update
  9.5 0.7 slice.44.g_ref
  10.3 1.0 slice.46.g_ref
  11.3 0.7 reshape.117.routes_ref
  13.0 1.0 pad_maximum_fusion.w_ref
  13.9 109.6 %gather_start.1 = (bf16[1024,2048]{1,0:T(8,128)(2,1)}, bf16[3,2048,512]{2,1,0:T(8,128)(2,1)}, bf16[512,2048]{1,0:T(8,128)(2,1)}, bf16[8,64,2048]{2,1,0:T(8,128)(...) custom-call(bf16[256,2048]{1,0:T(8,128)(2,1)} %x_ref.3, bf16[3,64,2048]{2,1,0:T(8,128)(2,1)} %pad_maximum_fusion.w_ref, ...), custom_call_target="tpu_custom_call" | custom-call | tf_op jit(solution)/shard_map/gather_start/pallas_call | solution.py:636
  123.5 0.9 copy.68
  124.6 0.7 convert_element_type.80.gain
  125.3 12.2 %project.1 = (bf16[1024,2048]{1,0:T(8,128)(2,1)}, f32[1024,512]{1,0:T(8,128)}, f32[1024,512]{1,0:T(8,128)}, bf16[1024,512]{1,0:T(8,128)(2,1)}, f32[1024,128]{1,0:T(8,128)}) custom-call(bf16[1024,2048]{1,0:T(8,128)(2,1)} %get-tuple-element.71.x_ref, f32[4,2048]{1,0:T(4,128)} %convert_element_type.80.gain, bf16[3,2048,512]{2,1,0:T(8,128)(2,1)} %get-tuple-element.73.w_ref), custom_call_target="tpu_custom_call" | custom-call | tf_op jit(solution)/shard_map/project/pallas_call | solution.py:1229
  137.5 7.4 norm_sums.1.squares
  146.8 0.8 copy.61
  147.6 1.3 constant_dynamic-slice_fusion.1.gain
  148.9 16.7 %attend.1 = (bf16[1024,512]{1,0:T(8,128)(2,1)}, f32[1024,128]{1,0:T(8,128)}, bf16[1024,512]{1,0:T(8,128)(2,1)}, bf16[1024,512]{1,0:T(8,128)(2,1)}) custom-call(f32[1024,512]{1,0:T(8,128)} %get-tuple-element.74.q_raw, f32[1024,512]{1,0:T(8,128)} %get-tuple-element.75.k_raw, bf16[1024,512]{1,0:T(8,128)(2,1)} %get-tuple-element.76.v_ref, ...), custom_call_target="tpu_custom_call" | custom-call | tf_op jit(solution)/shard_map/attend/pallas_call | solution.py:1274
  165.6 5.6 convolution_convert_fusion
  171.2 71.0 %branch_sum.1 = (f32[256,2048]{1,0:T(8,128)}, bf16[8,192,2048]{2,1,0:T(8,128)(2,1)}) custom-call(bf16[4,256,2048]{2,1,0:T(8,128)(2,1)} %bitcast.30, bf16[192,2048]{1,0:T(8,128)(2,1)} %slice.46.g_ref), custom_call_target="tpu_custom_call" | custom-call | tf_op jit(solution)/shard_map/branch_sum/pallas_call | solution.py:682
  242.1 1.4 fusion.3.picks
  244.2 1.9 multiply_reduce_fusion.2
  246.2 1.2 multiply_convert_fusion.x_ref
  247.4 70.7 %token_gather.1 = (bf16[8,256,2048]{2,1,0:T(8,128)(2,1)}, bf16[2,1152,2048]{2,1,0:T(8,128)(2,1)}, f32[2,1152,1024]{2,1,0:T(8,128)}) custom-call(bf16[256,2048]{1,0:T(8,128)(2,1)} %multiply_convert_fusion.x_ref, bf16[8,64,2048]{2,1,0:T(8,128)(2,1)} %get-tuple-element.82.g_first, bf16[8,192,2048]{2,1,0:T(8,128)(2,1)} %get-tuple-element.83.g_second, ...), custom_call_target="tpu_custom_call" | custom-call | tf_op jit(solution)/shard_map/token_gather/pallas_call | solution.py:778
  318.1 15.0 %route.1 = (bf16[2,1152,2048]{2,1,0:T(8,128)(2,1)}, f32[8,256,16]{2,1,0:T(8,128)}, f32[2,1152,1]{2,1,0:T(8,128)}) custom-call(bf16[8,288,256]{2,1,0:T(8,128)(2,1)} %fusion.3.picks, bf16[8,256,2048]{2,1,0:T(8,128)(2,1)} %get-tuple-element.84.rows_in.tokens, bf16[16,2048]{1,0:T(8,128)(2,1)} %bitcast.32, f32[2,16]{1,0:T(2,128)} %compare_convert_fusion.columns), custom_call_target="tpu_custom_call" | custom-call | tf_op jit(solution)/shard_map/route/pallas_call | solution.py:1509
  333.1 14.6 %all-gather.8.cloned.1.call-done.w_ref = bf16[2,2048,1024]{2,1,0:T(8,128)(2,1)} async-done(((bf16[2,512,1024]{2,1,0:T(8,128)(2,1)}), bf16[2,2048,1024]{2,1,0:T(8,128)(2,1)}) %all-gather.8.cloned.1.call-update) | async-done | bytes 8388624 | tf_op jit(solution)/shard_map/all_gather | solution.py:1690
  347.7 29.3 %active.1 = (bf16[2,1152,1024]{2,1,0:T(8,128)(2,1)}, bf16[2,1152,1024]{2,1,0:T(8,128)(2,1)}, bf16[2,1152,1024]{2,1,0:T(8,128)(2,1)}, f32[2,1152,1]{2,1,0:T(8,128)}) custom-call(bf16[2,1152,2048]{2,1,0:T(8,128)(2,1)} %get-tuple-element.85.x_ref, bf16[2,2048,1024]{2,1,0:T(8,128)(2,1)} %all-gather.6.cloned.1.call-done.g_ref, ...), custom_call_target="tpu_custom_call" | custom-call | tf_op jit(solution)/shard_map/active/pallas_call | solution.py:1561
  377.0 15.7 %down_grad.1 = bf16[2,1024,2048]{2,1,0:T(8,128)(2,1)} custom-call(bf16[2,1152,1024]{2,1,0:T(8,128)(2,1)} %get-tuple-element.93.gated_ref.a_ref, bf16[2,1152,2048]{2,1,0:T(8,128)(2,1)} %get-tuple-element.118.g_ref), custom_call_target="tpu_custom_call" | custom-call | tf_op jit(solution)/shard_map/down_grad/pallas_call | solution.py:1581
  392.7 0.8 copy-done.7
  394.1 2.6 fusion.1.turned
  396.7 26.5 %rows_back.1.rows_ref = bf16[2,1152,2048]{2,1,0:T(8,128)(2,1)} custom-call(bf16[2,1152,1024]{2,1,0:T(8,128)(2,1)} %get-tuple-element.88.a_ref.gg_ref, bf16[2,1152,1024]{2,1,0:T(8,128)(2,1)} %get-tuple-element.89.b_ref.gu_ref, bf16[2,2048,1024]{2,1,0:T(8,128)(2,1)} %all-gather.6.cloned.1.call-done.g_ref, bf16[2,2048,1024]{2,1,0:T(8,128)(2,1)} %all-gather.8.cloned.1.call-done.w_ref), custom_call_target="tpu_custom_call" | custom-call | tf_op jit(solution)/shard_map/rows_back/pallas_call | solution.py:1604
  423.4 1.2 fusion.6.dots
  424.6 16.8 %combine.1 = (bf16[8,256,2048]{2,1,0:T(8,128)(2,1)}, f32[32,2048]{1,0:T(8,128)}) custom-call(bf16[8,2,256,144]{3,2,1,0:T(8,128)(2,1)} %fusion.1.turned, bf16[2,1152,2048]{2,1,0:T(8,128)(2,1)} %rows_back.1.rows_ref, bf16[8,256,2048]{2,1,0:T(8,128)(2,1)} %get-tuple-element.84.rows_in.tokens, f32[8,256,16]{2,1,0:T(8,128)} %get-tuple-element.90.probs, ...), custom_call_target="tpu_custom_call" | custom-call | tf_op jit(solution)/shard_map/combine/pallas_call | solution.py:1639
  441.4 82.6 %token_back.1 = (f32[256,2048]{1,0:T(8,128)}, bf16[8,256,2048]{2,1,0:T(8,128)(2,1)}, bf16[2,2048,1024]{2,1,0:T(8,128)(2,1)}, bf16[2,2048,1024]{2,1,0:T(8,128)(2,1)}) custom-call(bf16[8,256,2048]{2,1,0:T(8,128)(2,1)} %get-tuple-element.92.p_ref, bf16[2,1152,1024]{2,1,0:T(8,128)(2,1)} %get-tuple-element.93.gated_ref.a_ref, ...), custom_call_target="tpu_custom_call" | custom-call | tf_op jit(solution)/shard_map/token_back/pallas_call | solution.py:923
  525.4 1.0 reshape.123.router_ref
  526.3 2.3 multiply_reduce_fusion
  528.8 2.3 fusion.14
  531.1 110.2 %branch_back.1 = (bf16[1024,2048]{1,0:T(8,128)(2,1)}, f32[256,2048]{1,0:T(8,128)}, f32[1024,512]{1,0:T(8,128)}, f32[1024,512]{1,0:T(8,128)}, bf16[1024,512]{1,0:...) custom-call(bf16[256,2048]{1,0:T(8,128)(2,1)} %get-tuple-element.165.x_ref, ...), custom_call_target="tpu_custom_call" | custom-call | tf_op jit(solution)/shard_map/branch_back/pallas_call | solution.py:1379
  641.3 0.7 constant_dynamic-update-slice_fusion
  642.2 25.2 %weight_parts.1 = (bf16[8,1024,512]{2,1,0:T(8,128)(2,1)}, bf16[1024,2048]{1,0:T(8,128)(2,1)}) custom-call(f32[1024,512]{1,0:T(8,128)} %get-tuple-element.100.q_scaled, f32[1024,512]{1,0:T(8,128)} %get-tuple-element.101.k_scaled, f32[1024,512]{1,0:T(8,128)} %get-tuple-element.74.q_raw, f32[1024,512]{1,0:T(8,128)} %get-tuple-element.75.k_raw, ...), custom_call_target="tpu_custom_call" | custom-call | tf_op jit(solution)/shard_map/weight_parts/pallas_call | solution.py:1447
  667.3 116.9 %end_exchange.1 = (f32[256,2048]{1,0:T(8,128)}, bf16[64,2048]{1,0:T(8,128)(2,1)}, bf16[64,2048]{1,0:T(8,128)(2,1)}, bf16[64,2048]{1,0:T(8,128)(2,1)}, bf16[64,2048]{1,0:T(8,128)(2,1)}, /*index=5*/f32[16,128]{1,0:T(8,128)}) custom-call(bf16[8,1024,512]{2,1,0:T(8,128)(2,1)} %get-tuple-element.106.p_ref, bf16[4,256,2048]{2,1,0:T(8,128)(2,1)} %bitcast.31, ...), custom_call_target="tpu_custom_call" | custom-call | tf_op jit(solution)/shard_map/end_exchange/pallas_call | solution.py:1141
  784.2 0.7 slice.52
  785.0 0.7 slice.51
  785.6 1.8 convert_element_type.93
  787.4 1.8 convert_element_type.94
  789.2 1.8 convert_element_type.95
  791.0 0.8 convert_element_type.96
  793.2 2.8 add_convert_fusion
  796.0 4.1 convert_element_type.99
  800.2 4.1 convert_element_type.97
  804.2 4.2 convert_element_type.98
  808.4 1.3 copy.72
  (82 shorter events, 8.4 us)
Async XLA Ops:
  7.2 240.2 %all-gather.4.cloned.1.call-start = ((), (), s32[]{:S(2)}) async-start(), calls=%async_computation.3 | async-start | bytes 10485760 | tf_op jit(solution)/shard_map/all_gather | solution.py:1688
  7.9 1.6 copy-start.2
  7.9 325.1 %all-gather.6.cloned.1.call-start = ((), (), s32[]{:S(2)}) async-start(), calls=%async_computation.4 | async-start | bytes 10485760 | tf_op jit(solution)/shard_map/all_gather | solution.py:1689
  8.7 2.5 copy-start.15
  8.7 3.4 copy-start.16
  8.7 3.6 copy-start.17
  8.7 4.2 copy-start.11
  8.7 4.2 copy-start.12
  8.7 4.2 copy-start.13
  8.7 338.9 %all-gather.8.cloned.1.call-start = ((), (), s32[]{:S(2)}) async-start(), calls=%async_computation.5 | async-start | bytes 10485760 | tf_op jit(solution)/shard_map/all_gather | solution.py:1690
  9.5 786.6 %reduce-scatter.8.cloned.1.call-start = ((), (), s32[]{:S(2)}) async-start(), calls=%async_computation.8 | async-start | bytes 10485760 | tf_op jit(solution)/shard_map/reduce_scatter | solution.py:1754
  125.3 19.7 %copy-start.14 = (s32[8,16,128]{2,1,0:T(8,128)S(1)}, s32[8,16,128]{2,1,0:T(8,128)}, u32[]{:S(2)}) copy-start(s32[8,16,128]{2,1,0:T(8,128)} %get-tuple-element.81) | copy-start | bytes 196612
  148.9 16.7 %copy-start.4 = (bf16[512,2048]{1,0:T(8,128)(2,1)S(1)}, bf16[512,2048]{1,0:T(8,128)(2,1)}, u32[]{:S(2)}) copy-start(bf16[512,2048]{1,0:T(8,128)(2,1)} %get-tuple-element.79.wo_ref) | copy-start | bytes 6291460
  171.2 73.1 %copy-start = (bf16[256,2048]{1,0:T(8,128)(2,1)S(1)}, bf16[256,2048]{1,0:T(8,128)(2,1)}, u32[]{:S(2)}) copy-start(bf16[256,2048]{1,0:T(8,128)(2,1)} %x_ref.3) | copy-start | bytes 3145732
  392.6 0.8 copy-start.7
  392.7 407.5 %reduce-scatter.4.cloned.1.call-start = ((), (), s32[]{:S(2)}) async-start(), calls=%async_computation.6 | async-start | bytes 10485760 | tf_op jit(solution)/shard_map/reduce_scatter | solution.py:1754
  396.7 26.5 %copy-start.6 = (f32[2,1152,1]{2,1,0:T(8,128)S(1)}, f32[2,1152,1]{2,1,0:T(8,128)}, u32[]{:S(2)}) copy-start(f32[2,1152,1]{2,1,0:T(8,128)} %get-tuple-element.91) | copy-start | bytes 27652
  524.0 280.2 %reduce-scatter.6.cloned.1.call-start = ((), (), s32[]{:S(2)}) async-start(), calls=%async_computation.7 | async-start | bytes 10485760 | tf_op jit(solution)/shard_map/reduce_scatter | solution.py:1754
  524.1 1.0 copy-start.10
  526.3 2.3 copy-start.1
  526.3 2.5 copy-start.3
  642.2 25.2 %copy-start.8 = (f32[8,2048]{1,0:T(8,128)}, f32[8,2048]{1,0:T(8,128)S(1)}, u32[]{:S(2)}) copy-start(f32[8,2048]{1,0:T(8,128)S(1)} %scatter.4.gains_in) | copy-start | bytes 196612
  784.2 6.8 copy-start.9
  804.2 4.2 copy-start.5
Sparse Core Ops, SparseCore 0:
  9.9 129.1 all-gather.3
  140.9 115.0 all-gather.5
  257.9 89.7 all-gather.7
  392.8 86.3 reduce-scatter.7
  524.1 119.5 reduce-scatter.3
  646.7 125.9 reduce-scatter.5

commit v4 on v3

--- a/solution.py
+++ b/solution.py
@@ -214,7 +214,7 @@
         )
 
     def start(self):
-        for i in self.order:
+        for i in self.order[:2]:
             self.swap(i).start()
         for i in self.order:
             self.load(i).start()
@@ -258,27 +258,44 @@
 
             self.left(e).start()
 
+        if t == 0:
+            for i in self.order[2:]:
+                self.swap(i).start()
         self.add_pairs(2 * t + 4)
 
     def finish(self, out_ref):
         place, lines, rows = self.place, self.lines, self.rows
 
-        def first(i, carry):
-            at = pl.ds(pl.multiple_of(i * 32, 32), 32)
-            out_ref[at, :] = self.own[place, at, :].astype(F32)
-            return carry
-
-        lax.fori_loop(0, rows // 32, first, 0)
+        def total(*extra):
+            def step(i, carry):
+                at = pl.ds(pl.multiple_of(i * 32, 32), 32)
+                value = self.own[place, at, :].astype(F32)
+                for ref in extra:
+                    value += ref[at, :].astype(F32)
+                out_ref[at, :] = value.astype(out_ref.dtype)
+                return carry
+
+            lax.fori_loop(0, rows // 32, step, 0)
 
         @pl.when(place > 0)
         def _():
             landed(self.last, self.final)
-            add_rows(out_ref, out_ref, self.last, rows)
 
         @pl.when(place < lines - 1)
         def _():
             landed(self.got.at[place], self.recv.at[place])
-            add_rows(out_ref, out_ref, self.got.at[place], rows)
+
+        @pl.when(place == 0)
+        def _():
+            total(self.got.at[place])
+
+        @pl.when(place == lines - 1)
+        def _():
+            total(self.last)
+
+        @pl.when(jnp.logical_and(place > 0, place < lines - 1))
+        def _():
+            total(self.last, self.got.at[place])
 
         for i in range(lines):
             self.swap(i).wait_send()
@@ -655,7 +672,7 @@
     )(x, w, wo, g, misc, routes)
 
 
-def branch_kernel(fsdp, sp, p_ref, g_ref, out_ref, g_all, *scratch):
+def branch_kernel(fsdp, sp, p_ref, g_ref, x_ref, gain, out_ref, second_ref, g_all, *scratch):
     f, s = lax.axis_index("fsdp"), lax.axis_index("sp")
     lines = fsdp // 2
     barrier = pltpu.get_barrier_semaphore()
@@ -673,21 +690,35 @@
         if k == min(2, lines - 1):
             plane.forward()
     plane.finish()
+
+    def norm(i, carry):
+        at = pl.ds(pl.multiple_of(i * 32, 32), 32)
+        mid = x_ref[at, :].astype(F32) + out_ref[at, :]
+        out_ref[at, :] = mid
+        inverse = lax.rsqrt(jnp.mean(mid * mid, axis=-1, keepdims=True) + EPSILON)
+        second_ref[at, :] = (mid * inverse * gain[1:2, :]).astype(BF16)
+        return carry
+
+    lax.fori_loop(0, TOK_DEV // 32, norm, 0)
     line.finish(0)
     own.wait()
 
 
-def branch_sum(fsdp, partial, g):
+def branch_sum(fsdp, partial, g, x, gains):
     sp, block = partial.shape[0], partial.shape[1:]
     return pl.pallas_call(
         functools.partial(branch_kernel, fsdp, sp),
-        out_shape=(jax.ShapeDtypeStruct(block, F32), jax.ShapeDtypeStruct((fsdp,) + g.shape, BF16)),
-        in_specs=[ANY, VMEM],
-        out_specs=[VMEM, ANY],
+        out_shape=(
+            jax.ShapeDtypeStruct(block, F32),
+            jax.ShapeDtypeStruct(block, BF16),
+            jax.ShapeDtypeStruct((fsdp,) + g.shape, BF16),
+        ),
+        in_specs=[ANY, VMEM, VMEM, VMEM],
+        out_specs=[VMEM, VMEM, ANY],
         scratch_shapes=plane_scratch(block, sp) + line_sems(1, fsdp) + [pltpu.SemaphoreType.DMA],
         compiler_params=comm_params(2),
         name="branch_sum",
-    )(partial, g)
+    )(partial, g, x, gains)
 
 
 def token_kernel(
@@ -798,9 +829,8 @@
 
 
 def token_back_kernel(
-    fsdp, p_ref, gated_ref, w_ref, turned, x_ref, gg_ref, gu_ref,
-    out_ref, part_ref, wg_ref, wu_ref,
-    wide, narrow, w_buf, tile, grad_tile, loads, tile_sem, grad_sem, *scratch,
+    fsdp, p_ref, gated_ref, w_ref, turned, x_ref, gu_ref, mid_ref, g_ref, gain,
+    out_ref, low_ref, gain_out, part_ref, wu_ref, wide, narrow, w_buf, tile, grad_tile, loads, tile_sem, grad_sem, *scratch,
 ):
     f, s = lax.axis_index("fsdp"), lax.axis_index("sp")
     lines = fsdp // 2
@@ -810,12 +840,10 @@
     expected = greet_line(barrier, lines, f, s)
     reads = [
         pltpu.make_async_copy(gated_ref, narrow, loads.at[0]),
-        pltpu.make_async_copy(w_ref, w_buf, loads.at[1]),
+        pltpu.make_async_copy(w_ref.at[0], w_buf, loads.at[1]),
         pltpu.make_async_copy(x_ref, wide, loads.at[2]),
-        pltpu.make_async_copy(gg_ref.at[0], narrow.at[0], loads.at[3]),
-        pltpu.make_async_copy(gu_ref.at[0], narrow.at[1], loads.at[4]),
-        pltpu.make_async_copy(gg_ref.at[1], narrow.at[0], loads.at[3]),
-        pltpu.make_async_copy(gu_ref.at[1], narrow.at[1], loads.at[4]),
+        pltpu.make_async_copy(gu_ref, narrow, loads.at[3]),
+        pltpu.make_async_copy(w_ref.at[1], w_buf, loads.at[1]),
     ]
     reads[0].start()
     reads[1].start()
@@ -827,20 +855,23 @@
         if e == 0:
             reads[0].wait()
             reads[1].wait()
+        else:
+            reads[4].wait()
 
         def columns(n, carry):
             at = pl.ds(pl.multiple_of(n * 512, 512), 512)
-            wide[e, :, at] = dot_nn(narrow[e], w_buf[e, :, at]).astype(BF16)
+            wide[e, :, at] = dot_nn(narrow[e], w_buf[:, at]).astype(BF16)
             return carry
 
         lax.fori_loop(0, D // 512, columns, 0)
+        if e == 0:
+            reads[4].start()
 
     def tile_copy(b, slot):
         return pltpu.make_async_copy(tile.at[slot], part_ref.at[b], tile_sem.at[slot])
 
     def sum_all():
         reads[3].start()
-        reads[4].start()
 
         def pair(i, carry):
             for slot in range(2):
@@ -863,44 +894,35 @@
         lax.fori_loop(0, fsdp // 2, pair, 0)
         reads[2].start()
 
-    def grad_copy(to, e, i, slot):
+    def grad_copy(e, i, slot):
         at = pl.ds(pl.multiple_of(i * height, height), height)
-        return pltpu.make_async_copy(grad_tile.at[slot], to.at[e, at, :], grad_sem.at[slot])
-
-    def grad_of(e, n, to, first):
-        if n == 0 and e == 0:
+        return pltpu.make_async_copy(grad_tile.at[slot], wu_ref.at[e, at, :], grad_sem.at[slot])
+
+    def grad_of(e):
+        if e == 0:
             reads[2].wait()
             reads[3].wait()
-            reads[4].wait()
-        if n == 0 and e == 1:
-            reads[5].wait()
-            reads[6].wait()
 
         def pair(i, carry):
             for slot in range(2):
                 part = 2 * i + slot
 
                 def before():
-                    grad_copy(to, e, part, slot).wait()
-
-                if first:
+                    grad_copy(e, part, slot).wait()
+
+                if e == 0:
                     pl.when(i > 0)(before)
                 else:
                     before()
                 at = pl.ds(pl.multiple_of(part * height, height), height)
-                grad_tile[slot] = dot_tn(wide[e, :, at], narrow[n]).astype(BF16)
-                grad_copy(to, e, part, slot).start()
+                grad_tile[slot] = dot_tn(wide[e, :, at], narrow[e]).astype(BF16)
+                grad_copy(e, part, slot).start()
             return carry
 
         lax.fori_loop(0, D // height // 2, pair, 0)
-        if n == 1 and e == 0:
-            reads[5].start()
-            reads[6].start()
 
     work = [functools.partial(down_of, e) for e in range(EXP_DEV)] + [sum_all]
-    for e in range(EXP_DEV):
-        for n, to in ((0, wg_ref), (1, wu_ref)):
-            work.append(functools.partial(grad_of, e, n, to, e == 0 and n == 0))
+    work += [functools.partial(grad_of, e) for e in range(EXP_DEV)]
     done = 0
     for t in range(lines - 1):
         line.step(t)
@@ -909,41 +931,58 @@
             unit()
         done = until
     line.finish(out_ref)
+    gain_out[...] = jnp.zeros_like(gain_out)
+
+    def norm_back(i, carry):
+        at = pl.ds(pl.multiple_of(i * 32, 32), 32)
+        mid = mid_ref[at, :]
+        inverse = lax.rsqrt(jnp.mean(mid * mid, axis=-1, keepdims=True) + EPSILON)
+        normed = mid * inverse
+        grad_y = out_ref[at, :]
+        scaled = grad_y * gain[1:2, :]
+        mean = jnp.mean(scaled * normed, axis=-1, keepdims=True)
+        grad = g_ref[at, :].astype(F32) + inverse * (scaled - normed * mean)
+        out_ref[at, :] = grad
+        low_ref[at, :] = grad.astype(BF16)
+        gain_out[1:2, :] += jnp.sum(grad_y * normed, axis=0, keepdims=True)
+        return carry
+
+    lax.fori_loop(0, TOK_DEV // 32, norm_back, 0)
     for slot in range(2):
         tile_copy(slot, slot).wait()
-        grad_copy(wg_ref, 0, slot, slot).wait()
-
-
-def token_back(fsdp, partial, gated, w_down, turned, received, grad_gate_pre, grad_up_pre):
+        grad_copy(0, slot, slot).wait()
+
+
+def token_back(fsdp, partial, gated, w_down, turned, received, grad_up_pre, mid, g, gains):
     block = partial.shape[1:]
     total, ff = gated.shape[1:]
     height = 256
     dma = pltpu.SemaphoreType.DMA
-    weight = jax.ShapeDtypeStruct((EXP_DEV, D, ff), BF16)
     return pl.pallas_call(
         functools.partial(token_back_kernel, fsdp),
         out_shape=(
             jax.ShapeDtypeStruct(block, F32),
+            jax.ShapeDtypeStruct(block, BF16),
+            jax.ShapeDtypeStruct((8, D), F32),
             jax.ShapeDtypeStruct(partial.shape, BF16),
-            weight,
-            weight,
+            jax.ShapeDtypeStruct((EXP_DEV, D, ff), BF16),
         ),
-        in_specs=[ANY, ANY, ANY, VMEM, ANY, ANY, ANY],
-        out_specs=[VMEM, ANY, ANY, ANY],
+        in_specs=[ANY, ANY, ANY, VMEM, ANY, ANY, VMEM, VMEM, VMEM],
+        out_specs=[VMEM, VMEM, VMEM, ANY, ANY],
         scratch_shapes=[
             pltpu.VMEM((EXP_DEV, total, D), BF16),
             pltpu.VMEM((EXP_DEV, total, ff), BF16),
-            pltpu.VMEM((EXP_DEV, ff, D), BF16),
+            pltpu.VMEM((ff, D), BF16),
             pltpu.VMEM((2,) + block, BF16),
             pltpu.VMEM((2, height, ff), BF16),
-            dma((5,)),
+            dma((4,)),
             dma((2,)),
             dma((2,)),
         ]
         + LineReduce.scratch(fsdp, block),
         compiler_params=comm_params(4),
         name="token_back",
-    )(partial, gated, w_down, turned, received, grad_gate_pre, grad_up_pre)
+    )(partial, gated, w_down, turned, received, grad_up_pre, mid, g, gains)
 
 
 class PlaneSum:
@@ -983,32 +1022,10 @@
         out_ref[...] = jnp.concatenate([terms[0], jnp.zeros((120, seq), F32)], axis=0).T
 
 
-def plane_sum_kernel(sp, x_ref, out_ref, *scratch):
-    f, s = lax.axis_index("fsdp"), lax.axis_index("sp")
-    total = PlaneSum(scratch, f, s, sp)
-    barrier = pltpu.get_barrier_semaphore()
-    pl.semaphore_wait(barrier, total.greet(barrier))
-    total.start(x_ref)
-    total.finish(out_ref)
-
-
-def plane_sum(sp, x, number, name):
-    seq = x.shape[0]
-    return pl.pallas_call(
-        functools.partial(plane_sum_kernel, sp),
-        out_shape=jax.ShapeDtypeStruct(x.shape, F32),
-        in_specs=[VMEM],
-        out_specs=VMEM,
-        scratch_shapes=PlaneSum.scratch(seq, sp),
-        compiler_params=comm_params(number),
-        name=name,
-    )(x)
-
-
 def end_kernel(
-    fsdp, sp, p_ref, b_ref, x_ref, mid_ref, gain, gains_in, router_ref,
+    fsdp, sp, p_ref, low_ref, w_ref, x_ref, mid_ref, gain, gains_in, router_ref,
     grad_out, qkv_0, qkv_1, qkv_2, o_out, small_out,
-    back, summed, low, o_low, gain_sum, pay, small,
+    first, low_in, w_buf, back, low, o_low, gain_sum, pay, small, loads,
     qsend, qrecv, osend, orecv, msend, mrecv, local, *scratch,
 ):
     f, s = lax.axis_index("fsdp"), lax.axis_index("sp")
@@ -1018,12 +1035,33 @@
     height = D // fsdp
     barrier = pltpu.get_barrier_semaphore()
     greet_all(barrier, me, count, sp)
+    reads = [
+        pltpu.make_async_copy(low_ref, low_in, loads.at[0]),
+        pltpu.make_async_copy(w_ref, w_buf, loads.at[1]),
+    ]
+    for copy in reads:
+        copy.start()
     pl.semaphore_wait(barrier, count - 1)
     plane_parts = 6 if sp == 4 else 5
-    plane = plane_reduce_of(b_ref, back, scratch[:plane_parts], f, s, sp)
+    plane = plane_reduce_of(first, back, scratch[:plane_parts], f, s, sp)
     line = LineReduce(p_ref, scratch[plane_parts:], lines, f, s)
-    plane.start()
     line.start()
+
+    def first_grads():
+        for copy in reads:
+            copy.wait()
+
+        def columns(n, carry):
+            at = pl.ds(pl.multiple_of(n * 256, 256), 256)
+            for d in range(sp):
+                rows_at = slice(d * TOK_DEV, (d + 1) * TOK_DEV)
+                total = dot_nt(low_in[rows_at, :cols], w_buf[0, at, :])
+                total += dot_nt(low_in[rows_at, cols : 2 * cols], w_buf[1, at, :])
+                total += dot_nt(low_in[rows_at, 2 * cols :], w_buf[2, at, :])
+                first[d, :, at] = total.astype(BF16)
+            return carry
+
+        lax.fori_loop(0, D // 256, columns, 0)
 
     def input_grads():
         gain_sum[...] = jnp.zeros_like(gain_sum)
@@ -1063,22 +1101,17 @@
 
     for t in range(lines - 1):
         line.step(t)
-        if t == min(1, lines - 2):
-            plane.forward()
+        if t == 0:
+            first_grads()
+            plane.start()
+    plane.forward()
     plane.finish()
     input_grads()
     lax.fori_loop(1, count, m_go, 0)
-    line.finish(summed)
-
-    def cast(i, carry):
-        at = pl.ds(pl.multiple_of(i * 32, 32), 32)
-        low[at, :] = summed[at, :].astype(BF16)
-        return carry
-
-    lax.fori_loop(0, summed.shape[0] // 32, cast, 0)
+    line.finish(low)
     for c in range(sp):
-        first = 3 * height + c * rows
-        o_low[:, c * cols : (c + 1) * cols] = low[first : first + rows, :]
+        top = 3 * height + c * rows
+        o_low[:, c * cols : (c + 1) * cols] = low[top : top + rows, :]
 
     def q_from(i, place):
         return low.at[pl.ds(pl.multiple_of(i * height + place * rows, rows), rows), :]
@@ -1133,7 +1166,7 @@
         q_own(i).wait()
 
 
-def end_exchange(fsdp, sp, partial, back, x, grad_mid, gains, gains_in, router, number):
+def end_exchange(fsdp, sp, partial, low, w, x, grad_mid, gains, gains_in, router, number):
     count = fsdp * sp
     block = partial.shape[1:]
     rows = D // count
@@ -1148,23 +1181,26 @@
             jax.ShapeDtypeStruct((rows, D), BF16),
             jax.ShapeDtypeStruct((16, 128), F32),
         ),
-        in_specs=[ANY, ANY, VMEM, VMEM, VMEM, VMEM, VMEM],
+        in_specs=[ANY, ANY, ANY, VMEM, VMEM, VMEM, VMEM, VMEM],
         out_specs=[VMEM, ANY, ANY, ANY, ANY, VMEM],
         scratch_shapes=[
+            pltpu.VMEM((sp, TOK_DEV, D), BF16),
+            pltpu.VMEM(low.shape, BF16),
+            pltpu.VMEM(w.shape, BF16),
             pltpu.VMEM((TOK_DEV, D), F32),
-            pltpu.VMEM(block, F32),
             pltpu.VMEM(block, BF16),
             pltpu.VMEM((rows, D), BF16),
             pltpu.VMEM((8, D), F32),
             pltpu.VMEM((count, 16, 128), F32),
             pltpu.VMEM((count, 16, 128), F32),
+            dma((2,)),
             dma((sp, 3)), dma((sp, 3)), dma, dma, dma((count,)), dma((count,)), dma((3,)),
         ]
         + plane_scratch((TOK_DEV, D), sp)
         + LineReduce.scratch(fsdp, block),
         compiler_params=comm_params(number),
         name="end_exchange",
-    )(partial, back, x, grad_mid, gains, gains_in, router)
+    )(partial, low, w, x, grad_mid, gains, gains_in, router)
 
 
 def dot_nt(a, b):
@@ -1205,7 +1241,15 @@
     return turn(v, table, -1.0)
 
 
-def project_kernel(x_ref, gain, w_ref, first_out, q_out, k_out, v_out, squares):
+def project_kernel(sp, x_ref, gain, w_ref, first_out, q_out, k_out, v_out, sums_out, squares, *scratch):
+    step = pl.program_id(0)
+    total = PlaneSum(scratch, lax.axis_index("fsdp"), lax.axis_index("sp"), sp)
+    barrier = pltpu.get_barrier_semaphore()
+
+    @pl.when(step == 0)
+    def _():
+        total.greet(barrier)
+
     x = x_ref[...].astype(F32)
     inverse = lax.rsqrt(jnp.mean(x * x, axis=-1, keepdims=True) + EPSILON)
     first = (x * inverse * gain[0:1, :]).astype(BF16)
@@ -1214,20 +1258,32 @@
     q_out[...] = q
     k = dot_nn(first, w_ref[1])
     k_out[...] = k
-    squares[...] = lanes(
+    at = pl.ds(pl.multiple_of(step * TOK_DEV, TOK_DEV), TOK_DEV)
+    squares[at, :] = lanes(
         jnp.sum(q * q, axis=-1, keepdims=True), jnp.sum(k * k, axis=-1, keepdims=True)
     )
+    last = step == pl.num_programs(0) - 1
+
+    @pl.when(last)
+    def _():
+        pl.semaphore_wait(barrier, sp - 1)
+        total.start(squares)
+
     v_out[...] = dot_nn(first, w_ref[2]).astype(BF16)
 
-
-def project(x, gains, w):
+    @pl.when(last)
+    def _():
+        total.finish(sums_out)
+
+
+def project(sp, x, gains, w):
     seq, cols = x.shape[0], w.shape[2]
 
     def block(width):
         return pl.BlockSpec((TOK_DEV, width), lambda i: (i, 0))
 
     return pl.pallas_call(
-        project_kernel,
+        functools.partial(project_kernel, sp),
         grid=(seq // TOK_DEV,),
         out_shape=(
             jax.ShapeDtypeStruct((seq, D), BF16),
@@ -1237,8 +1293,9 @@
             jax.ShapeDtypeStruct((seq, 128), F32),
         ),
         in_specs=[block(D), whole(gains.shape), whole(w.shape)],
-        out_specs=[block(D), block(cols), block(cols), block(cols), block(128)],
-        compiler_params=pltpu.CompilerParams(vmem_limit_bytes=VLIM),
+        out_specs=[block(D), block(cols), block(cols), block(cols), whole((seq, 128))],
+        scratch_shapes=[pltpu.VMEM((seq, 128), F32)] + PlaneSum.scratch(seq, sp),
+        compiler_params=comm_params(1),
         name="project",
     )(x, gains, w)
 
@@ -1406,8 +1463,7 @@
 
 
 def weight_kernel(
-    q_scaled, k_scaled, q_raw, k_raw, squares, dots, dv_ref, first, attended, g_ref, w_ref,
-    out, back, low, square,
+    q_scaled, k_scaled, q_raw, k_raw, squares, dots, dv_ref, first, attended, g_ref, out, low, square
 ):
     f = pl.program_id(0)
     height = first.shape[1]
@@ -1436,11 +1492,9 @@
     for c in range(sp):
         at = 3 * height + c * each
         out[0, at : at + each, :] = square[from_rows, c * cols : (c + 1) * cols]
-    total = dot_nt(low[:, :cols], w_ref[0]) + dot_nt(low[:, cols : 2 * cols], w_ref[1])
-    back[...] = (total + dot_nt(low[:, 2 * cols :], w_ref[2])).astype(BF16)
-
-
-def weight_parts(fsdp, q_scaled, k_scaled, q_raw, k_raw, squares, dots, dv, first, attended, g, w):
+
+
+def weight_parts(fsdp, q_scaled, k_scaled, q_raw, k_raw, squares, dots, dv, first, attended, g):
     seq, cols = dv.shape
     height = D // fsdp
     each = cols // fsdp
@@ -1449,7 +1503,7 @@
         grid=(fsdp,),
         out_shape=(
             jax.ShapeDtypeStruct((fsdp, 3 * height + D // cols * each, cols), BF16),
-            jax.ShapeDtypeStruct((seq, D), BF16),
+            jax.ShapeDtypeStruct((seq, 3 * cols), BF16),
         ),
         in_specs=[held((seq, cols))] * 4
         + [held((seq, 128))] * 2
@@ -1458,16 +1512,15 @@
             pl.BlockSpec((seq, height), lambda f: (0, f)),
             held((seq, cols)),
             held((seq, D)),
-            pl.BlockSpec((3, height, cols), lambda f: (0, f, 0)),
         ],
         out_specs=[
             pl.BlockSpec((1, 3 * height + D // cols * each, cols), lambda f: (f, 0, 0)),
-            pl.BlockSpec((seq, height), lambda f: (0, f)),
+            whole((seq, 3 * cols)),
         ],
-        scratch_shapes=[pltpu.VMEM((seq, 3 * cols), BF16), pltpu.VMEM((cols, D), BF16)],
+        scratch_shapes=[pltpu.VMEM((cols, D), BF16)],
         compiler_params=pltpu.CompilerParams(vmem_limit_bytes=VLIM),
         name="weight_parts",
-    )(q_scaled, k_scaled, q_raw, k_raw, squares, dots, dv, first, attended, g, w)
+    )(q_scaled, k_scaled, q_raw, k_raw, squares, dots, dv, first, attended, g)
 
 
 def two_parts(x, axis):
@@ -1571,25 +1624,26 @@
     )(x, w_gate, w_up, u, gates)
 
 
-def down_grad_kernel(a_ref, g_ref, out):
-    out[0] = dot_tn(a_ref[0], g_ref[0]).astype(BF16)
-
-
-def down_grad(gated, g):
-    _, total, ff = gated.shape
-    size = D // 2
+def weight_grad_kernel(a_ref, b_ref, out):
+    out[0] = dot_tn(a_ref[0], b_ref[0]).astype(BF16)
+
+
+def weight_grad(a, b, name):
+    _, total, height = a.shape
+    width = b.shape[2]
+    size = 1024
     return pl.pallas_call(
-        down_grad_kernel,
-        grid=(EXP_DEV, D // size),
-        out_shape=jax.ShapeDtypeStruct((EXP_DEV, ff, D), BF16),
+        weight_grad_kernel,
+        grid=(EXP_DEV, height // size, width // size),
+        out_shape=jax.ShapeDtypeStruct((EXP_DEV, height, width), BF16),
         in_specs=[
-            pl.BlockSpec((1, total, ff), lambda e, j: (e, 0, 0)),
-            pl.BlockSpec((1, total, size), lambda e, j: (e, 0, j)),
+            pl.BlockSpec((1, total, size), lambda e, i, j: (e, 0, i)),
+            pl.BlockSpec((1, total, size), lambda e, i, j: (e, 0, j)),
         ],
-        out_specs=pl.BlockSpec((1, ff, size), lambda e, j: (e, 0, j)),
+        out_specs=pl.BlockSpec((1, size, size), lambda e, i, j: (e, i, j)),
         compiler_params=pltpu.CompilerParams(vmem_limit_bytes=VLIM),
-        name="down_grad",
-    )(gated, g)
+        name=name,
+    )(a, b)
 
 
 def rows_back_kernel(a_ref, b_ref, g_ref, w_ref, out):
@@ -1654,15 +1708,31 @@
     )(turned, grad_rows, tokens, probs, dots, router_two, columns)
 
 
-def rms_parts(values_in):
-    inverse = lax.rsqrt(jnp.mean(values_in * values_in, axis=-1, keepdims=True) + EPSILON)
-    return (values_in * inverse, inverse)
-
-
-def rms_back(grad_out, normed, inverse, gain_row):
-    scaled = grad_out * gain_row
-    grad_in = inverse * (scaled - normed * jnp.mean(scaled * normed, axis=-1, keepdims=True))
-    return (grad_in, jnp.sum(grad_out * normed, axis=0))
+def widen_kernel(*refs):
+    count = len(refs) // 2
+    for low, out in zip(refs[:count], refs[count:]):
+        out[...] = low[...].astype(F32)
+
+
+def widen(arrays):
+    flat = [x.reshape(-1, x.shape[-1]) for x in arrays]
+    steps = 4
+    specs = [
+        whole(x.shape)
+        if x.shape[0] % (16 * steps)
+        else pl.BlockSpec((x.shape[0] // steps, x.shape[1]), lambda i: (i, 0))
+        for x in flat
+    ]
+    wide = pl.pallas_call(
+        widen_kernel,
+        grid=(steps,),
+        out_shape=tuple(jax.ShapeDtypeStruct(x.shape, F32) for x in flat),
+        in_specs=specs,
+        out_specs=specs,
+        compiler_params=pltpu.CompilerParams(vmem_limit_bytes=VLIM),
+        name="widen",
+    )(*flat)
+    return [x.reshape(like.shape) for x, like in zip(wide, arrays)]
 
 
 def angles(seq):
@@ -1694,7 +1764,7 @@
     misc_rows = -(-misc.shape[0] // 2048) * 16
     misc = jnp.pad(misc, (0, misc_rows * 128 - misc.shape[0])).reshape(misc_rows, 128)
     routes = expert_routes.reshape(TOK_DEV * TOP // 128, 128)
-    early = TOK_DEV // 4
+    early = TOK_DEV // 8
     x_all, w_all, wo_s, grad_first_half, misc_all, routes_all = gather_start(
         fsdp, sp, layer_input, jnp.stack([w_query, w_key, w_value]), w_output, output_grad[:early],
         misc, routes,
@@ -1722,18 +1792,15 @@
     ).astype(BF16)
     columns = (jnp.arange(experts, dtype=jnp.int32)[None, :] == own_ids[:, None]).astype(F32)
 
-    first_in, q_raw, k_raw, values, squares = project(x_all, gains32, w_all)
-    squares = plane_sum(sp, squares, 1, "norm_sums")
+    first_in, q_raw, k_raw, values, squares = project(sp, x_all, gains32, w_all)
     table = angles(seq)
     attended, sums, queries, keys = attend(
         q_raw, k_raw, values, squares, gains_own, table
     )
     branch = dot_nn(attended, wo_s).astype(BF16).reshape(sp, TOK_DEV, D)
-    inputs = layer_input.astype(F32)
-    branch, grad_second_half = branch_sum(fsdp, branch, output_grad[early:])
-    mid = inputs + branch
-    normed_m, inverse_m = rms_parts(mid)
-    second_in = (normed_m * gains32[1]).astype(BF16)
+    mid, second_in, grad_second_half = branch_sum(
+        fsdp, branch, output_grad[early:], layer_input, gains32
+    )
 
     tokens, grad_taken, unscaled = token_gather(
         fsdp, second_in, grad_first_half, grad_second_half, picks, down_full
@@ -1751,36 +1818,33 @@
     grad_router = (router_two[:experts] + router_two[experts:]).T
 
     def shed(grad):
-        return lax.psum_scatter(grad, "sp", scatter_dimension=1, tiled=True).astype(F32)
-
-    grad_down = shed(down_grad(gated, grad_taken))
-    grad_second, out_part, gate_part, up_part = token_back(
-        fsdp, second_part, gated, down_full, turned, received, grad_gate_pre, grad_up_pre
+        return lax.psum_scatter(grad, "sp", scatter_dimension=1, tiled=True)
+
+    grad_down = shed(weight_grad(gated, grad_taken, "down_grad"))
+    grad_gate = shed(weight_grad(received, grad_gate_pre, "gate_grad"))
+    grad_mid, grad_mid_low, gain_rows, out_part, up_part = token_back(
+        fsdp, second_part, gated, down_full, turned, received, grad_up_pre, mid, output_grad, gains32
     )
-    grad_gate, grad_up = shed(gate_part), shed(up_part)
-
-    grad_final = output_grad.astype(F32)
-    grad_mid_norm, gain_m = rms_back(grad_second, normed_m, inverse_m, gains32[1])
-    grad_mid = grad_final + grad_mid_norm
+    grad_up = shed(up_part)
+
     grad_branch, out_sum, q_scaled, k_scaled, grad_values, dots, gain_qk = branch_back(
-        fsdp, sp, grad_mid.astype(BF16), out_part, wo_s, queries, keys, values, sums, q_raw, k_raw,
+        fsdp, sp, grad_mid_low, out_part, wo_s, queries, keys, values, sums, q_raw, k_raw,
         gains_own, table,
     )
     layer_out = (mid + out_sum).astype(BF16)
-    weight_part, first_part = weight_parts(
-        fsdp, q_scaled, k_scaled, q_raw, k_raw, squares, dots, grad_values, first_in, attended,
-        grad_branch, w_all,
+    weight_part, grads_low = weight_parts(
+        fsdp, q_scaled, k_scaled, q_raw, k_raw, squares, dots, grad_values, first_in, attended, grad_branch
     )
 
-    gain_rows = lax.dynamic_update_slice(jnp.zeros((8, D), F32), gain_qk, (2, s * cols))
-    gain_rows = gain_rows.at[1].set(gain_m)
+    gain_rows = lax.dynamic_update_slice(gain_rows, gain_qk, (2, s * cols))
     router_part = grad_router.reshape(count, router_size)
     router_part = jnp.pad(router_part, ((0, 0), (0, 1024 - router_size))).reshape(count, 8, 128)
     input_grad, *weight_grads, small = end_exchange(
-        fsdp, sp, weight_part, first_part.reshape(sp, TOK_DEV, D), layer_input, grad_mid, gains32,
-        gain_rows, router_part, 8,
+        fsdp, sp, weight_part, grads_low, w_all, layer_input, grad_mid, gains32, gain_rows, router_part, 8
     )
-    weight_grads = [grad.astype(F32) for grad in weight_grads]
+    *weight_grads, grad_gate, grad_up, grad_down = widen(
+        [*weight_grads, grad_gate, grad_up, grad_down]
+    )
     grad_router_own = small[:8].reshape(1024)[:router_size].reshape(rows, experts)
     first_lane = (f * sp + s) * rows % 128
     grad_gains = lax.dynamic_slice(small[8:12], (0, first_lane), (4, rows))

time: 826 us -> 803 us (0.972)
  other arithmetic: 37.6 us -> 11.4 us
    pallas_call x3 -> x4, Pallas kernels: 35.2 us -> 59.5 us  [the longest x2 31.8 us: weight_grad(): pl.pallas_call(weight_grad_kernel, grid=(EXP_DEV, height // size, width /...]
    convert_element_type x9 -> x0, other arithmetic: 22.1 us -> none  [the longest x3 12.4 us: shed(): lax.psum_scatter(grad, 'sp', scatter_dimension=1, tiled=True).astype(F32)]
    pallas_call x1, Pallas kernels: 110 us -> 97 us  [branch_back(): pl.pallas_call(functools.partial(branch_back_kernel, fsdp, sp), out_shape...]
  transfers between devices with their start and end apart: 6 -> 6, of which waited for: 1 -> 1; matrix products, arithmetic and copies ran while one was open for 6% -> 4% of each run, Pallas kernels for 83% -> 85%
where the time goes in v4:
time: 803 us; the launch traced here: 794 us
  Pallas kernels  727 us (91%)
  waiting for transfers between devices  18.5 us (2%)
  local copies, waits for them, and re-layouts  16.5 us (2%)
  between operations  14.9 us (2%)
  other arithmetic  11.4 us (1%)
    pallas_call x1, Pallas kernels, end_exchange(): pl.pallas_call(functools.partial(end_kernel, fsdp, sp), out_shape=(jax.Sh...  110 us
    pallas_call x1, Pallas kernels, gather_start(): pl.pallas_call(functools.partial(start_kernel, fsdp, sp), out_shape=(jax....  104 us
    pallas_call x1, Pallas kernels, branch_back(): pl.pallas_call(functools.partial(branch_back_kernel, fsdp, sp), out_shape...  97 us
    pallas_call x1, Pallas kernels, token_back(): pl.pallas_call(functools.partial(token_back_kernel, fsdp), out_shape=(jax...  86.1 us
    pallas_call x1, Pallas kernels, branch_sum(): pl.pallas_call(functools.partial(branch_kernel, fsdp, sp), out_shape=(jax...  75.7 us
    pallas_call x1, Pallas kernels, token_gather(): pl.pallas_call(functools.partial(token_kernel, fsdp), out_shape=(jax.Shap...  70.7 us
    pallas_call x2, Pallas kernels, weight_grad(): pl.pallas_call(weight_grad_kernel, grid=(EXP_DEV, height // size, width /...  31.8 us
    pallas_call x1, Pallas kernels, active(): pl.pallas_call(active_kernel, grid=(EXP_DEV, ff // wide), out_shape=(low,...  29.4 us
  transfers between devices with their start and end apart: 6, of which 1 were waited for; matrix products, arithmetic and copies ran while one was open for 4% of the time, Pallas kernels for 85%

profile of v4, /device:TPU:12, one launch (start us, length us, event | category | flops | bytes accessed | tf_op | source)
XLA Modules:
  0.0 794.1 jit_solution(15111762037315923921)
XLA Ops:
  7.2 0.7 all-gather.4.cloned.1.call-update
  8.0 0.7 all-gather.6.cloned.1.call-update
  8.8 0.7 all-gather.8.cloned.1.call-update
  9.5 0.7 slice.24.g_ref
  10.2 1.0 slice.26.g_ref
  11.3 0.7 reshape.92.routes_ref
  12.3 0.6 fusion.13.misc_ref
  12.9 1.0 pad_maximum_fusion.w_ref
  13.9 104.3 %gather_start.1 = (bf16[1024,2048]{1,0:T(8,128)(2,1)}, bf16[3,2048,512]{2,1,0:T(8,128)(2,1)}, bf16[512,2048]{1,0:T(8,128)(2,1)}, bf16[8,32,2048]{2,1,0:T(8,128)(...) custom-call(bf16[256,2048]{1,0:T(8,128)(2,1)} %x_ref.5, bf16[3,64,2048]{2,1,0:T(8,128)(2,1)} %pad_maximum_fusion.w_ref, ...), custom_call_target="tpu_custom_call" | custom-call | tf_op jit(solution)/shard_map/gather_start/pallas_call | solution.py:653
  118.2 0.9 copy.68
  119.3 0.7 reshape.103.gain
  120.0 1.4 eq.63
  122.2 0.4 reshape.95
  122.6 0.8 copy.61
  123.4 19.1 %project.1 = (bf16[1024,2048]{1,0:T(8,128)(2,1)}, f32[1024,512]{1,0:T(8,128)}, f32[1024,512]{1,0:T(8,128)}, bf16[1024,512]{1,0:T(8,128)(2,1)}, f32[1024,128]{1,0:T(8,128)}) custom-call(bf16[1024,2048]{1,0:T(8,128)(2,1)} %get-tuple-element.68.x_ref, f32[4,2048]{1,0:T(4,128)} %reshape.103.gain, bf16[3,2048,512]{2,1,0:T(8,128)(2,1)} %get-tuple-element.70.w_ref), custom_call_target="tpu_custom_call" | custom-call | tf_op jit(solution)/shard_map/project/pallas_call | solution.py:1285
  142.5 1.3 constant_dynamic-slice_fusion.1.gain
  143.8 16.1 %attend.1 = (bf16[1024,512]{1,0:T(8,128)(2,1)}, f32[1024,128]{1,0:T(8,128)}, bf16[1024,512]{1,0:T(8,128)(2,1)}, bf16[1024,512]{1,0:T(8,128)(2,1)}) custom-call(f32[1024,512]{1,0:T(8,128)} %get-tuple-element.71.q_raw, f32[1024,512]{1,0:T(8,128)} %get-tuple-element.72.k_raw, bf16[1024,512]{1,0:T(8,128)(2,1)} %get-tuple-element.73.v_ref, ...), custom_call_target="tpu_custom_call" | custom-call | tf_op jit(solution)/shard_map/attend/pallas_call | solution.py:1331
  159.9 5.6 convolution_convert_fusion
  165.5 75.7 %branch_sum.1 = (f32[256,2048]{1,0:T(8,128)}, bf16[256,2048]{1,0:T(8,128)(2,1)}, bf16[8,224,2048]{2,1,0:T(8,128)(2,1)}) custom-call(bf16[4,256,2048]{2,1,0:T(8,128)(2,1)} %bitcast.34, bf16[224,2048]{1,0:T(8,128)(2,1)} %slice.26.g_ref, bf16[256,2048]{1,0:T(8,128)(2,1)} %x_ref.5, f32[4,2048]{1,0:T(4,128)} %reshape.103.gain), custom_call_target="tpu_custom_call" | custom-call | tf_op jit(solution)/shard_map/branch_sum/pallas_call | solution.py:709
  241.2 1.4 fusion.3.picks
  242.6 0.6 compare_convert_fusion.columns
  243.3 70.7 %token_gather.1 = (bf16[8,256,2048]{2,1,0:T(8,128)(2,1)}, bf16[2,1152,2048]{2,1,0:T(8,128)(2,1)}, f32[2,1152,1024]{2,1,0:T(8,128)}) custom-call(bf16[256,2048]{1,0:T(8,128)(2,1)} %get-tuple-element.79.x_ref, bf16[8,32,2048]{2,1,0:T(8,128)(2,1)} %get-tuple-element.80.g_first, bf16[8,224,2048]{2,1,0:T(8,128)(2,1)} %get-tuple-element.81.g_second, ...), custom_call_target="tpu_custom_call" | custom-call | tf_op jit(solution)/shard_map/token_gather/pallas_call | solution.py:809
  313.9 15.0 %route.1 = (bf16[2,1152,2048]{2,1,0:T(8,128)(2,1)}, f32[8,256,16]{2,1,0:T(8,128)}, f32[2,1152,1]{2,1,0:T(8,128)}) custom-call(bf16[8,288,256]{2,1,0:T(8,128)(2,1)} %fusion.3.picks, bf16[8,256,2048]{2,1,0:T(8,128)(2,1)} %get-tuple-element.82.rows_in.tokens, bf16[16,2048]{1,0:T(8,128)(2,1)} %bitcast.38, f32[2,16]{1,0:T(2,128)} %compare_convert_fusion.columns), custom_call_target="tpu_custom_call" | custom-call | tf_op jit(solution)/shard_map/route/pallas_call | solution.py:1562
  328.9 16.4 %all-gather.8.cloned.1.call-done.w_ref = bf16[2,2048,1024]{2,1,0:T(8,128)(2,1)} async-done(((bf16[2,512,1024]{2,1,0:T(8,128)(2,1)}), bf16[2,2048,1024]{2,1,0:T(8,128)(2,1)}) %all-gather.8.cloned.1.call-update) | async-done | bytes 8388624 | tf_op jit(solution)/shard_map/all_gather | solution.py:1760
  345.2 29.4 %active.1 = (bf16[2,1152,1024]{2,1,0:T(8,128)(2,1)}, bf16[2,1152,1024]{2,1,0:T(8,128)(2,1)}, bf16[2,1152,1024]{2,1,0:T(8,128)(2,1)}, f32[2,1152,1]{2,1,0:T(8,128)}) custom-call(bf16[2,1152,2048]{2,1,0:T(8,128)(2,1)} %get-tuple-element.83.x_ref.a_ref, bf16[2,2048,1024]{2,1,0:T(8,128)(2,1)} %all-gather.6.cloned.1.call-done.g_ref, ...), custom_call_target="tpu_custom_call" | custom-call | tf_op jit(solution)/shard_map/active/pallas_call | solution.py:1614
  374.7 15.6 %down_grad.1 = bf16[2,1024,2048]{2,1,0:T(8,128)(2,1)} custom-call(bf16[2,1152,1024]{2,1,0:T(8,128)(2,1)} %get-tuple-element.91.gated_ref.a_ref, bf16[2,1152,2048]{2,1,0:T(8,128)(2,1)} %get-tuple-element.116.b_ref), custom_call_target="tpu_custom_call" | custom-call | tf_op jit(solution)/shard_map/down_grad/pallas_call | solution.py:1635
  390.4 16.1 %gate_grad.1 = bf16[2,2048,1024]{2,1,0:T(8,128)(2,1)} custom-call(bf16[2,1152,2048]{2,1,0:T(8,128)(2,1)} %get-tuple-element.83.x_ref.a_ref, bf16[2,1152,1024]{2,1,0:T(8,128)(2,1)} %get-tuple-element.86.a_ref.b_ref), custom_call_target="tpu_custom_call" | custom-call | tf_op jit(solution)/shard_map/gate_grad/pallas_call | solution.py:1635
  406.6 0.8 copy-done.5
  407.4 0.7 pad_maximum_fusion.1.router
  408.0 2.8 fusion.1.turned
  410.8 26.7 %rows_back.1.rows_ref = bf16[2,1152,2048]{2,1,0:T(8,128)(2,1)} custom-call(bf16[2,1152,1024]{2,1,0:T(8,128)(2,1)} %get-tuple-element.86.a_ref.b_ref, bf16[2,1152,1024]{2,1,0:T(8,128)(2,1)} %get-tuple-element.87.b_ref.gu_ref, bf16[2,2048,1024]{2,1,0:T(8,128)(2,1)} %all-gather.6.cloned.1.call-done.g_ref, bf16[2,2048,1024]{2,1,0:T(8,128)(2,1)} %all-gather.8.cloned.1.call-done.w_ref), custom_call_target="tpu_custom_call" | custom-call | tf_op jit(solution)/shard_map/rows_back/pallas_call | solution.py:1658
  437.7 1.2 fusion.6.dots
  438.9 16.6 %combine.1 = (bf16[8,256,2048]{2,1,0:T(8,128)(2,1)}, f32[32,2048]{1,0:T(8,128)}) custom-call(bf16[8,2,256,144]{3,2,1,0:T(8,128)(2,1)} %fusion.1.turned, bf16[2,1152,2048]{2,1,0:T(8,128)(2,1)} %rows_back.1.rows_ref, bf16[8,256,2048]{2,1,0:T(8,128)(2,1)} %get-tuple-element.82.rows_in.tokens, f32[8,256,16]{2,1,0:T(8,128)} %get-tuple-element.88.probs, ...), custom_call_target="tpu_custom_call" | custom-call | tf_op jit(solution)/shard_map/combine/pallas_call | solution.py:1693
  455.5 86.1 %token_back.1 = (f32[256,2048]{1,0:T(8,128)}, bf16[256,2048]{1,0:T(8,128)(2,1)}, f32[8,2048]{1,0:T(8,128)}, bf16[8,256,2048]{2,1,0:T(8,128)(2,1)}, bf16[2,2048,1024]{2,1,0:T(8,128)(2,1)}) custom-call(bf16[8,256,2048]{2,1,0:T(8,128)(2,1)} %get-tuple-element.90.p_ref, bf16[2,1152,1024]{2,1,0:T(8,128)(2,1)} %get-tuple-element.91.gated_ref.a_ref, ...), custom_call_target="tpu_custom_call" | custom-call | tf_op jit(solution)/shard_map/token_back/pallas_call | solution.py:961
  541.7 0.9 copy-done.6
  542.6 0.3 copy.62
  542.9 1.0 reshape.96.router_ref
  543.9 97.0 %branch_back.1 = (bf16[1024,2048]{1,0:T(8,128)(2,1)}, f32[256,2048]{1,0:T(8,128)}, f32[1024,512]{1,0:T(8,128)}, f32[1024,512]{1,0:T(8,128)}, bf16[1024,512]{1,0:...) custom-call(bf16[256,2048]{1,0:T(8,128)(2,1)} %get-tuple-element.92.x_ref, ...), custom_call_target="tpu_custom_call" | custom-call | tf_op jit(solution)/shard_map/branch_back/pallas_call | solution.py:1436
  640.9 19.7 %weight_parts.1 = (bf16[8,1024,512]{2,1,0:T(8,128)(2,1)}, bf16[1024,1536]{1,0:T(8,128)(2,1)}) custom-call(f32[1024,512]{1,0:T(8,128)} %get-tuple-element.98.q_scaled, f32[1024,512]{1,0:T(8,128)} %get-tuple-element.99.k_scaled, f32[1024,512]{1,0:T(8,128)} %get-tuple-element.71.q_raw, f32[1024,512]{1,0:T(8,128)} %get-tuple-element.72.k_raw, ...), custom_call_target="tpu_custom_call" | custom-call | tf_op jit(solution)/shard_map/weight_parts/pallas_call | solution.py:1501
  660.6 0.6 constant_dynamic-update-slice_fusion.gains_in
  661.2 110.1 %end_exchange.1 = (f32[256,2048]{1,0:T(8,128)}, bf16[64,2048]{1,0:T(8,128)(2,1)}, bf16[64,2048]{1,0:T(8,128)(2,1)}, bf16[64,2048]{1,0:T(8,128)(2,1)}, bf16[64,2048]{1,0:T(8,128)(2,1)}, /*index=5*/f32[16,128]{1,0:T(8,128)}) custom-call(bf16[8,1024,512]{2,1,0:T(8,128)(2,1)} %get-tuple-element.104.p_ref, bf16[1024,1536]{1,0:T(8,128)(2,1)} %get-tuple-element.105.low_ref, ...), custom_call_target="tpu_custom_call" | custom-call | tf_op jit(solution)/shard_map/end_exchange/pallas_call | solution.py:1174
  771.3 0.7 slice.31
  771.9 0.7 slice.30
  772.7 0.7 copy.63
  773.4 0.6 constant_dynamic-slice_fusion
  774.0 2.8 add_convert_fusion
  776.8 8.6 %widen.1 = (f32[64,2048]{1,0:T(8,128)}, f32[64,2048]{1,0:T(8,128)}, f32[64,2048]{1,0:T(8,128)}, f32[64,2048]{1,0:T(8,128)}, f32[1024,1024]{1,0:T(8,128)}, /*index=5*/f32[1024,1024]{1,0:T(8,128)}, f32[512,2048]{1,0:T(8,128)}) custom-call(bf16[64,2048]{1,0:T(8,128)(2,1)} %get-tuple-element.111.refs_0_, bf16[64,2048]{1,0:T(8,128)(2,1)} %get-tuple-element.112.refs_1_, ...), custom_call_target="tpu_custom_call" | custom-call | tf_op jit(solution)/shard_map/widen/pallas_call | solution.py:1726
  785.5 1.3 copy.71
  (58 shorter events, 1.8 us)
Async XLA Ops:
  7.2 236.1 %all-gather.4.cloned.1.call-start = ((), (), s32[]{:S(2)}) async-start(), calls=%async_computation.3 | async-start | bytes 10485760 | tf_op jit(solution)/shard_map/all_gather | solution.py:1758
  7.9 1.6 copy-start.1
  7.9 321.0 %all-gather.6.cloned.1.call-start = ((), (), s32[]{:S(2)}) async-start(), calls=%async_computation.4 | async-start | bytes 10485760 | tf_op jit(solution)/shard_map/all_gather | solution.py:1759
  8.7 2.5 copy-start.10
  8.7 3.3 copy-start.11
  8.7 3.5 copy-start.13
  8.7 4.2 copy-start.7
  8.7 4.2 copy-start.8
  8.7 4.2 copy-start.9
  8.7 336.5 %all-gather.8.cloned.1.call-start = ((), (), s32[]{:S(2)}) async-start(), calls=%async_computation.5 | async-start | bytes 10485760 | tf_op jit(solution)/shard_map/all_gather | solution.py:1760
  9.5 767.4 %reduce-scatter.8.cloned.1.call-start = ((), (), s32[]{:S(2)}) async-start(), calls=%async_computation.8 | async-start | bytes 10485760 | tf_op jit(solution)/shard_map/reduce_scatter | solution.py:1821
  143.8 16.1 %copy-start.2 = (bf16[512,2048]{1,0:T(8,128)(2,1)S(1)}, bf16[512,2048]{1,0:T(8,128)(2,1)}, u32[]{:S(2)}) copy-start(bf16[512,2048]{1,0:T(8,128)(2,1)} %get-tuple-element.76.wo_ref) | copy-start | bytes 6291460
  390.3 386.5 %reduce-scatter.4.cloned.1.call-start = ((), (), s32[]{:S(2)}) async-start(), calls=%async_computation.6 | async-start | bytes 10485760 | tf_op jit(solution)/shard_map/reduce_scatter | solution.py:1821
  406.5 0.8 copy-start.5
  406.6 370.3 %reduce-scatter.6.cloned.1.call-start = ((), (), s32[]{:S(2)}) async-start(), calls=%async_computation.7 | async-start | bytes 10485760 | tf_op jit(solution)/shard_map/reduce_scatter | solution.py:1821
  410.8 26.7 %copy-start.4 = (f32[2,1152,1]{2,1,0:T(8,128)S(1)}, f32[2,1152,1]{2,1,0:T(8,128)}, u32[]{:S(2)}) copy-start(f32[2,1152,1]{2,1,0:T(8,128)} %get-tuple-element.89) | copy-start | bytes 27652
  541.6 1.0 copy-start.6
  640.9 19.7 %copy-start.12 = (f32[2,512]{1,0:T(2,128)S(1)}, f32[2,512]{1,0:T(2,128)}, u32[]{:S(2)}) copy-start(f32[2,512]{1,0:T(2,128)} %get-tuple-element.108) | copy-start | bytes 12292
  661.2 112.8 %copy-start = (f32[256,2048]{1,0:T(8,128)S(1)}, f32[256,2048]{1,0:T(8,128)}, u32[]{:S(2)}) copy-start(f32[256,2048]{1,0:T(8,128)} %get-tuple-element.77.mid_ref) | copy-start | bytes 6291460
  776.8 8.6 %copy-start.3 = (f32[256,2048]{1,0:T(8,128)S(1)}, f32[256,2048]{1,0:T(8,128)}, u32[]{:S(2)}) copy-start(f32[256,2048]{1,0:T(8,128)} %get-tuple-element.183) | copy-start | bytes 6291460
Sparse Core Ops, SparseCore 0:
  9.9 129.5 all-gather.3
  141.3 113.8 all-gather.5
  257.1 88.1 all-gather.7
  390.5 86.2 reduce-scatter.7
  480.0 100.4 reduce-scatter.3
  583.4 96.3 reduce-scatter.5

commit v5 on v4

--- a/solution.py
+++ b/solution.py
@@ -392,9 +392,11 @@
     def load(self):
         return pltpu.make_async_copy(self.p_ref.at[self.s], self.own, self.local)
 
-    def start(self):
-        for k in range(1, self.sp):
+    def start(self, make=lambda d: None):
+        for k in range(self.sp - 1, 0, -1):
+            make(self.s ^ k)
             self.copy(k).start()
+        make(self.s)
         self.load().start()
 
     def forward(self):
@@ -462,10 +464,15 @@
             self.recv.at[h, 2], (self.f, self.s ^ (3 - k)),
         )
 
-    def start(self):
-        for far in (True, False):
-            for h, k, _ in self.WAYS:
-                self.hop(h, k, far).start()
+    def start(self, make=lambda d: None):
+        make(self.s ^ 3)
+        for h, k, _ in self.WAYS:
+            self.hop(h, k, True).start()
+        make(self.s ^ 1)
+        make(self.s ^ 2)
+        for h, k, _ in self.WAYS:
+            self.hop(h, k, False).start()
+        make(self.s)
         for n in range(3):
             self.load(n).start()
 
@@ -525,23 +532,36 @@
     )
 
 
+def row_target(i, rows, sp):
+    parts = HEAD_DIM // rows
+    head, part = i // parts, lax.rem(i, parts)
+    return head // sp * parts + part, lax.rem(head, sp)
+
+
+def row_owner(f, s, rows, sp):
+    parts = HEAD_DIM // rows
+    return (f // parts * sp + s) * parts + lax.rem(f, parts)
+
+
 def start_kernel(
     fsdp, sp, x_ref, w_ref, wo_ref, g_ref, misc_ref, routes_ref,
     x_all, w_all, wo_all, g_all, misc_all, routes_all,
-    send, recv, xsend, xrecv, psend, precv, wsend, wrecv, msend, mrecv, rsend, rrecv, local,
+    send, recv, xsend, xrecv, psend, precv, wsend, wrecv, msend, mrecv, rsend, rrecv, local, wlocal,
 ):
     f, s = lax.axis_index("fsdp"), lax.axis_index("sp")
     count, lines = fsdp * sp, fsdp // 2
     me = f * sp + s
     rows = w_ref.shape[1]
-    cols = D // sp
+    heads = D // sp // HEAD_DIM
     barrier = pltpu.get_barrier_semaphore()
 
-    def w_block(s_to):
-        return w_ref.at[:, :, pl.ds(pl.multiple_of(s_to * cols, cols), cols)]
-
-    def w_rows(i):
-        return w_all.at[:, pl.ds(pl.multiple_of(i * rows, rows), rows), :]
+    def w_block(s_to, g):
+        at = pl.multiple_of((g * sp + s_to) * HEAD_DIM, HEAD_DIM)
+        return w_ref.at[:, :, pl.ds(at, HEAD_DIM)]
+
+    def w_rows(i, g):
+        at = pl.ds(pl.multiple_of(i * rows, rows), rows)
+        return w_all.at[:, at, pl.ds(g * HEAD_DIM, HEAD_DIM)]
 
     def w_view(b):
         size = rows * sp
@@ -549,14 +569,16 @@
 
     wo_view = rows_view(wo_all, rows)
     x_view = rows_view(x_all, TOK_DEV)
+    w_owns = [
+        pltpu.make_async_copy(w_block(s, g), w_rows(me, g), wlocal.at[g]) for g in range(heads)
+    ]
     owns = [
-        pltpu.make_async_copy(w_block(s), w_rows(me), local.at[0]),
-        pltpu.make_async_copy(x_ref, x_view(s), local.at[1]),
-        pltpu.make_async_copy(misc_ref, misc_all.at[me], local.at[2]),
-        pltpu.make_async_copy(routes_ref, routes_all.at[f], local.at[3]),
-        pltpu.make_async_copy(g_ref, g_all.at[f], local.at[4]),
+        pltpu.make_async_copy(x_ref, x_view(s), local.at[0]),
+        pltpu.make_async_copy(misc_ref, misc_all.at[me], local.at[1]),
+        pltpu.make_async_copy(routes_ref, routes_all.at[f], local.at[2]),
+        pltpu.make_async_copy(g_ref, g_all.at[f], local.at[3]),
     ]
-    for copy in owns:
+    for copy in w_owns + owns:
         copy.start()
     greet_all(barrier, me, count, sp)
     pl.semaphore_wait(barrier, count - 1)
@@ -566,10 +588,13 @@
     w_copies = []
     for k in range(sp - 1, 0, -1):
         s_to = s ^ k
-        copy = remote(w_block(s_to), w_rows(me), psend.at[k], precv.at[k], (f, s_to))
-        copy.start()
-        w_copies.append(copy)
-    target_s, target_f = me // fsdp, lax.rem(me, fsdp)
+        for g in range(heads):
+            copy = remote(
+                w_block(s_to, g), w_rows(me, g), psend.at[k, g], precv.at[k, g], (f, s_to)
+            )
+            copy.start()
+            w_copies.append(copy)
+    target_f, target_s = row_target(me, rows, sp)
     stays = jnp.logical_and(target_s == s, target_f == f)
     wo_copy = remote(wo_ref, wo_view(target_f), wsend, wrecv, (target_f, target_s))
     wo_own = pltpu.make_async_copy(wo_ref, wo_view(f), wrecv)
@@ -604,9 +629,11 @@
 
     lax.fori_loop(1, fsdp, routes_go, 0)
 
-    owns[0].wait()
+    for copy in w_owns:
+        copy.wait()
     for k in range(1, sp):
-        landed(w_rows(f * sp + (s ^ k)), precv.at[k])
+        for g in range(heads):
+            landed(w_rows(f * sp + (s ^ k), g), precv.at[k, g])
     line.start_own(0)
     tokens = plane_gather_of(x_ref, x_all, f, s, sp, xsend, xrecv)
     tokens.start()
@@ -643,12 +670,13 @@
     def _():
         wo_copy.wait_send()
 
-    for copy in owns[1:]:
+    for copy in owns:
         copy.wait()
 
 
 def gather_start(fsdp, sp, x, w, wo, g, misc, routes):
     count = fsdp * sp
+    heads = D // sp // HEAD_DIM
     dma = pltpu.SemaphoreType.DMA
     return pl.pallas_call(
         functools.partial(start_kernel, fsdp, sp),
@@ -664,15 +692,17 @@
         out_specs=[ANY] * 6,
         scratch_shapes=line_sems(3, fsdp)
         + [
-            dma((sp,)), dma((sp,)), dma((sp,)), dma((sp,)), dma, dma,
-            dma((count,)), dma((count,)), dma((fsdp,)), dma((fsdp,)), dma((5,)),
+            dma((sp,)), dma((sp,)), dma((sp, heads)), dma((sp, heads)), dma, dma,
+            dma((count,)), dma((count,)), dma((fsdp,)), dma((fsdp,)), dma((4,)), dma((heads,)),
         ],
         compiler_params=comm_params(0),
         name="gather_start",
     )(x, w, wo, g, misc, routes)
 
 
-def branch_kernel(fsdp, sp, p_ref, g_ref, x_ref, gain, out_ref, second_ref, g_all, *scratch):
+def branch_kernel(
+    fsdp, sp, a_ref, w_ref, g_ref, x_ref, gain, out_ref, second_ref, g_all, terms, *scratch
+):
     f, s = lax.axis_index("fsdp"), lax.axis_index("sp")
     lines = fsdp // 2
     barrier = pltpu.get_barrier_semaphore()
@@ -681,10 +711,17 @@
     own = pltpu.make_async_copy(g_ref, g_all.at[f], own_sem)
     own.start()
     pl.semaphore_wait(barrier, expected)
-    plane = plane_reduce_of(p_ref, out_ref, scratch[:-3], f, s, sp)
+    plane = plane_reduce_of(terms, out_ref, scratch[:-3], f, s, sp)
     line = LineGather([block_view(g_all)], [g_ref], lines, f, s, send, recv)
-    plane.start()
     line.start_own(0)
+
+    def branch_of(d):
+        rows = pl.ds(pl.multiple_of(d * TOK_DEV, TOK_DEV), TOK_DEV)
+        for n in range(D // 512):
+            at = pl.ds(n * 512, 512)
+            terms[d, :, at] = dot_nn(a_ref[rows, :], w_ref[:, at]).astype(BF16)
+
+    plane.start(branch_of)
     for k in range(1, lines):
         line.forward(0, k)
         if k == min(2, lines - 1):
@@ -704,8 +741,8 @@
     own.wait()
 
 
-def branch_sum(fsdp, partial, g, x, gains):
-    sp, block = partial.shape[0], partial.shape[1:]
+def branch_sum(fsdp, attended, w, g, x, gains):
+    sp, block = attended.shape[0] // TOK_DEV, x.shape
     return pl.pallas_call(
         functools.partial(branch_kernel, fsdp, sp),
         out_shape=(
@@ -713,12 +750,13 @@
             jax.ShapeDtypeStruct(block, BF16),
             jax.ShapeDtypeStruct((fsdp,) + g.shape, BF16),
         ),
-        in_specs=[ANY, VMEM, VMEM, VMEM],
+        in_specs=[VMEM] * 5,
         out_specs=[VMEM, VMEM, ANY],
-        scratch_shapes=plane_scratch(block, sp) + line_sems(1, fsdp) + [pltpu.SemaphoreType.DMA],
+        scratch_shapes=[pltpu.VMEM((sp,) + block, BF16)]
+        + plane_scratch(block, sp) + line_sems(1, fsdp) + [pltpu.SemaphoreType.DMA],
         compiler_params=comm_params(2),
         name="branch_sum",
-    )(partial, g, x, gains)
+    )(attended, w, g, x, gains)
 
 
 def token_kernel(
@@ -1117,7 +1155,7 @@
         return low.at[pl.ds(pl.multiple_of(i * height + place * rows, rows), rows), :]
 
     def q_to(i, place):
-        return (qkv_0, qkv_1, qkv_2)[i].at[:, pl.ds(pl.multiple_of(place * cols, cols), cols)]
+        return (qkv_0, qkv_1, qkv_2)[i].at[place]
 
     def q_copy(i, k):
         return remote(q_from(i, s ^ k), q_to(i, s), qsend.at[k, i], qrecv.at[k, i], (f, s ^ k))
@@ -1128,8 +1166,8 @@
     for k in range(sp - 1, 0, -1):
         for i in range(3):
             q_copy(i, k).start()
-    flat = s * fsdp + f
-    target_f, target_s = flat // sp, lax.rem(flat, sp)
+    owner = row_owner(f, s, rows, sp)
+    target_f, target_s = owner // sp, lax.rem(owner, sp)
     stays = jnp.logical_and(target_s == s, target_f == f)
     o_copy = remote(o_low, o_out, osend, orecv, (target_f, target_s))
     o_own = pltpu.make_async_copy(o_low, o_out, orecv)
@@ -1175,9 +1213,9 @@
         functools.partial(end_kernel, fsdp, sp),
         out_shape=(
             jax.ShapeDtypeStruct((TOK_DEV, D), F32),
-            jax.ShapeDtypeStruct((rows, D), BF16),
-            jax.ShapeDtypeStruct((rows, D), BF16),
-            jax.ShapeDtypeStruct((rows, D), BF16),
+            jax.ShapeDtypeStruct((sp, rows, D // sp), BF16),
+            jax.ShapeDtypeStruct((sp, rows, D // sp), BF16),
+            jax.ShapeDtypeStruct((sp, rows, D // sp), BF16),
             jax.ShapeDtypeStruct((rows, D), BF16),
             jax.ShapeDtypeStruct((16, 128), F32),
         ),
@@ -1404,20 +1442,22 @@
     line.start()
     dots[...] = jnp.zeros_like(dots)
     out_all = pltpu.make_async_copy(g_all, all_ref, all_sem)
+    def back_of(place):
+        at = pl.ds(pl.multiple_of(place * TOK_DEV, TOK_DEV), TOK_DEV)
+        dv_out[at, :] = dot_nt(g_all[at, :], wo_ref[...]).astype(BF16)
+
+    early = (0, 1, 2) if sp == 4 else (0,)
     for t in range(lines - 1):
         line.step(t)
         if t == min(1, lines - 2):
             plane.forward()
+            own.wait()
+            for k in early:
+                back_of(s ^ k)
     plane.finish()
-    own.wait()
     out_all.start()
-
-    def block(i, carry):
-        at = pl.ds(pl.multiple_of(i * TOK_DEV, TOK_DEV), TOK_DEV)
-        dv_out[at, :] = dot_nt(g_all[at, :], wo_ref[...]).astype(BF16)
-        return carry
-
-    lax.fori_loop(0, sp, block, 0)
+    for k in range(len(early), sp):
+        back_of(s ^ k)
     for h in range(q_ref.shape[1] // HEAD_DIM):
         attend_back_head(
             h, q_ref, k_ref, v_ref, sums, q_raw, k_raw, gain, table,
@@ -1580,7 +1620,29 @@
 FT = 256
 
 
-def active_kernel(x_ref, g_ref, w_ref, u_ref, gates, gated, grad_gate, grad_up, dots):
+def gate_kernel(x_ref, w_ref, out):
+    out[0] = dot_nn(x_ref[0], w_ref[0])
+
+
+def gate_product(x, w_gate):
+    _, total, _ = x.shape
+    ff = w_gate.shape[2]
+    wide = 2 * FT
+    return pl.pallas_call(
+        gate_kernel,
+        grid=(EXP_DEV, ff // wide),
+        out_shape=jax.ShapeDtypeStruct((EXP_DEV, total, ff), F32),
+        in_specs=[
+            pl.BlockSpec((1, total, D), lambda e, j: (e, 0, 0)),
+            pl.BlockSpec((1, D, wide), lambda e, j: (e, 0, j)),
+        ],
+        out_specs=pl.BlockSpec((1, total, wide), lambda e, j: (e, 0, j)),
+        compiler_params=pltpu.CompilerParams(vmem_limit_bytes=VLIM),
+        name="gate_product",
+    )(x, w_gate)
+
+
+def active_kernel(x_ref, pre_ref, w_ref, u_ref, gates, gated, grad_gate, grad_up, dots):
     @pl.when(pl.program_id(1) == 0)
     def _():
         dots[...] = jnp.zeros_like(dots)
@@ -1589,7 +1651,7 @@
     chunk = total // 4
     for first in range(0, total, chunk):
         at = slice(first, first + chunk)
-        gate_pre = dot_nn(x_ref[0, at, :], g_ref[0])
+        gate_pre = pre_ref[0, at, :]
         up_pre = dot_nn(x_ref[0, at, :], w_ref[0])
         sig = jax.nn.sigmoid(gate_pre)
         silu = gate_pre * sig
@@ -1603,7 +1665,7 @@
         grad_up[0, at, :] = (back * silu).astype(BF16)
 
 
-def active(x, w_gate, w_up, u, gates):
+def active(x, gate_pre, w_up, u, gates):
     _, total, _ = x.shape
     ff = w_up.shape[2]
     wide = 2 * FT
@@ -1616,12 +1678,12 @@
         grid=(EXP_DEV, ff // wide),
         out_shape=(low, low, low, jax.ShapeDtypeStruct((EXP_DEV, total, 1), F32)),
         in_specs=[
-            pl.BlockSpec((1, total, D), lambda e, j: (e, 0, 0)), weight, weight, tile, column,
+            pl.BlockSpec((1, total, D), lambda e, j: (e, 0, 0)), tile, weight, tile, column,
         ],
         out_specs=[tile, tile, tile, column],
         compiler_params=pltpu.CompilerParams(vmem_limit_bytes=VLIM),
         name="active",
-    )(x, w_gate, w_up, u, gates)
+    )(x, gate_pre, w_up, u, gates)
 
 
 def weight_grad_kernel(a_ref, b_ref, out):
@@ -1708,31 +1770,53 @@
     )(turned, grad_rows, tokens, probs, dots, router_two, columns)
 
 
-def widen_kernel(*refs):
+def widen_kernel(mid, total, *refs):
+    *refs, layer_out = refs
+    layer_out[...] = (mid[...] + total[...]).astype(BF16)
     count = len(refs) // 2
     for low, out in zip(refs[:count], refs[count:]):
-        out[...] = low[...].astype(F32)
-
-
-def widen(arrays):
+        if len(low.shape) == 2:
+            out[...] = low[...].astype(F32)
+            continue
+        sp, _, cols = low.shape
+        for s in range(sp):
+            for g in range(cols // HEAD_DIM):
+                head = g * sp + s
+                out[:, head * HEAD_DIM : (head + 1) * HEAD_DIM] = low[
+                    s, :, g * HEAD_DIM : (g + 1) * HEAD_DIM
+                ].astype(F32)
+
+
+def widen(mid, total, by_heads, arrays):
+    steps = 4
     flat = [x.reshape(-1, x.shape[-1]) for x in arrays]
-    steps = 4
-    specs = [
-        whole(x.shape)
-        if x.shape[0] % (16 * steps)
-        else pl.BlockSpec((x.shape[0] // steps, x.shape[1]), lambda i: (i, 0))
-        for x in flat
-    ]
+
+    def rows_of(shape, axis):
+        tall = shape[axis] // steps if shape[axis] % (16 * steps) == 0 else shape[axis]
+        block = shape[:axis] + (tall,) + shape[axis + 1 :]
+        moving = tall != shape[axis]
+        return pl.BlockSpec(
+            block, lambda i: tuple(i if moving and n == axis else 0 for n in range(len(shape)))
+        )
+
+    heads_out = [(x.shape[1], x.shape[0] * x.shape[2]) for x in by_heads]
     wide = pl.pallas_call(
         widen_kernel,
         grid=(steps,),
-        out_shape=tuple(jax.ShapeDtypeStruct(x.shape, F32) for x in flat),
-        in_specs=specs,
-        out_specs=specs,
+        out_shape=tuple(
+            jax.ShapeDtypeStruct(shape, F32) for shape in heads_out + [x.shape for x in flat]
+        )
+        + (jax.ShapeDtypeStruct(mid.shape, BF16),),
+        in_specs=[rows_of(mid.shape, 0)] * 2
+        + [rows_of(x.shape, 1) for x in by_heads]
+        + [rows_of(x.shape, 0) for x in flat],
+        out_specs=[rows_of(shape, 0) for shape in heads_out + [x.shape for x in flat] + [mid.shape]],
         compiler_params=pltpu.CompilerParams(vmem_limit_bytes=VLIM),
         name="widen",
-    )(*flat)
-    return [x.reshape(like.shape) for x, like in zip(wide, arrays)]
+    )(mid, total, *by_heads, *flat)
+    split = len(by_heads)
+    shaped = [x.reshape(like.shape) for x, like in zip(wide[split:-1], arrays)]
+    return list(wide[:split]) + shaped + [wide[-1]]
 
 
 def angles(seq):
@@ -1774,7 +1858,8 @@
     router_t = router_w.T
     gains_w = misc_all[:, router_size : router_size + 4 * rows].reshape(count, 4, rows)
     gains32 = gains_w.transpose(1, 0, 2).reshape(4, D).astype(F32)
-    gains_own = lax.dynamic_slice_in_dim(gains32, s * cols, cols, axis=1)
+    by_head = gains32.reshape(4, cols // HEAD_DIM, sp, HEAD_DIM)
+    gains_own = lax.dynamic_index_in_dim(by_head, s, axis=2, keepdims=False).reshape(4, cols)
 
     routes_block = routes_all.reshape(fsdp, TOK_DEV, TOP)
     own_ids = f * EXP_DEV + jnp.arange(EXP_DEV, dtype=jnp.int32)
@@ -1797,17 +1882,17 @@
     attended, sums, queries, keys = attend(
         q_raw, k_raw, values, squares, gains_own, table
     )
-    branch = dot_nn(attended, wo_s).astype(BF16).reshape(sp, TOK_DEV, D)
     mid, second_in, grad_second_half = branch_sum(
-        fsdp, branch, output_grad[early:], layer_input, gains32
+        fsdp, attended, wo_s, output_grad[early:], layer_input, gains32
     )
 
     tokens, grad_taken, unscaled = token_gather(
         fsdp, second_in, grad_first_half, grad_second_half, picks, down_full
     )
     received, probs, slot_gates = route(picks, tokens, router_t, columns)
+    gate_pre = gate_product(received, gate_full)
     gated, grad_gate_pre, grad_up_pre, slot_dots = active(
-        received, gate_full, up_full, unscaled, slot_gates
+        received, gate_pre, up_full, unscaled, slot_gates
     )
     dots_two = jnp.pad(two_parts(slot_dots, 2), ((0, 0), (0, 0), (0, 126)))
     grad_rows = rows_back(grad_gate_pre, grad_up_pre, gate_full, up_full)
@@ -1831,19 +1916,22 @@
         fsdp, sp, grad_mid_low, out_part, wo_s, queries, keys, values, sums, q_raw, k_raw,
         gains_own, table,
     )
-    layer_out = (mid + out_sum).astype(BF16)
     weight_part, grads_low = weight_parts(
         fsdp, q_scaled, k_scaled, q_raw, k_raw, squares, dots, grad_values, first_in, attended, grad_branch
     )
 
-    gain_rows = lax.dynamic_update_slice(gain_rows, gain_qk, (2, s * cols))
+    gain_rows = lax.dynamic_update_slice(
+        gain_rows.reshape(8, cols // HEAD_DIM, sp, HEAD_DIM),
+        gain_qk.reshape(2, cols // HEAD_DIM, 1, HEAD_DIM),
+        (2, 0, s, 0),
+    ).reshape(8, D)
     router_part = grad_router.reshape(count, router_size)
     router_part = jnp.pad(router_part, ((0, 0), (0, 1024 - router_size))).reshape(count, 8, 128)
     input_grad, *weight_grads, small = end_exchange(
         fsdp, sp, weight_part, grads_low, w_all, layer_input, grad_mid, gains32, gain_rows, router_part, 8
     )
-    *weight_grads, grad_gate, grad_up, grad_down = widen(
-        [*weight_grads, grad_gate, grad_up, grad_down]
+    *weight_grads, grad_gate, grad_up, grad_down, layer_out = widen(
+        mid, out_sum, weight_grads[:3], [weight_grads[3], grad_gate, grad_up, grad_down]
     )
     grad_router_own = small[:8].reshape(1024)[:router_size].reshape(rows, experts)
     first_lane = (f * sp + s) * rows % 128

time: 803 us -> 782 us (0.974)
    pallas_call x0 -> x1, Pallas kernels: none -> 16.8 us  [gate_product(): pl.pallas_call(gate_kernel, grid=(EXP_DEV, ff // wide), out_shape=jax.Sha...]
    pallas_call x1, Pallas kernels: 110 us -> 101 us  [end_exchange(): pl.pallas_call(functools.partial(end_kernel, fsdp, sp), out_shape=(jax.Sh...]
  transfers between devices with their start and end apart: 6 -> 6, of which waited for: 1 -> 1; matrix products, arithmetic and copies ran while one was open for 4% -> 3% of each run, Pallas kernels for 85% -> 87%
where the time goes in v5:
time: 782 us; the launch traced here: 773 us
  Pallas kernels  723 us (92%)
  local copies, waits for them, and re-layouts  15.1 us (2%)
  between operations  14.9 us (2%)
  waiting for transfers between devices  10.5 us (1%)
  other arithmetic  8.62 us (1%)
    pallas_call x1, Pallas kernels, end_exchange(): pl.pallas_call(functools.partial(end_kernel, fsdp, sp), out_shape=(jax.Sh...  101 us
    pallas_call x1, Pallas kernels, gather_start(): pl.pallas_call(functools.partial(start_kernel, fsdp, sp), out_shape=(jax....  98.7 us
    pallas_call x1, Pallas kernels, branch_back(): pl.pallas_call(functools.partial(branch_back_kernel, fsdp, sp), out_shape...  93.8 us
    pallas_call x1, Pallas kernels, token_back(): pl.pallas_call(functools.partial(token_back_kernel, fsdp), out_shape=(jax...  86.1 us
    pallas_call x1, Pallas kernels, branch_sum(): pl.pallas_call(functools.partial(branch_kernel, fsdp, sp), out_shape=(jax...  75.4 us
    pallas_call x1, Pallas kernels, token_gather(): pl.pallas_call(functools.partial(token_kernel, fsdp), out_shape=(jax.Shap...  70.7 us
    pallas_call x2, Pallas kernels, weight_grad(): pl.pallas_call(weight_grad_kernel, grid=(EXP_DEV, height // size, width /...  31.8 us
    pallas_call x1, Pallas kernels, rows_back(): pl.pallas_call(rows_back_kernel, grid=(EXP_DEV, D // size), out_shape=jax...  26.7 us
  transfers between devices with their start and end apart: 6, of which 1 were waited for; matrix products, arithmetic and copies ran while one was open for 3% of the time, Pallas kernels for 87%

profile of v5, /device:TPU:12, one launch (start us, length us, event | category | flops | bytes accessed | tf_op | source)
XLA Modules:
  0.0 772.8 jit_solution(7789224152881629662)
XLA Ops:
  7.2 0.7 all-gather.4.cloned.1.call-update
  8.0 0.7 all-gather.6.cloned.1.call-update
  8.8 0.7 all-gather.8.cloned.1.call-update
  9.7 0.7 reshape.108.routes_ref
  10.4 0.7 slice.24.g_ref
  11.3 0.6 fusion.13.misc_ref
  11.9 1.0 pad_maximum_fusion.w_ref
  12.9 98.7 %gather_start.1 = (bf16[1024,2048]{1,0:T(8,128)(2,1)}, bf16[3,2048,512]{2,1,0:T(8,128)(2,1)}, bf16[512,2048]{1,0:T(8,128)(2,1)}, bf16[8,32,2048]{2,1,0:T(8,128)(...) custom-call(bf16[256,2048]{1,0:T(8,128)(2,1)} %x_ref.5, bf16[3,64,2048]{2,1,0:T(8,128)(2,1)} %pad_maximum_fusion.w_ref, ...), custom_call_target="tpu_custom_call" | custom-call | tf_op jit(solution)/shard_map/gather_start/pallas_call | solution.py:681
  111.6 1.0 copy.89
  112.7 0.7 reshape.122.gain
  113.5 1.0 slice.26.g_ref
  114.5 0.6 copy.90
  115.1 0.6 eq.63
  115.7 0.3 copy.75
  116.4 0.4 reshape.111
  116.8 0.8 copy.79
  117.6 20.5 %project.1 = (bf16[1024,2048]{1,0:T(8,128)(2,1)}, f32[1024,512]{1,0:T(8,128)}, f32[1024,512]{1,0:T(8,128)}, bf16[1024,512]{1,0:T(8,128)(2,1)}, f32[1024,128]{1,0:T(8,128)}) custom-call(bf16[1024,2048]{1,0:T(8,128)(2,1)} %get-tuple-element.69.x_ref, f32[4,2048]{1,0:T(4,128)} %reshape.122.gain, bf16[3,2048,512]{2,1,0:T(8,128)(2,1)} %get-tuple-element.71.w_ref), custom_call_target="tpu_custom_call" | custom-call | tf_op jit(solution)/shard_map/project/pallas_call | solution.py:1323
  138.2 16.0 %attend.1 = (bf16[1024,512]{1,0:T(8,128)(2,1)}, f32[1024,128]{1,0:T(8,128)}, bf16[1024,512]{1,0:T(8,128)(2,1)}, bf16[1024,512]{1,0:T(8,128)(2,1)}) custom-call(f32[1024,512]{1,0:T(8,128)} %get-tuple-element.72.q_raw, f32[1024,512]{1,0:T(8,128)} %get-tuple-element.73.k_raw, bf16[1024,512]{1,0:T(8,128)(2,1)} %get-tuple-element.74.v_ref, ...), custom_call_target="tpu_custom_call" | custom-call | tf_op jit(solution)/shard_map/attend/pallas_call | solution.py:1369
  154.2 75.4 %branch_sum.1 = (f32[256,2048]{1,0:T(8,128)}, bf16[256,2048]{1,0:T(8,128)(2,1)}, bf16[8,224,2048]{2,1,0:T(8,128)(2,1)}) custom-call(bf16[1024,512]{1,0:T(8,128)(2,1)} %get-tuple-element.76.a_ref.attended, bf16[512,2048]{1,0:T(8,128)(2,1)} %get-tuple-element.77.w_ref.wo_ref, bf16[224,2048]{1,0:T(8,128)(2,1)} %slice.26.g_ref, bf16[256,2048]{1,0:T(8,128)(2,1)} %x_ref.5, ...), custom_call_target="tpu_custom_call" | custom-call | tf_op jit(solution)/shard_map/branch_sum/pallas_call | solution.py:746
  229.6 1.4 fusion.3.picks
  231.0 0.6 compare_convert_fusion.columns
  231.6 70.7 %token_gather.1 = (bf16[8,256,2048]{2,1,0:T(8,128)(2,1)}, bf16[2,1152,2048]{2,1,0:T(8,128)(2,1)}, f32[2,1152,1024]{2,1,0:T(8,128)}) custom-call(bf16[256,2048]{1,0:T(8,128)(2,1)} %get-tuple-element.80.x_ref, bf16[8,32,2048]{2,1,0:T(8,128)(2,1)} %get-tuple-element.81.g_first, bf16[8,224,2048]{2,1,0:T(8,128)(2,1)} %get-tuple-element.82.g_second, ...), custom_call_target="tpu_custom_call" | custom-call | tf_op jit(solution)/shard_map/token_gather/pallas_call | solution.py:847
  302.3 15.0 %route.1 = (bf16[2,1152,2048]{2,1,0:T(8,128)(2,1)}, f32[8,256,16]{2,1,0:T(8,128)}, f32[2,1152,1]{2,1,0:T(8,128)}) custom-call(bf16[8,288,256]{2,1,0:T(8,128)(2,1)} %fusion.3.picks, bf16[8,256,2048]{2,1,0:T(8,128)(2,1)} %get-tuple-element.83.rows_in.tokens, bf16[16,2048]{1,0:T(8,128)(2,1)} %bitcast.42, f32[2,16]{1,0:T(2,128)} %compare_convert_fusion.columns), custom_call_target="tpu_custom_call" | custom-call | tf_op jit(solution)/shard_map/route/pallas_call | solution.py:1602
  317.3 16.8 %gate_product.1.pre_ref = f32[2,1152,1024]{2,1,0:T(8,128)} custom-call(bf16[2,1152,2048]{2,1,0:T(8,128)(2,1)} %get-tuple-element.84.x_ref.a_ref, bf16[2,2048,1024]{2,1,0:T(8,128)(2,1)} %all-gather.6.cloned.1.call-done.w_ref.g_ref), custom_call_target="tpu_custom_call" | custom-call | tf_op jit(solution)/shard_map/gate_product/pallas_call | solution.py:1631
  334.0 8.4 %all-gather.8.cloned.1.call-done.w_ref = bf16[2,2048,1024]{2,1,0:T(8,128)(2,1)} async-done(((bf16[2,512,1024]{2,1,0:T(8,128)(2,1)}), bf16[2,2048,1024]{2,1,0:T(8,128)(2,1)}) %all-gather.8.cloned.1.call-update) | async-done | bytes 8388624 | tf_op jit(solution)/shard_map/all_gather | solution.py:1844
  342.4 24.4 %active.1 = (bf16[2,1152,1024]{2,1,0:T(8,128)(2,1)}, bf16[2,1152,1024]{2,1,0:T(8,128)(2,1)}, bf16[2,1152,1024]{2,1,0:T(8,128)(2,1)}, f32[2,1152,1]{2,1,0:T(8,128)}) custom-call(bf16[2,1152,2048]{2,1,0:T(8,128)(2,1)} %get-tuple-element.84.x_ref.a_ref, f32[2,1152,1024]{2,1,0:T(8,128)} %gate_product.1.pre_ref, ...), custom_call_target="tpu_custom_call" | custom-call | tf_op jit(solution)/shard_map/active/pallas_call | solution.py:1676
  366.8 15.7 %down_grad.1 = bf16[2,1024,2048]{2,1,0:T(8,128)(2,1)} custom-call(bf16[2,1152,1024]{2,1,0:T(8,128)(2,1)} %get-tuple-element.92.gated_ref.a_ref, bf16[2,1152,2048]{2,1,0:T(8,128)(2,1)} %get-tuple-element.116.b_ref), custom_call_target="tpu_custom_call" | custom-call | tf_op jit(solution)/shard_map/down_grad/pallas_call | solution.py:1697
  382.6 16.1 %gate_grad.1 = bf16[2,2048,1024]{2,1,0:T(8,128)(2,1)} custom-call(bf16[2,1152,2048]{2,1,0:T(8,128)(2,1)} %get-tuple-element.84.x_ref.a_ref, bf16[2,1152,1024]{2,1,0:T(8,128)(2,1)} %get-tuple-element.87.a_ref.b_ref), custom_call_target="tpu_custom_call" | custom-call | tf_op jit(solution)/shard_map/gate_grad/pallas_call | solution.py:1697
  398.8 0.8 copy-done.3
  399.5 0.7 pad_maximum_fusion.1.router
  400.2 2.8 fusion.1.turned
  403.0 26.7 %rows_back.1.rows_ref = bf16[2,1152,2048]{2,1,0:T(8,128)(2,1)} custom-call(bf16[2,1152,1024]{2,1,0:T(8,128)(2,1)} %get-tuple-element.87.a_ref.b_ref, bf16[2,1152,1024]{2,1,0:T(8,128)(2,1)} %get-tuple-element.88.b_ref.gu_ref, bf16[2,2048,1024]{2,1,0:T(8,128)(2,1)} %all-gather.6.cloned.1.call-done.w_ref.g_ref, ...), custom_call_target="tpu_custom_call" | custom-call | tf_op jit(solution)/shard_map/rows_back/pallas_call | solution.py:1720
  429.9 1.2 fusion.6.dots
  431.1 16.6 %combine.1 = (bf16[8,256,2048]{2,1,0:T(8,128)(2,1)}, f32[32,2048]{1,0:T(8,128)}) custom-call(bf16[8,2,256,144]{3,2,1,0:T(8,128)(2,1)} %fusion.1.turned, bf16[2,1152,2048]{2,1,0:T(8,128)(2,1)} %rows_back.1.rows_ref, bf16[8,256,2048]{2,1,0:T(8,128)(2,1)} %get-tuple-element.83.rows_in.tokens, f32[8,256,16]{2,1,0:T(8,128)} %get-tuple-element.89.probs, ...), custom_call_target="tpu_custom_call" | custom-call | tf_op jit(solution)/shard_map/combine/pallas_call | solution.py:1755
  447.7 86.1 %token_back.1 = (f32[256,2048]{1,0:T(8,128)}, bf16[256,2048]{1,0:T(8,128)(2,1)}, f32[8,2048]{1,0:T(8,128)}, bf16[8,256,2048]{2,1,0:T(8,128)(2,1)}, bf16[2,2048,1024]{2,1,0:T(8,128)(2,1)}) custom-call(bf16[8,256,2048]{2,1,0:T(8,128)(2,1)} %get-tuple-element.91.p_ref, bf16[2,1152,1024]{2,1,0:T(8,128)(2,1)} %get-tuple-element.92.gated_ref.a_ref, ...), custom_call_target="tpu_custom_call" | custom-call | tf_op jit(solution)/shard_map/token_back/pallas_call | solution.py:999
  533.8 0.9 copy-done.4
  534.7 0.3 copy.81
  535.1 1.0 reshape.115.router_ref
  536.0 93.8 %branch_back.1 = (bf16[1024,2048]{1,0:T(8,128)(2,1)}, f32[256,2048]{1,0:T(8,128)}, f32[1024,512]{1,0:T(8,128)}, f32[1024,512]{1,0:T(8,128)}, bf16[1024,512]{1,0:...) custom-call(bf16[256,2048]{1,0:T(8,128)(2,1)} %get-tuple-element.93.x_ref, ...), custom_call_target="tpu_custom_call" | custom-call | tf_op jit(solution)/shard_map/branch_back/pallas_call | solution.py:1476
  629.9 19.7 %weight_parts.1 = (bf16[8,1024,512]{2,1,0:T(8,128)(2,1)}, bf16[1024,1536]{1,0:T(8,128)(2,1)}) custom-call(f32[1024,512]{1,0:T(8,128)} %get-tuple-element.99.q_scaled, f32[1024,512]{1,0:T(8,128)} %get-tuple-element.100.k_scaled, f32[1024,512]{1,0:T(8,128)} %get-tuple-element.72.q_raw, f32[1024,512]{1,0:T(8,128)} %get-tuple-element.73.k_raw, ...), custom_call_target="tpu_custom_call" | custom-call | tf_op jit(solution)/shard_map/weight_parts/pallas_call | solution.py:1541
  649.5 0.6 bitcast_dynamic-update-slice_fusion
  650.1 101.4 %end_exchange.1 = (f32[256,2048]{1,0:T(8,128)}, bf16[4,64,512]{2,1,0:T(8,128)(2,1)}, bf16[4,64,512]{2,1,0:T(8,128)(2,1)}, bf16[4,64,512]{2,1,0:T(8,128)(2,1)}, b...) custom-call(bf16[8,1024,512]{2,1,0:T(8,128)(2,1)} %get-tuple-element.105.p_ref, ...), custom_call_target="tpu_custom_call" | custom-call | tf_op jit(solution)/shard_map/end_exchange/pallas_call | solution.py:1212
  751.5 0.7 slice.31
  752.2 0.7 slice.30
  753.0 0.7 copy.82
  753.6 0.6 constant_dynamic-slice_fusion
  754.3 9.9 %widen.1 = (f32[64,2048]{1,0:T(8,128)}, f32[64,2048]{1,0:T(8,128)}, f32[64,2048]{1,0:T(8,128)}, f32[64,2048]{1,0:T(8,128)}, f32[1024,1024]{1,0:T(8,128)}, /*inde...) custom-call(f32[256,2048]{1,0:T(8,128)} %get-tuple-element.78.mid_ref.mid, ...), custom_call_target="tpu_custom_call" | custom-call | tf_op jit(solution)/shard_map/widen/pallas_call | solution.py:1803
  764.2 1.3 copy.93
  (57 shorter events, 1.6 us)
Async XLA Ops:
  7.2 224.5 %all-gather.4.cloned.1.call-start = ((), (), s32[]{:S(2)}) async-start(), calls=%async_computation.3 | async-start | bytes 10485760 | tf_op jit(solution)/shard_map/all_gather | solution.py:1842
  7.9 1.6 copy-start.9
  7.9 2.5 copy-start
  7.9 3.1 copy-start.10
  7.9 3.3 copy-start.12
  8.0 4.0 copy-start.5
  8.0 4.0 copy-start.6
  8.0 4.0 copy-start.7
  8.0 309.3 %all-gather.6.cloned.1.call-start = ((), (), s32[]{:S(2)}) async-start(), calls=%async_computation.4 | async-start | bytes 10485760 | tf_op jit(solution)/shard_map/all_gather | solution.py:1843
  8.7 333.7 %all-gather.8.cloned.1.call-start = ((), (), s32[]{:S(2)}) async-start(), calls=%async_computation.5 | async-start | bytes 10485760 | tf_op jit(solution)/shard_map/all_gather | solution.py:1844
  9.5 744.8 %reduce-scatter.8.cloned.1.call-start = ((), (), s32[]{:S(2)}) async-start(), calls=%async_computation.8 | async-start | bytes 10485760 | tf_op jit(solution)/shard_map/reduce_scatter | solution.py:1906
  111.6 3.5 copy-start.8
  382.5 371.8 %reduce-scatter.4.cloned.1.call-start = ((), (), s32[]{:S(2)}) async-start(), calls=%async_computation.6 | async-start | bytes 10485760 | tf_op jit(solution)/shard_map/reduce_scatter | solution.py:1906
  398.7 0.8 copy-start.3
  398.7 355.6 %reduce-scatter.6.cloned.1.call-start = ((), (), s32[]{:S(2)}) async-start(), calls=%async_computation.7 | async-start | bytes 10485760 | tf_op jit(solution)/shard_map/reduce_scatter | solution.py:1906
  403.0 26.7 %copy-start.2 = (f32[2,1152,1]{2,1,0:T(8,128)S(1)}, f32[2,1152,1]{2,1,0:T(8,128)}, u32[]{:S(2)}) copy-start(f32[2,1152,1]{2,1,0:T(8,128)} %get-tuple-element.90) | copy-start | bytes 27652
  533.7 1.0 copy-start.4
  629.8 19.7 %copy-start.11 = (f32[2,512]{1,0:T(2,128)S(1)}, f32[2,512]{1,0:T(2,128)}, u32[]{:S(2)}) copy-start(f32[2,512]{1,0:T(2,128)} %get-tuple-element.109) | copy-start | bytes 12292
  754.3 9.9 %copy-start.1 = (f32[256,2048]{1,0:T(8,128)S(1)}, f32[256,2048]{1,0:T(8,128)}, u32[]{:S(2)}) copy-start(f32[256,2048]{1,0:T(8,128)} %get-tuple-element.196) | copy-start | bytes 6291460
Sparse Core Ops, SparseCore 0:
  9.9 129.0 all-gather.3
  140.8 111.5 all-gather.5
  254.3 88.1 all-gather.7
  382.6 86.3 reduce-scatter.7
  472.2 100.3 reduce-scatter.3
  575.6 96.4 reduce-scatter.5

commit v6 on v5

--- a/solution.py
+++ b/solution.py
@@ -760,8 +760,8 @@
 
 
 def token_kernel(
-    fsdp, x_ref, g_first, g_second, picks, w_ref, out_ref, taken_ref, back_ref,
-    g_buf, w_buf, taken, back, send, recv, local, loads, stores, back_sem,
+    fsdp, sp, x_ref, g_first, g_second, picks, w_ref, up_ref, out_ref, taken_ref, back_ref, up_all,
+    g_buf, w_buf, taken, back, send, recv, local, loads, stores, back_sem, usend, urecv, ulocal,
 ):
     f, s = lax.axis_index("fsdp"), lax.axis_index("sp")
     lines = fsdp // 2
@@ -771,7 +771,10 @@
     slots = picks.shape[1] // EXP_DEV
     ff = w_ref.shape[1]
     barrier = pltpu.get_barrier_semaphore()
-    expected = greet_line(barrier, lines, f, s)
+    expected = greet_line(barrier, lines, f, s) + greet_plane(barrier, f, s, sp)
+    plane = plane_gather_of(up_ref, up_all, f, s, sp, usend, urecv)
+    up_own = pltpu.make_async_copy(up_ref, plane.at(s, 0, up_ref.shape[0]), ulocal)
+    up_own.start()
     own = pltpu.make_async_copy(x_ref, out_ref.at[f], local)
     own.start()
     reads = [
@@ -790,6 +793,7 @@
     line = LineGather([view(p) for p in range(parts)], owns, lines, f, s, send, recv)
     for p in range(parts):
         line.start_own(p)
+    plane.start()
 
     def take_all():
         reads[0].wait()
@@ -828,10 +832,14 @@
             work[k - 1]()
         for p in range(parts):
             line.forward(p, k)
+        if k == min(2, lines - 1):
+            plane.forward()
     for unit in work[lines - 1 :]:
         unit()
     for p in range(parts):
         line.finish(p)
+    plane.finish()
+    up_own.wait()
     own.wait()
     for slot in range(2):
         back_copy(0, slot, slot).wait()
@@ -839,20 +847,21 @@
         pltpu.make_async_copy(taken.at[e], taken_ref.at[e], stores.at[e]).wait()
 
 
-def token_gather(fsdp, x, g_first, g_second, picks, w_down):
+def token_gather(fsdp, sp, x, g_first, g_second, picks, w_down, up):
     slots = picks.shape[1] // EXP_DEV
     total = fsdp * slots
     ff = w_down.shape[1]
     dma = pltpu.SemaphoreType.DMA
     return pl.pallas_call(
-        functools.partial(token_kernel, fsdp),
+        functools.partial(token_kernel, fsdp, sp),
         out_shape=(
             jax.ShapeDtypeStruct((fsdp, TOK_DEV, D), BF16),
             jax.ShapeDtypeStruct((EXP_DEV, total, D), BF16),
             jax.ShapeDtypeStruct((EXP_DEV, total, ff), F32),
+            jax.ShapeDtypeStruct((sp * up.shape[0], up.shape[1]), BF16),
         ),
-        in_specs=[VMEM, ANY, ANY, VMEM, ANY],
-        out_specs=[ANY, ANY, ANY],
+        in_specs=[VMEM, ANY, ANY, VMEM, ANY, VMEM],
+        out_specs=[ANY, ANY, ANY, ANY],
         scratch_shapes=[
             pltpu.VMEM((fsdp, TOK_DEV, D), BF16),
             pltpu.VMEM((EXP_DEV, ff, D), BF16),
@@ -860,10 +869,10 @@
             pltpu.VMEM((2, total, FT), F32),
         ]
         + line_sems(2, fsdp)
-        + [dma, dma((3,)), dma((EXP_DEV,)), dma((2,))],
+        + [dma, dma((3,)), dma((EXP_DEV,)), dma((2,)), dma((sp,)), dma((sp,)), dma],
         compiler_params=comm_params(3),
         name="token_gather",
-    )(x, g_first, g_second, picks, w_down)
+    )(x, g_first, g_second, picks, w_down, up)
 
 
 def token_back_kernel(
@@ -1620,39 +1629,13 @@
 FT = 256
 
 
-def gate_kernel(x_ref, w_ref, out):
-    out[0] = dot_nn(x_ref[0], w_ref[0])
-
-
-def gate_product(x, w_gate):
-    _, total, _ = x.shape
-    ff = w_gate.shape[2]
-    wide = 2 * FT
-    return pl.pallas_call(
-        gate_kernel,
-        grid=(EXP_DEV, ff // wide),
-        out_shape=jax.ShapeDtypeStruct((EXP_DEV, total, ff), F32),
-        in_specs=[
-            pl.BlockSpec((1, total, D), lambda e, j: (e, 0, 0)),
-            pl.BlockSpec((1, D, wide), lambda e, j: (e, 0, j)),
-        ],
-        out_specs=pl.BlockSpec((1, total, wide), lambda e, j: (e, 0, j)),
-        compiler_params=pltpu.CompilerParams(vmem_limit_bytes=VLIM),
-        name="gate_product",
-    )(x, w_gate)
-
-
-def active_kernel(x_ref, pre_ref, w_ref, u_ref, gates, gated, grad_gate, grad_up, dots):
-    @pl.when(pl.program_id(1) == 0)
-    def _():
-        dots[...] = jnp.zeros_like(dots)
-
+def active_tile(x_ref, g_ref, up, u_ref, gates, gated, grad_gate, grad_up, dots):
     total = x_ref.shape[1]
     chunk = total // 4
     for first in range(0, total, chunk):
         at = slice(first, first + chunk)
-        gate_pre = pre_ref[0, at, :]
-        up_pre = dot_nn(x_ref[0, at, :], w_ref[0])
+        gate_pre = dot_nn(x_ref[0, at, :], g_ref[0])
+        up_pre = dot_nn(x_ref[0, at, :], up)
         sig = jax.nn.sigmoid(gate_pre)
         silu = gate_pre * sig
         hidden = silu * up_pre
@@ -1665,25 +1648,42 @@
         grad_up[0, at, :] = (back * silu).astype(BF16)
 
 
-def active(x, gate_pre, w_up, u, gates):
+def active_kernel(x_ref, g_ref, first_ref, second_ref, u_ref, gates, gated, grad_gate, grad_up, dots):
+    rest = (u_ref, gates, gated, grad_gate, grad_up, dots)
+
+    @pl.when(pl.program_id(1) == 0)
+    def _():
+        dots[...] = jnp.zeros_like(dots)
+        active_tile(x_ref, g_ref, first_ref[0], *rest)
+
+    @pl.when(pl.program_id(1) == 1)
+    def _():
+        active_tile(x_ref, g_ref, second_ref[...].reshape(first_ref.shape[1:]), *rest)
+
+
+def active(x, w_gate, up_first, up_second, u, gates):
     _, total, _ = x.shape
-    ff = w_up.shape[2]
-    wide = 2 * FT
+    wide = up_first.shape[2]
+    sp, _, height, _ = up_second.shape
     tile = pl.BlockSpec((1, total, wide), lambda e, j: (e, 0, j))
-    weight = pl.BlockSpec((1, D, wide), lambda e, j: (e, 0, j))
     column = pl.BlockSpec((1, total, 1), lambda e, j: (e, 0, 0))
-    low = jax.ShapeDtypeStruct((EXP_DEV, total, ff), BF16)
+    low = jax.ShapeDtypeStruct((EXP_DEV, total, 2 * wide), BF16)
     return pl.pallas_call(
         active_kernel,
-        grid=(EXP_DEV, ff // wide),
+        grid=(EXP_DEV, 2),
         out_shape=(low, low, low, jax.ShapeDtypeStruct((EXP_DEV, total, 1), F32)),
         in_specs=[
-            pl.BlockSpec((1, total, D), lambda e, j: (e, 0, 0)), tile, weight, tile, column,
+            pl.BlockSpec((1, total, D), lambda e, j: (e, 0, 0)),
+            pl.BlockSpec((1, D, wide), lambda e, j: (e, 0, j)),
+            pl.BlockSpec((1, D, wide), lambda e, j: (e, 0, 0)),
+            pl.BlockSpec((sp, 1, height, wide), lambda e, j: (0, e, 0, 0)),
+            tile,
+            column,
         ],
         out_specs=[tile, tile, tile, column],
         compiler_params=pltpu.CompilerParams(vmem_limit_bytes=VLIM),
         name="active",
-    )(x, gate_pre, w_up, u, gates)
+    )(x, w_gate, up_first, up_second, u, gates)
 
 
 def weight_grad_kernel(a_ref, b_ref, out):
@@ -1708,24 +1708,34 @@
     )(a, b)
 
 
-def rows_back_kernel(a_ref, b_ref, g_ref, w_ref, out):
-    out[0] = (dot_nt(a_ref[0], g_ref[0]) + dot_nt(b_ref[0], w_ref[0])).astype(BF16)
-
-
-def rows_back(grad_gate_pre, grad_up_pre, w_gate, w_up):
+def rows_back_kernel(a_ref, b_ref, g_ref, first_ref, second_ref, out):
+    wide = first_ref.shape[2]
+    total = dot_nt(a_ref[0], g_ref[0]) + dot_nt(b_ref[0, :, :wide], first_ref[0])
+    second = second_ref[...].reshape(first_ref.shape[1:])
+    out[0] = (total + dot_nt(b_ref[0, :, wide:], second)).astype(BF16)
+
+
+def rows_back(grad_gate_pre, grad_up_pre, w_gate, up_first, up_second):
     _, total, ff = grad_up_pre.shape
     size = 512
+    wide = up_first.shape[2]
+    height = up_second.shape[2]
     row = pl.BlockSpec((1, total, ff), lambda e, j: (e, 0, 0))
-    weight = pl.BlockSpec((1, size, ff), lambda e, j: (e, j, 0))
     return pl.pallas_call(
         rows_back_kernel,
         grid=(EXP_DEV, D // size),
         out_shape=jax.ShapeDtypeStruct((EXP_DEV, total, D), BF16),
-        in_specs=[row, row, weight, weight],
+        in_specs=[
+            row,
+            row,
+            pl.BlockSpec((1, size, ff), lambda e, j: (e, j, 0)),
+            pl.BlockSpec((1, size, wide), lambda e, j: (e, j, 0)),
+            pl.BlockSpec((size // height, 1, height, wide), lambda e, j: (j, e, 0, 0)),
+        ],
         out_specs=pl.BlockSpec((1, total, size), lambda e, j: (e, 0, j)),
         compiler_params=pltpu.CompilerParams(vmem_limit_bytes=VLIM),
         name="rows_back",
-    )(grad_gate_pre, grad_up_pre, w_gate, w_up)
+    )(grad_gate_pre, grad_up_pre, w_gate, up_first, up_second)
 
 
 def combine_kernel(turned, rows_ref, tokens, probs, dots, router, columns, out, router_out):
@@ -1841,7 +1851,8 @@
 
     down_full = lax.all_gather(w_down, "sp", axis=1, tiled=True)
     gate_full = lax.all_gather(w_gate, "sp", axis=1, tiled=True)
-    up_full = lax.all_gather(w_up, "sp", axis=1, tiled=True)
+    wide = w_up.shape[2] // 2
+    up_first = lax.all_gather(w_up[:, :, :wide], "sp", axis=1, tiled=True)
 
     router_size = rows * experts
     misc = jnp.concatenate([w_router.reshape(router_size), norm_gains.reshape(4 * rows)])
@@ -1886,16 +1897,17 @@
         fsdp, attended, wo_s, output_grad[early:], layer_input, gains32
     )
 
-    tokens, grad_taken, unscaled = token_gather(
-        fsdp, second_in, grad_first_half, grad_second_half, picks, down_full
+    tokens, grad_taken, unscaled, up_second = token_gather(
+        fsdp, sp, second_in, grad_first_half, grad_second_half, picks, down_full,
+        w_up[:, :, wide:].reshape(-1, wide),
     )
+    up_second = up_second.reshape(sp, EXP_DEV, D // sp, wide)
     received, probs, slot_gates = route(picks, tokens, router_t, columns)
-    gate_pre = gate_product(received, gate_full)
     gated, grad_gate_pre, grad_up_pre, slot_dots = active(
-        received, gate_pre, up_full, unscaled, slot_gates
+        received, gate_full, up_first, up_second, unscaled, slot_gates
     )
     dots_two = jnp.pad(two_parts(slot_dots, 2), ((0, 0), (0, 0), (0, 126)))
-    grad_rows = rows_back(grad_gate_pre, grad_up_pre, gate_full, up_full)
+    grad_rows = rows_back(grad_gate_pre, grad_up_pre, gate_full, up_first, up_second)
     second_part, router_two = combine(
         turned, grad_rows, tokens, probs, dots_two, jnp.concatenate([router_t, router_t], axis=0),
         columns,

time: 782 us -> 775 us (level)
    all_gather x1, waiting for transfers between devices: 8.4 us -> 0.01 us  [body(): up_first = lax.all_gather(w_up[:, :, :wide], 'sp', axis=1, tiled=True)]
    pallas_call x3 -> x2, Pallas kernels: 112 us -> 110 us  [the longest x1 79.3 us: token_gather(): pl.pallas_call(functools.partial(token_kernel, fsdp, sp), out_shape=(jax....]
  transfers between devices with their start and end apart: 6 -> 6, of which waited for: 1 -> 1; matrix products, arithmetic and copies ran while one was open for 3% -> 3% of each run, Pallas kernels for 87% -> 86%
where the time goes in v6:
time: 775 us; the launch traced here: 765 us
  Pallas kernels  717 us (93%)
  local copies, waits for them, and re-layouts  17.5 us (2%)
  between operations  14.6 us (2%)
  other arithmetic  8.45 us (1%)
    pallas_call x1, Pallas kernels, end_exchange(): pl.pallas_call(functools.partial(end_kernel, fsdp, sp), out_shape=(jax.Sh...  101 us
    pallas_call x1, Pallas kernels, gather_start(): pl.pallas_call(functools.partial(start_kernel, fsdp, sp), out_shape=(jax....  100 us
    pallas_call x1, Pallas kernels, branch_back(): pl.pallas_call(functools.partial(branch_back_kernel, fsdp, sp), out_shape...  94.1 us
    pallas_call x1, Pallas kernels, token_back(): pl.pallas_call(functools.partial(token_back_kernel, fsdp), out_shape=(jax...  85.9 us
    pallas_call x1, Pallas kernels, token_gather(): pl.pallas_call(functools.partial(token_kernel, fsdp, sp), out_shape=(jax....  79.3 us
    pallas_call x1, Pallas kernels, branch_sum(): pl.pallas_call(functools.partial(branch_kernel, fsdp, sp), out_shape=(jax...  68.2 us
    pallas_call x2, Pallas kernels, weight_grad(): pl.pallas_call(weight_grad_kernel, grid=(EXP_DEV, height // size, width /...  32.1 us
    pallas_call x1, Pallas kernels, active(): pl.pallas_call(active_kernel, grid=(EXP_DEV, 2), out_shape=(low, low, low...  30.3 us
  transfers between devices with their start and end apart: 6, of which 1 were waited for; matrix products, arithmetic and copies ran while one was open for 3% of the time, Pallas kernels for 86%

profile of v6, /device:TPU:12, one launch (start us, length us, event | category | flops | bytes accessed | tf_op | source)
XLA Modules:
  0.0 765.0 jit_solution(1744221071021849718)
XLA Ops:
  7.2 0.7 all-gather.4.cloned.1.call-update
  8.0 0.8 copy-done.1
  8.8 1.5 fusion.14
  10.4 0.7 all-gather.6.cloned.1.call-update
  11.3 0.7 reshape.114.routes_ref
  12.0 0.7 slice.30.g_ref
  12.9 0.6 fusion.13.misc_ref
  13.6 1.0 pad_maximum_fusion.w_ref
  14.5 100.2 %gather_start.1 = (bf16[1024,2048]{1,0:T(8,128)(2,1)}, bf16[3,2048,512]{2,1,0:T(8,128)(2,1)}, bf16[512,2048]{1,0:T(8,128)(2,1)}, bf16[8,32,2048]{2,1,0:T(8,128)(...) custom-call(bf16[256,2048]{1,0:T(8,128)(2,1)} %x_ref.5, bf16[3,64,2048]{2,1,0:T(8,128)(2,1)} %pad_maximum_fusion.w_ref, ...), custom_call_target="tpu_custom_call" | custom-call | tf_op jit(solution)/shard_map/gather_start/pallas_call | solution.py:681
  114.8 1.0 copy.89
  115.9 0.7 reshape.130.gain
  116.6 1.0 slice.32.g_ref
  117.7 0.6 copy.90
  118.3 0.6 eq.63
  118.9 0.3 copy.75
  119.6 0.4 reshape.118
  120.0 0.8 copy.79
  120.8 20.9 %project.1 = (bf16[1024,2048]{1,0:T(8,128)(2,1)}, f32[1024,512]{1,0:T(8,128)}, f32[1024,512]{1,0:T(8,128)}, bf16[1024,512]{1,0:T(8,128)(2,1)}, f32[1024,128]{1,0:T(8,128)}) custom-call(bf16[1024,2048]{1,0:T(8,128)(2,1)} %get-tuple-element.70.x_ref, f32[4,2048]{1,0:T(4,128)} %reshape.130.gain, bf16[3,2048,512]{2,1,0:T(8,128)(2,1)} %get-tuple-element.72.w_ref), custom_call_target="tpu_custom_call" | custom-call | tf_op jit(solution)/shard_map/project/pallas_call | solution.py:1332
  141.7 16.0 %attend.1 = (bf16[1024,512]{1,0:T(8,128)(2,1)}, f32[1024,128]{1,0:T(8,128)}, bf16[1024,512]{1,0:T(8,128)(2,1)}, bf16[1024,512]{1,0:T(8,128)(2,1)}) custom-call(f32[1024,512]{1,0:T(8,128)} %get-tuple-element.73.q_raw, f32[1024,512]{1,0:T(8,128)} %get-tuple-element.74.k_raw, bf16[1024,512]{1,0:T(8,128)(2,1)} %get-tuple-element.75.v_ref, ...), custom_call_target="tpu_custom_call" | custom-call | tf_op jit(solution)/shard_map/attend/pallas_call | solution.py:1378
  157.7 68.2 %branch_sum.1 = (f32[256,2048]{1,0:T(8,128)}, bf16[256,2048]{1,0:T(8,128)(2,1)}, bf16[8,224,2048]{2,1,0:T(8,128)(2,1)}) custom-call(bf16[1024,512]{1,0:T(8,128)(2,1)} %get-tuple-element.77.a_ref.attended, bf16[512,2048]{1,0:T(8,128)(2,1)} %get-tuple-element.78.w_ref.wo_ref, bf16[224,2048]{1,0:T(8,128)(2,1)} %slice.32.g_ref, bf16[256,2048]{1,0:T(8,128)(2,1)} %x_ref.5, ...), custom_call_target="tpu_custom_call" | custom-call | tf_op jit(solution)/shard_map/branch_sum/pallas_call | solution.py:746
  225.9 1.4 fusion.3.picks
  227.3 0.6 compare_convert_fusion.columns
  228.0 79.3 %token_gather.1 = (bf16[8,256,2048]{2,1,0:T(8,128)(2,1)}, bf16[2,1152,2048]{2,1,0:T(8,128)(2,1)}, f32[2,1152,1024]{2,1,0:T(8,128)}, bf16[4096,512]{1,0:T(8,128)(2,1)}) custom-call(bf16[256,2048]{1,0:T(8,128)(2,1)} %get-tuple-element.81.x_ref, bf16[8,32,2048]{2,1,0:T(8,128)(2,1)} %get-tuple-element.82.g_first, ...), custom_call_target="tpu_custom_call" | custom-call | tf_op jit(solution)/shard_map/token_gather/pallas_call | solution.py:855
  307.2 15.0 %route.1 = (bf16[2,1152,2048]{2,1,0:T(8,128)(2,1)}, f32[8,256,16]{2,1,0:T(8,128)}, f32[2,1152,1]{2,1,0:T(8,128)}) custom-call(bf16[8,288,256]{2,1,0:T(8,128)(2,1)} %fusion.3.picks, bf16[8,256,2048]{2,1,0:T(8,128)(2,1)} %get-tuple-element.84.rows_in.tokens, bf16[16,2048]{1,0:T(8,128)(2,1)} %bitcast.47, f32[2,16]{1,0:T(2,128)} %compare_convert_fusion.columns), custom_call_target="tpu_custom_call" | custom-call | tf_op jit(solution)/shard_map/route/pallas_call | solution.py:1611
  322.2 6.1 all-gather.6.cloned.1.call-done.g_ref
  328.3 30.3 %active.1 = (bf16[2,1152,1024]{2,1,0:T(8,128)(2,1)}, bf16[2,1152,1024]{2,1,0:T(8,128)(2,1)}, bf16[2,1152,1024]{2,1,0:T(8,128)(2,1)}, f32[2,1152,1]{2,1,0:T(8,128)}) custom-call(bf16[2,1152,2048]{2,1,0:T(8,128)(2,1)} %get-tuple-element.85.x_ref.a_ref, bf16[2,2048,1024]{2,1,0:T(8,128)(2,1)} %all-gather.6.cloned.1.call-done.g_ref, ...), custom_call_target="tpu_custom_call" | custom-call | tf_op jit(solution)/shard_map/active/pallas_call | solution.py:1671
  358.7 15.6 %down_grad.1 = bf16[2,1024,2048]{2,1,0:T(8,128)(2,1)} custom-call(bf16[2,1152,1024]{2,1,0:T(8,128)(2,1)} %get-tuple-element.94.gated_ref.a_ref, bf16[2,1152,2048]{2,1,0:T(8,128)(2,1)} %get-tuple-element.118.b_ref), custom_call_target="tpu_custom_call" | custom-call | tf_op jit(solution)/shard_map/down_grad/pallas_call | solution.py:1697
  374.4 16.4 %gate_grad.1 = bf16[2,2048,1024]{2,1,0:T(8,128)(2,1)} custom-call(bf16[2,1152,2048]{2,1,0:T(8,128)(2,1)} %get-tuple-element.85.x_ref.a_ref, bf16[2,1152,1024]{2,1,0:T(8,128)(2,1)} %get-tuple-element.89.a_ref.b_ref), custom_call_target="tpu_custom_call" | custom-call | tf_op jit(solution)/shard_map/gate_grad/pallas_call | solution.py:1697
  390.9 0.8 copy-done.4
  391.7 0.7 pad_maximum_fusion.1.router
  392.4 2.6 fusion.1.turned
  395.0 26.8 %rows_back.1.rows_ref = bf16[2,1152,2048]{2,1,0:T(8,128)(2,1)} custom-call(bf16[2,1152,1024]{2,1,0:T(8,128)(2,1)} %get-tuple-element.89.a_ref.b_ref, bf16[2,1152,1024]{2,1,0:T(8,128)(2,1)} %get-tuple-element.90.b_ref.gu_ref, bf16[2,2048,1024]{2,1,0:T(8,128)(2,1)} %all-gather.6.cloned.1.call-done.g_ref, ...), custom_call_target="tpu_custom_call" | custom-call | tf_op jit(solution)/shard_map/rows_back/pallas_call | solution.py:1724
  421.9 1.2 fusion.6.dots
  423.1 16.8 %combine.1 = (bf16[8,256,2048]{2,1,0:T(8,128)(2,1)}, f32[32,2048]{1,0:T(8,128)}) custom-call(bf16[8,2,256,144]{3,2,1,0:T(8,128)(2,1)} %fusion.1.turned, bf16[2,1152,2048]{2,1,0:T(8,128)(2,1)} %rows_back.1.rows_ref, bf16[8,256,2048]{2,1,0:T(8,128)(2,1)} %get-tuple-element.84.rows_in.tokens, f32[8,256,16]{2,1,0:T(8,128)} %get-tuple-element.91.probs, ...), custom_call_target="tpu_custom_call" | custom-call | tf_op jit(solution)/shard_map/combine/pallas_call | solution.py:1765
  439.9 85.9 %token_back.1 = (f32[256,2048]{1,0:T(8,128)}, bf16[256,2048]{1,0:T(8,128)(2,1)}, f32[8,2048]{1,0:T(8,128)}, bf16[8,256,2048]{2,1,0:T(8,128)(2,1)}, bf16[2,2048,1024]{2,1,0:T(8,128)(2,1)}) custom-call(bf16[8,256,2048]{2,1,0:T(8,128)(2,1)} %get-tuple-element.93.p_ref, bf16[2,1152,1024]{2,1,0:T(8,128)(2,1)} %get-tuple-element.94.gated_ref.a_ref, ...), custom_call_target="tpu_custom_call" | custom-call | tf_op jit(solution)/shard_map/token_back/pallas_call | solution.py:1008
  525.9 0.9 copy-done.5
  526.8 0.3 copy.81
  527.2 1.0 reshape.123.router_ref
  528.1 94.1 %branch_back.1 = (bf16[1024,2048]{1,0:T(8,128)(2,1)}, f32[256,2048]{1,0:T(8,128)}, f32[1024,512]{1,0:T(8,128)}, f32[1024,512]{1,0:T(8,128)}, bf16[1024,512]{1,0:...) custom-call(bf16[256,2048]{1,0:T(8,128)(2,1)} %get-tuple-element.95.x_ref, ...), custom_call_target="tpu_custom_call" | custom-call | tf_op jit(solution)/shard_map/branch_back/pallas_call | solution.py:1485
  622.3 19.7 %weight_parts.1 = (bf16[8,1024,512]{2,1,0:T(8,128)(2,1)}, bf16[1024,1536]{1,0:T(8,128)(2,1)}) custom-call(f32[1024,512]{1,0:T(8,128)} %get-tuple-element.101.q_scaled, f32[1024,512]{1,0:T(8,128)} %get-tuple-element.102.k_scaled, f32[1024,512]{1,0:T(8,128)} %get-tuple-element.73.q_raw, f32[1024,512]{1,0:T(8,128)} %get-tuple-element.74.k_raw, ...), custom_call_target="tpu_custom_call" | custom-call | tf_op jit(solution)/shard_map/weight_parts/pallas_call | solution.py:1550
  641.9 0.6 bitcast_dynamic-update-slice_fusion
  642.5 101.4 %end_exchange.1 = (f32[256,2048]{1,0:T(8,128)}, bf16[4,64,512]{2,1,0:T(8,128)(2,1)}, bf16[4,64,512]{2,1,0:T(8,128)(2,1)}, bf16[4,64,512]{2,1,0:T(8,128)(2,1)}, b...) custom-call(bf16[8,1024,512]{2,1,0:T(8,128)(2,1)} %get-tuple-element.107.p_ref, ...), custom_call_target="tpu_custom_call" | custom-call | tf_op jit(solution)/shard_map/end_exchange/pallas_call | solution.py:1221
  744.0 0.7 slice.39
  744.7 0.7 slice.38
  745.4 0.7 copy.82
  746.1 0.6 constant_dynamic-slice_fusion
  746.7 9.9 %widen.1 = (f32[64,2048]{1,0:T(8,128)}, f32[64,2048]{1,0:T(8,128)}, f32[64,2048]{1,0:T(8,128)}, f32[64,2048]{1,0:T(8,128)}, f32[1024,1024]{1,0:T(8,128)}, /*inde...) custom-call(f32[256,2048]{1,0:T(8,128)} %get-tuple-element.79.mid_ref.mid, ...), custom_call_target="tpu_custom_call" | custom-call | tf_op jit(solution)/shard_map/widen/pallas_call | solution.py:1813
  756.6 1.3 copy.93
  (59 shorter events, 1.7 us)
Async XLA Ops:
  7.2 1.6 copy-start.1
  7.2 220.8 %all-gather.4.cloned.1.call-start = ((), (), s32[]{:S(2)}) async-start(), calls=%async_computation.3 | async-start | bytes 10485760 | tf_op jit(solution)/shard_map/all_gather | solution.py:1852
  7.9 314.3 %all-gather.8.cloned.1.call-start = ((), (), s32[]{:S(2)}) async-start(), calls=%async_computation.5 | async-start | bytes 5242880 | tf_op jit(solution)/shard_map/all_gather | solution.py:1855
  10.3 0.9 copy-start.10
  10.3 1.7 copy-start
  10.3 2.4 copy-start.11
  10.3 2.6 copy-start.13
  10.3 3.3 copy-start.6
  10.3 3.3 copy-start.7
  10.3 3.2 copy-start.8
  10.4 318.0 %all-gather.6.cloned.1.call-start = ((), (), s32[]{:S(2)}) async-start(), calls=%async_computation.4 | async-start | bytes 10485760 | tf_op jit(solution)/shard_map/all_gather | solution.py:1853
  11.1 735.6 %reduce-scatter.8.cloned.1.call-start = ((), (), s32[]{:S(2)}) async-start(), calls=%async_computation.8 | async-start | bytes 10485760 | tf_op jit(solution)/shard_map/reduce_scatter | solution.py:1918
  114.7 3.5 copy-start.9
  374.4 372.4 %reduce-scatter.4.cloned.1.call-start = ((), (), s32[]{:S(2)}) async-start(), calls=%async_computation.6 | async-start | bytes 10485760 | tf_op jit(solution)/shard_map/reduce_scatter | solution.py:1918
  390.9 0.8 copy-start.4
  390.9 355.9 %reduce-scatter.6.cloned.1.call-start = ((), (), s32[]{:S(2)}) async-start(), calls=%async_computation.7 | async-start | bytes 10485760 | tf_op jit(solution)/shard_map/reduce_scatter | solution.py:1918
  395.0 26.8 %copy-start.3 = (f32[2,1152,1]{2,1,0:T(8,128)S(1)}, f32[2,1152,1]{2,1,0:T(8,128)}, u32[]{:S(2)}) copy-start(f32[2,1152,1]{2,1,0:T(8,128)} %get-tuple-element.92) | copy-start | bytes 27652
  525.8 1.0 copy-start.5
  622.3 19.7 %copy-start.12 = (f32[2,512]{1,0:T(2,128)S(1)}, f32[2,512]{1,0:T(2,128)}, u32[]{:S(2)}) copy-start(f32[2,512]{1,0:T(2,128)} %get-tuple-element.111) | copy-start | bytes 12292
  746.7 9.9 %copy-start.2 = (f32[256,2048]{1,0:T(8,128)S(1)}, f32[256,2048]{1,0:T(8,128)}, u32[]{:S(2)}) copy-start(f32[256,2048]{1,0:T(8,128)} %get-tuple-element.200) | copy-start | bytes 6291460
Sparse Core Ops, SparseCore 0:
  9.9 130.6 all-gather.3
  143.0 70.5 all-gather.7
  215.4 112.8 all-gather.5
  374.5 86.7 reduce-scatter.7
  464.5 100.3 reduce-scatter.3
  567.8 96.6 reduce-scatter.5

commit v7 on v6

--- a/solution.py
+++ b/solution.py
@@ -191,7 +191,7 @@
             pltpu.VMEM((lines,) + block, BF16),
             pltpu.VMEM((lines,) + block, BF16),
             pltpu.VMEM(block, BF16),
-            dma((lines,)), dma((lines,)), dma((lines,)), dma((lines,)), dma, dma((lines,)),
+            dma((lines,)), dma((lines,)), dma((lines, 2)), dma((lines, 2)), dma((2,)), dma((lines,)),
         ]
 
     def load(self, i):
@@ -203,15 +203,23 @@
             self.precv.at[i], (self.f + 1 - 2 * self.core, self.s),
         )
 
-    def right(self, d, last):
+    def half(self, ref, h):
+        return ref.at[pl.ds(h * (self.rows // 2), self.rows // 2), :]
+
+    def right(self, d, last, h):
         dst = self.last if last else self.got.at[d]
-        sem = self.final if last else self.recv.at[d]
-        return remote(self.own.at[d], dst, self.send.at[d], sem, (self.f + 2, self.s))
-
-    def left(self, d):
-        return remote(
-            self.own.at[d], self.got.at[d], self.send.at[d], self.recv.at[d], (self.f - 2, self.s)
-        )
+        sem = self.final.at[h] if last else self.recv.at[d, h]
+        own = self.half(self.own.at[d], h)
+        return remote(own, self.half(dst, h), self.send.at[d, h], sem, (self.f + 2, self.s))
+
+    def left(self, d, h):
+        own, dst = self.half(self.own.at[d], h), self.half(self.got.at[d], h)
+        return remote(own, dst, self.send.at[d, h], self.recv.at[d, h], (self.f - 2, self.s))
+
+    def add_got(self, d, h):
+        own, got = self.half(self.own.at[d], h), self.half(self.got.at[d], h)
+        landed(got, self.recv.at[d, h])
+        add_rows(own, own, got, self.rows // 2)
 
     def start(self):
         for i in self.order[:2]:
@@ -231,32 +239,30 @@
     def step(self, t):
         place, lines = self.place, self.lines
         d = lines - 1 - t + place
-
-        @pl.when(t >= place)
-        def _():
-            @pl.when(place > 0)
+        e = t - (lines - 1 - place)
+        for h in range(2):
+
+            @pl.when(t >= place)
             def _():
-                landed(self.got.at[d], self.recv.at[d])
-                add_rows(self.own.at[d], self.own.at[d], self.got.at[d], self.rows)
-
-            @pl.when(d == place + 1)
+                @pl.when(place > 0)
+                def _():
+                    self.add_got(d, h)
+
+                @pl.when(d == place + 1)
+                def _():
+                    self.right(d, True, h).start()
+
+                @pl.when(d != place + 1)
+                def _():
+                    self.right(d, False, h).start()
+
+            @pl.when(e >= 0)
             def _():
-                self.right(d, True).start()
-
-            @pl.when(d != place + 1)
-            def _():
-                self.right(d, False).start()
-
-        e = t - (lines - 1 - place)
-
-        @pl.when(e >= 0)
-        def _():
-            @pl.when(place < lines - 1)
-            def _():
-                landed(self.got.at[e], self.recv.at[e])
-                add_rows(self.own.at[e], self.own.at[e], self.got.at[e], self.rows)
-
-            self.left(e).start()
+                @pl.when(place < lines - 1)
+                def _():
+                    self.add_got(e, h)
+
+                self.left(e, h).start()
 
         if t == 0:
             for i in self.order[2:]:
@@ -279,11 +285,13 @@
 
         @pl.when(place > 0)
         def _():
-            landed(self.last, self.final)
+            for h in range(2):
+                landed(self.half(self.last, h), self.final.at[h])
 
         @pl.when(place < lines - 1)
         def _():
-            landed(self.got.at[place], self.recv.at[place])
+            for h in range(2):
+                landed(self.half(self.got.at[place], h), self.recv.at[place, h])
 
         @pl.when(place == 0)
         def _():
@@ -302,11 +310,13 @@
 
             @pl.when(place < i)
             def _():
-                self.right(i, False).wait_send()
+                for h in range(2):
+                    self.right(i, False, h).wait_send()
 
             @pl.when(place > i)
             def _():
-                self.left(i).wait_send()
+                for h in range(2):
+                    self.left(i, h).wait_send()
 
 
 class PlaneGather:

time: 775 us -> 767 us (0.990)
  Pallas kernels: 717 us -> 709 us
where the time goes in v7:
time: 767 us; the launch traced here: 758 us
  Pallas kernels  709 us (92%)
  local copies, waits for them, and re-layouts  17.4 us (2%)
  between operations  14.6 us (2%)
  other arithmetic  8.45 us (1%)
    pallas_call x1, Pallas kernels, gather_start(): pl.pallas_call(functools.partial(start_kernel, fsdp, sp), out_shape=(jax....  100 us
    pallas_call x1, Pallas kernels, end_exchange(): pl.pallas_call(functools.partial(end_kernel, fsdp, sp), out_shape=(jax.Sh...  96.5 us
    pallas_call x1, Pallas kernels, branch_back(): pl.pallas_call(functools.partial(branch_back_kernel, fsdp, sp), out_shape...  95.5 us
    pallas_call x1, Pallas kernels, token_back(): pl.pallas_call(functools.partial(token_back_kernel, fsdp), out_shape=(jax...  82.1 us
    pallas_call x1, Pallas kernels, token_gather(): pl.pallas_call(functools.partial(token_kernel, fsdp, sp), out_shape=(jax....  79.3 us
    pallas_call x1, Pallas kernels, branch_sum(): pl.pallas_call(functools.partial(branch_kernel, fsdp, sp), out_shape=(jax...  68.2 us
    pallas_call x2, Pallas kernels, weight_grad(): pl.pallas_call(weight_grad_kernel, grid=(EXP_DEV, height // size, width /...  32.1 us
    pallas_call x1, Pallas kernels, active(): pl.pallas_call(active_kernel, grid=(EXP_DEV, 2), out_shape=(low, low, low...  30.3 us
  transfers between devices with their start and end apart: 6, of which 1 were waited for; matrix products, arithmetic and copies ran while one was open for 3% of the time, Pallas kernels for 86%

profile of v7, /device:TPU:12, one launch (start us, length us, event | category | flops | bytes accessed | tf_op | source)
XLA Modules:
  0.0 757.6 jit_solution(6844296356281195417)
XLA Ops:
  7.2 0.7 all-gather.4.cloned.1.call-update
  8.0 0.8 copy-done.1
  8.8 1.5 fusion.14
  10.4 0.7 all-gather.6.cloned.1.call-update
  11.3 0.7 reshape.114.routes_ref
  12.0 0.7 slice.30.g_ref
  12.9 0.6 fusion.13.misc_ref
  13.6 1.0 pad_maximum_fusion.w_ref
  14.5 100.2 %gather_start.1 = (bf16[1024,2048]{1,0:T(8,128)(2,1)}, bf16[3,2048,512]{2,1,0:T(8,128)(2,1)}, bf16[512,2048]{1,0:T(8,128)(2,1)}, bf16[8,32,2048]{2,1,0:T(8,128)(...) custom-call(bf16[256,2048]{1,0:T(8,128)(2,1)} %x_ref.5, bf16[3,64,2048]{2,1,0:T(8,128)(2,1)} %pad_maximum_fusion.w_ref, ...), custom_call_target="tpu_custom_call" | custom-call | tf_op jit(solution)/shard_map/gather_start/pallas_call | solution.py:691
  114.8 1.0 copy.89
  115.9 0.7 reshape.130.gain
  116.6 1.0 slice.32.g_ref
  117.7 0.6 copy.90
  118.3 0.6 eq.63
  118.9 0.3 copy.75
  119.6 0.4 reshape.118
  120.0 0.8 copy.79
  120.8 20.9 %project.1 = (bf16[1024,2048]{1,0:T(8,128)(2,1)}, f32[1024,512]{1,0:T(8,128)}, f32[1024,512]{1,0:T(8,128)}, bf16[1024,512]{1,0:T(8,128)(2,1)}, f32[1024,128]{1,0:T(8,128)}) custom-call(bf16[1024,2048]{1,0:T(8,128)(2,1)} %get-tuple-element.70.x_ref, f32[4,2048]{1,0:T(4,128)} %reshape.130.gain, bf16[3,2048,512]{2,1,0:T(8,128)(2,1)} %get-tuple-element.72.w_ref), custom_call_target="tpu_custom_call" | custom-call | tf_op jit(solution)/shard_map/project/pallas_call | solution.py:1342
  141.7 16.0 %attend.1 = (bf16[1024,512]{1,0:T(8,128)(2,1)}, f32[1024,128]{1,0:T(8,128)}, bf16[1024,512]{1,0:T(8,128)(2,1)}, bf16[1024,512]{1,0:T(8,128)(2,1)}) custom-call(f32[1024,512]{1,0:T(8,128)} %get-tuple-element.73.q_raw, f32[1024,512]{1,0:T(8,128)} %get-tuple-element.74.k_raw, bf16[1024,512]{1,0:T(8,128)(2,1)} %get-tuple-element.75.v_ref, ...), custom_call_target="tpu_custom_call" | custom-call | tf_op jit(solution)/shard_map/attend/pallas_call | solution.py:1388
  157.7 68.2 %branch_sum.1 = (f32[256,2048]{1,0:T(8,128)}, bf16[256,2048]{1,0:T(8,128)(2,1)}, bf16[8,224,2048]{2,1,0:T(8,128)(2,1)}) custom-call(bf16[1024,512]{1,0:T(8,128)(2,1)} %get-tuple-element.77.a_ref.attended, bf16[512,2048]{1,0:T(8,128)(2,1)} %get-tuple-element.78.w_ref.wo_ref, bf16[224,2048]{1,0:T(8,128)(2,1)} %slice.32.g_ref, bf16[256,2048]{1,0:T(8,128)(2,1)} %x_ref.5, ...), custom_call_target="tpu_custom_call" | custom-call | tf_op jit(solution)/shard_map/branch_sum/pallas_call | solution.py:756
  225.9 1.4 fusion.3.picks
  227.3 0.6 compare_convert_fusion.columns
  228.0 79.3 %token_gather.1 = (bf16[8,256,2048]{2,1,0:T(8,128)(2,1)}, bf16[2,1152,2048]{2,1,0:T(8,128)(2,1)}, f32[2,1152,1024]{2,1,0:T(8,128)}, bf16[4096,512]{1,0:T(8,128)(2,1)}) custom-call(bf16[256,2048]{1,0:T(8,128)(2,1)} %get-tuple-element.81.x_ref, bf16[8,32,2048]{2,1,0:T(8,128)(2,1)} %get-tuple-element.82.g_first, ...), custom_call_target="tpu_custom_call" | custom-call | tf_op jit(solution)/shard_map/token_gather/pallas_call | solution.py:865
  307.2 15.0 %route.1 = (bf16[2,1152,2048]{2,1,0:T(8,128)(2,1)}, f32[8,256,16]{2,1,0:T(8,128)}, f32[2,1152,1]{2,1,0:T(8,128)}) custom-call(bf16[8,288,256]{2,1,0:T(8,128)(2,1)} %fusion.3.picks, bf16[8,256,2048]{2,1,0:T(8,128)(2,1)} %get-tuple-element.84.rows_in.tokens, bf16[16,2048]{1,0:T(8,128)(2,1)} %bitcast.47, f32[2,16]{1,0:T(2,128)} %compare_convert_fusion.columns), custom_call_target="tpu_custom_call" | custom-call | tf_op jit(solution)/shard_map/route/pallas_call | solution.py:1621
  322.2 6.1 all-gather.6.cloned.1.call-done.g_ref
  328.3 30.3 %active.1 = (bf16[2,1152,1024]{2,1,0:T(8,128)(2,1)}, bf16[2,1152,1024]{2,1,0:T(8,128)(2,1)}, bf16[2,1152,1024]{2,1,0:T(8,128)(2,1)}, f32[2,1152,1]{2,1,0:T(8,128)}) custom-call(bf16[2,1152,2048]{2,1,0:T(8,128)(2,1)} %get-tuple-element.85.x_ref.a_ref, bf16[2,2048,1024]{2,1,0:T(8,128)(2,1)} %all-gather.6.cloned.1.call-done.g_ref, ...), custom_call_target="tpu_custom_call" | custom-call | tf_op jit(solution)/shard_map/active/pallas_call | solution.py:1681
  358.7 15.6 %down_grad.1 = bf16[2,1024,2048]{2,1,0:T(8,128)(2,1)} custom-call(bf16[2,1152,1024]{2,1,0:T(8,128)(2,1)} %get-tuple-element.94.gated_ref.a_ref, bf16[2,1152,2048]{2,1,0:T(8,128)(2,1)} %get-tuple-element.118.b_ref), custom_call_target="tpu_custom_call" | custom-call | tf_op jit(solution)/shard_map/down_grad/pallas_call | solution.py:1707
  374.4 16.4 %gate_grad.1 = bf16[2,2048,1024]{2,1,0:T(8,128)(2,1)} custom-call(bf16[2,1152,2048]{2,1,0:T(8,128)(2,1)} %get-tuple-element.85.x_ref.a_ref, bf16[2,1152,1024]{2,1,0:T(8,128)(2,1)} %get-tuple-element.89.a_ref.b_ref), custom_call_target="tpu_custom_call" | custom-call | tf_op jit(solution)/shard_map/gate_grad/pallas_call | solution.py:1707
  390.9 0.8 copy-done.4
  391.7 0.7 pad_maximum_fusion.1.router
  392.4 2.6 fusion.1.turned
  395.0 26.8 %rows_back.1.rows_ref = bf16[2,1152,2048]{2,1,0:T(8,128)(2,1)} custom-call(bf16[2,1152,1024]{2,1,0:T(8,128)(2,1)} %get-tuple-element.89.a_ref.b_ref, bf16[2,1152,1024]{2,1,0:T(8,128)(2,1)} %get-tuple-element.90.b_ref.gu_ref, bf16[2,2048,1024]{2,1,0:T(8,128)(2,1)} %all-gather.6.cloned.1.call-done.g_ref, ...), custom_call_target="tpu_custom_call" | custom-call | tf_op jit(solution)/shard_map/rows_back/pallas_call | solution.py:1734
  421.9 1.2 fusion.6.dots
  423.1 16.8 %combine.1 = (bf16[8,256,2048]{2,1,0:T(8,128)(2,1)}, f32[32,2048]{1,0:T(8,128)}) custom-call(bf16[8,2,256,144]{3,2,1,0:T(8,128)(2,1)} %fusion.1.turned, bf16[2,1152,2048]{2,1,0:T(8,128)(2,1)} %rows_back.1.rows_ref, bf16[8,256,2048]{2,1,0:T(8,128)(2,1)} %get-tuple-element.84.rows_in.tokens, f32[8,256,16]{2,1,0:T(8,128)} %get-tuple-element.91.probs, ...), custom_call_target="tpu_custom_call" | custom-call | tf_op jit(solution)/shard_map/combine/pallas_call | solution.py:1775
  439.9 82.1 %token_back.1 = (f32[256,2048]{1,0:T(8,128)}, bf16[256,2048]{1,0:T(8,128)(2,1)}, f32[8,2048]{1,0:T(8,128)}, bf16[8,256,2048]{2,1,0:T(8,128)(2,1)}, bf16[2,2048,1024]{2,1,0:T(8,128)(2,1)}) custom-call(bf16[8,256,2048]{2,1,0:T(8,128)(2,1)} %get-tuple-element.93.p_ref, bf16[2,1152,1024]{2,1,0:T(8,128)(2,1)} %get-tuple-element.94.gated_ref.a_ref, ...), custom_call_target="tpu_custom_call" | custom-call | tf_op jit(solution)/shard_map/token_back/pallas_call | solution.py:1018
  522.1 0.9 copy-done.5
  523.0 0.3 copy.81
  523.3 1.0 reshape.123.router_ref
  524.3 95.5 %branch_back.1 = (bf16[1024,2048]{1,0:T(8,128)(2,1)}, f32[256,2048]{1,0:T(8,128)}, f32[1024,512]{1,0:T(8,128)}, f32[1024,512]{1,0:T(8,128)}, bf16[1024,512]{1,0:...) custom-call(bf16[256,2048]{1,0:T(8,128)(2,1)} %get-tuple-element.95.x_ref, ...), custom_call_target="tpu_custom_call" | custom-call | tf_op jit(solution)/shard_map/branch_back/pallas_call | solution.py:1495
  619.8 19.8 %weight_parts.1 = (bf16[8,1024,512]{2,1,0:T(8,128)(2,1)}, bf16[1024,1536]{1,0:T(8,128)(2,1)}) custom-call(f32[1024,512]{1,0:T(8,128)} %get-tuple-element.101.q_scaled, f32[1024,512]{1,0:T(8,128)} %get-tuple-element.102.k_scaled, f32[1024,512]{1,0:T(8,128)} %get-tuple-element.73.q_raw, f32[1024,512]{1,0:T(8,128)} %get-tuple-element.74.k_raw, ...), custom_call_target="tpu_custom_call" | custom-call | tf_op jit(solution)/shard_map/weight_parts/pallas_call | solution.py:1560
  639.6 0.6 bitcast_dynamic-update-slice_fusion
  640.1 96.5 %end_exchange.1 = (f32[256,2048]{1,0:T(8,128)}, bf16[4,64,512]{2,1,0:T(8,128)(2,1)}, bf16[4,64,512]{2,1,0:T(8,128)(2,1)}, bf16[4,64,512]{2,1,0:T(8,128)(2,1)}, b...) custom-call(bf16[8,1024,512]{2,1,0:T(8,128)(2,1)} %get-tuple-element.107.p_ref, ...), custom_call_target="tpu_custom_call" | custom-call | tf_op jit(solution)/shard_map/end_exchange/pallas_call | solution.py:1231
  736.6 0.7 slice.39
  737.3 0.7 slice.38
  738.1 0.7 copy.82
  738.7 0.6 constant_dynamic-slice_fusion
  739.4 9.9 %widen.1 = (f32[64,2048]{1,0:T(8,128)}, f32[64,2048]{1,0:T(8,128)}, f32[64,2048]{1,0:T(8,128)}, f32[64,2048]{1,0:T(8,128)}, f32[1024,1024]{1,0:T(8,128)}, /*inde...) custom-call(f32[256,2048]{1,0:T(8,128)} %get-tuple-element.79.mid_ref.mid, ...), custom_call_target="tpu_custom_call" | custom-call | tf_op jit(solution)/shard_map/widen/pallas_call | solution.py:1823
  749.3 1.3 copy.93
  (59 shorter events, 1.7 us)
Async XLA Ops:
  7.2 1.6 copy-start.1
  7.2 220.8 %all-gather.4.cloned.1.call-start = ((), (), s32[]{:S(2)}) async-start(), calls=%async_computation.3 | async-start | bytes 10485760 | tf_op jit(solution)/shard_map/all_gather | solution.py:1862
  7.9 314.3 %all-gather.8.cloned.1.call-start = ((), (), s32[]{:S(2)}) async-start(), calls=%async_computation.5 | async-start | bytes 5242880 | tf_op jit(solution)/shard_map/all_gather | solution.py:1865
  10.3 0.9 copy-start.10
  10.3 1.7 copy-start
  10.3 2.4 copy-start.11
  10.3 2.6 copy-start.13
  10.3 3.3 copy-start.6
  10.3 3.3 copy-start.7
  10.3 3.2 copy-start.8
  10.4 318.0 %all-gather.6.cloned.1.call-start = ((), (), s32[]{:S(2)}) async-start(), calls=%async_computation.4 | async-start | bytes 10485760 | tf_op jit(solution)/shard_map/all_gather | solution.py:1863
  11.1 728.3 %reduce-scatter.8.cloned.1.call-start = ((), (), s32[]{:S(2)}) async-start(), calls=%async_computation.8 | async-start | bytes 10485760 | tf_op jit(solution)/shard_map/reduce_scatter | solution.py:1928
  114.7 3.5 copy-start.9
  374.4 365.0 %reduce-scatter.4.cloned.1.call-start = ((), (), s32[]{:S(2)}) async-start(), calls=%async_computation.6 | async-start | bytes 10485760 | tf_op jit(solution)/shard_map/reduce_scatter | solution.py:1928
  390.9 0.8 copy-start.4
  390.9 348.5 %reduce-scatter.6.cloned.1.call-start = ((), (), s32[]{:S(2)}) async-start(), calls=%async_computation.7 | async-start | bytes 10485760 | tf_op jit(solution)/shard_map/reduce_scatter | solution.py:1928
  395.0 26.8 %copy-start.3 = (f32[2,1152,1]{2,1,0:T(8,128)S(1)}, f32[2,1152,1]{2,1,0:T(8,128)}, u32[]{:S(2)}) copy-start(f32[2,1152,1]{2,1,0:T(8,128)} %get-tuple-element.92) | copy-start | bytes 27652
  522.0 1.0 copy-start.5
  619.8 19.8 %copy-start.12 = (f32[2,512]{1,0:T(2,128)S(1)}, f32[2,512]{1,0:T(2,128)}, u32[]{:S(2)}) copy-start(f32[2,512]{1,0:T(2,128)} %get-tuple-element.111) | copy-start | bytes 12292
  739.4 9.9 %copy-start.2 = (f32[256,2048]{1,0:T(8,128)S(1)}, f32[256,2048]{1,0:T(8,128)}, u32[]{:S(2)}) copy-start(f32[256,2048]{1,0:T(8,128)} %get-tuple-element.200) | copy-start | bytes 6291460
Sparse Core Ops, SparseCore 0:
  9.9 130.6 all-gather.3
  143.0 70.5 all-gather.7
  215.4 112.8 all-gather.5
  374.5 86.7 reduce-scatter.7
  464.5 103.3 reduce-scatter.3
  570.8 93.4 reduce-scatter.5

commit v8 on v7

--- a/solution.py
+++ b/solution.py
@@ -191,7 +191,7 @@
             pltpu.VMEM((lines,) + block, BF16),
             pltpu.VMEM((lines,) + block, BF16),
             pltpu.VMEM(block, BF16),
-            dma((lines,)), dma((lines,)), dma((lines, 2)), dma((lines, 2)), dma((2,)), dma((lines,)),
+            dma((lines,)), dma((lines,)), dma((lines, 4)), dma((lines, 4)), dma((4,)), dma((lines,)),
         ]
 
     def load(self, i):
@@ -203,23 +203,23 @@
             self.precv.at[i], (self.f + 1 - 2 * self.core, self.s),
         )
 
-    def half(self, ref, h):
-        return ref.at[pl.ds(h * (self.rows // 2), self.rows // 2), :]
+    def part(self, ref, h):
+        return ref.at[pl.ds(h * (self.rows // 4), self.rows // 4), :]
 
     def right(self, d, last, h):
         dst = self.last if last else self.got.at[d]
         sem = self.final.at[h] if last else self.recv.at[d, h]
-        own = self.half(self.own.at[d], h)
-        return remote(own, self.half(dst, h), self.send.at[d, h], sem, (self.f + 2, self.s))
+        own = self.part(self.own.at[d], h)
+        return remote(own, self.part(dst, h), self.send.at[d, h], sem, (self.f + 2, self.s))
 
     def left(self, d, h):
-        own, dst = self.half(self.own.at[d], h), self.half(self.got.at[d], h)
+        own, dst = self.part(self.own.at[d], h), self.part(self.got.at[d], h)
         return remote(own, dst, self.send.at[d, h], self.recv.at[d, h], (self.f - 2, self.s))
 
     def add_got(self, d, h):
-        own, got = self.half(self.own.at[d], h), self.half(self.got.at[d], h)
+        own, got = self.part(self.own.at[d], h), self.part(self.got.at[d], h)
         landed(got, self.recv.at[d, h])
-        add_rows(own, own, got, self.rows // 2)
+        add_rows(own, own, got, self.rows // 4)
 
     def start(self):
         for i in self.order[:2]:
@@ -240,7 +240,7 @@
         place, lines = self.place, self.lines
         d = lines - 1 - t + place
         e = t - (lines - 1 - place)
-        for h in range(2):
+        for h in range(4):
 
             @pl.when(t >= place)
             def _():
@@ -285,13 +285,13 @@
 
         @pl.when(place > 0)
         def _():
-            for h in range(2):
-                landed(self.half(self.last, h), self.final.at[h])
+            for h in range(4):
+                landed(self.part(self.last, h), self.final.at[h])
 
         @pl.when(place < lines - 1)
         def _():
-            for h in range(2):
-                landed(self.half(self.got.at[place], h), self.recv.at[place, h])
+            for h in range(4):
+                landed(self.part(self.got.at[place], h), self.recv.at[place, h])
 
         @pl.when(place == 0)
         def _():
@@ -310,12 +310,12 @@
 
             @pl.when(place < i)
             def _():
-                for h in range(2):
+                for h in range(4):
                     self.right(i, False, h).wait_send()
 
             @pl.when(place > i)
             def _():
-                for h in range(2):
+                for h in range(4):
                     self.left(i, h).wait_send()
 
 

time: 767 us -> 768 us (level)
  no operation moved by 1% of the time
where the time goes in v8:
time: 768 us; the launch traced here: 758 us
  Pallas kernels  710 us (92%)
  local copies, waits for them, and re-layouts  17.4 us (2%)
  between operations  14.6 us (2%)
  other arithmetic  8.45 us (1%)
    pallas_call x1, Pallas kernels, gather_start(): pl.pallas_call(functools.partial(start_kernel, fsdp, sp), out_shape=(jax....  100 us
    pallas_call x1, Pallas kernels, end_exchange(): pl.pallas_call(functools.partial(end_kernel, fsdp, sp), out_shape=(jax.Sh...  96.6 us
    pallas_call x1, Pallas kernels, branch_back(): pl.pallas_call(functools.partial(branch_back_kernel, fsdp, sp), out_shape...  95.6 us
    pallas_call x1, Pallas kernels, token_back(): pl.pallas_call(functools.partial(token_back_kernel, fsdp), out_shape=(jax...  82.3 us
    pallas_call x1, Pallas kernels, token_gather(): pl.pallas_call(functools.partial(token_kernel, fsdp, sp), out_shape=(jax....  79.3 us
    pallas_call x1, Pallas kernels, branch_sum(): pl.pallas_call(functools.partial(branch_kernel, fsdp, sp), out_shape=(jax...  68.2 us
    pallas_call x2, Pallas kernels, weight_grad(): pl.pallas_call(weight_grad_kernel, grid=(EXP_DEV, height // size, width /...  32.1 us
    pallas_call x1, Pallas kernels, active(): pl.pallas_call(active_kernel, grid=(EXP_DEV, 2), out_shape=(low, low, low...  30.3 us
  transfers between devices with their start and end apart: 6, of which 1 were waited for; matrix products, arithmetic and copies ran while one was open for 3% of the time, Pallas kernels for 86%

profile of v8, /device:TPU:12, one launch (start us, length us, event | category | flops | bytes accessed | tf_op | source)
XLA Modules:
  0.0 758.1 jit_solution(10929869332950379292)
XLA Ops:
  7.2 0.7 all-gather.4.cloned.1.call-update
  8.0 0.8 copy-done.1
  8.8 1.5 fusion.14
  10.4 0.7 all-gather.6.cloned.1.call-update
  11.3 0.7 reshape.114.routes_ref
  12.0 0.7 slice.30.g_ref
  12.9 0.6 fusion.13.misc_ref
  13.6 1.0 pad_maximum_fusion.w_ref
  14.5 100.2 %gather_start.1 = (bf16[1024,2048]{1,0:T(8,128)(2,1)}, bf16[3,2048,512]{2,1,0:T(8,128)(2,1)}, bf16[512,2048]{1,0:T(8,128)(2,1)}, bf16[8,32,2048]{2,1,0:T(8,128)(...) custom-call(bf16[256,2048]{1,0:T(8,128)(2,1)} %x_ref.5, bf16[3,64,2048]{2,1,0:T(8,128)(2,1)} %pad_maximum_fusion.w_ref, ...), custom_call_target="tpu_custom_call" | custom-call | tf_op jit(solution)/shard_map/gather_start/pallas_call | solution.py:691
  114.8 1.0 copy.89
  115.9 0.7 reshape.130.gain
  116.6 1.0 slice.32.g_ref
  117.7 0.6 copy.90
  118.3 0.6 eq.63
  118.9 0.3 copy.75
  119.6 0.4 reshape.118
  120.0 0.8 copy.79
  120.8 20.9 %project.1 = (bf16[1024,2048]{1,0:T(8,128)(2,1)}, f32[1024,512]{1,0:T(8,128)}, f32[1024,512]{1,0:T(8,128)}, bf16[1024,512]{1,0:T(8,128)(2,1)}, f32[1024,128]{1,0:T(8,128)}) custom-call(bf16[1024,2048]{1,0:T(8,128)(2,1)} %get-tuple-element.70.x_ref, f32[4,2048]{1,0:T(4,128)} %reshape.130.gain, bf16[3,2048,512]{2,1,0:T(8,128)(2,1)} %get-tuple-element.72.w_ref), custom_call_target="tpu_custom_call" | custom-call | tf_op jit(solution)/shard_map/project/pallas_call | solution.py:1342
  141.7 16.0 %attend.1 = (bf16[1024,512]{1,0:T(8,128)(2,1)}, f32[1024,128]{1,0:T(8,128)}, bf16[1024,512]{1,0:T(8,128)(2,1)}, bf16[1024,512]{1,0:T(8,128)(2,1)}) custom-call(f32[1024,512]{1,0:T(8,128)} %get-tuple-element.73.q_raw, f32[1024,512]{1,0:T(8,128)} %get-tuple-element.74.k_raw, bf16[1024,512]{1,0:T(8,128)(2,1)} %get-tuple-element.75.v_ref, ...), custom_call_target="tpu_custom_call" | custom-call | tf_op jit(solution)/shard_map/attend/pallas_call | solution.py:1388
  157.7 68.2 %branch_sum.1 = (f32[256,2048]{1,0:T(8,128)}, bf16[256,2048]{1,0:T(8,128)(2,1)}, bf16[8,224,2048]{2,1,0:T(8,128)(2,1)}) custom-call(bf16[1024,512]{1,0:T(8,128)(2,1)} %get-tuple-element.77.a_ref.attended, bf16[512,2048]{1,0:T(8,128)(2,1)} %get-tuple-element.78.w_ref.wo_ref, bf16[224,2048]{1,0:T(8,128)(2,1)} %slice.32.g_ref, bf16[256,2048]{1,0:T(8,128)(2,1)} %x_ref.5, ...), custom_call_target="tpu_custom_call" | custom-call | tf_op jit(solution)/shard_map/branch_sum/pallas_call | solution.py:756
  225.9 1.4 fusion.3.picks
  227.3 0.6 compare_convert_fusion.columns
  228.0 79.3 %token_gather.1 = (bf16[8,256,2048]{2,1,0:T(8,128)(2,1)}, bf16[2,1152,2048]{2,1,0:T(8,128)(2,1)}, f32[2,1152,1024]{2,1,0:T(8,128)}, bf16[4096,512]{1,0:T(8,128)(2,1)}) custom-call(bf16[256,2048]{1,0:T(8,128)(2,1)} %get-tuple-element.81.x_ref, bf16[8,32,2048]{2,1,0:T(8,128)(2,1)} %get-tuple-element.82.g_first, ...), custom_call_target="tpu_custom_call" | custom-call | tf_op jit(solution)/shard_map/token_gather/pallas_call | solution.py:865
  307.2 15.0 %route.1 = (bf16[2,1152,2048]{2,1,0:T(8,128)(2,1)}, f32[8,256,16]{2,1,0:T(8,128)}, f32[2,1152,1]{2,1,0:T(8,128)}) custom-call(bf16[8,288,256]{2,1,0:T(8,128)(2,1)} %fusion.3.picks, bf16[8,256,2048]{2,1,0:T(8,128)(2,1)} %get-tuple-element.84.rows_in.tokens, bf16[16,2048]{1,0:T(8,128)(2,1)} %bitcast.47, f32[2,16]{1,0:T(2,128)} %compare_convert_fusion.columns), custom_call_target="tpu_custom_call" | custom-call | tf_op jit(solution)/shard_map/route/pallas_call | solution.py:1621
  322.2 6.1 all-gather.6.cloned.1.call-done.g_ref
  328.3 30.3 %active.1 = (bf16[2,1152,1024]{2,1,0:T(8,128)(2,1)}, bf16[2,1152,1024]{2,1,0:T(8,128)(2,1)}, bf16[2,1152,1024]{2,1,0:T(8,128)(2,1)}, f32[2,1152,1]{2,1,0:T(8,128)}) custom-call(bf16[2,1152,2048]{2,1,0:T(8,128)(2,1)} %get-tuple-element.85.x_ref.a_ref, bf16[2,2048,1024]{2,1,0:T(8,128)(2,1)} %all-gather.6.cloned.1.call-done.g_ref, ...), custom_call_target="tpu_custom_call" | custom-call | tf_op jit(solution)/shard_map/active/pallas_call | solution.py:1681
  358.7 15.6 %down_grad.1 = bf16[2,1024,2048]{2,1,0:T(8,128)(2,1)} custom-call(bf16[2,1152,1024]{2,1,0:T(8,128)(2,1)} %get-tuple-element.94.gated_ref.a_ref, bf16[2,1152,2048]{2,1,0:T(8,128)(2,1)} %get-tuple-element.118.b_ref), custom_call_target="tpu_custom_call" | custom-call | tf_op jit(solution)/shard_map/down_grad/pallas_call | solution.py:1707
  374.4 16.4 %gate_grad.1 = bf16[2,2048,1024]{2,1,0:T(8,128)(2,1)} custom-call(bf16[2,1152,2048]{2,1,0:T(8,128)(2,1)} %get-tuple-element.85.x_ref.a_ref, bf16[2,1152,1024]{2,1,0:T(8,128)(2,1)} %get-tuple-element.89.a_ref.b_ref), custom_call_target="tpu_custom_call" | custom-call | tf_op jit(solution)/shard_map/gate_grad/pallas_call | solution.py:1707
  390.9 0.8 copy-done.4
  391.7 0.7 pad_maximum_fusion.1.router
  392.4 2.6 fusion.1.turned
  395.0 26.8 %rows_back.1.rows_ref = bf16[2,1152,2048]{2,1,0:T(8,128)(2,1)} custom-call(bf16[2,1152,1024]{2,1,0:T(8,128)(2,1)} %get-tuple-element.89.a_ref.b_ref, bf16[2,1152,1024]{2,1,0:T(8,128)(2,1)} %get-tuple-element.90.b_ref.gu_ref, bf16[2,2048,1024]{2,1,0:T(8,128)(2,1)} %all-gather.6.cloned.1.call-done.g_ref, ...), custom_call_target="tpu_custom_call" | custom-call | tf_op jit(solution)/shard_map/rows_back/pallas_call | solution.py:1734
  421.9 1.2 fusion.6.dots
  423.1 16.8 %combine.1 = (bf16[8,256,2048]{2,1,0:T(8,128)(2,1)}, f32[32,2048]{1,0:T(8,128)}) custom-call(bf16[8,2,256,144]{3,2,1,0:T(8,128)(2,1)} %fusion.1.turned, bf16[2,1152,2048]{2,1,0:T(8,128)(2,1)} %rows_back.1.rows_ref, bf16[8,256,2048]{2,1,0:T(8,128)(2,1)} %get-tuple-element.84.rows_in.tokens, f32[8,256,16]{2,1,0:T(8,128)} %get-tuple-element.91.probs, ...), custom_call_target="tpu_custom_call" | custom-call | tf_op jit(solution)/shard_map/combine/pallas_call | solution.py:1775
  439.9 82.3 %token_back.1 = (f32[256,2048]{1,0:T(8,128)}, bf16[256,2048]{1,0:T(8,128)(2,1)}, f32[8,2048]{1,0:T(8,128)}, bf16[8,256,2048]{2,1,0:T(8,128)(2,1)}, bf16[2,2048,1024]{2,1,0:T(8,128)(2,1)}) custom-call(bf16[8,256,2048]{2,1,0:T(8,128)(2,1)} %get-tuple-element.93.p_ref, bf16[2,1152,1024]{2,1,0:T(8,128)(2,1)} %get-tuple-element.94.gated_ref.a_ref, ...), custom_call_target="tpu_custom_call" | custom-call | tf_op jit(solution)/shard_map/token_back/pallas_call | solution.py:1018
  522.2 0.9 copy-done.5
  523.2 0.3 copy.81
  523.5 1.0 reshape.123.router_ref
  524.5 95.6 %branch_back.1 = (bf16[1024,2048]{1,0:T(8,128)(2,1)}, f32[256,2048]{1,0:T(8,128)}, f32[1024,512]{1,0:T(8,128)}, f32[1024,512]{1,0:T(8,128)}, bf16[1024,512]{1,0:...) custom-call(bf16[256,2048]{1,0:T(8,128)(2,1)} %get-tuple-element.95.x_ref, ...), custom_call_target="tpu_custom_call" | custom-call | tf_op jit(solution)/shard_map/branch_back/pallas_call | solution.py:1495
  620.1 19.8 %weight_parts.1 = (bf16[8,1024,512]{2,1,0:T(8,128)(2,1)}, bf16[1024,1536]{1,0:T(8,128)(2,1)}) custom-call(f32[1024,512]{1,0:T(8,128)} %get-tuple-element.101.q_scaled, f32[1024,512]{1,0:T(8,128)} %get-tuple-element.102.k_scaled, f32[1024,512]{1,0:T(8,128)} %get-tuple-element.73.q_raw, f32[1024,512]{1,0:T(8,128)} %get-tuple-element.74.k_raw, ...), custom_call_target="tpu_custom_call" | custom-call | tf_op jit(solution)/shard_map/weight_parts/pallas_call | solution.py:1560
  639.9 0.6 bitcast_dynamic-update-slice_fusion
  640.5 96.6 %end_exchange.1 = (f32[256,2048]{1,0:T(8,128)}, bf16[4,64,512]{2,1,0:T(8,128)(2,1)}, bf16[4,64,512]{2,1,0:T(8,128)(2,1)}, bf16[4,64,512]{2,1,0:T(8,128)(2,1)}, b...) custom-call(bf16[8,1024,512]{2,1,0:T(8,128)(2,1)} %get-tuple-element.107.p_ref, ...), custom_call_target="tpu_custom_call" | custom-call | tf_op jit(solution)/shard_map/end_exchange/pallas_call | solution.py:1231
  737.1 0.7 slice.39
  737.8 0.7 slice.38
  738.5 0.7 copy.82
  739.2 0.6 constant_dynamic-slice_fusion
  739.9 9.9 %widen.1 = (f32[64,2048]{1,0:T(8,128)}, f32[64,2048]{1,0:T(8,128)}, f32[64,2048]{1,0:T(8,128)}, f32[64,2048]{1,0:T(8,128)}, f32[1024,1024]{1,0:T(8,128)}, /*inde...) custom-call(f32[256,2048]{1,0:T(8,128)} %get-tuple-element.79.mid_ref.mid, ...), custom_call_target="tpu_custom_call" | custom-call | tf_op jit(solution)/shard_map/widen/pallas_call | solution.py:1823
  749.8 1.3 copy.93
  (59 shorter events, 1.7 us)
Async XLA Ops:
  7.2 1.6 copy-start.1
  7.2 220.8 %all-gather.4.cloned.1.call-start = ((), (), s32[]{:S(2)}) async-start(), calls=%async_computation.3 | async-start | bytes 10485760 | tf_op jit(solution)/shard_map/all_gather | solution.py:1862
  7.9 314.3 %all-gather.8.cloned.1.call-start = ((), (), s32[]{:S(2)}) async-start(), calls=%async_computation.5 | async-start | bytes 5242880 | tf_op jit(solution)/shard_map/all_gather | solution.py:1865
  10.3 0.9 copy-start.10
  10.3 1.7 copy-start
  10.3 2.4 copy-start.11
  10.3 2.6 copy-start.13
  10.3 3.3 copy-start.6
  10.3 3.3 copy-start.7
  10.3 3.2 copy-start.8
  10.4 318.0 %all-gather.6.cloned.1.call-start = ((), (), s32[]{:S(2)}) async-start(), calls=%async_computation.4 | async-start | bytes 10485760 | tf_op jit(solution)/shard_map/all_gather | solution.py:1863
  11.1 728.8 %reduce-scatter.8.cloned.1.call-start = ((), (), s32[]{:S(2)}) async-start(), calls=%async_computation.8 | async-start | bytes 10485760 | tf_op jit(solution)/shard_map/reduce_scatter | solution.py:1928
  114.7 3.5 copy-start.9
  374.4 365.5 %reduce-scatter.4.cloned.1.call-start = ((), (), s32[]{:S(2)}) async-start(), calls=%async_computation.6 | async-start | bytes 10485760 | tf_op jit(solution)/shard_map/reduce_scatter | solution.py:1928
  390.9 0.8 copy-start.4
  390.9 349.0 %reduce-scatter.6.cloned.1.call-start = ((), (), s32[]{:S(2)}) async-start(), calls=%async_computation.7 | async-start | bytes 10485760 | tf_op jit(solution)/shard_map/reduce_scatter | solution.py:1928
  395.0 26.8 %copy-start.3 = (f32[2,1152,1]{2,1,0:T(8,128)S(1)}, f32[2,1152,1]{2,1,0:T(8,128)}, u32[]{:S(2)}) copy-start(f32[2,1152,1]{2,1,0:T(8,128)} %get-tuple-element.92) | copy-start | bytes 27652
  522.2 1.0 copy-start.5
  620.1 19.8 %copy-start.12 = (f32[2,512]{1,0:T(2,128)S(1)}, f32[2,512]{1,0:T(2,128)}, u32[]{:S(2)}) copy-start(f32[2,512]{1,0:T(2,128)} %get-tuple-element.111) | copy-start | bytes 12292
  739.9 9.9 %copy-start.2 = (f32[256,2048]{1,0:T(8,128)S(1)}, f32[256,2048]{1,0:T(8,128)}, u32[]{:S(2)}) copy-start(f32[256,2048]{1,0:T(8,128)} %get-tuple-element.200) | copy-start | bytes 6291460
Sparse Core Ops, SparseCore 0:
  9.9 130.6 all-gather.3
  143.0 70.5 all-gather.7
  215.4 112.8 all-gather.5
  374.5 86.7 reduce-scatter.7
  464.5 103.1 reduce-scatter.3
  570.6 93.6 reduce-scatter.5
